TPU v7x, 32 devices: a whole 2x2x4 slice. The times are simulated.
32 devices in a mesh: groups: 2 (over x), dom: 16 (over z, y, core).
Axes of the slice: x: 2, y: 2, z: 4, core: 2. Of those that a mesh axis runs over, the one named last changes fastest.
Arguments:
- grid_latent: bfloat16 [32768, 512], P(('groups', 'dom')), parts along dimension 0, may hold values from -6 to 6
- mesh_latent: bfloat16 [16384, 512], P(('groups', 'dom')), parts along dimension 0, may hold values from -6 to 6
- encoder_weight: bfloat16 [512, 512], replicated, may hold values from -0.25 to 0.25
- processor_weights: bfloat16 [2, 512, 512], replicated, may hold values from -0.25 to 0.25
- decoder_weight: bfloat16 [512, 512], replicated, may hold values from -0.25 to 0.25
- cotangent: bfloat16 [32768, 512], P(('groups', 'dom')), parts along dimension 0, may hold values from -6 to 6
- grid_halo_rows: int32 [16, 2, 64], P('dom'), may hold values from 0 to 1023
- encoder_neighbours: int32 [8192, 4], P('dom'), may hold values from 0 to 1151
- halo_rows: int32 [16, 2, 64], P('dom'), may hold values from 0 to 511
- far_sources: int32 [16, 16, 4], P('dom'), may hold values from 0 to 511, as said below
- mesh_neighbours: int32 [8192, 8], P('dom'), may hold values from 0 to 703, as said below
- decoder_neighbours: int32 [16384, 3], P('dom'), may hold values from 0 to 639
Outputs:
- output: bfloat16 [32768, 512], P(('groups', 'dom')), parts along dimension 0
- grid_grad: bfloat16 [32768, 512], P(('groups', 'dom')), parts along dimension 0
- mesh_grad: bfloat16 [16384, 512], P(('groups', 'dom')), parts along dimension 0
There are 2 independent parts, one for each index of `groups`. A program takes and returns all parts, laid end to end along the dimension named above; an argument that names none is the same for every part. Nothing has to cross between parts.
Inputs may be any that keep to these rules, and one draw needn't show every extreme that they name: `far_sources`: slots j at or beyond the number of mesh nodes that p sends to r hold 0; every partition sends at least one mesh node to every partition; in every draw some partition sends 4 to every partition and some partition receives 4 from every partition. `mesh_neighbours`: the first 6 entries of a row are below 640; the last 2 are at least 640 and name only filled slots.
All inputs are finite; a program needn't handle non-finite values.
Results may differ from a plain program's by a relative error of at most 0.012.
Values may be sent and summed in bfloat16 or wider, within the bound.
No kernel may reach another device: no remote copies, remote signals or barrier semaphores. Data moves between devices by JAX's collectives and lax.ppermute only.
A program may use at most 64 MiB of HBM per device.

v0:
```python
import jax
import jax.numpy as jnp
from jax import lax
from jax.sharding import PartitionSpec as P


def padded(shard, sides, width):
    for axis, dim in sides:
        peers, length = (lax.axis_size(axis), shard.shape[dim])
        up = [(i, (i + 1) % peers) for i in range(peers)]
        down = [(j, i) for i, j in up]
        last = lax.slice_in_dim(shard, length - width, length, axis=dim)
        initial = lax.slice_in_dim(shard, 0, width, axis=dim)
        before = lax.ppermute(last, axis, up)
        after = lax.ppermute(initial, axis, down)
        shard = jnp.concatenate([before, shard, after], axis=dim)
    return shard


def silu_grad(value):
    sigma = jax.nn.sigmoid(value)
    return sigma * (1.0 + value * (1.0 - sigma))


def block_sum(targets, values, count):
    block_rows = min(count, 512)
    starts = jnp.arange(count // block_rows, dtype=jnp.int32) * block_rows

    def one_block(start):
        wanted = start + jnp.arange(block_rows, dtype=jnp.int32)
        onehot = (wanted[:, None] == targets[None, :]).astype(values.dtype)
        return jnp.dot(
            onehot, values, preferred_element_type=jnp.float32, precision=lax.Precision.HIGHEST
        )

    return lax.map(one_block, starts).reshape(count, values.shape[1])


def edge_counts(entries, columns):
    wanted = jnp.arange(columns, dtype=jnp.int32)
    return jnp.sum((entries[:, :, None] == wanted[None, None, :]).astype(jnp.int32), axis=1).astype(
        jnp.bfloat16
    )


def rim_pair(arrived):
    return jnp.concatenate([arrived[0], arrived[3]], axis=0)


def spread_back(counts, values):
    return lax.dot_general(
        counts, values, (((0,), (0,)), ((), ())), preferred_element_type=jnp.float32
    )


def on_device(
    grid_latent,
    mesh_latent,
    encoder_weight,
    processor_weights,
    decoder_weight,
    cotangent,
    grid_halo_rows,
    encoder_neighbours,
    halo_rows,
    far_sources,
    mesh_neighbours,
    decoder_neighbours,
):
    devices = lax.axis_size("dom")
    grid_rows, feature_width = grid_latent.shape
    mesh_rows = mesh_latent.shape[0]
    grid_rim_size = grid_halo_rows.shape[2]
    mesh_rim_size = halo_rows.shape[2]
    far_slots = far_sources.shape[2]
    degree = mesh_neighbours.shape[1]
    layer_count = processor_weights.shape[0]
    inverse_degree = 1.0 / degree
    grid_lists = grid_halo_rows[0].reshape(-1)
    rim_lists = halo_rows[0].reshape(-1)
    far_lists = far_sources[0].reshape(-1)
    near_columns = mesh_rows + 2 * mesh_rim_size
    pre_encoder = jnp.dot(grid_latent, encoder_weight, preferred_element_type=jnp.float32)
    grid_message = jax.nn.silu(pre_encoder).astype(jnp.bfloat16)
    grid_out = jnp.take(grid_message, grid_lists, axis=0).reshape(2, grid_rim_size, feature_width)
    grid_in = padded(grid_out, (("dom", 0),), 1)
    encoder_counts = edge_counts(encoder_neighbours, grid_rows + 2 * grid_rim_size)
    grid_extended = jnp.concatenate([grid_message, rim_pair(grid_in)], axis=0)
    encoder_sum = jnp.dot(encoder_counts, grid_extended, preferred_element_type=jnp.float32)
    hidden = (mesh_latent.astype(jnp.float32) + encoder_sum).astype(jnp.bfloat16)
    mesh_counts = edge_counts(mesh_neighbours, near_columns + devices * far_slots)
    pre_layers = []
    for layer in range(layer_count):
        weight = processor_weights[layer]
        pre_layer = jnp.dot(hidden, weight, preferred_element_type=jnp.float32)
        message = jax.nn.silu(pre_layer).astype(jnp.bfloat16)
        rim_out = jnp.take(message, rim_lists, axis=0).reshape(2, mesh_rim_size, feature_width)
        far_out = jnp.take(message, far_lists, axis=0).reshape(devices, far_slots, feature_width)
        rim_in = padded(rim_out, (("dom", 0),), 1)
        far_in = lax.all_to_all(far_out, "dom", split_axis=0, concat_axis=0, tiled=True)
        remote = jnp.concatenate([rim_pair(rim_in), far_in.reshape(-1, feature_width)], axis=0)
        extended = jnp.concatenate([message, remote], axis=0)
        gathered = jnp.dot(mesh_counts, extended, preferred_element_type=jnp.float32)
        hidden = (hidden.astype(jnp.float32) + gathered * inverse_degree).astype(jnp.bfloat16)
        pre_layers.append(pre_layer)
    pre_decoder = jnp.dot(hidden, decoder_weight, preferred_element_type=jnp.float32)
    decoder_message = jax.nn.silu(pre_decoder).astype(jnp.bfloat16)
    decoder_out = jnp.take(decoder_message, rim_lists, axis=0).reshape(
        2, mesh_rim_size, feature_width
    )
    decoder_in = padded(decoder_out, (("dom", 0),), 1)
    decoder_counts = edge_counts(decoder_neighbours, near_columns)
    mesh_extended = jnp.concatenate([decoder_message, rim_pair(decoder_in)], axis=0)
    decoder_sum = jnp.dot(decoder_counts, mesh_extended, preferred_element_type=jnp.float32)
    output = (grid_latent.astype(jnp.float32) + decoder_sum).astype(jnp.bfloat16)
    decoder_spread = spread_back(decoder_counts, cotangent)
    decoder_returning = jnp.stack(
        [
            decoder_spread[mesh_rows : mesh_rows + mesh_rim_size],
            decoder_spread[mesh_rows + mesh_rim_size :],
        ]
    )
    decoder_returned = padded(decoder_returning, (("dom", 0),), 1)
    back_decoder = decoder_spread[:mesh_rows] + block_sum(
        rim_lists, rim_pair(decoder_returned), mesh_rows
    )
    decoder_grad = (back_decoder * silu_grad(pre_decoder)).astype(jnp.bfloat16)
    mesh_grad = jnp.dot(decoder_grad, decoder_weight.T, preferred_element_type=jnp.float32).astype(
        jnp.bfloat16
    )
    for layer in reversed(range(layer_count)):
        spread = spread_back(mesh_counts, mesh_grad)
        returning = jnp.stack(
            [
                spread[mesh_rows : mesh_rows + mesh_rim_size],
                spread[mesh_rows + mesh_rim_size : near_columns],
            ]
        )
        returned = padded(returning, (("dom", 0),), 1)
        far_returning = spread[near_columns:].reshape(devices, far_slots, feature_width)
        far_returned = lax.all_to_all(far_returning, "dom", split_axis=0, concat_axis=0, tiled=True)
        message_grad = spread[:mesh_rows] + block_sum(rim_lists, rim_pair(returned), mesh_rows)
        message_grad = (
            message_grad + block_sum(far_lists, far_returned.reshape(-1, feature_width), mesh_rows)
        ) * inverse_degree
        layer_grad = (message_grad * silu_grad(pre_layers[layer])).astype(jnp.bfloat16)
        mesh_grad = (
            mesh_grad.astype(jnp.float32)
            + jnp.dot(layer_grad, processor_weights[layer].T, preferred_element_type=jnp.float32)
        ).astype(jnp.bfloat16)
    encoder_spread = spread_back(encoder_counts, mesh_grad)
    grid_returning = jnp.stack(
        [
            encoder_spread[grid_rows : grid_rows + grid_rim_size],
            encoder_spread[grid_rows + grid_rim_size :],
        ]
    )
    grid_returned = padded(grid_returning, (("dom", 0),), 1)
    back_encoder = encoder_spread[:grid_rows] + block_sum(
        grid_lists, rim_pair(grid_returned), grid_rows
    )
    encoder_grad = (back_encoder * silu_grad(pre_encoder)).astype(jnp.bfloat16)
    grid_grad = (
        cotangent.astype(jnp.float32)
        + jnp.dot(encoder_grad, encoder_weight.T, preferred_element_type=jnp.float32)
    ).astype(jnp.bfloat16)
    return (output, grid_grad, mesh_grad)


def solution(mesh):
    in_specs = (
        P(("groups", "dom"), None),
        P(("groups", "dom"), None),
        P(),
        P(),
        P(),
        P(("groups", "dom"), None),
        P("dom", None, None),
        P("dom", None),
        P("dom", None, None),
        P("dom", None, None),
        P("dom", None),
        P("dom", None),
    )
    out_specs = (P(("groups", "dom"), None), P(("groups", "dom"), None), P(("groups", "dom"), None))
    return jax.shard_map(
        on_device, mesh=mesh, in_specs=in_specs, out_specs=out_specs, check_vma=False
    )
```

profile of v0, /device:TPU:0, one launch (start us, length us, event | category | flops | bytes accessed | tf_op | source)
XLA Modules:
  0.0 147.2 jit_solution(15216381831461072137)
XLA Ops:
  2.3 3.5 %multiply_convert_fusion = (bf16[1024,512]{1,0:T(8,128)(2,1)S(1)}, f32[1024,512]{1,0:T(8,128)}) fusion(bf16[1024,512]{1,0:T(8,128)(2,1)} %param.18, bf16[512,512]{1,0:T(8,128)(2,1)S(1)} %copy-done), kind=kOutput, calls=%fused_computation.23 | convolution fusion | flops 539492352 | bytes 4718592 | tf_op jit(solution)/shard_map/dot_general | solution.py:83
  6.8 5.5 %collective-permute-start.1 = (bf16[1,64,512]{2,1,0:T(8,128)(2,1)S(1)}, bf16[1,64,512]{2,1,0:T(8,128)(2,1)S(1)}, u32[]{:S(2)}, u32[]{:S(2)}) collective-permute-start(bf16[1,64,512]{2,1,0:T(8,128)(2,1)S(1)} %get-tuple-element.120), channel_id=1, source_target_pairs={{1,0},{2,1},{3,2},{4,3},{5,4},{6,5},{7,6},{8,7},{9,8},{10,9},{11,1... | collective-permute-start | bytes 196616 | tf_op jit(solution)/shard_map/ppermute | solution.py:15
  24.1 4.4 %all-to-all-start = ((bf16[16,4,512]{2,1,0:T(4,128)(2,1)}), bf16[16,4,512]{2,1,0:T(4,128)(2,1)S(1)}, u32[]{:S(2)}, u32[]{:S(2)}) async-start(bf16[16,4,512]{2,1,0:T(4,128)(2,1)} %reshape.110), calls=%async_computation | async-start | bytes 131072 | tf_op jit(solution)/shard_map/all_to_all | solution.py:100
  30.7 4.4 %collective-permute-start.3 = (bf16[1,64,512]{2,1,0:T(8,128)(2,1)S(1)}, bf16[1,64,512]{2,1,0:T(8,128)(2,1)S(1)}, u32[]{:S(2)}, u32[]{:S(2)}) collective-permute-start(bf16[1,64,512]{2,1,0:T(8,128)(2,1)S(1)} %get-tuple-element.118), channel_id=1, source_target_pairs={{1,0},{2,1},{3,2},{4,3},{5,4},{6,5},{7,6},{8,7},{9,8},{10,9},{11,1... | collective-permute-start | bytes 196616 | tf_op jit(solution)/shard_map/ppermute | solution.py:15
  37.8 3.8 %collective-permute-done.2 = bf16[1,64,512]{2,1,0:T(8,128)(2,1)} collective-permute-done((bf16[1,64,512]{2,1,0:T(8,128)(2,1)S(1)}, bf16[1,64,512]{2,1,0:T(8,128)(2,1)}, u32[]{:S(2)}, u32[]{:S(2)}) %collective-permute-start.2) | collective-permute-done | bytes 65568 | tf_op jit(solution)/shard_map/ppermute | solution.py:14
  50.0 3.5 %all-to-all-start.1 = ((bf16[16,4,512]{2,1,0:T(4,128)(2,1)}), bf16[16,4,512]{2,1,0:T(4,128)(2,1)S(1)}, u32[]{:S(2)}, u32[]{:S(2)}) async-start(bf16[16,4,512]{2,1,0:T(4,128)(2,1)} %reshape.112), calls=%async_computation.1 | async-start | bytes 131072 | tf_op jit(solution)/shard_map/all_to_all | solution.py:100
  54.3 4.3 %collective-permute-start.5 = (bf16[1,64,512]{2,1,0:T(8,128)(2,1)}, bf16[1,64,512]{2,1,0:T(8,128)(2,1)}, u32[]{:S(2)}, u32[]{:S(2)}) collective-permute-start(bf16[1,64,512]{2,1,0:T(8,128)(2,1)} %get-tuple-element.116), channel_id=1, source_target_pairs={{1,0},{2,1},{3,2},{4,3},{5,4},{6,5},{7,6},{8,7},{9,8},{10,9},{11,1... | collective-permute-start | bytes 196616 | tf_op jit(solution)/shard_map/ppermute | solution.py:15
  59.6 4.5 %collective-permute-start.9 = (f32[1,64,512]{2,1,0:T(8,128)S(1)}, f32[1,64,512]{2,1,0:T(8,128)}, u32[]{:S(2)}, u32[]{:S(2)}) collective-permute-start(f32[1,64,512]{2,1,0:T(8,128)S(1)} %get-tuple-element.112), channel_id=1, source_target_pairs={{1,0},{2,1},{3,2},{4,3},{5,4},{6,5},{7,6},{8,7},{9,8},{10,9},{11,1... | collective-permute-start | bytes 393224 | tf_op jit(solution)/shard_map/ppermute | solution.py:15
  65.3 3.7 %multiply_convert_fusion.1 = (bf16[512,512]{1,0:T(8,128)(2,1)}, f32[512,512]{1,0:T(8,128)}) fusion(bf16[512,512]{1,0:T(8,128)(2,1)} %param.22, bf16[512,704]{0,1:T(8,128)(2,1)} %convert_element_type.108, bf16[512,512]{1,0:T(8,128)(2,1)} %copy-done.35, bf16[64,512]{1,0:T(8,128)(2,1)S(1)} %reshape.113, bf16[64,512]{1,0:T(8,128)(2,1)} %bitcast.16, ...), kind=kOutput, calls=%fused_computation.57 | convolution fusion | flops 642777088 | bytes 4063232 | tf_op jit(solution)/shard_map/dot_general | solution.py:106
  69.0 2.2 %collective-permute-done.8 = f32[1,64,512]{2,1,0:T(8,128)} collective-permute-done((f32[1,64,512]{2,1,0:T(8,128)S(1)}, f32[1,64,512]{2,1,0:T(8,128)}, u32[]{:S(2)}, u32[]{:S(2)}) %collective-permute-start.8) | collective-permute-done | bytes 131104 | tf_op jit(solution)/shard_map/ppermute | solution.py:14
  71.3 2.6 %fusion.16 = bf16[512,512]{1,0:T(8,128)(2,1)S(1)} fusion(f32[640,512]{1,0:T(8,128)} %fusion.56, f32[512,512]{1,0:T(8,128)} %get-tuple-element.128, f32[64,512]{1,0:T(8,128)} %bitcast.24, f32[64,512]{1,0:T(8,128)} %bitcast.22, s32[128]{0:T(128)S(1)} %reshape_squeeze.13), kind=kOutput, calls=%fused_computation.44 | convolution fusion | flops 405405696 | bytes 2884096 | tf_op jit(solution)/shard_map/while/body/eval_jaxpr/dot_general | solution.py:32
  77.6 3.5 %all-to-all-start.2 = ((f32[16,4,512]{2,1,0:T(4,128)}), f32[16,4,512]{2,1,0:T(4,128)S(1)}, u32[]{:S(2)}, u32[]{:S(2)}) async-start(f32[16,4,512]{2,1,0:T(4,128)} %reshape.114), calls=%async_computation.2 | async-start | bytes 262144 | tf_op jit(solution)/shard_map/all_to_all | solution.py:141
  83.7 4.4 %collective-permute-start.11 = (f32[1,64,512]{2,1,0:T(8,128)}, f32[1,64,512]{2,1,0:T(8,128)}, u32[]{:S(2)}, u32[]{:S(2)}) collective-permute-start(f32[1,64,512]{2,1,0:T(8,128)} %get-tuple-element.110), channel_id=1, source_target_pairs={{1,0},{2,1},{3,2},{4,3},{5,4},{6,5},{7,6},{8,7},{9,8},{10,9},{11,1... | collective-permute-start | bytes 393224 | tf_op jit(solution)/shard_map/ppermute | solution.py:15
  90.9 4.6 %collective-permute-done.10 = f32[1,64,512]{2,1,0:T(8,128)} collective-permute-done((f32[1,64,512]{2,1,0:T(8,128)}, f32[1,64,512]{2,1,0:T(8,128)}, u32[]{:S(2)}, u32[]{:S(2)}) %collective-permute-start.10) | collective-permute-done | bytes 131104 | tf_op jit(solution)/shard_map/ppermute | solution.py:14
  95.5 2.7 %fusion.17 = bf16[512,512]{1,0:T(8,128)(2,1)S(1)} fusion(f32[512,512]{1,0:T(8,128)S(1)} %fusion.83, f32[704,512]{1,0:T(8,128)} %copy-done.8, f32[512,512]{1,0:T(8,128)} %get-tuple-element.126, f32[64,512]{1,0:T(8,128)} %bitcast.28, f32[64,512]{1,0:T(8,128)} %bitcast.26, s32[128]{0:T(128)} %copy-done.31), kind=kOutput, calls=%fused_computation.45 | convolution fusion | flops 405929984 | bytes 3932672 | tf_op jit(solution)/shard_map/while/body/eval_jaxpr/dot_general | solution.py:32
  102.4 3.5 %all-to-all-start.3 = ((f32[16,4,512]{2,1,0:T(4,128)}), f32[16,4,512]{2,1,0:T(4,128)S(1)}, u32[]{:S(2)}, u32[]{:S(2)}) async-start(f32[16,4,512]{2,1,0:T(4,128)} %reshape.116), calls=%async_computation.3 | async-start | bytes 262144 | tf_op jit(solution)/shard_map/all_to_all | solution.py:141
  106.7 4.3 %collective-permute-start.7 = (bf16[1,64,512]{2,1,0:T(8,128)(2,1)}, bf16[1,64,512]{2,1,0:T(8,128)(2,1)}, u32[]{:S(2)}, u32[]{:S(2)}) collective-permute-start(bf16[1,64,512]{2,1,0:T(8,128)(2,1)} %get-tuple-element.114), channel_id=1, source_target_pairs={{1,0},{2,1},{3,2},{4,3},{5,4},{6,5},{7,6},{8,7},{9,8},{10,9},{11,1... | collective-permute-start | bytes 196616 | tf_op jit(solution)/shard_map/ppermute | solution.py:15
  111.1 4.4 %collective-permute-start.13 = (f32[1,64,512]{2,1,0:T(8,128)}, f32[1,64,512]{2,1,0:T(8,128)}, u32[]{:S(2)}, u32[]{:S(2)}) collective-permute-start(f32[1,64,512]{2,1,0:T(8,128)} %get-tuple-element.107), channel_id=1, source_target_pairs={{1,0},{2,1},{3,2},{4,3},{5,4},{6,5},{7,6},{8,7},{9,8},{10,9},{11,1... | collective-permute-start | bytes 393224 | tf_op jit(solution)/shard_map/ppermute | solution.py:15
  118.4 4.4 %collective-permute-done.12 = f32[1,64,512]{2,1,0:T(8,128)} collective-permute-done((f32[1,64,512]{2,1,0:T(8,128)S(1)}, f32[1,64,512]{2,1,0:T(8,128)}, u32[]{:S(2)}, u32[]{:S(2)}) %collective-permute-start.12) | collective-permute-done | bytes 131104 | tf_op jit(solution)/shard_map/ppermute | solution.py:14
  122.7 2.7 %fusion.18 = bf16[512,512]{1,0:T(8,128)(2,1)S(1)} fusion(f32[512,512]{1,0:T(8,128)S(1)} %fusion.82, f32[704,512]{1,0:T(8,128)} %copy-done.7, f32[512,512]{1,0:T(8,128)} %get-tuple-element.124, f32[64,512]{1,0:T(8,128)} %bitcast.32, f32[64,512]{1,0:T(8,128)} %bitcast.30, s32[128]{0:T(128)S(1)} %copy-done.32), kind=kOutput, calls=%fused_computation.46 | convolution fusion | flops 405929984 | bytes 3932672 | tf_op jit(solution)/shard_map/while/body/eval_jaxpr/dot_general | solution.py:32
  128.9 2.8 %add_convert_fusion.1 = bf16[1024,512]{1,0:T(8,128)(2,1)} fusion(bf16[1024,512]{1,0:T(8,128)(2,1)S(1)} %copy-done.15, bf16[64,512]{1,0:T(8,128)(2,1)} %bitcast.20, bf16[64,512]{1,0:T(8,128)(2,1)} %bitcast.18, bf16[512,512]{1,0:T(8,128)(2,1)S(1)} %copy-done.6, s32[1024,640]{1,0:T(8,128)S(1)} %convert_reduce_fusion.2), kind=kOutput, calls=%fused_computation.22 | convolution fusion | flops 675282944 | bytes 5373952 | tf_op jit(solution)/shard_map/dot_general | solution.py:114
  131.7 3.9 %collective-permute-done.14 = f32[1,64,512]{2,1,0:T(8,128)S(1)} collective-permute-done((f32[1,64,512]{2,1,0:T(8,128)S(1)}, f32[1,64,512]{2,1,0:T(8,128)S(1)}, u32[]{:S(2)}, u32[]{:S(2)}) %collective-permute-start.14) | collective-permute-done | bytes 131104 | tf_op jit(solution)/shard_map/ppermute | solution.py:14
  135.7 5.8 %while.3 = (s32[]{:T(128)}, f32[2,512,512]{2,1,0:T(8,128)}, s32[2]{0:T(128)S(1)}, s32[1,2,64]{2,1,0:T(2,128)}, f32[128,512]{1,0:T(8,128)S(1)}, /*index=5*/s32[128]{0:T(128)S(1)}, s32[]{:T(128)}) while((s32[]{:T(128)}, f32[2,512,512]{2,1,0:T(8,128)}, s32[2]{0:T(128)S(1)}, s32[1,2,64]{2,1,0:T(2,128)}, f32[128,512]{1,0:T(8,128)S(1)}, ...), condition=%wide.wide.region_4.7_spmd, body=%wide.wide.region_3.6_spmd.sunk | while | flops 402719232 | bytes 1315433 | solution.py:36
  141.4 4.0 %fusion.5 = bf16[1024,512]{1,0:T(8,128)(2,1)S(1)} fusion(f32[1152,512]{1,0:T(8,128)} %copy-done.1, f32[2,512,512]{2,1,0:T(8,128)} %get-tuple-element.82, f32[1024,512]{1,0:T(8,128)} %get-tuple-element.122), kind=kLoop, calls=%fused_computation.20 | loop fusion | flops 5242880 | bytes 7340032 | tf_op jit(solution)/shard_map/convert_element_type | solution.py:162
  (166 shorter events, 58.0 us)
Async XLA Ops:
  2.3 10.3 %copy-start.22 = (s32[512,4]{0,1:T(4,128)S(1)}, s32[512,4]{0,1:T(4,128)}, u32[]{:S(2)}) copy-start(s32[512,4]{0,1:T(4,128)} %param.25) | copy-start | bytes 24580
  6.8 10.5 %collective-permute-start.1 = (bf16[1,64,512]{2,1,0:T(8,128)(2,1)S(1)}, bf16[1,64,512]{2,1,0:T(8,128)(2,1)S(1)}, u32[]{:S(2)}, u32[]{:S(2)}) collective-permute-start(bf16[1,64,512]{2,1,0:T(8,128)(2,1)S(1)} %get-tuple-element.120), channel_id=1, source_target_pairs={{1,0},{2,1},{3,2},{4,3},{5,4},{6,5},{7,6},{8,7},{9,8},{10,9},{11,1... | collective-permute-start | bytes 196616 | tf_op jit(solution)/shard_map/ppermute | solution.py:15
  12.3 6.4 %collective-permute-start = (bf16[1,64,512]{2,1,0:T(8,128)(2,1)S(1)}, bf16[1,64,512]{2,1,0:T(8,128)(2,1)S(1)}, u32[]{:S(2)}, u32[]{:S(2)}) collective-permute-start(bf16[1,64,512]{2,1,0:T(8,128)(2,1)S(1)} %get-tuple-element.119), channel_id=1, source_target_pairs={{0,1},{1,2},{2,3},{3,4},{4,5},{5,6},{6,7},{7,8},{8,9},{9,10},{10,1... | collective-permute-start | bytes 196616 | tf_op jit(solution)/shard_map/ppermute | solution.py:14
  12.6 58.7 %copy-start.31 = (s32[128]{0:T(128)}, s32[128]{0:T(128)S(1)}, u32[]{:S(2)}) copy-start(s32[128]{0:T(128)S(1)} %reshape_squeeze.13) | copy-start | bytes 1540
  21.6 13.5 %copy-start.21 = (s32[512,8]{0,1:T(8,128)S(1)}, s32[512,8]{0,1:T(8,128)}, u32[]{:S(2)}) copy-start(s32[512,8]{0,1:T(8,128)} %param.28) | copy-start | bytes 49156
  24.1 13.6 %all-to-all-start = ((bf16[16,4,512]{2,1,0:T(4,128)(2,1)}), bf16[16,4,512]{2,1,0:T(4,128)(2,1)S(1)}, u32[]{:S(2)}, u32[]{:S(2)}) async-start(bf16[16,4,512]{2,1,0:T(4,128)(2,1)} %reshape.110), calls=%async_computation | async-start | bytes 131072 | tf_op jit(solution)/shard_map/all_to_all | solution.py:100
  30.7 7.1 %collective-permute-start.3 = (bf16[1,64,512]{2,1,0:T(8,128)(2,1)S(1)}, bf16[1,64,512]{2,1,0:T(8,128)(2,1)S(1)}, u32[]{:S(2)}, u32[]{:S(2)}) collective-permute-start(bf16[1,64,512]{2,1,0:T(8,128)(2,1)S(1)} %get-tuple-element.118), channel_id=1, source_target_pairs={{1,0},{2,1},{3,2},{4,3},{5,4},{6,5},{7,6},{8,7},{9,8},{10,9},{11,1... | collective-permute-start | bytes 196616 | tf_op jit(solution)/shard_map/ppermute | solution.py:15
  35.1 6.5 %collective-permute-start.2 = (bf16[1,64,512]{2,1,0:T(8,128)(2,1)S(1)}, bf16[1,64,512]{2,1,0:T(8,128)(2,1)}, u32[]{:S(2)}, u32[]{:S(2)}) collective-permute-start(bf16[1,64,512]{2,1,0:T(8,128)(2,1)S(1)} %get-tuple-element.117), channel_id=1, source_target_pairs={{0,1},{1,2},{2,3},{3,4},{4,5},{5,6},{6,7},{7,8},{8,9},{9,10},{10,1... | collective-permute-start | bytes 196616 | tf_op jit(solution)/shard_map/ppermute | solution.py:14
  50.0 14.1 %all-to-all-start.1 = ((bf16[16,4,512]{2,1,0:T(4,128)(2,1)}), bf16[16,4,512]{2,1,0:T(4,128)(2,1)S(1)}, u32[]{:S(2)}, u32[]{:S(2)}) async-start(bf16[16,4,512]{2,1,0:T(4,128)(2,1)} %reshape.112), calls=%async_computation.1 | async-start | bytes 131072 | tf_op jit(solution)/shard_map/all_to_all | solution.py:100
  54.3 9.9 %collective-permute-start.5 = (bf16[1,64,512]{2,1,0:T(8,128)(2,1)}, bf16[1,64,512]{2,1,0:T(8,128)(2,1)}, u32[]{:S(2)}, u32[]{:S(2)}) collective-permute-start(bf16[1,64,512]{2,1,0:T(8,128)(2,1)} %get-tuple-element.116), channel_id=1, source_target_pairs={{1,0},{2,1},{3,2},{4,3},{5,4},{6,5},{7,6},{8,7},{9,8},{10,9},{11,1... | collective-permute-start | bytes 196616 | tf_op jit(solution)/shard_map/ppermute | solution.py:15
  58.6 6.7 %collective-permute-start.4 = (bf16[1,64,512]{2,1,0:T(8,128)(2,1)}, bf16[1,64,512]{2,1,0:T(8,128)(2,1)}, u32[]{:S(2)}, u32[]{:S(2)}) collective-permute-start(bf16[1,64,512]{2,1,0:T(8,128)(2,1)} %get-tuple-element.115), channel_id=1, source_target_pairs={{0,1},{1,2},{2,3},{3,4},{4,5},{5,6},{6,7},{7,8},{8,9},{9,10},{10,1... | collective-permute-start | bytes 196616 | tf_op jit(solution)/shard_map/ppermute | solution.py:14
  59.6 9.4 %collective-permute-start.9 = (f32[1,64,512]{2,1,0:T(8,128)S(1)}, f32[1,64,512]{2,1,0:T(8,128)}, u32[]{:S(2)}, u32[]{:S(2)}) collective-permute-start(f32[1,64,512]{2,1,0:T(8,128)S(1)} %get-tuple-element.112), channel_id=1, source_target_pairs={{1,0},{2,1},{3,2},{4,3},{5,4},{6,5},{7,6},{8,7},{9,8},{10,9},{11,1... | collective-permute-start | bytes 393224 | tf_op jit(solution)/shard_map/ppermute | solution.py:15
  64.1 7.2 %collective-permute-start.8 = (f32[1,64,512]{2,1,0:T(8,128)S(1)}, f32[1,64,512]{2,1,0:T(8,128)}, u32[]{:S(2)}, u32[]{:S(2)}) collective-permute-start(f32[1,64,512]{2,1,0:T(8,128)S(1)} %get-tuple-element.111), channel_id=1, source_target_pairs={{0,1},{1,2},{2,3},{3,4},{4,5},{5,6},{6,7},{7,8},{8,9},{9,10},{10,1... | collective-permute-start | bytes 393224 | tf_op jit(solution)/shard_map/ppermute | solution.py:14
  77.6 11.4 %all-to-all-start.2 = ((f32[16,4,512]{2,1,0:T(4,128)}), f32[16,4,512]{2,1,0:T(4,128)S(1)}, u32[]{:S(2)}, u32[]{:S(2)}) async-start(f32[16,4,512]{2,1,0:T(4,128)} %reshape.114), calls=%async_computation.2 | async-start | bytes 262144 | tf_op jit(solution)/shard_map/all_to_all | solution.py:141
  83.7 7.2 %collective-permute-start.11 = (f32[1,64,512]{2,1,0:T(8,128)}, f32[1,64,512]{2,1,0:T(8,128)}, u32[]{:S(2)}, u32[]{:S(2)}) collective-permute-start(f32[1,64,512]{2,1,0:T(8,128)} %get-tuple-element.110), channel_id=1, source_target_pairs={{1,0},{2,1},{3,2},{4,3},{5,4},{6,5},{7,6},{8,7},{9,8},{10,9},{11,1... | collective-permute-start | bytes 393224 | tf_op jit(solution)/shard_map/ppermute | solution.py:15
  88.1 7.4 %collective-permute-start.10 = (f32[1,64,512]{2,1,0:T(8,128)}, f32[1,64,512]{2,1,0:T(8,128)}, u32[]{:S(2)}, u32[]{:S(2)}) collective-permute-start(f32[1,64,512]{2,1,0:T(8,128)} %get-tuple-element.108), channel_id=1, source_target_pairs={{0,1},{1,2},{2,3},{3,4},{4,5},{5,6},{6,7},{7,8},{8,9},{9,10},{10,1... | collective-permute-start | bytes 393224 | tf_op jit(solution)/shard_map/ppermute | solution.py:14
  101.1 21.6 %copy-start.32 = (s32[128]{0:T(128)S(1)}, s32[128]{0:T(128)}, u32[]{:S(2)}) copy-start(s32[128]{0:T(128)} %copy-done.31) | copy-start | bytes 1540
  102.4 13.1 %all-to-all-start.3 = ((f32[16,4,512]{2,1,0:T(4,128)}), f32[16,4,512]{2,1,0:T(4,128)S(1)}, u32[]{:S(2)}, u32[]{:S(2)}) async-start(f32[16,4,512]{2,1,0:T(4,128)} %reshape.116), calls=%async_computation.3 | async-start | bytes 262144 | tf_op jit(solution)/shard_map/all_to_all | solution.py:141
  106.7 22.1 %collective-permute-start.7 = (bf16[1,64,512]{2,1,0:T(8,128)(2,1)}, bf16[1,64,512]{2,1,0:T(8,128)(2,1)}, u32[]{:S(2)}, u32[]{:S(2)}) collective-permute-start(bf16[1,64,512]{2,1,0:T(8,128)(2,1)} %get-tuple-element.114), channel_id=1, source_target_pairs={{1,0},{2,1},{3,2},{4,3},{5,4},{6,5},{7,6},{8,7},{9,8},{10,9},{11,1... | collective-permute-start | bytes 196616 | tf_op jit(solution)/shard_map/ppermute | solution.py:15
  111.1 17.8 %collective-permute-start.6 = (bf16[1,64,512]{2,1,0:T(8,128)(2,1)}, bf16[1,64,512]{2,1,0:T(8,128)(2,1)}, u32[]{:S(2)}, u32[]{:S(2)}) collective-permute-start(bf16[1,64,512]{2,1,0:T(8,128)(2,1)} %get-tuple-element.113), channel_id=1, source_target_pairs={{0,1},{1,2},{2,3},{3,4},{4,5},{5,6},{6,7},{7,8},{8,9},{9,10},{10,1... | collective-permute-start | bytes 196616 | tf_op jit(solution)/shard_map/ppermute | solution.py:14
  111.1 7.3 %collective-permute-start.13 = (f32[1,64,512]{2,1,0:T(8,128)}, f32[1,64,512]{2,1,0:T(8,128)}, u32[]{:S(2)}, u32[]{:S(2)}) collective-permute-start(f32[1,64,512]{2,1,0:T(8,128)} %get-tuple-element.107), channel_id=1, source_target_pairs={{1,0},{2,1},{3,2},{4,3},{5,4},{6,5},{7,6},{8,7},{9,8},{10,9},{11,1... | collective-permute-start | bytes 393224 | tf_op jit(solution)/shard_map/ppermute | solution.py:15
  115.5 7.2 %collective-permute-start.12 = (f32[1,64,512]{2,1,0:T(8,128)S(1)}, f32[1,64,512]{2,1,0:T(8,128)}, u32[]{:S(2)}, u32[]{:S(2)}) collective-permute-start(f32[1,64,512]{2,1,0:T(8,128)S(1)} %get-tuple-element.105), channel_id=1, source_target_pairs={{0,1},{1,2},{2,3},{3,4},{4,5},{5,6},{6,7},{7,8},{8,9},{9,10},{10,1... | collective-permute-start | bytes 393224 | tf_op jit(solution)/shard_map/ppermute | solution.py:14
  128.3 3.4 %collective-permute-start.15 = (f32[1,64,512]{2,1,0:T(8,128)S(1)}, f32[1,64,512]{2,1,0:T(8,128)S(1)}, u32[]{:S(2)}, u32[]{:S(2)}) collective-permute-start(f32[1,64,512]{2,1,0:T(8,128)S(1)} %get-tuple-element.104), channel_id=1, source_target_pairs={{1,0},{2,1},{3,2},{4,3},{5,4},{6,5},{7,6},{8,7},{9,8},{10,9},{11,1... | collective-permute-start | bytes 393224 | tf_op jit(solution)/shard_map/ppermute | solution.py:15
  128.6 7.1 %collective-permute-start.14 = (f32[1,64,512]{2,1,0:T(8,128)S(1)}, f32[1,64,512]{2,1,0:T(8,128)S(1)}, u32[]{:S(2)}, u32[]{:S(2)}) collective-permute-start(f32[1,64,512]{2,1,0:T(8,128)S(1)} %get-tuple-element.103), channel_id=1, source_target_pairs={{0,1},{1,2},{2,3},{3,4},{4,5},{5,6},{6,7},{7,8},{8,9},{9,10},{10,1... | collective-permute-start | bytes 393224 | tf_op jit(solution)/shard_map/ppermute | solution.py:14
  (32 other events, 113.1 us)
where the time goes:
time: 148 us; the launch traced here: 147 us
  starting transfers between devices  47.5 us (32%)
  matrix products  35.8 us (24%)
  waiting for transfers between devices  25.9 us (18%)
  local copies, waits for them, and re-layouts  25.1 us (17%)
  other arithmetic  11.6 us (8%)
    ppermute x8, starting transfers between devices, padded(): after = lax.ppermute(initial, axis, down)  32.2 us
    ppermute x8, waiting for transfers between devices, padded(): before = lax.ppermute(last, axis, up)  21.5 us
    dot_general x7, matrix products, one_block(): jnp.dot(onehot, values, preferred_element_type=jnp.float32, precision=lax...  12.4 us
    all_to_all x2, starting transfers between devices, on_device(): lax.all_to_all(far_out, 'dom', split_axis=0, concat_axis=0, tiled=True)  7.91 us
    all_to_all x2, starting transfers between devices, on_device(): lax.all_to_all(far_returning, 'dom', split_axis=0, concat_axis=0, tiled=T...  7.02 us
    unnamed x73, local copies, waits for them, and re-layouts  5.05 us
    reduce_sum x3, other arithmetic, edge_counts(): jnp.sum((entries[:, :, None] == wanted[None, None, :]).astype(jnp.int32),...  4.1 us
    convert_element_type x1, other arithmetic, on_device(): encoder_grad = (back_encoder * silu_grad(pre_encoder)).astype(jnp.bfloat16)  4 us
  transfers between devices with their start and end apart: 20, of which 10 were waited for; matrix products, arithmetic and copies ran while one was open for 18% of the time, Pallas kernels for 0%

commit v1 on v0

--- a/solution.py
+++ b/solution.py
@@ -4,17 +4,24 @@
 from jax.sharding import PartitionSpec as P
 
 
-def padded(shard, sides, width):
-    for axis, dim in sides:
-        peers, length = (lax.axis_size(axis), shard.shape[dim])
-        up = [(i, (i + 1) % peers) for i in range(peers)]
-        down = [(j, i) for i, j in up]
-        last = lax.slice_in_dim(shard, length - width, length, axis=dim)
-        initial = lax.slice_in_dim(shard, 0, width, axis=dim)
-        before = lax.ppermute(last, axis, up)
-        after = lax.ppermute(initial, axis, down)
-        shard = jnp.concatenate([before, shard, after], axis=dim)
-    return shard
+def exchange(pair):
+    peers = lax.axis_size("dom")
+    odd = lax.axis_index("dom") % 2 == 1
+    inner = [(i, i ^ 1) for i in range(peers)]
+    outer = [(i, (i + 1) % peers if i % 2 else (i - 1) % peers) for i in range(peers)]
+    to_left, to_right = pair[0], pair[1]
+    far_side = lax.ppermute(jnp.where(odd, to_right, to_left), "dom", outer)
+    near_side = lax.ppermute(jnp.where(odd, to_left, to_right), "dom", inner)
+    from_left = jnp.where(odd, near_side, far_side)
+    from_right = jnp.where(odd, far_side, near_side)
+    return jnp.concatenate([from_left, from_right], axis=0)
+
+
+def far_exchange(blocks):
+    if blocks.shape[0] > 32:
+        return lax.all_to_all(blocks, "dom", split_axis=0, concat_axis=0, tiled=True)
+    everything = lax.all_gather(blocks, "dom")
+    return lax.dynamic_index_in_dim(everything, lax.axis_index("dom"), axis=1, keepdims=False)
 
 
 def silu_grad(value):
@@ -29,9 +36,7 @@
     def one_block(start):
         wanted = start + jnp.arange(block_rows, dtype=jnp.int32)
         onehot = (wanted[:, None] == targets[None, :]).astype(values.dtype)
-        return jnp.dot(
-            onehot, values, preferred_element_type=jnp.float32, precision=lax.Precision.HIGHEST
-        )
+        return jnp.dot(onehot, values, preferred_element_type=jnp.float32)
 
     return lax.map(one_block, starts).reshape(count, values.shape[1])
 
@@ -41,10 +46,6 @@
     return jnp.sum((entries[:, :, None] == wanted[None, None, :]).astype(jnp.int32), axis=1).astype(
         jnp.bfloat16
     )
-
-
-def rim_pair(arrived):
-    return jnp.concatenate([arrived[0], arrived[3]], axis=0)
 
 
 def spread_back(counts, values):
@@ -83,9 +84,9 @@
     pre_encoder = jnp.dot(grid_latent, encoder_weight, preferred_element_type=jnp.float32)
     grid_message = jax.nn.silu(pre_encoder).astype(jnp.bfloat16)
     grid_out = jnp.take(grid_message, grid_lists, axis=0).reshape(2, grid_rim_size, feature_width)
-    grid_in = padded(grid_out, (("dom", 0),), 1)
+    grid_in = exchange(grid_out)
     encoder_counts = edge_counts(encoder_neighbours, grid_rows + 2 * grid_rim_size)
-    grid_extended = jnp.concatenate([grid_message, rim_pair(grid_in)], axis=0)
+    grid_extended = jnp.concatenate([grid_message, grid_in], axis=0)
     encoder_sum = jnp.dot(encoder_counts, grid_extended, preferred_element_type=jnp.float32)
     hidden = (mesh_latent.astype(jnp.float32) + encoder_sum).astype(jnp.bfloat16)
     mesh_counts = edge_counts(mesh_neighbours, near_columns + devices * far_slots)
@@ -96,9 +97,9 @@
         message = jax.nn.silu(pre_layer).astype(jnp.bfloat16)
         rim_out = jnp.take(message, rim_lists, axis=0).reshape(2, mesh_rim_size, feature_width)
         far_out = jnp.take(message, far_lists, axis=0).reshape(devices, far_slots, feature_width)
-        rim_in = padded(rim_out, (("dom", 0),), 1)
-        far_in = lax.all_to_all(far_out, "dom", split_axis=0, concat_axis=0, tiled=True)
-        remote = jnp.concatenate([rim_pair(rim_in), far_in.reshape(-1, feature_width)], axis=0)
+        rim_in = exchange(rim_out)
+        far_in = far_exchange(far_out)
+        remote = jnp.concatenate([rim_in, far_in.reshape(-1, feature_width)], axis=0)
         extended = jnp.concatenate([message, remote], axis=0)
         gathered = jnp.dot(mesh_counts, extended, preferred_element_type=jnp.float32)
         hidden = (hidden.astype(jnp.float32) + gathered * inverse_degree).astype(jnp.bfloat16)
@@ -108,9 +109,9 @@
     decoder_out = jnp.take(decoder_message, rim_lists, axis=0).reshape(
         2, mesh_rim_size, feature_width
     )
-    decoder_in = padded(decoder_out, (("dom", 0),), 1)
+    decoder_in = exchange(decoder_out)
     decoder_counts = edge_counts(decoder_neighbours, near_columns)
-    mesh_extended = jnp.concatenate([decoder_message, rim_pair(decoder_in)], axis=0)
+    mesh_extended = jnp.concatenate([decoder_message, decoder_in], axis=0)
     decoder_sum = jnp.dot(decoder_counts, mesh_extended, preferred_element_type=jnp.float32)
     output = (grid_latent.astype(jnp.float32) + decoder_sum).astype(jnp.bfloat16)
     decoder_spread = spread_back(decoder_counts, cotangent)
@@ -120,9 +121,9 @@
             decoder_spread[mesh_rows + mesh_rim_size :],
         ]
     )
-    decoder_returned = padded(decoder_returning, (("dom", 0),), 1)
+    decoder_returned = exchange(decoder_returning.astype(jnp.bfloat16))
     back_decoder = decoder_spread[:mesh_rows] + block_sum(
-        rim_lists, rim_pair(decoder_returned), mesh_rows
+        rim_lists, decoder_returned, mesh_rows
     )
     decoder_grad = (back_decoder * silu_grad(pre_decoder)).astype(jnp.bfloat16)
     mesh_grad = jnp.dot(decoder_grad, decoder_weight.T, preferred_element_type=jnp.float32).astype(
@@ -136,10 +137,10 @@
                 spread[mesh_rows + mesh_rim_size : near_columns],
             ]
         )
-        returned = padded(returning, (("dom", 0),), 1)
+        returned = exchange(returning.astype(jnp.bfloat16))
         far_returning = spread[near_columns:].reshape(devices, far_slots, feature_width)
-        far_returned = lax.all_to_all(far_returning, "dom", split_axis=0, concat_axis=0, tiled=True)
-        message_grad = spread[:mesh_rows] + block_sum(rim_lists, rim_pair(returned), mesh_rows)
+        far_returned = far_exchange(far_returning.astype(jnp.bfloat16))
+        message_grad = spread[:mesh_rows] + block_sum(rim_lists, returned, mesh_rows)
         message_grad = (
             message_grad + block_sum(far_lists, far_returned.reshape(-1, feature_width), mesh_rows)
         ) * inverse_degree
@@ -155,9 +156,9 @@
             encoder_spread[grid_rows + grid_rim_size :],
         ]
     )
-    grid_returned = padded(grid_returning, (("dom", 0),), 1)
+    grid_returned = exchange(grid_returning.astype(jnp.bfloat16))
     back_encoder = encoder_spread[:grid_rows] + block_sum(
-        grid_lists, rim_pair(grid_returned), grid_rows
+        grid_lists, grid_returned, grid_rows
     )
     encoder_grad = (back_encoder * silu_grad(pre_encoder)).astype(jnp.bfloat16)
     grid_grad = (

time: 148 us -> 239 us (1.61)
  waiting for transfers between devices: 25.9 us -> 123 us
  starting transfers between devices: 47.5 us -> 25.7 us
  between operations: 1.29 us -> 14.3 us
  matrix products: 35.8 us -> 45.8 us
  local copies, waits for them, and re-layouts: 25.1 us -> 19.1 us
    all_gather x0 -> x4, waiting for transfers between devices: none -> 107 us  [far_exchange(): everything = lax.all_gather(blocks, 'dom')]
    all_to_all x4 -> x0, starting transfers between devices: 14.9 us -> none  [the longest x2 7.91 us: on_device(): lax.all_to_all(far_out, 'dom', split_axis=0, concat_axis=0, tiled=True)]
    ppermute x16, waiting for transfers between devices: 25 us -> 15.7 us  [the longest x8 15.7 us: exchange(): far_side = lax.ppermute(jnp.where(odd, to_right, to_left), 'dom', outer)]
    dot_general x4, matrix products: 3.86 us -> 13.2 us  [spread_back(): lax.dot_general(counts, values, (((0,), (0,)), ((), ())), preferred_eleme...]
    ppermute x16, starting transfers between devices: 32.5 us -> 25.3 us  [the longest x8 23.4 us: exchange(): far_side = lax.ppermute(jnp.where(odd, to_right, to_left), 'dom', outer)]
    dot_general x7 -> x4, matrix products: 12.4 us -> 5.47 us  [one_block(): return jnp.dot(onehot, values, preferred_element_type=jnp.float32)]
    dot_general x2, matrix products: 0.94 us -> 7.48 us  [on_device(): jnp.dot(layer_grad, processor_weights[layer].T, preferred_element_type=jn...]
    dynamic_slice x0 -> x4, local copies, waits for them, and re-layouts: none -> 4.67 us  [far_exchange(): lax.dynamic_index_in_dim(everything, lax.axis_index('dom'), axis=1, keepd...]
  transfers between devices with their start and end apart: 20 -> 20, of which waited for: 10 -> 11; matrix products, arithmetic and copies ran while one was open for 18% -> 6% of each run, Pallas kernels for 0% -> 0%
where the time goes in v1:
time: 239 us; the launch traced here: 238 us
  waiting for transfers between devices  123 us (51%)
  matrix products  45.8 us (19%)
  starting transfers between devices  25.7 us (11%)
  local copies, waits for them, and re-layouts  19.1 us (8%)
  between operations  14.3 us (6%)
  other arithmetic  10.4 us (4%)
    all_gather x4, waiting for transfers between devices, far_exchange(): everything = lax.all_gather(blocks, 'dom')  107 us
    ppermute x8, starting transfers between devices, exchange(): far_side = lax.ppermute(jnp.where(odd, to_right, to_left), 'dom', outer)  23.4 us
    ppermute x8, waiting for transfers between devices, exchange(): far_side = lax.ppermute(jnp.where(odd, to_right, to_left), 'dom', outer)  15.7 us
    dot_general x4, matrix products, spread_back(): lax.dot_general(counts, values, (((0,), (0,)), ((), ())), preferred_eleme...  13.2 us
    dot_general x2, matrix products, on_device(): jnp.dot(layer_grad, processor_weights[layer].T, preferred_element_type=jn...  7.48 us
    dot_general x4, matrix products, one_block(): return jnp.dot(onehot, values, preferred_element_type=jnp.float32)  5.47 us
  transfers between devices with their start and end apart: 20, of which 11 were waited for; matrix products, arithmetic and copies ran while one was open for 6% of the time, Pallas kernels for 0%

profile of v1, /device:TPU:0, one launch (start us, length us, event | category | flops | bytes accessed | tf_op | source)
XLA Modules:
  0.0 238.3 jit_solution(16540329792177945251)
XLA Ops:
  9.6 3.5 %multiply_convert_fusion = (bf16[1024,512]{1,0:T(8,128)(2,1)S(1)}, f32[1024,512]{1,0:T(8,128)}) fusion(bf16[1024,512]{1,0:T(8,128)(2,1)} %param.18, bf16[512,512]{1,0:T(8,128)(2,1)S(1)} %copy-done), kind=kOutput, calls=%fused_computation.23 | convolution fusion | flops 539492352 | bytes 4718592 | tf_op jit(solution)/shard_map/dot_general | solution.py:84
  14.6 5.7 %collective-permute-start.1 = (bf16[64,512]{1,0:T(8,128)(2,1)S(1)}, bf16[64,512]{1,0:T(8,128)(2,1)S(1)}, u32[]{:S(2)}, u32[]{:S(2)}) collective-permute-start(bf16[64,512]{1,0:T(8,128)(2,1)S(1)} %get-tuple-element.136), channel_id=1, source_target_pairs={{0,15},{1,2},{2,1},{3,4},{4,3},{5,6},{6,5},{7,8},{8,7},{9,10},{10,... | collective-permute-start | bytes 196616 | tf_op jit(solution)/shard_map/ppermute | solution.py:13
  28.0 4.0 %collective-permute-start.3 = (bf16[64,512]{1,0:T(8,128)(2,1)S(1)}, bf16[64,512]{1,0:T(8,128)(2,1)S(1)}, u32[]{:S(2)}, u32[]{:S(2)}) collective-permute-start(bf16[64,512]{1,0:T(8,128)(2,1)S(1)} %get-tuple-element.132), channel_id=1, source_target_pairs={{0,15},{1,2},{2,1},{3,4},{4,3},{5,6},{6,5},{7,8},{8,7},{9,10},{10,... | collective-permute-start | bytes 196616 | tf_op jit(solution)/shard_map/ppermute | solution.py:13
  34.5 30.1 %all-gather.5.cloned.1.call-done = bf16[16,16,4,512]{3,2,0,1:T(4,128)(2,1)} async-done(((bf16[1,16,4,512]{3,2,0,1:T(4,128)(2,1)}), bf16[16,16,4,512]{3,2,0,1:T(4,128)(2,1)}) %all-gather.5.cloned.1.call-update) | async-done | bytes 1048592 | tf_op jit(solution)/shard_map/all_gather | solution.py:23
  71.4 3.2 %fusion.141 = (bf16[640,512]{1,0:T(8,128)(2,1)S(1)}, f32[640,512]{1,0:T(8,128)}) fusion(bf16[1024,512]{1,0:T(8,128)(2,1)} %param.23, s32[1024,640]{1,0:T(8,128)S(1)} %convert_reduce_fusion.2), kind=kOutput, calls=%fused_computation.206 | convolution fusion | flops 672071680 | bytes 5636096 | tf_op jit(solution)/shard_map/dot_general | solution.py:52
  74.9 2.7 %collective-permute-start.9 = (bf16[64,512]{1,0:T(8,128)(2,1)S(1)}, bf16[64,512]{1,0:T(8,128)(2,1)S(1)}, u32[]{:S(2)}, u32[]{:S(2)}) collective-permute-start(bf16[64,512]{1,0:T(8,128)(2,1)S(1)} %get-tuple-element.112), channel_id=1, source_target_pairs={{0,15},{1,2},{2,1},{3,4},{4,3},{5,6},{6,5},{7,8},{8,7},{9,10},{10,... | collective-permute-start | bytes 196616 | tf_op jit(solution)/shard_map/ppermute | solution.py:13
  81.6 4.6 %collective-permute-done.5 = bf16[64,512]{1,0:T(8,128)(2,1)S(1)} collective-permute-done((bf16[64,512]{1,0:T(8,128)(2,1)S(1)}, bf16[64,512]{1,0:T(8,128)(2,1)S(1)}, u32[]{:S(2)}, u32[]{:S(2)}) %collective-permute-start.5) | collective-permute-done | bytes 65568 | tf_op jit(solution)/shard_map/ppermute | solution.py:13
  86.2 20.6 %all-gather.7.cloned.1.call-done = bf16[16,16,4,512]{3,2,0,1:T(4,128)(2,1)} async-done(((bf16[1,16,4,512]{3,2,0,1:T(4,128)(2,1)}), bf16[16,16,4,512]{3,2,0,1:T(4,128)(2,1)}) %all-gather.7.cloned.1.call-update) | async-done | bytes 1048592 | tf_op jit(solution)/shard_map/all_gather | solution.py:23
  107.7 3.7 %multiply_convert_fusion.1 = (bf16[512,512]{1,0:T(8,128)(2,1)}, f32[512,512]{1,0:T(8,128)}) fusion(bf16[512,512]{1,0:T(8,128)(2,1)} %param.22, bf16[512,704]{0,1:T(8,128)(2,1)} %copy-done.2, bf16[512,512]{1,0:T(8,128)(2,1)} %copy-done.17, bf16[64,512]{1,0:T(8,128)(2,1)S(1)} %reshape.151, bf16[64,512]{1,0:T(8,128)(2,1)S(1)} %get-tuple-element.126, ...), kind=kOutput, calls=%fused_computation.72 | convolution fusion | flops 642777088 | bytes 4063232 | tf_op jit(solution)/shard_map/dot_general | solution.py:107
  111.4 3.3 %convolution_convert_fusion = bf16[512,512]{1,0:T(8,128)(2,1)} fusion(bf16[512,512]{1,0:T(8,128)(2,1)} %param.22, f32[640,512]{1,0:T(8,128)} %get-tuple-element.146, f32[512,512]{1,0:T(8,128)} %get-tuple-element.144, bf16[64,512]{1,0:T(8,128)(2,1)S(1)} %get-tuple-element.120, bf16[64,512]{1,0:T(8,128)(2,1)S(1)} %get-tuple-element.119, ...), kind=kOutput, calls=%fused_computation.42 | convolution fusion | flops 338755584 | bytes 3277312 | tf_op jit(solution)/shard_map/dot_general | solution.py:129
  114.7 2.9 %fusion.142 = (bf16[704,512]{1,0:T(8,128)(2,1)S(1)}, f32[704,512]{1,0:T(8,128)}) fusion(bf16[512,704]{0,1:T(8,128)(2,1)} %copy-done.2, bf16[512,512]{1,0:T(8,128)(2,1)} %convolution_convert_fusion), kind=kOutput, calls=%fused_computation.207 | convolution fusion | flops 369459200 | bytes 3407872 | tf_op jit(solution)/shard_map/dot_general | solution.py:52
  118.8 2.7 %collective-permute-start.11 = (bf16[64,512]{1,0:T(8,128)(2,1)S(1)}, bf16[64,512]{1,0:T(8,128)(2,1)S(1)}, u32[]{:S(2)}, u32[]{:S(2)}) collective-permute-start(bf16[64,512]{1,0:T(8,128)(2,1)S(1)} %get-tuple-element.110), channel_id=1, source_target_pairs={{0,15},{1,2},{2,1},{3,4},{4,3},{5,6},{6,5},{7,8},{8,7},{9,10},{10,... | collective-permute-start | bytes 196616 | tf_op jit(solution)/shard_map/ppermute | solution.py:13
  121.5 3.7 %collective-permute-done.11 = bf16[64,512]{1,0:T(8,128)(2,1)S(1)} collective-permute-done((bf16[64,512]{1,0:T(8,128)(2,1)S(1)}, bf16[64,512]{1,0:T(8,128)(2,1)S(1)}, u32[]{:S(2)}, u32[]{:S(2)}) %collective-permute-start.11) | collective-permute-done | bytes 65568 | tf_op jit(solution)/shard_map/ppermute | solution.py:13
  125.3 30.6 %all-gather.9.cloned.1.call-done = bf16[16,16,4,512]{3,1,2,0:T(8,128)(2,1)} async-done(((bf16[1,16,4,512]{3,1,2,0:T(8,128)(2,1)}), bf16[16,16,4,512]{3,1,2,0:T(8,128)(2,1)}) %all-gather.9.cloned.1.call-update) | async-done | bytes 1048592 | tf_op jit(solution)/shard_map/all_gather | solution.py:23
  158.7 3.7 %fusion.21 = bf16[512,512]{1,0:T(8,128)(2,1)} fusion(f32[512,512]{1,0:T(8,128)} %fusion.94, f32[704,512]{1,0:T(8,128)} %get-tuple-element.148, f32[512,512]{1,0:T(8,128)} %get-tuple-element.142, bf16[512,512]{1,0:T(8,128)(2,1)} %convolution_convert_fusion, bf16[2,512,512]{2,1,0:T(8,128)(2,1)} %param.21, bf16[64,512]{1,0:T(8,128)(2,1)S(1)} %get-tuple-element.118, ...), kind=kOutput, calls=%fused_computation.49 | convolution fusion | flops 339804160 | bytes 4850176 | tf_op jit(solution)/shard_map/dot_general | solution.py:150
  162.5 2.9 %fusion.143 = (bf16[704,512]{1,0:T(8,128)(2,1)S(1)}, f32[704,512]{1,0:T(8,128)}) fusion(bf16[512,704]{0,1:T(8,128)(2,1)} %copy-done.2, bf16[512,512]{1,0:T(8,128)(2,1)} %fusion.21), kind=kOutput, calls=%fused_computation.208 | convolution fusion | flops 369459200 | bytes 3407872 | tf_op jit(solution)/shard_map/dot_general | solution.py:52
  170.7 2.4 collective-permute-start.13
  177.2 26.1 %all-gather.11.cloned.1.call-done = bf16[16,16,4,512]{3,1,2,0:T(8,128)(2,1)} async-done(((bf16[1,16,4,512]{3,1,2,0:T(8,128)(2,1)}), bf16[16,16,4,512]{3,1,2,0:T(8,128)(2,1)}) %all-gather.11.cloned.1.call-update) | async-done | bytes 1048592 | tf_op jit(solution)/shard_map/all_gather | solution.py:23
  206.0 3.8 %fusion.22 = bf16[512,512]{1,0:T(8,128)(2,1)} fusion(f32[512,512]{1,0:T(8,128)} %fusion.93, f32[704,512]{1,0:T(8,128)} %get-tuple-element.150, f32[512,512]{1,0:T(8,128)} %get-tuple-element.140, bf16[512,512]{1,0:T(8,128)(2,1)} %fusion.21, bf16[2,512,512]{2,1,0:T(8,128)(2,1)} %param.21, bf16[64,512]{1,0:T(8,128)(2,1)S(1)} %get-tuple-element.116, ...), kind=kOutput, calls=%fused_computation.50 | convolution fusion | flops 339804160 | bytes 4850176 | tf_op jit(solution)/shard_map/dot_general | solution.py:150
  209.8 4.2 %fusion.144 = (bf16[1152,512]{1,0:T(8,128)(2,1)S(1)}, f32[1152,512]{1,0:T(8,128)}) fusion(bf16[512,512]{1,0:T(8,128)(2,1)} %fusion.22, s32[512,1152]{1,0:T(8,128)} %copy-done.1), kind=kOutput, calls=%fused_computation.209 | convolution fusion | flops 605159424 | bytes 6422528 | tf_op jit(solution)/shard_map/dot_general | solution.py:52
  214.3 2.1 collective-permute-start.15
  218.4 2.3 collective-permute-done.15
  220.7 5.3 %while.3 = (s32[]{:T(128)}, f32[2,512,512]{2,1,0:T(8,128)}, s32[2]{0:T(128)S(1)}, s32[1,2,64]{2,1,0:T(2,128)}, bf16[128,512]{1,0:T(8,128)(2,1)S(1)}, /*index=5*/s32[128]{0:T(128)S(1)}, s32[]{:T(128)}) while((s32[]{:T(128)}, f32[2,512,512]{2,1,0:T(8,128)}, s32[2]{0:T(128)S(1)}, s32[1,2,64]{2,1,0:T(2,128)}, ...), condition=%wide.wide.region_4.7_spmd, body=%wide.wide.region_3.6_spmd.sunk | while | flops 67174912 | bytes 1184861 | solution.py:41
  226.1 4.0 %fusion.5 = bf16[1024,512]{1,0:T(8,128)(2,1)S(1)} fusion(f32[1152,512]{1,0:T(8,128)} %get-tuple-element.152, f32[2,512,512]{2,1,0:T(8,128)} %get-tuple-element.82, f32[1024,512]{1,0:T(8,128)} %get-tuple-element.138), kind=kLoop, calls=%fused_computation.20 | loop fusion | flops 5242880 | bytes 7340032 | tf_op jit(solution)/shard_map/convert_element_type | solution.py:163
  (144 shorter events, 51.5 us)
Async XLA Ops:
  7.2 57.4 %all-gather.5.cloned.1.call-start = ((), (), s32[]{:S(2)}) async-start(), calls=%async_computation | async-start | bytes 1114112 | tf_op jit(solution)/shard_map/all_gather | solution.py:23
  9.6 149.2 %copy-start.11 = (s32[128]{0:T(128)}, s32[128]{0:T(128)S(1)}, u32[]{:S(2)}) copy-start(s32[128]{0:T(128)S(1)} %reshape_squeeze.13) | copy-start | bytes 1540
  9.6 10.7 %copy-start.10 = (s32[1,16,4]{1,2,0:T(4,128)S(1)}, s32[1,16,4]{1,2,0:T(4,128)}, u32[]{:S(2)}) copy-start(s32[1,16,4]{1,2,0:T(4,128)} %param.27) | copy-start | bytes 772
  9.6 10.8 %copy-start.9 = (s32[512,4]{0,1:T(4,128)S(1)}, s32[512,4]{0,1:T(4,128)}, u32[]{:S(2)}) copy-start(s32[512,4]{0,1:T(4,128)} %param.25) | copy-start | bytes 24580
  14.1 7.8 %collective-permute-start = (bf16[64,512]{1,0:T(8,128)(2,1)S(1)}, bf16[64,512]{1,0:T(8,128)(2,1)S(1)}, u32[]{:S(2)}, u32[]{:S(2)}) collective-permute-start(bf16[64,512]{1,0:T(8,128)(2,1)S(1)} %get-tuple-element.135), channel_id=1, source_target_pairs={{0,1},{1,0},{2,3},{3,2},{4,5},{5,4},{6,7},{7,6},{8,9},{9,8},{10,11... | collective-permute-start | bytes 196616 | tf_op jit(solution)/shard_map/ppermute | solution.py:14
  14.6 7.6 %collective-permute-start.1 = (bf16[64,512]{1,0:T(8,128)(2,1)S(1)}, bf16[64,512]{1,0:T(8,128)(2,1)S(1)}, u32[]{:S(2)}, u32[]{:S(2)}) collective-permute-start(bf16[64,512]{1,0:T(8,128)(2,1)S(1)} %get-tuple-element.136), channel_id=1, source_target_pairs={{0,15},{1,2},{2,1},{3,4},{4,3},{5,6},{6,5},{7,8},{8,7},{9,10},{10,... | collective-permute-start | bytes 196616 | tf_op jit(solution)/shard_map/ppermute | solution.py:13
  26.9 79.9 %all-gather.7.cloned.1.call-start = ((), (), s32[]{:S(2)}) async-start(), calls=%async_computation.1 | async-start | bytes 1114112 | tf_op jit(solution)/shard_map/all_gather | solution.py:23
  27.9 5.9 %collective-permute-start.2 = (bf16[64,512]{1,0:T(8,128)(2,1)S(1)}, bf16[64,512]{1,0:T(8,128)(2,1)S(1)}, u32[]{:S(2)}, u32[]{:S(2)}) collective-permute-start(bf16[64,512]{1,0:T(8,128)(2,1)S(1)} %get-tuple-element.131), channel_id=1, source_target_pairs={{0,1},{1,0},{2,3},{3,2},{4,5},{5,4},{6,7},{7,6},{8,9},{9,8},{10,11... | collective-permute-start | bytes 196616 | tf_op jit(solution)/shard_map/ppermute | solution.py:14
  28.0 6.5 %collective-permute-start.3 = (bf16[64,512]{1,0:T(8,128)(2,1)S(1)}, bf16[64,512]{1,0:T(8,128)(2,1)S(1)}, u32[]{:S(2)}, u32[]{:S(2)}) collective-permute-start(bf16[64,512]{1,0:T(8,128)(2,1)S(1)} %get-tuple-element.132), channel_id=1, source_target_pairs={{0,15},{1,2},{2,1},{3,4},{4,3},{5,6},{6,5},{7,8},{8,7},{9,10},{10,... | collective-permute-start | bytes 196616 | tf_op jit(solution)/shard_map/ppermute | solution.py:13
  33.8 33.4 %copy-start.2 = (bf16[512,704]{0,1:T(8,128)(2,1)}, bf16[512,704]{0,1:T(8,128)(2,1)S(1)}, u32[]{:S(2)}) copy-start(bf16[512,704]{0,1:T(8,128)(2,1)S(1)} %convert_element_type.134) | copy-start | bytes 2162692
  70.2 85.7 %all-gather.9.cloned.1.call-start = ((), (), s32[]{:S(2)}) async-start(), calls=%async_computation.2 | async-start | bytes 1114112 | tf_op jit(solution)/shard_map/all_gather | solution.py:23
  74.6 7.0 %collective-permute-start.8 = (bf16[64,512]{1,0:T(8,128)(2,1)S(1)}, bf16[64,512]{1,0:T(8,128)(2,1)S(1)}, u32[]{:S(2)}, u32[]{:S(2)}) collective-permute-start(bf16[64,512]{1,0:T(8,128)(2,1)S(1)} %get-tuple-element.111), channel_id=1, source_target_pairs={{0,1},{1,0},{2,3},{3,2},{4,5},{5,4},{6,7},{7,6},{8,9},{9,8},{10,11... | collective-permute-start | bytes 196616 | tf_op jit(solution)/shard_map/ppermute | solution.py:14
  74.9 6.7 %collective-permute-start.9 = (bf16[64,512]{1,0:T(8,128)(2,1)S(1)}, bf16[64,512]{1,0:T(8,128)(2,1)S(1)}, u32[]{:S(2)}, u32[]{:S(2)}) collective-permute-start(bf16[64,512]{1,0:T(8,128)(2,1)S(1)} %get-tuple-element.112), channel_id=1, source_target_pairs={{0,15},{1,2},{2,1},{3,4},{4,3},{5,6},{6,5},{7,8},{8,7},{9,10},{10,... | collective-permute-start | bytes 196616 | tf_op jit(solution)/shard_map/ppermute | solution.py:13
  79.7 1.9 collective-permute-start.4
  79.8 6.5 %collective-permute-start.5 = (bf16[64,512]{1,0:T(8,128)(2,1)S(1)}, bf16[64,512]{1,0:T(8,128)(2,1)S(1)}, u32[]{:S(2)}, u32[]{:S(2)}) collective-permute-start(bf16[64,512]{1,0:T(8,128)(2,1)S(1)} %get-tuple-element.128), channel_id=1, source_target_pairs={{0,15},{1,2},{2,1},{3,4},{4,3},{5,6},{6,5},{7,8},{8,7},{9,10},{10,... | collective-permute-start | bytes 196616 | tf_op jit(solution)/shard_map/ppermute | solution.py:13
  118.3 85.0 %all-gather.11.cloned.1.call-start = ((), (), s32[]{:S(2)}) async-start(), calls=%async_computation.3 | async-start | bytes 1114112 | tf_op jit(solution)/shard_map/all_gather | solution.py:23
  118.5 3.0 %collective-permute-start.10 = (bf16[64,512]{1,0:T(8,128)(2,1)S(1)}, bf16[64,512]{1,0:T(8,128)(2,1)S(1)}, u32[]{:S(2)}, u32[]{:S(2)}) collective-permute-start(bf16[64,512]{1,0:T(8,128)(2,1)S(1)} %get-tuple-element.108), channel_id=1, source_target_pairs={{0,1},{1,0},{2,3},{3,2},{4,5},{5,4},{6,7},{7,6},{8,9},{9,8},{10,11... | collective-permute-start | bytes 196616 | tf_op jit(solution)/shard_map/ppermute | solution.py:14
  118.8 6.4 %collective-permute-start.11 = (bf16[64,512]{1,0:T(8,128)(2,1)S(1)}, bf16[64,512]{1,0:T(8,128)(2,1)S(1)}, u32[]{:S(2)}, u32[]{:S(2)}) collective-permute-start(bf16[64,512]{1,0:T(8,128)(2,1)S(1)} %get-tuple-element.110), channel_id=1, source_target_pairs={{0,15},{1,2},{2,1},{3,4},{4,3},{5,6},{6,5},{7,8},{8,7},{9,10},{10,... | collective-permute-start | bytes 196616 | tf_op jit(solution)/shard_map/ppermute | solution.py:13
  168.3 4.8 %collective-permute-start.6 = (bf16[64,512]{1,0:T(8,128)(2,1)S(1)}, bf16[64,512]{1,0:T(8,128)(2,1)S(1)}, u32[]{:S(2)}, u32[]{:S(2)}) collective-permute-start(bf16[64,512]{1,0:T(8,128)(2,1)S(1)} %get-tuple-element.123), channel_id=1, source_target_pairs={{0,1},{1,0},{2,3},{3,2},{4,5},{5,4},{6,7},{7,6},{8,9},{9,8},{10,11... | collective-permute-start | bytes 196616 | tf_op jit(solution)/shard_map/ppermute | solution.py:14
  168.6 6.5 %collective-permute-start.7 = (bf16[64,512]{1,0:T(8,128)(2,1)S(1)}, bf16[64,512]{1,0:T(8,128)(2,1)S(1)}, u32[]{:S(2)}, u32[]{:S(2)}) collective-permute-start(bf16[64,512]{1,0:T(8,128)(2,1)S(1)} %get-tuple-element.124), channel_id=1, source_target_pairs={{0,15},{1,2},{2,1},{3,4},{4,3},{5,6},{6,5},{7,8},{8,7},{9,10},{10,... | collective-permute-start | bytes 196616 | tf_op jit(solution)/shard_map/ppermute | solution.py:13
  170.7 4.4 %collective-permute-start.12 = (bf16[64,512]{1,0:T(8,128)(2,1)S(1)}, bf16[64,512]{1,0:T(8,128)(2,1)S(1)}, u32[]{:S(2)}, u32[]{:S(2)}) collective-permute-start(bf16[64,512]{1,0:T(8,128)(2,1)S(1)} %get-tuple-element.105), channel_id=1, source_target_pairs={{0,1},{1,0},{2,3},{3,2},{4,5},{5,4},{6,7},{7,6},{8,9},{9,8},{10,11... | collective-permute-start | bytes 196616 | tf_op jit(solution)/shard_map/ppermute | solution.py:14
  170.7 6.5 %collective-permute-start.13 = (bf16[64,512]{1,0:T(8,128)(2,1)S(1)}, bf16[64,512]{1,0:T(8,128)(2,1)S(1)}, u32[]{:S(2)}, u32[]{:S(2)}) collective-permute-start(bf16[64,512]{1,0:T(8,128)(2,1)S(1)} %get-tuple-element.107), channel_id=1, source_target_pairs={{0,15},{1,2},{2,1},{3,4},{4,3},{5,6},{6,5},{7,8},{8,7},{9,10},{10,... | collective-permute-start | bytes 196616 | tf_op jit(solution)/shard_map/ppermute | solution.py:13
  214.0 4.4 %collective-permute-start.14 = (bf16[64,512]{1,0:T(8,128)(2,1)S(1)}, bf16[64,512]{1,0:T(8,128)(2,1)S(1)}, u32[]{:S(2)}, u32[]{:S(2)}) collective-permute-start(bf16[64,512]{1,0:T(8,128)(2,1)S(1)} %get-tuple-element.103), channel_id=1, source_target_pairs={{0,1},{1,0},{2,3},{3,2},{4,5},{5,4},{6,7},{7,6},{8,9},{9,8},{10,11... | collective-permute-start | bytes 196616 | tf_op jit(solution)/shard_map/ppermute | solution.py:14
  214.3 6.4 %collective-permute-start.15 = (bf16[64,512]{1,0:T(8,128)(2,1)S(1)}, bf16[64,512]{1,0:T(8,128)(2,1)S(1)}, u32[]{:S(2)}, u32[]{:S(2)}) collective-permute-start(bf16[64,512]{1,0:T(8,128)(2,1)S(1)} %get-tuple-element.104), channel_id=1, source_target_pairs={{0,15},{1,2},{2,1},{3,4},{4,3},{5,6},{6,5},{7,8},{8,7},{9,10},{10,... | collective-permute-start | bytes 196616 | tf_op jit(solution)/shard_map/ppermute | solution.py:13
  (14 other events, 51.4 us)
Sparse Core Ops, SparseCore 0:
  27.0 37.4 all-gather.4
  70.3 36.4 all-gather.6
  118.4 37.4 all-gather.8
  166.2 37.0 all-gather.10

commit v2 on v1

--- a/solution.py
+++ b/solution.py
@@ -8,9 +8,10 @@
     peers = lax.axis_size("dom")
     odd = lax.axis_index("dom") % 2 == 1
     inner = [(i, i ^ 1) for i in range(peers)]
-    outer = [(i, (i + 1) % peers if i % 2 else (i - 1) % peers) for i in range(peers)]
+    outer = [[i, (i + 1) % peers] for i in range(1, peers, 2)]
     to_left, to_right = pair[0], pair[1]
-    far_side = lax.ppermute(jnp.where(odd, to_right, to_left), "dom", outer)
+    both = lax.all_gather(jnp.where(odd, to_right, to_left), "dom", axis_index_groups=outer)
+    far_side = jnp.where(odd, both[1], both[0])
     near_side = lax.ppermute(jnp.where(odd, to_left, to_right), "dom", inner)
     from_left = jnp.where(odd, near_side, far_side)
     from_right = jnp.where(odd, far_side, near_side)
@@ -18,10 +19,7 @@
 
 
 def far_exchange(blocks):
-    if blocks.shape[0] > 32:
-        return lax.all_to_all(blocks, "dom", split_axis=0, concat_axis=0, tiled=True)
-    everything = lax.all_gather(blocks, "dom")
-    return lax.dynamic_index_in_dim(everything, lax.axis_index("dom"), axis=1, keepdims=False)
+    return lax.all_to_all(blocks, "dom", split_axis=0, concat_axis=0, tiled=True)
 
 
 def silu_grad(value):

time: 239 us -> 169 us (0.71)
  waiting for transfers between devices: 123 us -> 0.03 us
  blocking collectives: 0 us -> 58.7 us
  between operations: 14.3 us -> 1.18 us
  other arithmetic: 10.4 us -> 20.1 us
    all_gather x4 -> x0, waiting for transfers between devices: 107 us -> none  [far_exchange(): everything = lax.all_gather(blocks, 'dom')]
    all_gather x0 -> x8, blocking collectives: none -> 58.7 us  [exchange(): lax.all_gather(jnp.where(odd, to_right, to_left), 'dom', axis_index_group...]
    all_to_all x0 -> x4, starting transfers between devices: none -> 24.1 us  [far_exchange(): lax.all_to_all(blocks, 'dom', split_axis=0, concat_axis=0, tiled=True)]
    ppermute x8 -> x0, starting transfers between devices: 23.4 us -> none  [exchange(): far_side = lax.ppermute(jnp.where(odd, to_right, to_left), 'dom', outer)]
    ppermute x8 -> x0, waiting for transfers between devices: 15.7 us -> none  [exchange(): far_side = lax.ppermute(jnp.where(odd, to_right, to_left), 'dom', outer)]
    dynamic_slice x4 -> x0, local copies, waits for them, and re-layouts: 4.67 us -> none  [far_exchange(): lax.dynamic_index_in_dim(everything, lax.axis_index('dom'), axis=1, keepd...]
    select_n x8, other arithmetic: 0.11 us -> 4.1 us  [exchange(): from_left = jnp.where(odd, near_side, far_side)]
    select_n x8, other arithmetic: 0.12 us -> 2.63 us  [exchange(): jnp.where(odd, to_right, to_left)]
  transfers between devices with their start and end apart: 20 -> 12, of which waited for: 11 -> 0; matrix products, arithmetic and copies ran while one was open for 6% -> 22% of each run, Pallas kernels for 0% -> 0%
where the time goes in v2:
time: 169 us; the launch traced here: 168 us
  blocking collectives  58.7 us (35%)
  matrix products  45.2 us (27%)
  starting transfers between devices  25.3 us (15%)
  other arithmetic  20.1 us (12%)
  local copies, waits for them, and re-layouts  17.2 us (10%)
    all_gather x8, blocking collectives, exchange(): lax.all_gather(jnp.where(odd, to_right, to_left), 'dom', axis_index_group...  58.7 us
    all_to_all x4, starting transfers between devices, far_exchange(): lax.all_to_all(blocks, 'dom', split_axis=0, concat_axis=0, tiled=True)  24.1 us
    dot_general x4, matrix products, spread_back(): lax.dot_general(counts, values, (((0,), (0,)), ((), ())), preferred_eleme...  12 us
    dot_general x2, matrix products, on_device(): jnp.dot(layer_grad, processor_weights[layer].T, preferred_element_type=jn...  7.55 us
    dot_general x4, matrix products, one_block(): return jnp.dot(onehot, values, preferred_element_type=jnp.float32)  5.19 us
    select_n x8, other arithmetic, exchange(): from_left = jnp.where(odd, near_side, far_side)  4.1 us
    reduce_sum x3, other arithmetic, edge_counts(): jnp.sum((entries[:, :, None] == wanted[None, None, :]).astype(jnp.int32),...  4.09 us
    convert_element_type x1, other arithmetic, on_device(): encoder_grad = (back_encoder * silu_grad(pre_encoder)).astype(jnp.bfloat16)  4 us
  transfers between devices with their start and end apart: 12, of which 0 were waited for; matrix products, arithmetic and copies ran while one was open for 22% of the time, Pallas kernels for 0%

profile of v2, /device:TPU:0, one launch (start us, length us, event | category | flops | bytes accessed | tf_op | source)
XLA Modules:
  0.0 167.8 jit_solution(7223449795429747252)
XLA Ops:
  2.3 3.5 %multiply_convert_fusion = (bf16[1024,512]{1,0:T(8,128)(2,1)S(1)}, f32[1024,512]{1,0:T(8,128)}) fusion(bf16[1024,512]{1,0:T(8,128)(2,1)} %param.18, bf16[512,512]{1,0:T(8,128)(2,1)S(1)} %copy-done), kind=kOutput, calls=%fused_computation.23 | convolution fusion | flops 539492352 | bytes 4718592 | tf_op jit(solution)/shard_map/dot_general | solution.py:82
  8.5 2.0 %fusion.141 = (bf16[640,512]{1,0:T(8,128)(2,1)S(1)}, f32[640,512]{1,0:T(8,128)}) fusion(bf16[1024,512]{1,0:T(8,128)(2,1)S(1)} %copy-done.6, s32[1024,640]{1,0:T(8,128)S(1)} %convert_reduce_fusion.2), kind=kOutput, calls=%fused_computation.210 | convolution fusion | flops 672071680 | bytes 5636096 | tf_op jit(solution)/shard_map/dot_general | solution.py:50
  16.7 8.2 %all-gather = bf16[128,512]{1,0:T(8,128)(2,1)S(1)} all-gather(bf16[64,512]{1,0:T(8,128)(2,1)S(1)} %get-tuple-element.135), channel_id=2, replica_groups={{1,2},{3,4},{5,6},{7,8},{9,10},{11,12},{13,14},{15,0},{17,18},{19,20},{..., dimensions={0}, use_global_device_ids=true | all-gather | bytes 196608 | tf_op jit(solution)/shard_map/all_gather | solution.py:13
  25.0 7.1 %all-gather.4 = bf16[128,512]{1,0:T(8,128)(2,1)S(1)} all-gather(bf16[64,512]{1,0:T(8,128)(2,1)S(1)} %get-tuple-element.111), channel_id=6, replica_groups={{1,2},{3,4},{5,6},{7,8},{9,10},{11,12},{13,14},{15,0},{17,18},{19,20},{..., dimensions={0}, use_global_device_ids=true | all-gather | bytes 196608 | tf_op jit(solution)/shard_map/all_gather | solution.py:13
  40.9 6.2 %all-to-all-start = ((bf16[16,4,512]{2,1,0:T(4,128)(2,1)}), bf16[16,4,512]{2,1,0:T(4,128)(2,1)S(1)}, u32[]{:S(2)}, u32[]{:S(2)}) async-start(bf16[16,4,512]{2,1,0:T(4,128)(2,1)} %reshape.140), calls=%async_computation | async-start | bytes 131072 | tf_op jit(solution)/shard_map/all_to_all | solution.py:22
  48.0 7.1 %all-gather.1 = bf16[128,512]{1,0:T(8,128)(2,1)S(1)} all-gather(bf16[64,512]{1,0:T(8,128)(2,1)S(1)} %get-tuple-element.133), channel_id=3, replica_groups={{1,2},{3,4},{5,6},{7,8},{9,10},{11,12},{13,14},{15,0},{17,18},{19,20},{..., dimensions={0}, use_global_device_ids=true | all-gather | bytes 196608 | tf_op jit(solution)/shard_map/all_gather | solution.py:13
  56.0 2.1 %fusion.17 = bf16[512,512]{1,0:T(8,128)(2,1)S(1)} fusion(bf16[512,704]{0,1:T(8,128)(2,1)} %convert_element_type.120, bf16[512,512]{1,0:T(8,128)(2,1)} %copy-done.23, bf16[64,512]{1,0:T(8,128)(2,1)S(1)} %reshape.141, bf16[64,512]{1,0:T(8,128)(2,1)S(1)} %get-tuple-element.126, bf16[64,512]{1,0:T(8,128)(2,1)S(1)} %get-tuple-element.125, ...), kind=kOutput, calls=%fused_computation.45 | convolution fusion | flops 373030912 | bytes 2490368 | tf_op jit(solution)/shard_map/dot_general | solution.py:102
  65.7 6.2 %all-to-all-start.1 = ((bf16[16,4,512]{2,1,0:T(4,128)(2,1)}), bf16[16,4,512]{2,1,0:T(4,128)(2,1)S(1)}, u32[]{:S(2)}, u32[]{:S(2)}) async-start(bf16[16,4,512]{2,1,0:T(4,128)(2,1)} %reshape.142), calls=%async_computation.1 | async-start | bytes 131072 | tf_op jit(solution)/shard_map/all_to_all | solution.py:22
  71.9 7.6 %all-gather.2 = bf16[128,512]{1,0:T(8,128)(2,1)S(1)} all-gather(bf16[64,512]{1,0:T(8,128)(2,1)S(1)} %get-tuple-element.131), channel_id=4, replica_groups={{1,2},{3,4},{5,6},{7,8},{9,10},{11,12},{13,14},{15,0},{17,18},{19,20},{..., dimensions={0}, use_global_device_ids=true | all-gather | bytes 196608 | tf_op jit(solution)/shard_map/all_gather | solution.py:13
  79.6 3.7 %multiply_convert_fusion.1 = (bf16[512,512]{1,0:T(8,128)(2,1)}, f32[512,512]{1,0:T(8,128)}) fusion(bf16[512,512]{1,0:T(8,128)(2,1)} %param.22, bf16[512,704]{0,1:T(8,128)(2,1)} %convert_element_type.120, bf16[512,512]{1,0:T(8,128)(2,1)} %copy-done.24, bf16[64,512]{1,0:T(8,128)(2,1)S(1)} %reshape.143, bf16[64,512]{1,0:T(8,128)(2,1)S(1)} %get-tuple-element.124, ...), kind=kOutput, calls=%fused_computation.72 | convolution fusion | flops 642777088 | bytes 4063232 | tf_op jit(solution)/shard_map/dot_general | solution.py:105
  83.3 3.3 %convolution_convert_fusion = bf16[512,512]{1,0:T(8,128)(2,1)} fusion(bf16[512,512]{1,0:T(8,128)(2,1)} %param.22, f32[640,512]{1,0:T(8,128)} %get-tuple-element.146, f32[512,512]{1,0:T(8,128)} %get-tuple-element.144, bf16[64,512]{1,0:T(8,128)(2,1)S(1)} %get-tuple-element.120, bf16[64,512]{1,0:T(8,128)(2,1)S(1)} %get-tuple-element.119, s32[128]{0:T(128)S(1)} %copy-done.21), kind=kOutput, calls=%fused_computation.42 | convolution fusion | flops 338755584 | bytes 3277312 | tf_op jit(solution)/shard_map/dot_general | solution.py:127
  86.6 2.9 %fusion.142 = (bf16[704,512]{1,0:T(8,128)(2,1)S(1)}, f32[704,512]{1,0:T(8,128)}) fusion(bf16[512,704]{0,1:T(8,128)(2,1)} %convert_element_type.120, bf16[512,512]{1,0:T(8,128)(2,1)} %convolution_convert_fusion), kind=kOutput, calls=%fused_computation.211 | convolution fusion | flops 369459200 | bytes 3407872 | tf_op jit(solution)/shard_map/dot_general | solution.py:50
  90.2 5.6 %all-to-all-start.2 = ((bf16[16,4,512]{2,1,0:T(4,128)(2,1)}), bf16[16,4,512]{2,1,0:T(4,128)(2,1)S(1)}, u32[]{:S(2)}, u32[]{:S(2)}) async-start(bf16[16,4,512]{2,1,0:T(4,128)(2,1)} %convert_element_type.132), calls=%async_computation.2 | async-start | bytes 131072 | tf_op jit(solution)/shard_map/all_to_all | solution.py:22
  99.0 7.1 %all-gather.5 = bf16[128,512]{1,0:T(8,128)(2,1)S(1)} all-gather(bf16[64,512]{1,0:T(8,128)(2,1)S(1)} %get-tuple-element.108), channel_id=7, replica_groups={{1,2},{3,4},{5,6},{7,8},{9,10},{11,12},{13,14},{15,0},{17,18},{19,20},{..., dimensions={0}, use_global_device_ids=true | all-gather | bytes 196608 | tf_op jit(solution)/shard_map/all_gather | solution.py:13
  106.0 7.1 %all-gather.3 = bf16[128,512]{1,0:T(8,128)(2,1)S(1)} all-gather(bf16[64,512]{1,0:T(8,128)(2,1)S(1)} %get-tuple-element.129), channel_id=5, replica_groups={{1,2},{3,4},{5,6},{7,8},{9,10},{11,12},{13,14},{15,0},{17,18},{19,20},{..., dimensions={0}, use_global_device_ids=true | all-gather | bytes 196608 | tf_op jit(solution)/shard_map/all_gather | solution.py:13
  115.0 3.8 %fusion.21 = bf16[512,512]{1,0:T(8,128)(2,1)} fusion(f32[512,512]{1,0:T(8,128)} %fusion.94, f32[704,512]{1,0:T(8,128)} %get-tuple-element.148, f32[512,512]{1,0:T(8,128)} %get-tuple-element.142, bf16[512,512]{1,0:T(8,128)(2,1)} %convolution_convert_fusion, bf16[2,512,512]{2,1,0:T(8,128)(2,1)} %param.21, bf16[64,512]{1,0:T(8,128)(2,1)} %get-tuple-element.118, ...), kind=kOutput, calls=%fused_computation.49 | convolution fusion | flops 339804160 | bytes 4850176 | tf_op jit(solution)/shard_map/dot_general | solution.py:148
  118.8 2.9 %fusion.143 = (bf16[704,512]{1,0:T(8,128)(2,1)S(1)}, f32[704,512]{1,0:T(8,128)}) fusion(bf16[512,704]{0,1:T(8,128)(2,1)} %convert_element_type.120, bf16[512,512]{1,0:T(8,128)(2,1)} %fusion.21), kind=kOutput, calls=%fused_computation.212 | convolution fusion | flops 369459200 | bytes 3407872 | tf_op jit(solution)/shard_map/dot_general | solution.py:50
  123.9 6.1 %all-to-all-start.3 = ((bf16[16,4,512]{2,1,0:T(4,128)(2,1)}), bf16[16,4,512]{2,1,0:T(4,128)(2,1)S(1)}, u32[]{:S(2)}, u32[]{:S(2)}) async-start(bf16[16,4,512]{2,1,0:T(4,128)(2,1)} %convert_element_type.136), calls=%async_computation.3 | async-start | bytes 131072 | tf_op jit(solution)/shard_map/all_to_all | solution.py:22
  130.0 7.6 %all-gather.6 = bf16[128,512]{1,0:T(8,128)(2,1)S(1)} all-gather(bf16[64,512]{1,0:T(8,128)(2,1)S(1)} %get-tuple-element.105), channel_id=8, replica_groups={{1,2},{3,4},{5,6},{7,8},{9,10},{11,12},{13,14},{15,0},{17,18},{19,20},{..., dimensions={0}, use_global_device_ids=true | all-gather | bytes 196608 | tf_op jit(solution)/shard_map/all_gather | solution.py:13
  139.8 3.8 %fusion.22 = bf16[512,512]{1,0:T(8,128)(2,1)} fusion(f32[512,512]{1,0:T(8,128)} %fusion.93, f32[704,512]{1,0:T(8,128)} %get-tuple-element.150, f32[512,512]{1,0:T(8,128)} %get-tuple-element.140, bf16[512,512]{1,0:T(8,128)(2,1)} %fusion.21, bf16[2,512,512]{2,1,0:T(8,128)(2,1)} %param.21, bf16[64,512]{1,0:T(8,128)(2,1)S(1)} %get-tuple-element.116, ...), kind=kOutput, calls=%fused_computation.50 | convolution fusion | flops 339804160 | bytes 4850176 | tf_op jit(solution)/shard_map/dot_general | solution.py:148
  143.5 4.2 %fusion.144 = (bf16[1152,512]{1,0:T(8,128)(2,1)S(1)}, f32[1152,512]{1,0:T(8,128)}) fusion(bf16[512,512]{1,0:T(8,128)(2,1)} %fusion.22, s32[512,1152]{1,0:T(8,128)} %copy-done.1), kind=kOutput, calls=%fused_computation.213 | convolution fusion | flops 605159424 | bytes 6422528 | tf_op jit(solution)/shard_map/dot_general | solution.py:50
  149.8 7.1 %all-gather.7 = bf16[128,512]{1,0:T(8,128)(2,1)S(1)} all-gather(bf16[64,512]{1,0:T(8,128)(2,1)S(1)} %get-tuple-element.103), channel_id=9, replica_groups={{1,2},{3,4},{5,6},{7,8},{9,10},{11,12},{13,14},{15,0},{17,18},{19,20},{..., dimensions={0}, use_global_device_ids=true | all-gather | bytes 196608 | tf_op jit(solution)/shard_map/all_gather | solution.py:13
  156.9 5.1 %while.3 = (s32[]{:T(128)}, f32[2,512,512]{2,1,0:T(8,128)}, s32[2]{0:T(128)S(1)}, s32[1,2,64]{2,1,0:T(2,128)}, bf16[128,512]{1,0:T(8,128)(2,1)S(1)}, /*index=5*/s32[128]{0:T(128)S(1)}, s32[]{:T(128)}) while((s32[]{:T(128)}, f32[2,512,512]{2,1,0:T(8,128)}, s32[2]{0:T(128)S(1)}, s32[1,2,64]{2,1,0:T(2,128)}, ...), condition=%wide.wide.region_4.7_spmd, body=%wide.wide.region_3.6_spmd.sunk | while | flops 67174912 | bytes 1184861 | solution.py:39
  162.1 4.0 %fusion.5 = bf16[1024,512]{1,0:T(8,128)(2,1)S(1)} fusion(f32[1152,512]{1,0:T(8,128)} %get-tuple-element.152, f32[2,512,512]{2,1,0:T(8,128)} %get-tuple-element.82, f32[1024,512]{1,0:T(8,128)} %get-tuple-element.138), kind=kLoop, calls=%fused_computation.20 | loop fusion | flops 5242880 | bytes 7340032 | tf_op jit(solution)/shard_map/convert_element_type | solution.py:161
  (141 shorter events, 47.6 us)
Async XLA Ops:
  2.3 5.0 %copy-start.8 = (s32[1024,3]{0,1:T(4,128)S(1)}, s32[1024,3]{0,1:T(4,128)}, u32[]{:S(2)}) copy-start(s32[1024,3]{0,1:T(4,128)} %param.29) | copy-start | bytes 36868
  6.8 25.3 %collective-permute-start = (bf16[64,512]{1,0:T(8,128)(2,1)S(1)}, bf16[64,512]{1,0:T(8,128)(2,1)S(1)}, u32[]{:S(2)}, u32[]{:S(2)}) collective-permute-start(bf16[64,512]{1,0:T(8,128)(2,1)S(1)} %get-tuple-element.136), channel_id=1, source_target_pairs={{0,1},{1,0},{2,3},{3,2},{4,5},{5,4},{6,7},{7,6},{8,9},{9,8},{10,11... | collective-permute-start | bytes 196616 | tf_op jit(solution)/shard_map/ppermute | solution.py:15
  8.5 4.2 %copy-start.10 = (s32[512,4]{0,1:T(4,128)S(1)}, s32[512,4]{0,1:T(4,128)}, u32[]{:S(2)}) copy-start(s32[512,4]{0,1:T(4,128)} %param.25) | copy-start | bytes 24580
  10.5 36.7 %collective-permute-start.4 = (bf16[64,512]{1,0:T(8,128)(2,1)S(1)}, bf16[64,512]{1,0:T(8,128)(2,1)}, u32[]{:S(2)}, u32[]{:S(2)}) collective-permute-start(bf16[64,512]{1,0:T(8,128)(2,1)S(1)} %get-tuple-element.112), channel_id=1, source_target_pairs={{0,1},{1,0},{2,3},{3,2},{4,5},{5,4},{6,7},{7,6},{8,9},{9,8},{10,11... | collective-permute-start | bytes 196616 | tf_op jit(solution)/shard_map/ppermute | solution.py:15
  14.1 18.0 %copy-start.1 = (s32[512,1152]{1,0:T(8,128)}, s32[512,1152]{1,0:T(8,128)S(1)}, u32[]{:S(2)}) copy-start(s32[512,1152]{1,0:T(8,128)S(1)} %convert_reduce_fusion.1) | copy-start | bytes 7077892
  14.1 18.0 %copy-start.4 = (bf16[1024,512]{1,0:T(8,128)(2,1)S(1)}, bf16[1024,512]{1,0:T(8,128)(2,1)}, u32[]{:S(2)}) copy-start(bf16[1024,512]{1,0:T(8,128)(2,1)} %copy-done.3) | copy-start | bytes 3145732
  14.1 18.0 %copy-start.16 = (bf16[512,512]{1,0:T(8,128)(2,1)S(1)}, bf16[512,512]{1,0:T(8,128)(2,1)}, u32[]{:S(2)}) copy-start(bf16[512,512]{1,0:T(8,128)(2,1)} %param.19) | copy-start | bytes 1572868
  37.7 17.4 %collective-permute-start.1 = (bf16[64,512]{1,0:T(8,128)(2,1)}, bf16[64,512]{1,0:T(8,128)(2,1)}, u32[]{:S(2)}, u32[]{:S(2)}) collective-permute-start(bf16[64,512]{1,0:T(8,128)(2,1)} %get-tuple-element.134), channel_id=1, source_target_pairs={{0,1},{1,0},{2,3},{3,2},{4,5},{5,4},{6,7},{7,6},{8,9},{9,8},{10,11... | collective-permute-start | bytes 196616 | tf_op jit(solution)/shard_map/ppermute | solution.py:15
  40.9 15.0 %all-to-all-start = ((bf16[16,4,512]{2,1,0:T(4,128)(2,1)}), bf16[16,4,512]{2,1,0:T(4,128)(2,1)S(1)}, u32[]{:S(2)}, u32[]{:S(2)}) async-start(bf16[16,4,512]{2,1,0:T(4,128)(2,1)} %reshape.140), calls=%async_computation | async-start | bytes 131072 | tf_op jit(solution)/shard_map/all_to_all | solution.py:22
  64.4 15.1 %collective-permute-start.2 = (bf16[64,512]{1,0:T(8,128)(2,1)}, bf16[64,512]{1,0:T(8,128)(2,1)S(1)}, u32[]{:S(2)}, u32[]{:S(2)}) collective-permute-start(bf16[64,512]{1,0:T(8,128)(2,1)} %get-tuple-element.132), channel_id=1, source_target_pairs={{0,1},{1,0},{2,3},{3,2},{4,5},{5,4},{6,7},{7,6},{8,9},{9,8},{10,11... | collective-permute-start | bytes 196616 | tf_op jit(solution)/shard_map/ppermute | solution.py:15
  65.7 13.8 %all-to-all-start.1 = ((bf16[16,4,512]{2,1,0:T(4,128)(2,1)}), bf16[16,4,512]{2,1,0:T(4,128)(2,1)S(1)}, u32[]{:S(2)}, u32[]{:S(2)}) async-start(bf16[16,4,512]{2,1,0:T(4,128)(2,1)} %reshape.142), calls=%async_computation.1 | async-start | bytes 131072 | tf_op jit(solution)/shard_map/all_to_all | solution.py:22
  79.6 3.7 %copy-start.21 = (s32[128]{0:T(128)S(1)}, s32[128]{0:T(128)}, u32[]{:S(2)}) copy-start(s32[128]{0:T(128)} %copy-done.20) | copy-start | bytes 1540
  89.5 24.2 %copy-start.12 = (s32[64]{0:T(128)S(1)}, s32[64]{0:T(128)}, u32[]{:S(2)}) copy-start(s32[64]{0:T(128)} %copy-done.11) | copy-start | bytes 772
  89.5 23.6 %collective-permute-start.5 = (bf16[64,512]{1,0:T(8,128)(2,1)S(1)}, bf16[64,512]{1,0:T(8,128)(2,1)S(1)}, u32[]{:S(2)}, u32[]{:S(2)}) collective-permute-start(bf16[64,512]{1,0:T(8,128)(2,1)S(1)} %get-tuple-element.110), channel_id=1, source_target_pairs={{0,1},{1,0},{2,3},{3,2},{4,5},{5,4},{6,7},{7,6},{8,9},{9,8},{10,11... | collective-permute-start | bytes 196616 | tf_op jit(solution)/shard_map/ppermute | solution.py:15
  90.2 23.5 %all-to-all-start.2 = ((bf16[16,4,512]{2,1,0:T(4,128)(2,1)}), bf16[16,4,512]{2,1,0:T(4,128)(2,1)S(1)}, u32[]{:S(2)}, u32[]{:S(2)}) async-start(bf16[16,4,512]{2,1,0:T(4,128)(2,1)} %convert_element_type.132), calls=%async_computation.2 | async-start | bytes 131072 | tf_op jit(solution)/shard_map/all_to_all | solution.py:22
  98.6 23.8 %collective-permute-start.3 = (bf16[64,512]{1,0:T(8,128)(2,1)}, bf16[64,512]{1,0:T(8,128)(2,1)}, u32[]{:S(2)}, u32[]{:S(2)}) collective-permute-start(bf16[64,512]{1,0:T(8,128)(2,1)} %get-tuple-element.130), channel_id=1, source_target_pairs={{0,1},{1,0},{2,3},{3,2},{4,5},{5,4},{6,7},{7,6},{8,9},{9,8},{10,11... | collective-permute-start | bytes 196616 | tf_op jit(solution)/shard_map/ppermute | solution.py:15
  121.7 18.0 %copy-start.22 = (s32[128]{0:T(128)S(1)}, s32[128]{0:T(128)}, u32[]{:S(2)}) copy-start(s32[128]{0:T(128)} %copy-done.20) | copy-start | bytes 1540
  122.4 15.2 %collective-permute-start.6 = (bf16[64,512]{1,0:T(8,128)(2,1)}, bf16[64,512]{1,0:T(8,128)(2,1)}, u32[]{:S(2)}, u32[]{:S(2)}) collective-permute-start(bf16[64,512]{1,0:T(8,128)(2,1)} %get-tuple-element.107), channel_id=1, source_target_pairs={{0,1},{1,0},{2,3},{3,2},{4,5},{5,4},{6,7},{7,6},{8,9},{9,8},{10,11... | collective-permute-start | bytes 196616 | tf_op jit(solution)/shard_map/ppermute | solution.py:15
  123.9 14.6 %all-to-all-start.3 = ((bf16[16,4,512]{2,1,0:T(4,128)(2,1)}), bf16[16,4,512]{2,1,0:T(4,128)(2,1)S(1)}, u32[]{:S(2)}, u32[]{:S(2)}) async-start(bf16[16,4,512]{2,1,0:T(4,128)(2,1)} %convert_element_type.136), calls=%async_computation.3 | async-start | bytes 131072 | tf_op jit(solution)/shard_map/all_to_all | solution.py:22
  143.5 4.3 %copy-start.2 = (bf16[512,512]{1,0:T(8,128)(2,1)S(1)}, bf16[512,512]{1,0:T(8,128)(2,1)}, u32[]{:S(2)}) copy-start(bf16[512,512]{1,0:T(8,128)(2,1)} %get-tuple-element.143) | copy-start | bytes 1572868
  143.5 4.3 %copy-start.5 = (bf16[1024,512]{1,0:T(8,128)(2,1)S(1)}, bf16[1024,512]{1,0:T(8,128)(2,1)}, u32[]{:S(2)}) copy-start(bf16[1024,512]{1,0:T(8,128)(2,1)} %param.18) | copy-start | bytes 3145732
  147.7 9.1 %collective-permute-start.7 = (bf16[64,512]{1,0:T(8,128)(2,1)S(1)}, bf16[64,512]{1,0:T(8,128)(2,1)S(1)}, u32[]{:S(2)}, u32[]{:S(2)}) collective-permute-start(bf16[64,512]{1,0:T(8,128)(2,1)S(1)} %get-tuple-element.104), channel_id=1, source_target_pairs={{0,1},{1,0},{2,3},{3,2},{4,5},{5,4},{6,7},{7,6},{8,9},{9,8},{10,11... | collective-permute-start | bytes 196616 | tf_op jit(solution)/shard_map/ppermute | solution.py:15
  147.8 9.1 %copy-start.19 = (s32[2]{0:T(128)S(1)}, s32[2]{0:T(128)}, u32[]{:S(2)}) copy-start(s32[2]{0:T(128)} %iota_multiply_fusion) | copy-start | bytes 28
  162.1 4.0 %copy-start.7 = (bf16[1024,512]{1,0:T(8,128)(2,1)S(1)}, bf16[1024,512]{1,0:T(8,128)(2,1)}, u32[]{:S(2)}) copy-start(bf16[1024,512]{1,0:T(8,128)(2,1)} %param.23) | copy-start | bytes 3145732
  (13 other events, 24.5 us)

commit v3 on v2

v3 whole, which is shorter than its diff:
```python
import functools

import jax
import jax.numpy as jnp
from jax import lax
from jax.experimental import pallas as pl
from jax.experimental.pallas import tpu as pltpu
from jax.sharding import PartitionSpec as P

BF = jnp.bfloat16
F32 = jnp.float32
VMEM_LIMIT = 24 * 1024 * 1024


def mm(a, b):
    return jnp.dot(a, b, preferred_element_type=F32)


def mm_t(a, b):
    return lax.dot_general(a, b, (((1,), (1,)), ((), ())), preferred_element_type=F32)


def silu_pair(value):
    sigma = 1.0 / (1.0 + jnp.exp(-value))
    message = value * sigma
    return message, sigma + message * (1.0 - sigma)


def pick(rows, wanted):
    places = lax.broadcasted_iota(jnp.int32, (rows, wanted.shape[1]), 0)
    return (places == wanted).astype(F32).astype(BF)


def counts(entries, first, columns):
    rows, degree = entries.shape
    places = lax.broadcasted_iota(jnp.int32, (rows, columns), 1) + first
    total = jnp.zeros((rows, columns), F32)
    for k in range(degree):
        total = total + (places == entries[:, k : k + 1]).astype(F32)
    return total.astype(BF)


def call(body, out_shapes, flops, *args, scratch=()):
    shapes = [jax.ShapeDtypeStruct(s, t) for s, t in out_shapes]
    size = sum(a.size * a.dtype.itemsize for a in args)
    size += sum(s.size * s.dtype.itemsize for s in shapes)
    return pl.pallas_call(
        body,
        out_shape=shapes,
        in_specs=[pl.BlockSpec(memory_space=pltpu.VMEM) for _ in args],
        out_specs=[pl.BlockSpec(memory_space=pltpu.VMEM) for _ in shapes],
        scratch_shapes=list(scratch),
        compiler_params=pltpu.CompilerParams(vmem_limit_bytes=VMEM_LIMIT),
        cost_estimate=pl.CostEstimate(flops=flops, bytes_accessed=size, transcendentals=0),
    )(*args)


def grid_send(latent, lists, outer, inner):
    half = outer.shape[0]
    chosen = pick(latent.shape[0], lists[...]).T
    rows = mm(chosen, latent[...]).astype(BF)
    outer[...] = rows[:half]
    inner[...] = rows[half:]


def encoder_local(latent, weight, mesh, entries, lists, near, rim, rim_t, slope, chosen, chosen_t):
    grid_rows = latent.shape[0]
    message, gradient = silu_pair(mm(latent[...], weight[...]))
    slope[...] = gradient.astype(BF)
    own = counts(entries[...], 0, grid_rows)
    near[...] = mesh[...].astype(F32) + mm(own, message.astype(BF))
    side = counts(entries[...], grid_rows, rim.shape[1])
    rim[...] = side
    rim_t[...] = side.T
    selected = pick(mesh.shape[0], lists[...])
    chosen[...] = selected
    chosen_t[...] = selected.T


def split_far(far, rows, scratch):
    scratch[...] = rows
    for peer in range(far.shape[0]):
        far[peer] = scratch[peer * far.shape[1] : (peer + 1) * far.shape[1]].astype(BF)


def first_hidden(near, rim, outer_in, inner_in, encoder, weight, chosen_t, hidden, message, slope, outer, inner, far, scratch):
    half = outer_in.shape[0]
    arrived = jnp.concatenate([outer_in[...], inner_in[...]], axis=0)
    far_message = silu_pair(mm(arrived, encoder[...]))[0].astype(BF)
    state = (near[...] + mm(rim[...], far_message)).astype(BF)
    hidden[...] = state
    value, gradient = silu_pair(mm(state, weight[...]))
    value = value.astype(BF)
    message[...] = value
    slope[...] = gradient
    slots = far.shape[0] * far.shape[1]
    rows = mm(chosen_t[...], value)
    outer[...] = rows[:half].astype(BF)
    inner[...] = rows[half : 2 * half].astype(BF)
    split_far(far, rows[2 * half : 2 * half + slots], scratch)


def mesh_tables(entries, own, rim, far, back_t):
    rows = own.shape[0]
    width = rim.shape[1]
    own[...] = counts(entries[...], 0, rows)
    side = counts(entries[...], rows, width)
    distant = counts(entries[...], rows + width, back_t.shape[0] - width)
    rim[...] = side
    far[...] = distant[:, : far.shape[1]]
    back_t[:width] = side.T
    back_t[width:] = distant.T


def decoder_back(entries, cotangent, own, rim, near, outer, inner):
    rows = near.shape[0]
    half = outer.shape[0]
    mine = counts(entries[...], 0, rows)
    side = counts(entries[...], rows, 2 * half)
    own[...] = mine
    rim[...] = side
    grads = cotangent[...]
    near[...] = mm(mine.T, grads)
    back = mm(side.T, grads).astype(BF)
    outer[...] = back[:half]
    inner[...] = back[half:]


def layer_local(hidden, own, message, near, *, scale):
    near[...] = hidden[...].astype(F32) + scale * mm(own[...], message[...])


def join(near, rim, far, outer_in, inner_in, far_in, scale):
    arrived = jnp.concatenate([outer_in, inner_in], axis=0)
    total = mm(rim[...], arrived) + mm(far[...], far_in[...])
    return (near[...] + scale * total).astype(BF)


def next_hidden(near, rim, far_counts, outer_in, inner_in, far_in, weight, chosen_t, outer_extra, inner_extra,
                hidden, message, slope, outer, inner, far, scratch, *, scale):
    half = outer_in.shape[0]
    state = join(near, rim, far_counts, outer_in[...], inner_in[...], far_in, scale)
    hidden[...] = state
    value, gradient = silu_pair(mm(state, weight[...]))
    value = value.astype(BF)
    message[...] = value
    slope[...] = gradient
    slots = far.shape[0] * far.shape[1]
    rows = mm(chosen_t[...], value)
    outer[:half] = rows[:half].astype(BF)
    inner[:half] = rows[half : 2 * half].astype(BF)
    outer[half:] = outer_extra[...]
    inner[half:] = inner_extra[...]
    split_far(far, rows[2 * half : 2 * half + slots], scratch)


def turn(near, rim, far_counts, outer_in, inner_in, far_in, weight, chosen, chosen_t, back_t, back_near,
         message, grad, outer, inner, far, scratch, *, scale):
    half = outer_in.shape[0] // 2
    state = join(near, rim, far_counts, outer_in[:half], inner_in[:half], far_in, scale)
    value, gradient = silu_pair(mm(state, weight[...]))
    value = value.astype(BF)
    message[...] = value
    returned = jnp.concatenate([outer_in[half:], inner_in[half:]], axis=0)
    back = back_near[...] + mm(chosen[:, : 2 * half], returned)
    change = mm_t((back * gradient).astype(BF), weight[...]).astype(BF)
    grad[...] = change
    slots = far.shape[0] * far.shape[1]
    rows = mm(back_t[...], change)
    outer[:half] = rows[:half].astype(BF)
    inner[:half] = rows[half : 2 * half].astype(BF)
    split_far(far, rows[2 * half : 2 * half + slots], scratch)
    rim_rows = mm(chosen_t[: 2 * half], value).astype(BF)
    outer[half:] = rim_rows[:half]
    inner[half:] = rim_rows[half:]


def back_local(own, grad, near):
    near[...] = lax.dot_general(
        own[...], grad[...], (((0,), (0,)), ((), ())), preferred_element_type=F32
    )


def layer_back(near, chosen, returned, far_in, slope, weight, grad, scale):
    width = returned.shape[0]
    total = near[...] + mm(chosen[:, :width], returned)
    total = total + mm(chosen[:, width : width + far_in.shape[0]], far_in[...])
    change = (total * scale * slope[...]).astype(BF)
    return (grad[...].astype(F32) + mm_t(change, weight[...])).astype(BF)


def middle_back(near, chosen, outer_in, inner_in, far_in, slope, weight, grad, back_t,
                new_grad, outer, inner, far, scratch, *, scale):
    half = outer.shape[0]
    returned = jnp.concatenate([outer_in[:half], inner_in[:half]], axis=0)
    change = layer_back(near, chosen, returned, far_in, slope, weight, grad, scale)
    new_grad[...] = change
    slots = far.shape[0] * far.shape[1]
    rows = mm(back_t[...], change)
    outer[...] = rows[:half].astype(BF)
    inner[...] = rows[half : 2 * half].astype(BF)
    split_far(far, rows[2 * half : 2 * half + slots], scratch)


def last_back(near, chosen, outer_in, inner_in, far_in, slope, weight, grad, grid_rim_t,
              new_grad, outer, inner, *, scale):
    half = outer.shape[0]
    returned = jnp.concatenate([outer_in[...], inner_in[...]], axis=0)
    change = layer_back(near, chosen, returned, far_in, slope, weight, grad, scale)
    new_grad[...] = change
    rows = mm(grid_rim_t[...], change).astype(BF)
    outer[...] = rows[:half]
    inner[...] = rows[half:]


def decode(latent, own, rim, message, outer_in, inner_in, output):
    half = outer_in.shape[0] // 2
    arrived = jnp.concatenate([outer_in[half:], inner_in[half:]], axis=0)
    total = mm(own[...], message[...]) + mm(rim[...], arrived)
    output[...] = (latent[...].astype(F32) + total).astype(BF)


def grid_local(entries, grad, near):
    own = counts(entries[...], 0, near.shape[0])
    near[...] = lax.dot_general(own, grad[...], (((0,), (0,)), ((), ())), preferred_element_type=F32)


def grid_back(near, lists, outer_in, inner_in, slope, weight, cotangent, output):
    returned = jnp.concatenate([outer_in[...], inner_in[...]], axis=0)
    total = near[...] + mm(pick(near.shape[0], lists[...]), returned)
    change = (total * slope[...].astype(F32)).astype(BF)
    output[...] = (cotangent[...].astype(F32) + mm_t(change, weight[...])).astype(BF)


def swap(outer, inner):
    peers = lax.axis_size("dom")
    across = [(i, (i + 1) % peers if i % 2 else (i - 1) % peers) for i in range(peers)]
    within = [(i, i ^ 1) for i in range(peers)]
    return lax.ppermute(outer, "dom", across), lax.ppermute(inner, "dom", within)


def spread(blocks):
    out = lax.all_to_all(blocks, "dom", split_axis=0, concat_axis=0, tiled=True)
    return out.reshape(-1, blocks.shape[2])


def on_device(
    grid_latent,
    mesh_latent,
    encoder_weight,
    processor_weights,
    decoder_weight,
    cotangent,
    grid_halo_rows,
    encoder_neighbours,
    halo_rows,
    far_sources,
    mesh_neighbours,
    decoder_neighbours,
):
    devices = lax.axis_size("dom")
    grid_rows, width = grid_latent.shape
    mesh_rows = mesh_latent.shape[0]
    ghalo = grid_halo_rows.shape[2]
    halo = halo_rows.shape[2]
    cap = far_sources.shape[2]
    slots = devices * cap
    padded = -(-slots // 128) * 128
    scale = 1.0 / mesh_neighbours.shape[1]
    odd = lax.axis_index("dom") % 2 == 1

    def in_order(lists):
        return jnp.where(odd, lists[0, ::-1], lists[0]).reshape(1, -1)

    def remap(entries, rows, size):
        swapped = jnp.where(entries < rows + size, entries + size, entries - size)
        near = (entries < rows) | (entries >= rows + 2 * size)
        return jnp.where(near | jnp.logical_not(odd), entries, swapped)

    def square(rows, depth):
        return 2 * rows * depth * width

    grid_lists = in_order(grid_halo_rows)
    outer, inner = call(
        grid_send, [((ghalo, width), BF)] * 2, square(2 * ghalo, grid_rows), grid_latent, grid_lists
    )
    outer_in, inner_in = swap(outer, inner)

    mesh_lists = jnp.concatenate(
        [in_order(halo_rows), far_sources[0].reshape(1, -1), jnp.full((1, padded - slots), -1, jnp.int32)], axis=1
    )
    listed = 2 * halo + padded
    encoder_entries = remap(encoder_neighbours, grid_rows, ghalo)
    near, grid_rim, grid_rim_t, grid_slope, chosen, chosen_t = call(
        encoder_local,
        [
            ((mesh_rows, width), F32),
            ((mesh_rows, 2 * ghalo), BF),
            ((2 * ghalo, mesh_rows), BF),
            ((grid_rows, width), BF),
            ((mesh_rows, listed), BF),
            ((listed, mesh_rows), BF),
        ],
        square(grid_rows, width) + square(mesh_rows, grid_rows),
        grid_latent, encoder_weight, mesh_latent, encoder_entries, mesh_lists,
    )

    far_shape = ((devices, cap, width), BF)
    state_shape = ((mesh_rows, width), BF)
    total_shape = ((mesh_rows, width), F32)
    rim_shape = ((halo, width), BF)
    wide_shape = ((2 * halo, width), BF)
    staging = [pltpu.VMEM((slots, width), F32)]
    step_flops = 3 * square(mesh_rows, width)
    hidden, message, slope_0, outer, inner, far = call(
        first_hidden,
        [state_shape, state_shape, total_shape, rim_shape, rim_shape, far_shape],
        step_flops,
        near, grid_rim, outer_in, inner_in, encoder_weight, processor_weights[0], chosen_t,
        scratch=staging,
    )
    outer_in, inner_in = swap(outer, inner)
    far_in = spread(far)

    mesh_entries = remap(mesh_neighbours, mesh_rows, halo)
    own, rim, far_counts, back_t = call(
        mesh_tables,
        [
            ((mesh_rows, mesh_rows), BF),
            ((mesh_rows, 2 * halo), BF),
            ((mesh_rows, slots), BF),
            ((listed, mesh_rows), BF),
        ],
        10 * mesh_rows * listed,
        mesh_entries,
    )
    local = functools.partial(layer_local, scale=scale)
    (near,) = call(local, [total_shape], square(mesh_rows, mesh_rows), hidden, own, message)
    decoder_entries = remap(decoder_neighbours, mesh_rows, halo)
    grid_own, decoder_rim, decoder_near, outer_back, inner_back = call(
        decoder_back,
        [
            ((grid_rows, mesh_rows), BF),
            ((grid_rows, 2 * halo), BF),
            total_shape,
            rim_shape,
            rim_shape,
        ],
        2 * square(grid_rows, mesh_rows),
        decoder_entries, cotangent,
    )
    hidden, message, slope_1, outer, inner, far = call(
        functools.partial(next_hidden, scale=scale),
        [state_shape, state_shape, total_shape, wide_shape, wide_shape, far_shape],
        step_flops,
        near, rim, far_counts, outer_in, inner_in, far_in, processor_weights[1], chosen_t, outer_back, inner_back,
        scratch=staging,
    )
    outer_in, inner_in = swap(outer, inner)
    far_in = spread(far)
    (near,) = call(local, [total_shape], square(mesh_rows, mesh_rows), hidden, own, message)
    message, grad, outer, inner, far = call(
        functools.partial(turn, scale=scale),
        [state_shape, state_shape, wide_shape, wide_shape, far_shape],
        2 * step_flops,
        near, rim, far_counts, outer_in, inner_in, far_in, decoder_weight, chosen, chosen_t, back_t, decoder_near,
        scratch=staging,
    )
    outer_in, inner_in = swap(outer, inner)
    far_in = spread(far)
    (near,) = call(back_local, [total_shape], square(mesh_rows, mesh_rows), own, grad)
    outer_decoder, inner_decoder = outer_in, inner_in
    grad, outer, inner, far = call(
        functools.partial(middle_back, scale=scale),
        [state_shape, rim_shape, rim_shape, far_shape],
        step_flops,
        near, chosen, outer_in, inner_in, far_in, slope_1, processor_weights[1], grad, back_t,
        scratch=staging,
    )
    outer_in, inner_in = swap(outer, inner)
    far_in = spread(far)
    (near,) = call(back_local, [total_shape], square(mesh_rows, mesh_rows), own, grad)
    (output,) = call(
        decode,
        [((grid_rows, width), BF)],
        square(grid_rows, mesh_rows),
        grid_latent, grid_own, decoder_rim, message, outer_decoder, inner_decoder,
    )
    mesh_grad, outer, inner = call(
        functools.partial(last_back, scale=scale),
        [state_shape, ((ghalo, width), BF), ((ghalo, width), BF)],
        step_flops,
        near, chosen, outer_in, inner_in, far_in, slope_0, processor_weights[0], grad, grid_rim_t,
    )
    outer_in, inner_in = swap(outer, inner)
    (near,) = call(
        grid_local, [((grid_rows, width), F32)], square(mesh_rows, grid_rows), encoder_entries, mesh_grad
    )
    (grid_grad,) = call(
        grid_back,
        [((grid_rows, width), BF)],
        square(grid_rows, width),
        near, grid_lists, outer_in, inner_in, grid_slope, encoder_weight, cotangent,
    )
    return (output, grid_grad, mesh_grad)


def solution(mesh):
    in_specs = (
        P(("groups", "dom"), None),
        P(("groups", "dom"), None),
        P(),
        P(),
        P(),
        P(("groups", "dom"), None),
        P("dom", None, None),
        P("dom", None),
        P("dom", None, None),
        P("dom", None, None),
        P("dom", None),
        P("dom", None),
    )
    out_specs = (P(("groups", "dom"), None), P(("groups", "dom"), None), P(("groups", "dom"), None))
    return jax.shard_map(
        on_device, mesh=mesh, in_specs=in_specs, out_specs=out_specs, check_vma=False
    )
```

time: 169 us -> 149 us (0.88)
  blocking collectives: 58.7 us -> 0 us
  local copies, waits for them, and re-layouts: 17.2 us -> 62.5 us
  matrix products: 45.2 us -> 0 us
  Pallas kernels: 0 us -> 27.2 us
  other arithmetic: 20.1 us -> 7.38 us
  starting transfers between devices: 25.3 us -> 36.9 us
  waiting for transfers between devices: 0.03 us -> 11.4 us
    all_gather x8 -> x0, blocking collectives: 58.7 us -> none  [exchange(): lax.all_gather(jnp.where(odd, to_right, to_left), 'dom', axis_index_group...]
    unnamed x51 -> x150, local copies, waits for them, and re-layouts: 1.1 us -> 46.8 us
    dot_general x19 -> x0, matrix products: 45.2 us -> none  [the longest x4 12 us: spread_back(): lax.dot_general(counts, values, (((0,), (0,)), ((), ())), preferred_eleme...]
    pallas_call x0 -> x16, Pallas kernels: none -> 27.2 us  [call(): pl.pallas_call(body, out_shape=shapes, in_specs=[pl.BlockSpec(memory_spac...]
    ppermute x8 -> x12, starting transfers between devices: 1.2 us -> 17.1 us  [the longest x6 17.1 us: swap(): lax.ppermute(outer, 'dom', across)]
    all_to_all x4, waiting for transfers between devices: 0.01 us -> 11.4 us  [spread(): out = lax.all_to_all(blocks, 'dom', split_axis=0, concat_axis=0, tiled=True)]
    gather x6 -> x0, local copies, waits for them, and re-layouts: 10.4 us -> none  [the longest x2 3.97 us: on_device(): jnp.take(message, rim_lists, axis=0)]
    select_n x25 -> x4, other arithmetic: 8.55 us -> 2.97 us  [the longest x3 2.27 us: remap(): return jnp.where(near | jnp.logical_not(odd), entries, swapped)]
  transfers between devices with their start and end apart: 12 -> 16, of which waited for: 0 -> 3; matrix products, arithmetic and copies ran while one was open for 22% -> 17% of each run, Pallas kernels for 0% -> 8%
where the time goes in v3:
time: 149 us; the launch traced here: 147 us
  local copies, waits for them, and re-layouts  62.5 us (42%)
  starting transfers between devices  36.9 us (25%)
  Pallas kernels  27.2 us (18%)
  waiting for transfers between devices  11.4 us (8%)
  other arithmetic  7.38 us (5%)
    unnamed x150, local copies, waits for them, and re-layouts  46.8 us
    pallas_call x16, Pallas kernels, call(): pl.pallas_call(body, out_shape=shapes, in_specs=[pl.BlockSpec(memory_spac...  27.2 us
    all_to_all x4, starting transfers between devices, spread(): out = lax.all_to_all(blocks, 'dom', split_axis=0, concat_axis=0, tiled=True)  19.8 us
    ppermute x6, starting transfers between devices, swap(): lax.ppermute(outer, 'dom', across)  17.1 us
    all_to_all x4, waiting for transfers between devices, spread(): out = lax.all_to_all(blocks, 'dom', split_axis=0, concat_axis=0, tiled=True)  11.4 us
    reshape x4, local copies, waits for them, and re-layouts, spread(): return out.reshape(-1, blocks.shape[2])  3.21 us
  transfers between devices with their start and end apart: 16, of which 3 were waited for; matrix products, arithmetic and copies ran while one was open for 17% of the time, Pallas kernels for 8%

profile of v3, /device:TPU:0, one launch (start us, length us, event | category | flops | bytes accessed | tf_op | source)
XLA Modules:
  0.0 146.6 jit_solution(445774572649777785)
XLA Ops:
  5.0 4.8 %collective-permute-start = (bf16[64,512]{1,0:T(8,128)(2,1)}, bf16[64,512]{1,0:T(8,128)(2,1)S(1)}, u32[]{:S(2)}, u32[]{:S(2)}) collective-permute-start(bf16[64,512]{1,0:T(8,128)(2,1)} %get-tuple-element.48), channel_id=1, source_target_pairs={{0,15},{1,2},{2,1},{3,4},{4,3},{5,6},{6,5},{7,8},{8,7},{9,10},{10,... | collective-permute-start | bytes 196616 | tf_op jit(solution)/shard_map/ppermute | solution.py:239
  15.9 1.7 %copy.88 = s32[1024,3]{1,0:T(8,128)} copy(s32[1024,3]{0,1:T(4,128)} %param.23) | data formatting | bytes 24576 | tf_op args[11]
  32.5 2.4 %shard_map.140 = (f32[512,512]{1,0:T(8,128)S(1)}, bf16[512,128]{1,0:T(8,128)(2,1)S(1)}, bf16[128,512]{1,0:T(8,128)(2,1)S(1)}, bf16[1024,512]{1,0:T(8,128)(2,1)S(...) custom-call(bf16[1024,512]{1,0:T(8,128)(2,1)S(1)} %copy-done.1, bf16[512,512]{1,0:T(8,128)(2,1)S(1)} %copy-done.24, ...), custom_call_target="tpu_custom_call" | custom-call | flops 1073741824 | bytes 4989952 | tf_op jit(solution)/shard_map/pallas_call | solution.py:47
  35.9 1.9 %shard_map.142 = (bf16[512,512]{1,0:T(8,128)(2,1)S(1)}, bf16[512,512]{1,0:T(8,128)(2,1)S(1)}, f32[512,512]{1,0:T(8,128)S(1)}, bf16[64,512]{1,0:T(8,128)(2,1)}, b...) custom-call(f32[512,512]{1,0:T(8,128)S(1)} %get-tuple-element.46.near, bf16[512,128]{1,0:T(8,128)(2,1)S(1)} %get-tuple-element.47.rim, ...), custom_call_target="tpu_custom_call" | custom-call | flops 805306368 | bytes 4915200 | tf_op jit(solution)/shard_map/pallas_call | solution.py:47
  40.4 4.1 %all-to-all-start = ((bf16[16,4,512]{2,1,0:T(4,128)(2,1)}), bf16[16,4,512]{2,1,0:T(4,128)(2,1)}, u32[]{:S(2)}, u32[]{:S(2)}) async-start(bf16[16,4,512]{2,1,0:T(4,128)(2,1)} %get-tuple-element.58), calls=%async_computation | async-start | bytes 131072 | tf_op jit(solution)/shard_map/all_to_all | solution.py:243
  44.5 4.3 %collective-permute-start.2 = (bf16[64,512]{1,0:T(8,128)(2,1)}, bf16[64,512]{1,0:T(8,128)(2,1)}, u32[]{:S(2)}, u32[]{:S(2)}) collective-permute-start(bf16[64,512]{1,0:T(8,128)(2,1)} %get-tuple-element.56), channel_id=1, source_target_pairs={{0,15},{1,2},{2,1},{3,4},{4,3},{5,6},{6,5},{7,8},{8,7},{9,10},{10,... | collective-permute-start | bytes 196616 | tf_op jit(solution)/shard_map/ppermute | solution.py:239
  50.1 1.8 %shard_map.139 = (bf16[1024,512]{1,0:T(8,128)(2,1)S(1)}, bf16[1024,128]{1,0:T(8,128)(2,1)S(1)}, f32[512,512]{1,0:T(8,128)S(1)}, bf16[64,512]{1,0:T(8,128)(2,1)S(1)}, bf16[64,512]{1,0:T(8,128)(2,1)S(1)}) custom-call(s32[1024,3]{1,0:T(8,128)S(1)} %select_select_fusion.entries, bf16[1024,512]{1,0:T(8,128)(2,1)S(1)} %copy-done.14), custom_call_target="tpu_custom_call" | custom-call | flops 1073741824 | bytes 3551232 | tf_op jit(solution)/shard_map/pallas_call | solution.py:47
  55.1 1.7 %shard_map.143 = (bf16[512,512]{1,0:T(8,128)(2,1)S(1)}, bf16[512,128]{1,0:T(8,128)(2,1)S(1)}, bf16[512,64]{1,0:T(8,128)(2,1)S(1)}, bf16[256,512]{1,0:T(8,128)(2,1)S(1)}) custom-call(s32[512,8]{1,0:T(8,128)S(1)} %select_select_fusion.1.entries), custom_call_target="tpu_custom_call" | custom-call | flops 1310720 | bytes 999424 | tf_op jit(solution)/shard_map/pallas_call | solution.py:47
  63.6 2.7 %shard_map.145 = (bf16[512,512]{1,0:T(8,128)(2,1)S(1)}, bf16[512,512]{1,0:T(8,128)(2,1)S(1)}, f32[512,512]{1,0:T(8,128)S(1)}, bf16[128,512]{1,0:T(8,128)(2,1)}, ...) custom-call(f32[512,512]{1,0:T(8,128)S(1)} %copy-done.13, bf16[512,128]{1,0:T(8,128)(2,1)S(1)} %get-tuple-element.54.rim, ...), custom_call_target="tpu_custom_call" | custom-call | flops 805306368 | bytes 4784128 | tf_op jit(solution)/shard_map/pallas_call | solution.py:47
  69.6 5.6 %all-to-all-start.1 = ((bf16[16,4,512]{2,1,0:T(4,128)(2,1)}), bf16[16,4,512]{2,1,0:T(4,128)(2,1)S(1)}, u32[]{:S(2)}, u32[]{:S(2)}) async-start(bf16[16,4,512]{2,1,0:T(4,128)(2,1)} %get-tuple-element.65), calls=%async_computation.1 | async-start | bytes 131072 | tf_op jit(solution)/shard_map/all_to_all | solution.py:243
  77.7 4.4 %all-to-all-done.1 = bf16[16,4,512]{2,1,0:T(4,128)(2,1)S(1)} async-done(((bf16[16,4,512]{2,1,0:T(4,128)(2,1)}), bf16[16,4,512]{2,1,0:T(4,128)(2,1)S(1)}, u32[]{:S(2)}, u32[]{:S(2)}) %all-to-all-start.1) | async-done | bytes 65568 | tf_op jit(solution)/shard_map/all_to_all | solution.py:243
  88.1 3.3 %shard_map.147 = (bf16[512,512]{1,0:T(8,128)(2,1)S(1)}, bf16[512,512]{1,0:T(8,128)(2,1)S(1)}, bf16[128,512]{1,0:T(8,128)(2,1)}, bf16[128,512]{1,0:T(8,128)(2,1)}, bf16[16,4,512]{2,1,0:T(4,128)(2,1)}) custom-call(f32[512,512]{1,0:T(8,128)S(1)} %shard_map.146.near, bf16[512,128]{1,0:T(8,128)(2,1)S(1)} %copy-done.49, bf16[512,64]{1,0:T(8,128)(2,1)S(1)} %copy-done.52, ...), custom_call_target="tpu_custom_call" | custom-call | flops 1610612736 | bytes 5308416 | tf_op jit(solution)/shard_map/pallas_call | solution.py:47
  93.3 5.9 %all-to-all-start.2 = ((bf16[16,4,512]{2,1,0:T(4,128)(2,1)}), bf16[16,4,512]{2,1,0:T(4,128)(2,1)}, u32[]{:S(2)}, u32[]{:S(2)}) async-start(bf16[16,4,512]{2,1,0:T(4,128)(2,1)} %get-tuple-element.73), calls=%async_computation.2 | async-start | bytes 131072 | tf_op jit(solution)/shard_map/all_to_all | solution.py:243
  100.8 5.4 %all-to-all-done.2 = bf16[16,4,512]{2,1,0:T(4,128)(2,1)} async-done(((bf16[16,4,512]{2,1,0:T(4,128)(2,1)}), bf16[16,4,512]{2,1,0:T(4,128)(2,1)}, u32[]{:S(2)}, u32[]{:S(2)}) %all-to-all-start.2) | async-done | bytes 65568 | tf_op jit(solution)/shard_map/all_to_all | solution.py:243
  106.2 1.5 %reshape.60.far_in = bf16[64,512]{1,0:T(8,128)(2,1)} reshape(bf16[16,4,512]{2,1,0:T(4,128)(2,1)} %all-to-all-done.2) | data formatting | bytes 131072 | tf_op jit(solution)/shard_map/reshape | solution.py:244
  112.8 1.8 %shard_map.150 = (bf16[512,512]{1,0:T(8,128)(2,1)S(1)}, bf16[64,512]{1,0:T(8,128)(2,1)S(1)}, bf16[64,512]{1,0:T(8,128)(2,1)S(1)}, bf16[16,4,512]{2,1,0:T(4,128)(2,1)S(1)}) custom-call(f32[512,512]{1,0:T(8,128)S(1)} %shard_map.149.near, bf16[512,256]{1,0:T(8,128)(2,1)S(1)} %get-tuple-element.66.chosen, bf16[128,512]{1,0:T(8,128)(2,1)S(1)} %collective-permute-done.6.outer_in, ...), custom_call_target="tpu_custom_call" | custom-call | flops 805306368 | bytes 4718592 | tf_op jit(solution)/shard_map/pallas_call | solution.py:47
  117.3 4.2 %all-to-all-start.3 = ((bf16[16,4,512]{2,1,0:T(4,128)(2,1)}), bf16[16,4,512]{2,1,0:T(4,128)(2,1)}, u32[]{:S(2)}, u32[]{:S(2)}) async-start(bf16[16,4,512]{2,1,0:T(4,128)(2,1)} %copy-done.45), calls=%async_computation.3 | async-start | bytes 131072 | tf_op jit(solution)/shard_map/all_to_all | solution.py:243
  121.4 4.3 %collective-permute-start.8 = (bf16[64,512]{1,0:T(8,128)(2,1)}, bf16[64,512]{1,0:T(8,128)(2,1)}, u32[]{:S(2)}, u32[]{:S(2)}) collective-permute-start(bf16[64,512]{1,0:T(8,128)(2,1)} %copy-done.54), channel_id=1, source_target_pairs={{0,15},{1,2},{2,1},{3,4},{4,3},{5,6},{6,5},{7,8},{8,7},{9,10},{10,... | collective-permute-start | bytes 196616 | tf_op jit(solution)/shard_map/ppermute | solution.py:239
  127.2 1.6 %all-to-all-done.3 = bf16[16,4,512]{2,1,0:T(4,128)(2,1)} async-done(((bf16[16,4,512]{2,1,0:T(4,128)(2,1)}), bf16[16,4,512]{2,1,0:T(4,128)(2,1)}, u32[]{:S(2)}, u32[]{:S(2)}) %all-to-all-start.3) | async-done | bytes 65568 | tf_op jit(solution)/shard_map/all_to_all | solution.py:243
  132.8 2.5 %shard_map.152 = (bf16[512,512]{1,0:T(8,128)(2,1)}, bf16[64,512]{1,0:T(8,128)(2,1)S(1)}, bf16[64,512]{1,0:T(8,128)(2,1)S(1)}) custom-call(f32[512,512]{1,0:T(8,128)S(1)} %shard_map.151.near, bf16[512,256]{1,0:T(8,128)(2,1)S(1)} %get-tuple-element.66.chosen, bf16[64,512]{1,0:T(8,128)(2,1)} %collective-permute-done.8.outer_in, ...), custom_call_target="tpu_custom_call" | custom-call | flops 805306368 | bytes 4390912 | tf_op jit(solution)/shard_map/pallas_call | solution.py:47
  135.3 2.7 %collective-permute-start.10 = (bf16[64,512]{1,0:T(8,128)(2,1)S(1)}, bf16[64,512]{1,0:T(8,128)(2,1)S(1)}, u32[]{:S(2)}, u32[]{:S(2)}) collective-permute-start(bf16[64,512]{1,0:T(8,128)(2,1)S(1)} %get-tuple-element.82), channel_id=1, source_target_pairs={{0,15},{1,2},{2,1},{3,4},{4,3},{5,6},{6,5},{7,8},{8,7},{9,10},{10,... | collective-permute-start | bytes 196616 | tf_op jit(solution)/shard_map/ppermute | solution.py:239
  140.1 2.9 %shard_map.148 = bf16[1024,512]{1,0:T(8,128)(2,1)} custom-call(bf16[1024,512]{1,0:T(8,128)(2,1)S(1)} %copy-done.1, bf16[1024,512]{1,0:T(8,128)(2,1)S(1)} %copy-done.19, bf16[1024,128]{1,0:T(8,128)(2,1)S(1)} %copy-done.39, bf16[512,512]{1,0:T(8,128)(2,1)S(1)} %copy-done.36, bf16[128,512]{1,0:T(8,128)(2,1)S(1)} %collective-permute-done.6.outer_in, ...), custom_call_target="tpu_custom_call" | custom-call | flops 536870912 | bytes 4194304 | tf_op jit(solution)/shard_map/pallas_call | solution.py:47
  143.0 1.5 %shard_map.153.near = f32[1024,512]{1,0:T(8,128)S(1)} custom-call(s32[512,4]{1,0:T(8,128)S(1)} %copy-done.23, bf16[512,512]{1,0:T(8,128)(2,1)S(1)} %copy-done.34), custom_call_target="tpu_custom_call" | custom-call | flops 536870912 | bytes 2629632 | tf_op jit(solution)/shard_map/pallas_call | solution.py:47
  144.6 1.9 %shard_map.154 = bf16[1024,512]{1,0:T(8,128)(2,1)} custom-call(f32[1024,512]{1,0:T(8,128)S(1)} %shard_map.153.near, s32[1,128]{1,0:T(1,128)S(1)} %select_n.69.lists, bf16[64,512]{1,0:T(8,128)(2,1)S(1)} %collective-permute-done.10.outer_in, bf16[64,512]{1,0:T(8,128)(2,1)S(1)} %collective-permute-done.11.inner_in, bf16[1024,512]{1,0:T(8,128)(2,1)S(1)} %copy-done.17, ...), custom_call_target="tpu_custom_call" | custom-call | flops 536870912 | bytes 5898752 | tf_op jit(solution)/shard_map/pallas_call | solution.py:47
  (212 shorter events, 70.5 us)
Async XLA Ops:
  0.6 17.1 %copy-start.72 = (s32[1,16,4]{1,2,0:T(4,128)S(1)}, s32[1,16,4]{1,2,0:T(4,128)}, u32[]{:S(2)}) copy-start(s32[1,16,4]{1,2,0:T(4,128)} %param.21) | copy-start | bytes 772
  5.0 30.9 %collective-permute-start = (bf16[64,512]{1,0:T(8,128)(2,1)}, bf16[64,512]{1,0:T(8,128)(2,1)S(1)}, u32[]{:S(2)}, u32[]{:S(2)}) collective-permute-start(bf16[64,512]{1,0:T(8,128)(2,1)} %get-tuple-element.48), channel_id=1, source_target_pairs={{0,15},{1,2},{2,1},{3,4},{4,3},{5,6},{6,5},{7,8},{8,7},{9,10},{10,... | collective-permute-start | bytes 196616 | tf_op jit(solution)/shard_map/ppermute | solution.py:239
  9.8 26.1 %collective-permute-start.1 = (bf16[64,512]{1,0:T(8,128)(2,1)S(1)}, bf16[64,512]{1,0:T(8,128)(2,1)S(1)}, u32[]{:S(2)}, u32[]{:S(2)}) collective-permute-start(bf16[64,512]{1,0:T(8,128)(2,1)S(1)} %get-tuple-element.49), channel_id=1, source_target_pairs={{0,1},{1,0},{2,3},{3,2},{4,5},{5,4},{6,7},{7,6},{8,9},{9,8},{10,11... | collective-permute-start | bytes 196616 | tf_op jit(solution)/shard_map/ppermute | solution.py:239
  13.3 15.4 %copy-start.67 = (bf16[2,512,512]{2,1,0:T(8,128)(2,1)S(1)}, bf16[2,512,512]{2,1,0:T(8,128)(2,1)}, u32[]{:S(2)}) copy-start(bf16[2,512,512]{2,1,0:T(8,128)(2,1)} %param.15) | copy-start | bytes 3145732
  28.9 30.9 %copy-start.2 = (bf16[512,512]{1,0:T(8,128)(2,1)}, bf16[512,512]{1,0:T(8,128)(2,1)S(1)}, u32[]{:S(2)}) copy-start(bf16[512,512]{1,0:T(8,128)(2,1)S(1)} %get-tuple-element.85.weight) | copy-start | bytes 1572868
  35.8 13.0 %copy-start.43 = (bf16[128,512]{1,0:T(8,128)(2,1)}, bf16[128,512]{1,0:T(8,128)(2,1)S(1)}, u32[]{:S(2)}) copy-start(bf16[128,512]{1,0:T(8,128)(2,1)S(1)} %get-tuple-element.80.grid_rim_t) | copy-start | bytes 393220
  40.4 18.5 %all-to-all-start = ((bf16[16,4,512]{2,1,0:T(4,128)(2,1)}), bf16[16,4,512]{2,1,0:T(4,128)(2,1)}, u32[]{:S(2)}, u32[]{:S(2)}) async-start(bf16[16,4,512]{2,1,0:T(4,128)(2,1)} %get-tuple-element.58), calls=%async_computation | async-start | bytes 131072 | tf_op jit(solution)/shard_map/all_to_all | solution.py:243
  44.5 15.2 %collective-permute-start.2 = (bf16[64,512]{1,0:T(8,128)(2,1)}, bf16[64,512]{1,0:T(8,128)(2,1)}, u32[]{:S(2)}, u32[]{:S(2)}) collective-permute-start(bf16[64,512]{1,0:T(8,128)(2,1)} %get-tuple-element.56), channel_id=1, source_target_pairs={{0,15},{1,2},{2,1},{3,4},{4,3},{5,6},{6,5},{7,8},{8,7},{9,10},{10,... | collective-permute-start | bytes 196616 | tf_op jit(solution)/shard_map/ppermute | solution.py:239
  48.8 10.9 %collective-permute-start.3 = (bf16[64,512]{1,0:T(8,128)(2,1)}, bf16[64,512]{1,0:T(8,128)(2,1)}, u32[]{:S(2)}, u32[]{:S(2)}) collective-permute-start(bf16[64,512]{1,0:T(8,128)(2,1)} %get-tuple-element.57), channel_id=1, source_target_pairs={{0,1},{1,0},{2,3},{3,2},{4,5},{5,4},{6,7},{7,6},{8,9},{9,8},{10,11... | collective-permute-start | bytes 196616 | tf_op jit(solution)/shard_map/ppermute | solution.py:239
  50.0 7.4 %copy-start.27 = (bf16[512,512]{1,0:T(8,128)(2,1)S(1)}, bf16[512,512]{1,0:T(8,128)(2,1)}, u32[]{:S(2)}) copy-start(bf16[512,512]{1,0:T(8,128)(2,1)} %copy-done.26) | copy-start | bytes 1572868
  50.1 7.4 %copy-start.29 = (bf16[512,512]{1,0:T(8,128)(2,1)S(1)}, bf16[512,512]{1,0:T(8,128)(2,1)}, u32[]{:S(2)}) copy-start(bf16[512,512]{1,0:T(8,128)(2,1)} %copy-done.28) | copy-start | bytes 1572868
  57.4 8.9 %copy-start.48 = (bf16[512,128]{1,0:T(8,128)(2,1)}, bf16[512,128]{1,0:T(8,128)(2,1)S(1)}, u32[]{:S(2)}) copy-start(bf16[512,128]{1,0:T(8,128)(2,1)S(1)} %get-tuple-element.54.rim) | copy-start | bytes 393220
  68.9 13.1 %collective-permute-start.4 = (bf16[128,512]{1,0:T(8,128)(2,1)}, bf16[128,512]{1,0:T(8,128)(2,1)}, u32[]{:S(2)}, u32[]{:S(2)}) collective-permute-start(bf16[128,512]{1,0:T(8,128)(2,1)} %get-tuple-element.63), channel_id=1, source_target_pairs={{0,15},{1,2},{2,1},{3,4},{4,3},{5,6},{6,5},{7,8},{8,7},{9,10},{10,... | collective-permute-start | bytes 393224 | tf_op jit(solution)/shard_map/ppermute | solution.py:239
  69.6 12.5 %collective-permute-start.5 = (bf16[128,512]{1,0:T(8,128)(2,1)}, bf16[128,512]{1,0:T(8,128)(2,1)}, u32[]{:S(2)}, u32[]{:S(2)}) collective-permute-start(bf16[128,512]{1,0:T(8,128)(2,1)} %get-tuple-element.64), channel_id=1, source_target_pairs={{0,1},{1,0},{2,3},{3,2},{4,5},{5,4},{6,7},{7,6},{8,9},{9,8},{10,11... | collective-permute-start | bytes 393224 | tf_op jit(solution)/shard_map/ppermute | solution.py:239
  69.6 12.5 %all-to-all-start.1 = ((bf16[16,4,512]{2,1,0:T(4,128)(2,1)}), bf16[16,4,512]{2,1,0:T(4,128)(2,1)S(1)}, u32[]{:S(2)}, u32[]{:S(2)}) async-start(bf16[16,4,512]{2,1,0:T(4,128)(2,1)} %get-tuple-element.65), calls=%async_computation.1 | async-start | bytes 131072 | tf_op jit(solution)/shard_map/all_to_all | solution.py:243
  93.0 14.7 %collective-permute-start.6 = (bf16[128,512]{1,0:T(8,128)(2,1)}, bf16[128,512]{1,0:T(8,128)(2,1)S(1)}, u32[]{:S(2)}, u32[]{:S(2)}) collective-permute-start(bf16[128,512]{1,0:T(8,128)(2,1)} %get-tuple-element.70), channel_id=1, source_target_pairs={{0,15},{1,2},{2,1},{3,4},{4,3},{5,6},{6,5},{7,8},{8,7},{9,10},{10,... | collective-permute-start | bytes 393224 | tf_op jit(solution)/shard_map/ppermute | solution.py:239
  93.3 14.3 %collective-permute-start.7 = (bf16[128,512]{1,0:T(8,128)(2,1)}, bf16[128,512]{1,0:T(8,128)(2,1)}, u32[]{:S(2)}, u32[]{:S(2)}) collective-permute-start(bf16[128,512]{1,0:T(8,128)(2,1)} %get-tuple-element.71), channel_id=1, source_target_pairs={{0,1},{1,0},{2,3},{3,2},{4,5},{5,4},{6,7},{7,6},{8,9},{9,8},{10,11... | collective-permute-start | bytes 393224 | tf_op jit(solution)/shard_map/ppermute | solution.py:239
  93.3 12.9 %all-to-all-start.2 = ((bf16[16,4,512]{2,1,0:T(4,128)(2,1)}), bf16[16,4,512]{2,1,0:T(4,128)(2,1)}, u32[]{:S(2)}, u32[]{:S(2)}) async-start(bf16[16,4,512]{2,1,0:T(4,128)(2,1)} %get-tuple-element.73), calls=%async_computation.2 | async-start | bytes 131072 | tf_op jit(solution)/shard_map/all_to_all | solution.py:243
  117.3 11.5 %all-to-all-start.3 = ((bf16[16,4,512]{2,1,0:T(4,128)(2,1)}), bf16[16,4,512]{2,1,0:T(4,128)(2,1)}, u32[]{:S(2)}, u32[]{:S(2)}) async-start(bf16[16,4,512]{2,1,0:T(4,128)(2,1)} %copy-done.45), calls=%async_computation.3 | async-start | bytes 131072 | tf_op jit(solution)/shard_map/all_to_all | solution.py:243
  121.4 8.2 %collective-permute-start.8 = (bf16[64,512]{1,0:T(8,128)(2,1)}, bf16[64,512]{1,0:T(8,128)(2,1)}, u32[]{:S(2)}, u32[]{:S(2)}) collective-permute-start(bf16[64,512]{1,0:T(8,128)(2,1)} %copy-done.54), channel_id=1, source_target_pairs={{0,15},{1,2},{2,1},{3,4},{4,3},{5,6},{6,5},{7,8},{8,7},{9,10},{10,... | collective-permute-start | bytes 196616 | tf_op jit(solution)/shard_map/ppermute | solution.py:239
  125.7 3.9 %collective-permute-start.9 = (bf16[64,512]{1,0:T(8,128)(2,1)}, bf16[64,512]{1,0:T(8,128)(2,1)}, u32[]{:S(2)}, u32[]{:S(2)}) collective-permute-start(bf16[64,512]{1,0:T(8,128)(2,1)} %copy-done.53), channel_id=1, source_target_pairs={{0,1},{1,0},{2,3},{3,2},{4,5},{5,4},{6,7},{7,6},{8,9},{9,8},{10,11... | collective-permute-start | bytes 196616 | tf_op jit(solution)/shard_map/ppermute | solution.py:239
  132.8 5.2 %copy-start.19 = (bf16[1024,512]{1,0:T(8,128)(2,1)S(1)}, bf16[1024,512]{1,0:T(8,128)(2,1)}, u32[]{:S(2)}) copy-start(bf16[1024,512]{1,0:T(8,128)(2,1)} %copy-done.18) | copy-start | bytes 3145732
  135.3 9.2 %collective-permute-start.10 = (bf16[64,512]{1,0:T(8,128)(2,1)S(1)}, bf16[64,512]{1,0:T(8,128)(2,1)S(1)}, u32[]{:S(2)}, u32[]{:S(2)}) collective-permute-start(bf16[64,512]{1,0:T(8,128)(2,1)S(1)} %get-tuple-element.82), channel_id=1, source_target_pairs={{0,15},{1,2},{2,1},{3,4},{4,3},{5,6},{6,5},{7,8},{8,7},{9,10},{10,... | collective-permute-start | bytes 196616 | tf_op jit(solution)/shard_map/ppermute | solution.py:239
  138.0 6.5 %collective-permute-start.11 = (bf16[64,512]{1,0:T(8,128)(2,1)S(1)}, bf16[64,512]{1,0:T(8,128)(2,1)S(1)}, u32[]{:S(2)}, u32[]{:S(2)}) collective-permute-start(bf16[64,512]{1,0:T(8,128)(2,1)S(1)} %get-tuple-element.83), channel_id=1, source_target_pairs={{0,1},{1,0},{2,3},{3,2},{4,5},{5,4},{6,7},{7,6},{8,9},{9,8},{10,11... | collective-permute-start | bytes 196616 | tf_op jit(solution)/shard_map/ppermute | solution.py:239
  (65 other events, 88.4 us)

commit v4 on v2

v4 whole, which is shorter than its diff:
```python
import functools

import jax
import jax.numpy as jnp
from jax import lax
from jax.experimental import pallas as pl
from jax.experimental.pallas import tpu as pltpu
from jax.sharding import PartitionSpec as P

BF = jnp.bfloat16
F32 = jnp.float32
VMEM_LIMIT = 24 * 1024 * 1024
PLANE = 4
STAGED = 16


def mm(a, b):
    return jnp.dot(a, b, preferred_element_type=F32)


def mm_t(a, b):
    return lax.dot_general(a, b, (((1,), (1,)), ((), ())), preferred_element_type=F32)


def t_mm(a, b):
    return lax.dot_general(a, b, (((0,), (0,)), ((), ())), preferred_element_type=F32)


def silu_pair(value):
    sigma = 0.5 + 0.5 * jnp.tanh(0.5 * value)
    message = value * sigma
    return message, sigma + message * (1.0 - sigma)


def pick(rows, wanted):
    places = lax.broadcasted_iota(jnp.int32, (rows, wanted.shape[1]), 0)
    return (places == wanted).astype(F32).astype(BF)


def counts_t(columns, first, entries):
    degree, rows = entries.shape
    places = lax.broadcasted_iota(jnp.int32, (columns, rows), 0) + first
    total = jnp.zeros((columns, rows), F32)
    for k in range(degree):
        total = total + (places == entries[k : k + 1]).astype(F32)
    return total.astype(BF)


def side_swap(entries, rows, size, me):
    swapped = jnp.where(entries < rows + size, entries + size, entries - size)
    rim = (entries >= rows) & (entries < rows + 2 * size)
    return jnp.where(rim & (me % 2 == 1), swapped, entries)


def pair_order(lists, me):
    left, right = lists[0, 0:1], lists[0, 1:2]
    odd = me % 2
    return left + odd * (right - left), right + odd * (left - right)


def by_stage(x, devices):
    return (x % PLANE) * (devices // PLANE) + x // PLANE


def call(body, out_shapes, flops, *args, scalars=0):
    shapes = [jax.ShapeDtypeStruct(s, t) for s, t in out_shapes]
    size = sum(a.size * a.dtype.itemsize for a in args)
    size += sum(s.size * s.dtype.itemsize for s in shapes)
    specs = [pl.BlockSpec(memory_space=pltpu.SMEM) for _ in range(scalars)]
    specs += [pl.BlockSpec(memory_space=pltpu.VMEM) for _ in args[scalars:]]
    return pl.pallas_call(
        body,
        out_shape=shapes,
        in_specs=specs,
        out_specs=[pl.BlockSpec(memory_space=pltpu.VMEM) for _ in shapes],
        compiler_params=pltpu.CompilerParams(vmem_limit_bytes=VMEM_LIMIT),
        cost_estimate=pl.CostEstimate(flops=flops, bytes_accessed=size, transcendentals=0),
    )(*args)


def grid_send(me, latent, lists, outer, inner):
    wanted_outer, wanted_inner = pair_order(lists, me[0])
    values = latent[...]
    outer[...] = t_mm(pick(latent.shape[0], wanted_outer), values).astype(BF)
    inner[...] = t_mm(pick(latent.shape[0], wanted_inner), values).astype(BF)


def encoder_local(me, latent, weight, mesh, entries, near, own_t, rim_t, slope, *, size):
    rows = latent.shape[0]
    message, gradient = silu_pair(mm(latent[...], weight[...]))
    slope[...] = gradient.astype(BF)
    columns = side_swap(entries[...], rows, size, me[0])
    own = counts_t(rows, 0, columns)
    own_t[...] = own
    rim_t[...] = counts_t(2 * size, rows, columns)
    near[...] = mesh[...].astype(F32) + t_mm(own, message.astype(BF))


def list_tables(me, lists, far_lists, send, receive, *, rows):
    size = lists.shape[2]
    cap, devices = far_lists.shape
    outer, inner = pair_order(lists, me[0])
    rim = [pick(rows, outer), pick(rows, inner)]
    for k in range(2):
        send[:, k * size : (k + 1) * size] = rim[k]
        receive[:, k * size : (k + 1) * size] = rim[k]
    partner = lax.broadcasted_iota(jnp.int32, (devices, devices * cap), 0)
    place = lax.broadcasted_iota(jnp.int32, (devices, devices * cap), 1)
    if devices == STAGED:
        x = partner ^ me[0]
        send_place, receive_place = by_stage(x, devices) * cap, x * cap
    else:
        send_place, receive_place = partner * cap, partner * cap
    send_far = jnp.zeros((rows, devices * cap), F32)
    receive_far = jnp.zeros((rows, devices * cap), F32)
    for j in range(cap):
        chosen = pick(rows, far_lists[j : j + 1])
        send_far += mm(chosen, (place == send_place + j).astype(F32).astype(BF))
        receive_far += mm(chosen, (place == receive_place + j).astype(F32).astype(BF))
    send[:, 2 * size :] = send_far.astype(BF)
    receive[:, 2 * size :] = receive_far.astype(BF)


def mesh_tables(me, entries, own_t, forth_t, back_t, *, size, devices):
    rows = own_t.shape[0]
    slots = forth_t.shape[0] - 2 * size
    cap = slots // devices
    columns = side_swap(entries[...], rows, size, me[0])
    own_t[...] = counts_t(rows, 0, columns)
    rim = counts_t(2 * size, rows, columns)
    forth_t[: 2 * size] = rim
    back_t[: 2 * size] = rim
    far = jnp.maximum(columns - rows - 2 * size, 0)
    partner, slot = far // cap, far % cap
    if devices == STAGED:
        partner = partner ^ me[0]
        send_place, receive_place = by_stage(partner, devices) * cap + slot, partner * cap + slot
    else:
        send_place, receive_place = far, far
    is_far = columns >= rows + 2 * size
    forth_t[2 * size :] = counts_t(slots, 0, jnp.where(is_far, receive_place, -1))
    back_t[2 * size :] = counts_t(slots, 0, jnp.where(is_far, send_place, -1))


def decoder_back(me, entries, cotangent, own_t, rim_t, near, outer, inner):
    rows = near.shape[0]
    size = outer.shape[0]
    columns = side_swap(entries[...], rows, size, me[0])
    own = counts_t(rows, 0, columns)
    side = counts_t(2 * size, rows, columns)
    own_t[...] = own
    rim_t[...] = side
    grads = cotangent[...]
    near[...] = mm(own, grads)
    back = mm(side, grads).astype(BF)
    outer[...] = back[:size]
    inner[...] = back[size:]


def emit(outs, rows, size, extra=None):
    outer, inner = outs[:2]
    rows = rows.astype(BF)
    outer[:size] = rows[:size]
    inner[:size] = rows[size : 2 * size]
    used = size
    if extra is not None:
        outer[size:] = extra[0]
        inner[size : 2 * size] = extra[1]
        used = 2 * size
    far = rows[2 * size :]
    if len(outs) == 3:
        outs[2][...] = far
        return
    block = far.shape[0] // PLANE
    inner[used:] = far[block : 2 * block]
    outs[2][...] = far[:block]
    for k in range(2, PLANE):
        outs[k + 1][...] = far[k * block : (k + 1) * block]


def arrived(ins, size):
    return jnp.concatenate([ins[0][:size], ins[1][:size]] + [ref[...] for ref in ins[2:]], axis=0)


def shuffle(own, first, second, third, *outs):
    block = own.shape[0]
    parts = [own[...], first[first.shape[0] - block :], second[...], third[...]]
    rows = jnp.concatenate(parts, axis=0)
    count = rows.shape[0]
    cap = count // (PLANE * len(outs))
    target = lax.broadcasted_iota(jnp.int32, (count, count), 0)
    source = lax.broadcasted_iota(jnp.int32, (count, count), 1)
    place, slot = target // cap, target % cap
    wanted = ((place % PLANE) * len(outs) + place // PLANE) * cap + slot
    moved = mm((source == wanted).astype(F32).astype(BF), rows).astype(BF)
    for m, out in enumerate(outs):
        out[...] = moved[m * PLANE * cap : (m + 1) * PLANE * cap]


def layer_local(hidden, own_t, message, near, *, scale):
    near[...] = hidden[...].astype(F32) + scale * t_mm(own_t[...], message[...])


def back_local(own_t, grad, near):
    near[...] = mm(own_t[...], grad[...])


def first_hidden(near, rim_t, outer_in, inner_in, encoder, weight, send, hidden, message, slope, *outs):
    size = outs[0].shape[0]
    incoming = silu_pair(mm(arrived([outer_in, inner_in], outer_in.shape[0]), encoder[...]))[0].astype(BF)
    state = (near[...] + t_mm(rim_t[...], incoming)).astype(BF)
    hidden[...] = state
    value, gradient = silu_pair(mm(state, weight[0]))
    value = value.astype(BF)
    message[...] = value
    slope[...] = gradient
    emit(outs, t_mm(send[...], value), size)


def next_hidden(near, forth_t, weight, send, outer_extra, inner_extra, *refs, ins, layer, scale):
    size = outer_extra.shape[0]
    rows = arrived(refs[:ins], size)
    hidden, message, slope = refs[ins : ins + 3]
    state = (near[...] + scale * t_mm(forth_t[...], rows)).astype(BF)
    hidden[...] = state
    value, gradient = silu_pair(mm(state, weight[layer]))
    value = value.astype(BF)
    message[...] = value
    slope[...] = gradient
    emit(refs[ins + 3 :], t_mm(send[...], value), size, (outer_extra[...], inner_extra[...]))


def turn(near, forth_t, weight, send, receive, back_t, back_near, *refs, ins, scale):
    size = refs[0].shape[0] // 2
    rows = arrived(refs[:ins], size)
    message, grad = refs[ins : ins + 2]
    state = (near[...] + scale * t_mm(forth_t[...], rows)).astype(BF)
    value, gradient = silu_pair(mm(state, weight[...]))
    value = value.astype(BF)
    message[...] = value
    returned = jnp.concatenate([refs[0][size : 2 * size], refs[1][size : 2 * size]], axis=0)
    back = back_near[...] + mm(receive[:, : 2 * size], returned)
    change = mm_t((back * gradient).astype(BF), weight[...]).astype(BF)
    grad[...] = change
    rim = t_mm(send[:, : 2 * size], value).astype(BF)
    emit(refs[ins + 2 :], mm(back_t[...], change), size, (rim[:size], rim[size:]))


def layer_back(near, receive, rows, slope, weight, grad, scale):
    total = near[...] + mm(receive[...], rows)
    change = (total * scale * slope[...]).astype(BF)
    return (grad[...].astype(F32) + mm_t(change, weight)).astype(BF)


def middle_back(near, receive, slope, weight, grad, back_t, *refs, ins, layer, scale):
    size = refs[ins + 1].shape[0]
    rows = arrived(refs[:ins], size)
    change = layer_back(near, receive, rows, slope, weight[layer], grad, scale)
    refs[ins][...] = change
    emit(refs[ins + 1 :], mm(back_t[...], change), size)


def last_back(near, receive, slope, weight, grad, grid_rim_t, *refs, ins, scale):
    new_grad, outer, inner = refs[ins:]
    rows = arrived(refs[:ins], refs[0].shape[0])
    change = layer_back(near, receive, rows, slope, weight[0], grad, scale)
    new_grad[...] = change
    back = mm(grid_rim_t[...], change).astype(BF)
    outer[...] = back[: outer.shape[0]]
    inner[...] = back[outer.shape[0] :]


def decode(latent, own_t, rim_t, message, outer_in, inner_in, output):
    size = outer_in.shape[0] // 2
    incoming = jnp.concatenate([outer_in[size:], inner_in[size : 2 * size]], axis=0)
    total = t_mm(own_t[...], message[...]) + t_mm(rim_t[...], incoming)
    output[...] = (latent[...].astype(F32) + total).astype(BF)


def grid_back(me, near, lists, outer_in, inner_in, slope, weight, cotangent, output):
    outer, inner = pair_order(lists, me[0])
    rows = near.shape[0]
    total = near[...] + mm(pick(rows, outer), outer_in[...]) + mm(pick(rows, inner), inner_in[...])
    change = (total * slope[...].astype(F32)).astype(BF)
    output[...] = (cotangent[...].astype(F32) + mm_t(change, weight[...])).astype(BF)


def toggle(value, bits):
    peers = lax.axis_size("dom")
    return lax.ppermute(value, "dom", [(i, i ^ bits) for i in range(peers)])


def across(value):
    peers = lax.axis_size("dom")
    pairs = [(i, (i + 1) % peers if i % 2 else (i - 1) % peers) for i in range(peers)]
    return lax.ppermute(value, "dom", pairs)


def exchange(outs, cap):
    width = outs[0].shape[1]
    if len(outs) == 3:
        outer, inner, far = outs
        peers = lax.axis_size("dom")
        blocks = far.reshape(peers, cap, width)
        blocks = lax.all_to_all(blocks, "dom", split_axis=0, concat_axis=0, tiled=True)
        return [across(outer), toggle(inner, 1), blocks.reshape(-1, width)]
    outer, inner, own, second, third = outs
    third_in = toggle(third, 3)
    second_in = toggle(second, 2)
    inner_in = toggle(inner, 1)
    outer_in = across(outer)
    columns = STAGED // PLANE
    blocks = call(
        shuffle,
        [((PLANE * cap, width), BF)] * columns,
        2 * (STAGED * cap) ** 2 * width,
        own, inner_in, second_in, third_in,
    )
    moved = [toggle(blocks[m], m * PLANE) for m in reversed(range(1, columns))]
    return [outer_in, inner_in, blocks[0]] + moved[::-1]


def on_device(
    grid_latent,
    mesh_latent,
    encoder_weight,
    processor_weights,
    decoder_weight,
    cotangent,
    grid_halo_rows,
    encoder_neighbours,
    halo_rows,
    far_sources,
    mesh_neighbours,
    decoder_neighbours,
):
    devices = lax.axis_size("dom")
    grid_rows, width = grid_latent.shape
    mesh_rows = mesh_latent.shape[0]
    ghalo = grid_halo_rows.shape[2]
    halo = halo_rows.shape[2]
    cap = far_sources.shape[2]
    slots = devices * cap
    listed = 2 * halo + slots
    scale = 1.0 / mesh_neighbours.shape[1]
    me = lax.axis_index("dom").astype(jnp.int32).reshape(1)

    def square(rows, depth):
        return 2 * rows * depth * width

    def sends(per_side):
        if devices != STAGED:
            return [((per_side, width), BF)] * 2 + [((slots, width), BF)]
        block = slots // PLANE
        return [((per_side, width), BF), ((per_side + block, width), BF)] + [((block, width), BF)] * (PLANE - 1)

    state = ((mesh_rows, width), BF)
    total = ((mesh_rows, width), F32)
    step = 3 * square(mesh_rows, width)

    outer, inner = call(
        grid_send, [((ghalo, width), BF)] * 2, square(2 * ghalo, grid_rows), me, grid_latent, grid_halo_rows,
        scalars=1,
    )
    outer_in, inner_in = across(outer), toggle(inner, 1)

    near, grid_own_t, grid_rim_t, grid_slope = call(
        functools.partial(encoder_local, size=ghalo),
        [total, ((grid_rows, mesh_rows), BF), ((2 * ghalo, mesh_rows), BF), ((grid_rows, width), BF)],
        square(grid_rows, width) + square(mesh_rows, grid_rows),
        me, grid_latent, encoder_weight, mesh_latent, encoder_neighbours.T,
        scalars=1,
    )
    send, receive = call(
        functools.partial(list_tables, rows=mesh_rows),
        [((mesh_rows, listed), BF)] * 2,
        16 * mesh_rows * listed,
        me, halo_rows, far_sources[0].T,
        scalars=1,
    )

    hidden, message, slope_0, *outs = call(
        first_hidden,
        [state, state, total] + sends(halo),
        step,
        near, grid_rim_t, outer_in, inner_in, encoder_weight, processor_weights, send,
    )
    ins = exchange(outs, cap)

    own_t, forth_t, back_t = call(
        functools.partial(mesh_tables, size=halo, devices=devices),
        [((mesh_rows, mesh_rows), BF)] + [((listed, mesh_rows), BF)] * 2,
        30 * mesh_rows * listed,
        me, mesh_neighbours.T,
        scalars=1,
    )
    local = functools.partial(layer_local, scale=scale)
    (near,) = call(local, [total], square(mesh_rows, mesh_rows), hidden, own_t, message)
    decoder_own_t, decoder_rim_t, decoder_near, outer_back, inner_back = call(
        decoder_back,
        [((mesh_rows, grid_rows), BF), ((2 * halo, grid_rows), BF), total, ((halo, width), BF), ((halo, width), BF)],
        square(grid_rows, mesh_rows),
        me, decoder_neighbours.T, cotangent,
        scalars=1,
    )

    hidden, message, slope_1, *outs = call(
        functools.partial(next_hidden, ins=len(ins), layer=1, scale=scale),
        [state, state, total] + sends(2 * halo),
        step,
        near, forth_t, processor_weights, send, outer_back, inner_back, *ins,
    )
    ins = exchange(outs, cap)
    (near,) = call(local, [total], square(mesh_rows, mesh_rows), hidden, own_t, message)

    message, grad, *outs = call(
        functools.partial(turn, ins=len(ins), scale=scale),
        [state, state] + sends(2 * halo),
        2 * step,
        near, forth_t, decoder_weight, send, receive, back_t, decoder_near, *ins,
    )
    ins = exchange(outs, cap)
    outer_decoder, inner_decoder = ins[:2]
    (near,) = call(back_local, [total], square(mesh_rows, mesh_rows), own_t, grad)

    grad, *outs = call(
        functools.partial(middle_back, ins=len(ins), layer=1, scale=scale),
        [state] + sends(halo),
        step,
        near, receive, slope_1, processor_weights, grad, back_t, *ins,
    )
    ins = exchange(outs, cap)
    (near,) = call(back_local, [total], square(mesh_rows, mesh_rows), own_t, grad)
    (output,) = call(
        decode,
        [((grid_rows, width), BF)],
        square(grid_rows, mesh_rows),
        grid_latent, decoder_own_t, decoder_rim_t, message, outer_decoder, inner_decoder,
    )

    mesh_grad, outer, inner = call(
        functools.partial(last_back, ins=len(ins), scale=scale),
        [state, ((ghalo, width), BF), ((ghalo, width), BF)],
        step,
        near, receive, slope_0, processor_weights, grad, grid_rim_t, *ins,
    )
    outer_in, inner_in = across(outer), toggle(inner, 1)
    (near,) = call(
        back_local, [((grid_rows, width), F32)], square(mesh_rows, grid_rows), grid_own_t, mesh_grad
    )
    (grid_grad,) = call(
        grid_back,
        [((grid_rows, width), BF)],
        square(grid_rows, width),
        me, near, grid_halo_rows, outer_in, inner_in, grid_slope, encoder_weight, cotangent,
        scalars=1,
    )
    return (output, grid_grad, mesh_grad)


def solution(mesh):
    in_specs = (
        P(("groups", "dom"), None),
        P(("groups", "dom"), None),
        P(),
        P(),
        P(),
        P(("groups", "dom"), None),
        P("dom", None, None),
        P("dom", None),
        P("dom", None, None),
        P("dom", None, None),
        P("dom", None),
        P("dom", None),
    )
    out_specs = (P(("groups", "dom"), None), P(("groups", "dom"), None), P(("groups", "dom"), None))
    return jax.shard_map(
        on_device, mesh=mesh, in_specs=in_specs, out_specs=out_specs, check_vma=False
    )
```

time: 169 us -> 90.4 us (0.53)
  blocking collectives: 58.7 us -> 0 us
  matrix products: 45.2 us -> 0 us
  waiting for transfers between devices: 0.03 us -> 27.4 us
  other arithmetic: 20.1 us -> 0 us
  Pallas kernels: 0 us -> 19 us
  starting transfers between devices: 25.3 us -> 35.2 us
  local copies, waits for them, and re-layouts: 17.2 us -> 7.3 us
    all_gather x8 -> x0, blocking collectives: 58.7 us -> none  [exchange(): lax.all_gather(jnp.where(odd, to_right, to_left), 'dom', axis_index_group...]
    dot_general x19 -> x0, matrix products: 45.2 us -> none  [the longest x4 12 us: spread_back(): lax.dot_general(counts, values, (((0,), (0,)), ((), ())), preferred_eleme...]
    ppermute x8 -> x32, starting transfers between devices: 1.2 us -> 35.2 us  [the longest x26 21 us: toggle(): return lax.ppermute(value, 'dom', [(i, i ^ bits) for i in range(peers)])]
    ppermute x8 -> x32, waiting for transfers between devices: 0.02 us -> 27.4 us  [the longest x26 24.6 us: toggle(): return lax.ppermute(value, 'dom', [(i, i ^ bits) for i in range(peers)])]
    all_to_all x4 -> x0, starting transfers between devices: 24.1 us -> none  [far_exchange(): lax.all_to_all(blocks, 'dom', split_axis=0, concat_axis=0, tiled=True)]
    pallas_call x0 -> x21, Pallas kernels: none -> 19 us  [call(): pl.pallas_call(body, out_shape=shapes, in_specs=specs, out_specs=[pl.Bloc...]
    gather x6 -> x0, local copies, waits for them, and re-layouts: 10.4 us -> none  [the longest x2 3.97 us: on_device(): jnp.take(message, rim_lists, axis=0)]
    select_n x25 -> x0, other arithmetic: 8.55 us -> none  [the longest x8 4.1 us: exchange(): from_left = jnp.where(odd, near_side, far_side)]
  transfers between devices with their start and end apart: 12 -> 32, of which waited for: 0 -> 9; matrix products, arithmetic and copies ran while one was open for 22% -> 0% of each run, Pallas kernels for 0% -> 12%
where the time goes in v4:
time: 90.4 us; the launch traced here: 90 us
  starting transfers between devices  35.2 us (39%)
  waiting for transfers between devices  27.4 us (30%)
  Pallas kernels  19 us (21%)
  local copies, waits for them, and re-layouts  7.3 us (8%)
  between operations  1.05 us (1%)
    ppermute x26, waiting for transfers between devices, toggle(): return lax.ppermute(value, 'dom', [(i, i ^ bits) for i in range(peers)])  24.6 us
    ppermute x26, starting transfers between devices, toggle(): return lax.ppermute(value, 'dom', [(i, i ^ bits) for i in range(peers)])  21 us
    pallas_call x21, Pallas kernels, call(): pl.pallas_call(body, out_shape=shapes, in_specs=specs, out_specs=[pl.Bloc...  19 us
    ppermute x6, starting transfers between devices, across(): return lax.ppermute(value, 'dom', pairs)  14.1 us
    unnamed x34, local copies, waits for them, and re-layouts  7.3 us
    ppermute x6, waiting for transfers between devices, across(): return lax.ppermute(value, 'dom', pairs)  2.85 us
  transfers between devices with their start and end apart: 32, of which 9 were waited for; matrix products, arithmetic and copies ran while one was open for 0% of the time, Pallas kernels for 12%

profile of v4, /device:TPU:0, one launch (start us, length us, event | category | flops | bytes accessed | tf_op | source)
XLA Modules:
  0.0 90.0 jit_solution(18065135717819691786)
XLA Ops:
  3.1 5.5 %collective-permute-start = (bf16[64,512]{1,0:T(8,128)(2,1)S(1)}, bf16[64,512]{1,0:T(8,128)(2,1)S(1)}, u32[]{:S(2)}, u32[]{:S(2)}) collective-permute-start(bf16[64,512]{1,0:T(8,128)(2,1)S(1)} %get-tuple-element.71), channel_id=1, source_target_pairs={{0,15},{1,2},{2,1},{3,4},{4,3},{5,6},{6,5},{7,8},{8,7},{9,10},{10,... | collective-permute-start | bytes 196616 | tf_op jit(solution)/shard_map/ppermute | solution.py:296
  14.4 2.6 %shard_map.140 = (f32[512,512]{1,0:T(8,128)S(1)}, bf16[1024,512]{1,0:T(8,128)(2,1)S(1)}, bf16[128,512]{1,0:T(8,128)(2,1)S(1)}, bf16[1024,512]{1,0:T(8,128)(2,1)S(1)}) custom-call(s32[1]{0:T(128)} %bitcast.me, bf16[1024,512]{1,0:T(8,128)(2,1)S(1)} %copy-done.2, bf16[512,512]{1,0:T(8,128)(2,1)S(1)} %copy-done.4, bf16[512,512]{1,0:T(8,128)(2,1)S(1)} %copy-done.11, ...), custom_call_target="tpu_custom_call" | custom-call | flops 1073741824 | bytes 5382148 | tf_op jit(solution)/shard_map/pallas_call | solution.py:71
  18.9 1.4 %collective-permute-start.5 = (bf16[16,512]{1,0:T(8,128)(2,1)S(1)}, bf16[16,512]{1,0:T(8,128)(2,1)S(1)}, u32[]{:S(2)}, u32[]{:S(2)}) collective-permute-start(bf16[16,512]{1,0:T(8,128)(2,1)S(1)} %get-tuple-element.84), channel_id=1, source_target_pairs={{0,3},{1,2},{2,1},{3,0},{4,7},{5,6},{6,5},{7,4},{8,11},{9,10},{10,... | collective-permute-start | bytes 49160 | tf_op jit(solution)/shard_map/ppermute | solution.py:290
  26.1 2.3 %collective-permute-start.8 = (bf16[16,512]{1,0:T(8,128)(2,1)S(1)}, bf16[16,512]{1,0:T(8,128)(2,1)S(1)}, u32[]{:S(2)}, u32[]{:S(2)}) collective-permute-start(bf16[16,512]{1,0:T(8,128)(2,1)S(1)} %get-tuple-element.88), channel_id=1, source_target_pairs={{0,12},{1,13},{2,14},{3,15},{4,8},{5,9},{6,10},{7,11},{8,4},{9,5},... | collective-permute-start | bytes 49160 | tf_op jit(solution)/shard_map/ppermute | solution.py:290
  29.5 2.2 %collective-permute-done.8.refs_5_ = bf16[16,512]{1,0:T(8,128)(2,1)S(1)} collective-permute-done((bf16[16,512]{1,0:T(8,128)(2,1)S(1)}, bf16[16,512]{1,0:T(8,128)(2,1)S(1)}, u32[]{:S(2)}, u32[]{:S(2)}) %collective-permute-start.8) | collective-permute-done | bytes 16416 | tf_op jit(solution)/shard_map/ppermute | solution.py:290
  32.7 3.2 %collective-permute-start.9 = (bf16[128,512]{1,0:T(8,128)(2,1)S(1)}, bf16[128,512]{1,0:T(8,128)(2,1)S(1)}, u32[]{:S(2)}, u32[]{:S(2)}) collective-permute-start(bf16[128,512]{1,0:T(8,128)(2,1)S(1)} %get-tuple-element.94), channel_id=1, source_target_pairs={{0,15},{1,2},{2,1},{3,4},{4,3},{5,6},{6,5},{7,8},{8,7},{9,10},{10,... | collective-permute-start | bytes 393224 | tf_op jit(solution)/shard_map/ppermute | solution.py:296
  35.9 4.3 %collective-permute-done.11.second = bf16[16,512]{1,0:T(8,128)(2,1)S(1)} collective-permute-done((bf16[16,512]{1,0:T(8,128)(2,1)S(1)}, bf16[16,512]{1,0:T(8,128)(2,1)S(1)}, u32[]{:S(2)}, u32[]{:S(2)}) %collective-permute-start.11) | collective-permute-done | bytes 16416 | tf_op jit(solution)/shard_map/ppermute | solution.py:290
  40.5 2.3 %collective-permute-start.14 = (bf16[16,512]{1,0:T(8,128)(2,1)S(1)}, bf16[16,512]{1,0:T(8,128)(2,1)S(1)}, u32[]{:S(2)}, u32[]{:S(2)}) collective-permute-start(bf16[16,512]{1,0:T(8,128)(2,1)S(1)} %get-tuple-element.101), channel_id=1, source_target_pairs={{0,8},{1,9},{2,10},{3,11},{4,12},{5,13},{6,14},{7,15},{8,0},{9,1},... | collective-permute-start | bytes 49160 | tf_op jit(solution)/shard_map/ppermute | solution.py:290
  42.8 2.1 %collective-permute-start.15 = (bf16[16,512]{1,0:T(8,128)(2,1)S(1)}, bf16[16,512]{1,0:T(8,128)(2,1)S(1)}, u32[]{:S(2)}, u32[]{:S(2)}) collective-permute-start(bf16[16,512]{1,0:T(8,128)(2,1)S(1)} %get-tuple-element.102), channel_id=1, source_target_pairs={{0,12},{1,13},{2,14},{3,15},{4,8},{5,9},{6,10},{7,11},{8,4},{9,5},... | collective-permute-start | bytes 49160 | tf_op jit(solution)/shard_map/ppermute | solution.py:290
  45.3 3.0 %collective-permute-done.15.refs_5_ = bf16[16,512]{1,0:T(8,128)(2,1)S(1)} collective-permute-done((bf16[16,512]{1,0:T(8,128)(2,1)S(1)}, bf16[16,512]{1,0:T(8,128)(2,1)S(1)}, u32[]{:S(2)}, u32[]{:S(2)}) %collective-permute-start.15) | collective-permute-done | bytes 16416 | tf_op jit(solution)/shard_map/ppermute | solution.py:290
  49.7 2.5 %collective-permute-start.16 = (bf16[128,512]{1,0:T(8,128)(2,1)S(1)}, bf16[128,512]{1,0:T(8,128)(2,1)S(1)}, u32[]{:S(2)}, u32[]{:S(2)}) collective-permute-start(bf16[128,512]{1,0:T(8,128)(2,1)S(1)} %get-tuple-element.104), channel_id=1, source_target_pairs={{0,15},{1,2},{2,1},{3,4},{4,3},{5,6},{6,5},{7,8},{8,7},{9,10},{10,... | collective-permute-start | bytes 393224 | tf_op jit(solution)/shard_map/ppermute | solution.py:296
  52.2 4.8 %collective-permute-done.18.second = bf16[16,512]{1,0:T(8,128)(2,1)S(1)} collective-permute-done((bf16[16,512]{1,0:T(8,128)(2,1)S(1)}, bf16[16,512]{1,0:T(8,128)(2,1)S(1)}, u32[]{:S(2)}, u32[]{:S(2)}) %collective-permute-start.18) | collective-permute-done | bytes 16416 | tf_op jit(solution)/shard_map/ppermute | solution.py:290
  57.3 2.3 %collective-permute-start.21 = (bf16[16,512]{1,0:T(8,128)(2,1)S(1)}, bf16[16,512]{1,0:T(8,128)(2,1)S(1)}, u32[]{:S(2)}, u32[]{:S(2)}) collective-permute-start(bf16[16,512]{1,0:T(8,128)(2,1)S(1)} %get-tuple-element.114), channel_id=1, source_target_pairs={{0,8},{1,9},{2,10},{3,11},{4,12},{5,13},{6,14},{7,15},{8,0},{9,1},... | collective-permute-start | bytes 49160 | tf_op jit(solution)/shard_map/ppermute | solution.py:290
  59.6 2.1 %collective-permute-start.22 = (bf16[16,512]{1,0:T(8,128)(2,1)S(1)}, bf16[16,512]{1,0:T(8,128)(2,1)S(1)}, u32[]{:S(2)}, u32[]{:S(2)}) collective-permute-start(bf16[16,512]{1,0:T(8,128)(2,1)S(1)} %get-tuple-element.115), channel_id=1, source_target_pairs={{0,12},{1,13},{2,14},{3,15},{4,8},{5,9},{6,10},{7,11},{8,4},{9,5},... | collective-permute-start | bytes 49160 | tf_op jit(solution)/shard_map/ppermute | solution.py:290
  62.1 3.0 %collective-permute-done.22.refs_5_ = bf16[16,512]{1,0:T(8,128)(2,1)S(1)} collective-permute-done((bf16[16,512]{1,0:T(8,128)(2,1)S(1)}, bf16[16,512]{1,0:T(8,128)(2,1)S(1)}, u32[]{:S(2)}, u32[]{:S(2)}) %collective-permute-start.22) | collective-permute-done | bytes 16416 | tf_op jit(solution)/shard_map/ppermute | solution.py:290
  66.0 2.0 %collective-permute-start.23 = (bf16[64,512]{1,0:T(8,128)(2,1)S(1)}, bf16[64,512]{1,0:T(8,128)(2,1)S(1)}, u32[]{:S(2)}, u32[]{:S(2)}) collective-permute-start(bf16[64,512]{1,0:T(8,128)(2,1)S(1)} %get-tuple-element.118), channel_id=1, source_target_pairs={{0,15},{1,2},{2,1},{3,4},{4,3},{5,6},{6,5},{7,8},{8,7},{9,10},{10,... | collective-permute-start | bytes 196616 | tf_op jit(solution)/shard_map/ppermute | solution.py:296
  68.1 3.6 %collective-permute-done.25.second = bf16[16,512]{1,0:T(8,128)(2,1)S(1)} collective-permute-done((bf16[16,512]{1,0:T(8,128)(2,1)S(1)}, bf16[16,512]{1,0:T(8,128)(2,1)S(1)}, u32[]{:S(2)}, u32[]{:S(2)}) %collective-permute-start.25) | collective-permute-done | bytes 16416 | tf_op jit(solution)/shard_map/ppermute | solution.py:290
  71.9 2.5 %collective-permute-start.28 = (bf16[16,512]{1,0:T(8,128)(2,1)S(1)}, bf16[16,512]{1,0:T(8,128)(2,1)S(1)}, u32[]{:S(2)}, u32[]{:S(2)}) collective-permute-start(bf16[16,512]{1,0:T(8,128)(2,1)S(1)} %get-tuple-element.125), channel_id=1, source_target_pairs={{0,8},{1,9},{2,10},{3,11},{4,12},{5,13},{6,14},{7,15},{8,0},{9,1},... | collective-permute-start | bytes 49160 | tf_op jit(solution)/shard_map/ppermute | solution.py:290
  74.4 1.9 %collective-permute-start.29 = (bf16[16,512]{1,0:T(8,128)(2,1)S(1)}, bf16[16,512]{1,0:T(8,128)(2,1)S(1)}, u32[]{:S(2)}, u32[]{:S(2)}) collective-permute-start(bf16[16,512]{1,0:T(8,128)(2,1)S(1)} %get-tuple-element.126), channel_id=1, source_target_pairs={{0,12},{1,13},{2,14},{3,15},{4,8},{5,9},{6,10},{7,11},{8,4},{9,5},... | collective-permute-start | bytes 49160 | tf_op jit(solution)/shard_map/ppermute | solution.py:290
  76.9 3.1 %collective-permute-done.29.refs_5_ = bf16[16,512]{1,0:T(8,128)(2,1)S(1)} collective-permute-done((bf16[16,512]{1,0:T(8,128)(2,1)S(1)}, bf16[16,512]{1,0:T(8,128)(2,1)S(1)}, u32[]{:S(2)}, u32[]{:S(2)}) %collective-permute-start.29) | collective-permute-done | bytes 16416 | tf_op jit(solution)/shard_map/ppermute | solution.py:290
  80.0 1.4 %shard_map.157 = (bf16[512,512]{1,0:T(8,128)(2,1)}, bf16[64,512]{1,0:T(8,128)(2,1)S(1)}, bf16[64,512]{1,0:T(8,128)(2,1)S(1)}) custom-call(f32[512,512]{1,0:T(8,128)S(1)} %shard_map.155.near, bf16[512,192]{1,0:T(8,128)(2,1)S(1)} %get-tuple-element.91.receive, f32[512,512]{1,0:T(8,128)S(1)} %get-tuple-element.117.slope, bf16[2,512,512]{2,1,0:T(8,128)(2,1)S(1)} %copy-done, ...), custom_call_target="tpu_custom_call" | custom-call | flops 805306368 | bytes 4866048 | tf_op jit(solution)/shard_map/pallas_call | solution.py:71
  82.2 2.0 %shard_map.151 = bf16[1024,512]{1,0:T(8,128)(2,1)} custom-call(bf16[1024,512]{1,0:T(8,128)(2,1)S(1)} %copy-done.3, bf16[512,1024]{1,0:T(8,128)(2,1)S(1)} %get-tuple-element.67.own_t, bf16[128,1024]{1,0:T(8,128)(2,1)S(1)} %get-tuple-element.68.rim_t, bf16[512,512]{1,0:T(8,128)(2,1)S(1)} %get-tuple-element.103.message, ...), custom_call_target="tpu_custom_call" | custom-call | flops 536870912 | bytes 4210688 | tf_op jit(solution)/shard_map/pallas_call | solution.py:71
  84.9 2.8 %collective-permute-done.30.outer_in = bf16[64,512]{1,0:T(8,128)(2,1)S(1)} collective-permute-done((bf16[64,512]{1,0:T(8,128)(2,1)S(1)}, bf16[64,512]{1,0:T(8,128)(2,1)S(1)}, u32[]{:S(2)}, u32[]{:S(2)}) %collective-permute-start.30) | collective-permute-done | bytes 65568 | tf_op jit(solution)/shard_map/ppermute | solution.py:296
  87.7 2.2 %shard_map.159 = bf16[1024,512]{1,0:T(8,128)(2,1)} custom-call(s32[1]{0:T(128)} %bitcast.me, f32[1024,512]{1,0:T(8,128)S(1)} %shard_map.158.near, s32[1,2,64]{2,1,0:T(2,128)S(1)} %copy-done.10, bf16[64,512]{1,0:T(8,128)(2,1)S(1)} %collective-permute-done.30.outer_in, bf16[64,512]{1,0:T(8,128)(2,1)S(1)} %collective-permute-done.31.inner_in, ...), custom_call_target="tpu_custom_call" | custom-call | flops 536870912 | bytes 5898756 | tf_op jit(solution)/shard_map/pallas_call | solution.py:71
  (95 shorter events, 24.0 us)
Async XLA Ops:
  3.1 14.0 %collective-permute-start = (bf16[64,512]{1,0:T(8,128)(2,1)S(1)}, bf16[64,512]{1,0:T(8,128)(2,1)S(1)}, u32[]{:S(2)}, u32[]{:S(2)}) collective-permute-start(bf16[64,512]{1,0:T(8,128)(2,1)S(1)} %get-tuple-element.71), channel_id=1, source_target_pairs={{0,15},{1,2},{2,1},{3,4},{4,3},{5,6},{6,5},{7,8},{8,7},{9,10},{10,... | collective-permute-start | bytes 196616 | tf_op jit(solution)/shard_map/ppermute | solution.py:296
  8.6 8.5 %collective-permute-start.1 = (bf16[64,512]{1,0:T(8,128)(2,1)S(1)}, bf16[64,512]{1,0:T(8,128)(2,1)S(1)}, u32[]{:S(2)}, u32[]{:S(2)}) collective-permute-start(bf16[64,512]{1,0:T(8,128)(2,1)S(1)} %get-tuple-element.72), channel_id=1, source_target_pairs={{0,1},{1,0},{2,3},{3,2},{4,5},{5,4},{6,7},{7,6},{8,9},{9,8},{10,11... | collective-permute-start | bytes 196616 | tf_op jit(solution)/shard_map/ppermute | solution.py:290
  18.3 5.4 %collective-permute-start.3 = (bf16[80,512]{1,0:T(8,128)(2,1)S(1)}, bf16[80,512]{1,0:T(8,128)(2,1)S(1)}, u32[]{:S(2)}, u32[]{:S(2)}) collective-permute-start(bf16[80,512]{1,0:T(8,128)(2,1)S(1)} %get-tuple-element.81), channel_id=1, source_target_pairs={{0,1},{1,0},{2,3},{3,2},{4,5},{5,4},{6,7},{7,6},{8,9},{9,8},{10,11... | collective-permute-start | bytes 245768 | tf_op jit(solution)/shard_map/ppermute | solution.py:290
  20.3 8.5 %collective-permute-start.2 = (bf16[64,512]{1,0:T(8,128)(2,1)S(1)}, bf16[64,512]{1,0:T(8,128)(2,1)S(1)}, u32[]{:S(2)}, u32[]{:S(2)}) collective-permute-start(bf16[64,512]{1,0:T(8,128)(2,1)S(1)} %get-tuple-element.80), channel_id=1, source_target_pairs={{0,15},{1,2},{2,1},{3,4},{4,3},{5,6},{6,5},{7,8},{8,7},{9,10},{10,... | collective-permute-start | bytes 196616 | tf_op jit(solution)/shard_map/ppermute | solution.py:296
  23.9 4.9 %collective-permute-start.6 = (bf16[16,512]{1,0:T(8,128)(2,1)S(1)}, bf16[16,512]{1,0:T(8,128)(2,1)S(1)}, u32[]{:S(2)}, u32[]{:S(2)}) collective-permute-start(bf16[16,512]{1,0:T(8,128)(2,1)S(1)} %get-tuple-element.86), channel_id=1, source_target_pairs={{0,4},{1,5},{2,6},{3,7},{4,0},{5,1},{6,2},{7,3},{8,12},{9,13},{10,... | collective-permute-start | bytes 49160 | tf_op jit(solution)/shard_map/ppermute | solution.py:290
  26.1 5.5 %collective-permute-start.8 = (bf16[16,512]{1,0:T(8,128)(2,1)S(1)}, bf16[16,512]{1,0:T(8,128)(2,1)S(1)}, u32[]{:S(2)}, u32[]{:S(2)}) collective-permute-start(bf16[16,512]{1,0:T(8,128)(2,1)S(1)} %get-tuple-element.88), channel_id=1, source_target_pairs={{0,12},{1,13},{2,14},{3,15},{4,8},{5,9},{6,10},{7,11},{8,4},{9,5},... | collective-permute-start | bytes 49160 | tf_op jit(solution)/shard_map/ppermute | solution.py:290
  32.6 7.6 %collective-permute-start.10 = (bf16[144,512]{1,0:T(8,128)(2,1)S(1)}, bf16[144,512]{1,0:T(8,128)(2,1)S(1)}, u32[]{:S(2)}, u32[]{:S(2)}) collective-permute-start(bf16[144,512]{1,0:T(8,128)(2,1)S(1)} %get-tuple-element.95), channel_id=1, source_target_pairs={{0,1},{1,0},{2,3},{3,2},{4,5},{5,4},{6,7},{7,6},{8,9},{9,8},{10,11... | collective-permute-start | bytes 442376 | tf_op jit(solution)/shard_map/ppermute | solution.py:290
  32.7 12.6 %collective-permute-start.9 = (bf16[128,512]{1,0:T(8,128)(2,1)S(1)}, bf16[128,512]{1,0:T(8,128)(2,1)S(1)}, u32[]{:S(2)}, u32[]{:S(2)}) collective-permute-start(bf16[128,512]{1,0:T(8,128)(2,1)S(1)} %get-tuple-element.94), channel_id=1, source_target_pairs={{0,15},{1,2},{2,1},{3,4},{4,3},{5,6},{6,5},{7,8},{8,7},{9,10},{10,... | collective-permute-start | bytes 393224 | tf_op jit(solution)/shard_map/ppermute | solution.py:296
  40.4 4.9 %collective-permute-start.13 = (bf16[16,512]{1,0:T(8,128)(2,1)S(1)}, bf16[16,512]{1,0:T(8,128)(2,1)S(1)}, u32[]{:S(2)}, u32[]{:S(2)}) collective-permute-start(bf16[16,512]{1,0:T(8,128)(2,1)S(1)} %get-tuple-element.100), channel_id=1, source_target_pairs={{0,4},{1,5},{2,6},{3,7},{4,0},{5,1},{6,2},{7,3},{8,12},{9,13},{10,... | collective-permute-start | bytes 49160 | tf_op jit(solution)/shard_map/ppermute | solution.py:290
  40.5 4.9 %collective-permute-start.14 = (bf16[16,512]{1,0:T(8,128)(2,1)S(1)}, bf16[16,512]{1,0:T(8,128)(2,1)S(1)}, u32[]{:S(2)}, u32[]{:S(2)}) collective-permute-start(bf16[16,512]{1,0:T(8,128)(2,1)S(1)} %get-tuple-element.101), channel_id=1, source_target_pairs={{0,8},{1,9},{2,10},{3,11},{4,12},{5,13},{6,14},{7,15},{8,0},{9,1},... | collective-permute-start | bytes 49160 | tf_op jit(solution)/shard_map/ppermute | solution.py:290
  42.8 5.5 %collective-permute-start.15 = (bf16[16,512]{1,0:T(8,128)(2,1)S(1)}, bf16[16,512]{1,0:T(8,128)(2,1)S(1)}, u32[]{:S(2)}, u32[]{:S(2)}) collective-permute-start(bf16[16,512]{1,0:T(8,128)(2,1)S(1)} %get-tuple-element.102), channel_id=1, source_target_pairs={{0,12},{1,13},{2,14},{3,15},{4,8},{5,9},{6,10},{7,11},{8,4},{9,5},... | collective-permute-start | bytes 49160 | tf_op jit(solution)/shard_map/ppermute | solution.py:290
  49.6 7.4 %collective-permute-start.17 = (bf16[144,512]{1,0:T(8,128)(2,1)S(1)}, bf16[144,512]{1,0:T(8,128)(2,1)S(1)}, u32[]{:S(2)}, u32[]{:S(2)}) collective-permute-start(bf16[144,512]{1,0:T(8,128)(2,1)S(1)} %get-tuple-element.105), channel_id=1, source_target_pairs={{0,1},{1,0},{2,3},{3,2},{4,5},{5,4},{6,7},{7,6},{8,9},{9,8},{10,11... | collective-permute-start | bytes 442376 | tf_op jit(solution)/shard_map/ppermute | solution.py:290
  49.7 12.4 %collective-permute-start.16 = (bf16[128,512]{1,0:T(8,128)(2,1)S(1)}, bf16[128,512]{1,0:T(8,128)(2,1)S(1)}, u32[]{:S(2)}, u32[]{:S(2)}) collective-permute-start(bf16[128,512]{1,0:T(8,128)(2,1)S(1)} %get-tuple-element.104), channel_id=1, source_target_pairs={{0,15},{1,2},{2,1},{3,4},{4,3},{5,6},{6,5},{7,8},{8,7},{9,10},{10,... | collective-permute-start | bytes 393224 | tf_op jit(solution)/shard_map/ppermute | solution.py:296
  52.2 4.8 %collective-permute-start.18 = (bf16[16,512]{1,0:T(8,128)(2,1)S(1)}, bf16[16,512]{1,0:T(8,128)(2,1)S(1)}, u32[]{:S(2)}, u32[]{:S(2)}) collective-permute-start(bf16[16,512]{1,0:T(8,128)(2,1)S(1)} %get-tuple-element.110), channel_id=1, source_target_pairs={{0,2},{1,3},{2,0},{3,1},{4,6},{5,7},{6,4},{7,5},{8,10},{9,11},{10,... | collective-permute-start | bytes 49160 | tf_op jit(solution)/shard_map/ppermute | solution.py:290
  52.2 4.8 %collective-permute-start.19 = (bf16[16,512]{1,0:T(8,128)(2,1)S(1)}, bf16[16,512]{1,0:T(8,128)(2,1)S(1)}, u32[]{:S(2)}, u32[]{:S(2)}) collective-permute-start(bf16[16,512]{1,0:T(8,128)(2,1)S(1)} %get-tuple-element.111), channel_id=1, source_target_pairs={{0,3},{1,2},{2,1},{3,0},{4,7},{5,6},{6,5},{7,4},{8,11},{9,10},{10,... | collective-permute-start | bytes 49160 | tf_op jit(solution)/shard_map/ppermute | solution.py:290
  57.2 4.9 %collective-permute-start.20 = (bf16[16,512]{1,0:T(8,128)(2,1)S(1)}, bf16[16,512]{1,0:T(8,128)(2,1)S(1)}, u32[]{:S(2)}, u32[]{:S(2)}) collective-permute-start(bf16[16,512]{1,0:T(8,128)(2,1)S(1)} %get-tuple-element.113), channel_id=1, source_target_pairs={{0,4},{1,5},{2,6},{3,7},{4,0},{5,1},{6,2},{7,3},{8,12},{9,13},{10,... | collective-permute-start | bytes 49160 | tf_op jit(solution)/shard_map/ppermute | solution.py:290
  59.6 5.5 %collective-permute-start.22 = (bf16[16,512]{1,0:T(8,128)(2,1)S(1)}, bf16[16,512]{1,0:T(8,128)(2,1)S(1)}, u32[]{:S(2)}, u32[]{:S(2)}) collective-permute-start(bf16[16,512]{1,0:T(8,128)(2,1)S(1)} %get-tuple-element.115), channel_id=1, source_target_pairs={{0,12},{1,13},{2,14},{3,15},{4,8},{5,9},{6,10},{7,11},{8,4},{9,5},... | collective-permute-start | bytes 49160 | tf_op jit(solution)/shard_map/ppermute | solution.py:290
  65.9 5.8 %collective-permute-start.24 = (bf16[80,512]{1,0:T(8,128)(2,1)S(1)}, bf16[80,512]{1,0:T(8,128)(2,1)S(1)}, u32[]{:S(2)}, u32[]{:S(2)}) collective-permute-start(bf16[80,512]{1,0:T(8,128)(2,1)S(1)} %get-tuple-element.119), channel_id=1, source_target_pairs={{0,1},{1,0},{2,3},{3,2},{4,5},{5,4},{6,7},{7,6},{8,9},{9,8},{10,11... | collective-permute-start | bytes 245768 | tf_op jit(solution)/shard_map/ppermute | solution.py:290
  66.0 10.9 %collective-permute-start.23 = (bf16[64,512]{1,0:T(8,128)(2,1)S(1)}, bf16[64,512]{1,0:T(8,128)(2,1)S(1)}, u32[]{:S(2)}, u32[]{:S(2)}) collective-permute-start(bf16[64,512]{1,0:T(8,128)(2,1)S(1)} %get-tuple-element.118), channel_id=1, source_target_pairs={{0,15},{1,2},{2,1},{3,4},{4,3},{5,6},{6,5},{7,8},{8,7},{9,10},{10,... | collective-permute-start | bytes 196616 | tf_op jit(solution)/shard_map/ppermute | solution.py:296
  71.8 5.0 %collective-permute-start.27 = (bf16[16,512]{1,0:T(8,128)(2,1)S(1)}, bf16[16,512]{1,0:T(8,128)(2,1)S(1)}, u32[]{:S(2)}, u32[]{:S(2)}) collective-permute-start(bf16[16,512]{1,0:T(8,128)(2,1)S(1)} %get-tuple-element.124), channel_id=1, source_target_pairs={{0,4},{1,5},{2,6},{3,7},{4,0},{5,1},{6,2},{7,3},{8,12},{9,13},{10,... | collective-permute-start | bytes 49160 | tf_op jit(solution)/shard_map/ppermute | solution.py:290
  71.9 5.0 %collective-permute-start.28 = (bf16[16,512]{1,0:T(8,128)(2,1)S(1)}, bf16[16,512]{1,0:T(8,128)(2,1)S(1)}, u32[]{:S(2)}, u32[]{:S(2)}) collective-permute-start(bf16[16,512]{1,0:T(8,128)(2,1)S(1)} %get-tuple-element.125), channel_id=1, source_target_pairs={{0,8},{1,9},{2,10},{3,11},{4,12},{5,13},{6,14},{7,15},{8,0},{9,1},... | collective-permute-start | bytes 49160 | tf_op jit(solution)/shard_map/ppermute | solution.py:290
  74.4 5.5 %collective-permute-start.29 = (bf16[16,512]{1,0:T(8,128)(2,1)S(1)}, bf16[16,512]{1,0:T(8,128)(2,1)S(1)}, u32[]{:S(2)}, u32[]{:S(2)}) collective-permute-start(bf16[16,512]{1,0:T(8,128)(2,1)S(1)} %get-tuple-element.126), channel_id=1, source_target_pairs={{0,12},{1,13},{2,14},{3,15},{4,8},{5,9},{6,10},{7,11},{8,4},{9,5},... | collective-permute-start | bytes 49160 | tf_op jit(solution)/shard_map/ppermute | solution.py:290
  81.3 6.4 %collective-permute-start.30 = (bf16[64,512]{1,0:T(8,128)(2,1)S(1)}, bf16[64,512]{1,0:T(8,128)(2,1)S(1)}, u32[]{:S(2)}, u32[]{:S(2)}) collective-permute-start(bf16[64,512]{1,0:T(8,128)(2,1)S(1)} %get-tuple-element.128), channel_id=1, source_target_pairs={{0,15},{1,2},{2,1},{3,4},{4,3},{5,6},{6,5},{7,8},{8,7},{9,10},{10,... | collective-permute-start | bytes 196616 | tf_op jit(solution)/shard_map/ppermute | solution.py:296
  81.3 6.4 %collective-permute-start.31 = (bf16[64,512]{1,0:T(8,128)(2,1)S(1)}, bf16[64,512]{1,0:T(8,128)(2,1)S(1)}, u32[]{:S(2)}, u32[]{:S(2)}) collective-permute-start(bf16[64,512]{1,0:T(8,128)(2,1)S(1)} %get-tuple-element.129), channel_id=1, source_target_pairs={{0,1},{1,0},{2,3},{3,2},{4,5},{5,4},{6,7},{7,6},{8,9},{9,8},{10,11... | collective-permute-start | bytes 196616 | tf_op jit(solution)/shard_map/ppermute | solution.py:290
  (25 other events, 108.1 us)

commit v5 on v4

--- a/solution.py
+++ b/solution.py
@@ -12,6 +12,7 @@
 VMEM_LIMIT = 24 * 1024 * 1024
 PLANE = 4
 STAGED = 16
+CHUNKS = 4
 
 
 def mm(a, b):
@@ -62,41 +63,84 @@
     return (x % PLANE) * (devices // PLANE) + x // PLANE
 
 
-def call(body, out_shapes, flops, *args, scalars=0):
+def call(body, out_shapes, flops, *args, scalars=0, hbm=0, free=0, hbm_out=0, scratch=()):
     shapes = [jax.ShapeDtypeStruct(s, t) for s, t in out_shapes]
     size = sum(a.size * a.dtype.itemsize for a in args)
     size += sum(s.size * s.dtype.itemsize for s in shapes)
-    specs = [pl.BlockSpec(memory_space=pltpu.SMEM) for _ in range(scalars)]
-    specs += [pl.BlockSpec(memory_space=pltpu.VMEM) for _ in args[scalars:]]
+    places = [pltpu.SMEM] * scalars + [pltpu.HBM] * hbm + [pltpu.VMEM] * (len(args) - scalars - hbm - free)
+    places += [pl.ANY] * free
+    out_places = [pltpu.HBM] * hbm_out + [pltpu.VMEM] * (len(shapes) - hbm_out)
     return pl.pallas_call(
         body,
         out_shape=shapes,
-        in_specs=specs,
-        out_specs=[pl.BlockSpec(memory_space=pltpu.VMEM) for _ in shapes],
+        in_specs=[pl.BlockSpec(memory_space=place) for place in places],
+        out_specs=[pl.BlockSpec(memory_space=place) for place in out_places],
+        scratch_shapes=list(scratch),
         compiler_params=pltpu.CompilerParams(vmem_limit_bytes=VMEM_LIMIT),
         cost_estimate=pl.CostEstimate(flops=flops, bytes_accessed=size, transcendentals=0),
     )(*args)
 
 
-def grid_send(me, latent, lists, outer, inner):
-    wanted_outer, wanted_inner = pair_order(lists, me[0])
-    values = latent[...]
-    outer[...] = t_mm(pick(latent.shape[0], wanted_outer), values).astype(BF)
-    inner[...] = t_mm(pick(latent.shape[0], wanted_inner), values).astype(BF)
-
-
-def encoder_local(me, latent, weight, mesh, entries, near, own_t, rim_t, slope, *, size):
+def copies_of(arrays):
+    return [pltpu.VMEM(a.shape, a.dtype) for a in arrays]
+
+
+def fetch(sources, targets, sems):
+    copies = [pltpu.make_async_copy(s, t, sems.at[i]) for i, (s, t) in enumerate(zip(sources, targets))]
+    for copy in copies:
+        copy.start()
+    return copies
+
+
+def row_chunks(rows):
+    step = rows // CHUNKS
+    return [pl.ds(i * step, step) for i in range(CHUNKS)]
+
+
+def grid_send(me, latent, lists, outer, inner, values, wanted, sems):
+    parts = row_chunks(latent.shape[0])
+    sources = [lists] + [latent.at[part] for part in parts]
+    copies = fetch(sources, [wanted] + [values.at[part] for part in parts], sems)
+    copies[0].wait()
+    wanted_outer, wanted_inner = pair_order(wanted, me[0])
+    step = latent.shape[0] // CHUNKS
+    outer_rows = inner_rows = 0.0
+    for i, part in enumerate(parts):
+        copies[i + 1].wait()
+        chunk = values[part]
+        outer_rows += t_mm(pick(step, wanted_outer - i * step), chunk)
+        inner_rows += t_mm(pick(step, wanted_inner - i * step), chunk)
+    outer[...] = outer_rows.astype(BF)
+    inner[...] = inner_rows.astype(BF)
+
+
+def encoder_local(me, entries, mesh_entries, lists, far_lists, weight, latent, mesh,
+                  near, grid_own_t, grid_rim_t, slope, send, receive, own_t, forth_t, back_t,
+                  entries_v, mesh_entries_v, lists_v, far_lists_v, weight_v, latent_v, mesh_v, sems, *, size):
+    sources = [entries, mesh_entries, lists, far_lists, weight, latent, mesh]
+    targets = [entries_v, mesh_entries_v, lists_v, far_lists_v, weight_v, latent_v, mesh_v]
+    copies = fetch(sources, targets, sems)
     rows = latent.shape[0]
-    message, gradient = silu_pair(mm(latent[...], weight[...]))
+    copies[0].wait()
+    columns = side_swap(entries_v[...], rows, size, me[0])
+    own = counts_t(rows, 0, columns)
+    grid_own_t[...] = own
+    grid_rim_t[...] = counts_t(2 * size, rows, columns)
+    copies[1].wait()
+    mesh_tables(me, mesh_entries_v, own_t, forth_t, back_t, lists.shape[2], far_lists.shape[1])
+    copies[2].wait()
+    copies[3].wait()
+    list_tables(me, lists_v, far_lists_v, send, receive)
+    copies[4].wait()
+    copies[5].wait()
+    message, gradient = silu_pair(mm(latent_v[...], weight_v[...]))
     slope[...] = gradient.astype(BF)
-    columns = side_swap(entries[...], rows, size, me[0])
-    own = counts_t(rows, 0, columns)
-    own_t[...] = own
-    rim_t[...] = counts_t(2 * size, rows, columns)
-    near[...] = mesh[...].astype(F32) + t_mm(own, message.astype(BF))
-
-
-def list_tables(me, lists, far_lists, send, receive, *, rows):
+    copies[6].wait()
+    near[...] = mesh_v[...].astype(F32) + t_mm(own, message.astype(BF))
+
+
+def list_tables(me, lists, far_lists, send, receive):
+    rows = send.shape[0]
     size = lists.shape[2]
     cap, devices = far_lists.shape
     outer, inner = pair_order(lists, me[0])
@@ -121,7 +165,7 @@
     receive[:, 2 * size :] = receive_far.astype(BF)
 
 
-def mesh_tables(me, entries, own_t, forth_t, back_t, *, size, devices):
+def mesh_tables(me, entries, own_t, forth_t, back_t, size, devices):
     rows = own_t.shape[0]
     slots = forth_t.shape[0] - 2 * size
     cap = slots // devices
@@ -158,31 +202,45 @@
 
 
 def emit(outs, rows, size, extra=None):
-    outer, inner = outs[:2]
+    inner = outs[0]
     rows = rows.astype(BF)
-    outer[:size] = rows[:size]
-    inner[:size] = rows[size : 2 * size]
+    inner[:size] = rows[:size]
     used = size
     if extra is not None:
-        outer[size:] = extra[0]
-        inner[size : 2 * size] = extra[1]
+        inner[size : 2 * size] = extra
         used = 2 * size
-    far = rows[2 * size :]
-    if len(outs) == 3:
-        outs[2][...] = far
+    far = rows[size:]
+    if len(outs) == 2:
+        outs[1][...] = far
         return
     block = far.shape[0] // PLANE
     inner[used:] = far[block : 2 * block]
-    outs[2][...] = far[:block]
+    outs[1][...] = far[:block]
     for k in range(2, PLANE):
-        outs[k + 1][...] = far[k * block : (k + 1) * block]
+        outs[k][...] = far[k * block : (k + 1) * block]
+
+
+def outer_forth(send, message, *refs, size):
+    outer = refs[-1]
+    outer[:size] = t_mm(send[:, :size], message[...]).astype(BF)
+    if len(refs) == 2:
+        outer[size:] = refs[0][...]
+
+
+def outer_back(back_t, grad, *refs, size):
+    outer = refs[-1]
+    outer[:size] = mm(back_t[:size], grad[...]).astype(BF)
+    if len(refs) == 3:
+        send, message = refs[:2]
+        outer[size:] = t_mm(send[:, :size], message[...]).astype(BF)
 
 
 def arrived(ins, size):
-    return jnp.concatenate([ins[0][:size], ins[1][:size]] + [ref[...] for ref in ins[2:]], axis=0)
-
-
-def shuffle(own, first, second, third, *outs):
+    far = list(ins[2:3]) + list(ins[3:])[::-1]
+    return jnp.concatenate([ins[0][:size], ins[1][:size]] + [ref[...] for ref in far], axis=0)
+
+
+def shuffle(own, third, second, first, _after, *outs):
     block = own.shape[0]
     parts = [own[...], first[first.shape[0] - block :], second[...], third[...]]
     rows = jnp.concatenate(parts, axis=0)
@@ -205,8 +263,7 @@
     near[...] = mm(own_t[...], grad[...])
 
 
-def first_hidden(near, rim_t, outer_in, inner_in, encoder, weight, send, hidden, message, slope, *outs):
-    size = outs[0].shape[0]
+def first_hidden(near, rim_t, outer_in, inner_in, encoder, weight, send, hidden, message, slope, *outs, size):
     incoming = silu_pair(mm(arrived([outer_in, inner_in], outer_in.shape[0]), encoder[...]))[0].astype(BF)
     state = (near[...] + t_mm(rim_t[...], incoming)).astype(BF)
     hidden[...] = state
@@ -214,11 +271,10 @@
     value = value.astype(BF)
     message[...] = value
     slope[...] = gradient
-    emit(outs, t_mm(send[...], value), size)
-
-
-def next_hidden(near, forth_t, weight, send, outer_extra, inner_extra, *refs, ins, layer, scale):
-    size = outer_extra.shape[0]
+    emit(outs, t_mm(send[:, size:], value), size)
+
+
+def next_hidden(near, forth_t, weight, send, inner_extra, *refs, ins, layer, scale, size):
     rows = arrived(refs[:ins], size)
     hidden, message, slope = refs[ins : ins + 3]
     state = (near[...] + scale * t_mm(forth_t[...], rows)).astype(BF)
@@ -227,11 +283,10 @@
     value = value.astype(BF)
     message[...] = value
     slope[...] = gradient
-    emit(refs[ins + 3 :], t_mm(send[...], value), size, (outer_extra[...], inner_extra[...]))
-
-
-def turn(near, forth_t, weight, send, receive, back_t, back_near, *refs, ins, scale):
-    size = refs[0].shape[0] // 2
+    emit(refs[ins + 3 :], t_mm(send[:, size:], value), size, inner_extra[...])
+
+
+def turn(near, forth_t, weight, send, receive, back_t, back_near, *refs, ins, scale, size):
     rows = arrived(refs[:ins], size)
     message, grad = refs[ins : ins + 2]
     state = (near[...] + scale * t_mm(forth_t[...], rows)).astype(BF)
@@ -242,8 +297,8 @@
     back = back_near[...] + mm(receive[:, : 2 * size], returned)
     change = mm_t((back * gradient).astype(BF), weight[...]).astype(BF)
     grad[...] = change
-    rim = t_mm(send[:, : 2 * size], value).astype(BF)
-    emit(refs[ins + 2 :], mm(back_t[...], change), size, (rim[:size], rim[size:]))
+    rim = t_mm(send[:, size : 2 * size], value).astype(BF)
+    emit(refs[ins + 2 :], mm(back_t[size:], change), size, rim)
 
 
 def layer_back(near, receive, rows, slope, weight, grad, scale):
@@ -252,12 +307,11 @@
     return (grad[...].astype(F32) + mm_t(change, weight)).astype(BF)
 
 
-def middle_back(near, receive, slope, weight, grad, back_t, *refs, ins, layer, scale):
-    size = refs[ins + 1].shape[0]
+def middle_back(near, receive, slope, weight, grad, back_t, *refs, ins, layer, scale, size):
     rows = arrived(refs[:ins], size)
     change = layer_back(near, receive, rows, slope, weight[layer], grad, scale)
     refs[ins][...] = change
-    emit(refs[ins + 1 :], mm(back_t[...], change), size)
+    emit(refs[ins + 1 :], mm(back_t[size:], change), size)
 
 
 def last_back(near, receive, slope, weight, grad, grid_rim_t, *refs, ins, scale):
@@ -277,12 +331,26 @@
     output[...] = (latent[...].astype(F32) + total).astype(BF)
 
 
-def grid_back(me, near, lists, outer_in, inner_in, slope, weight, cotangent, output):
-    outer, inner = pair_order(lists, me[0])
-    rows = near.shape[0]
-    total = near[...] + mm(pick(rows, outer), outer_in[...]) + mm(pick(rows, inner), inner_in[...])
-    change = (total * slope[...].astype(F32)).astype(BF)
-    output[...] = (cotangent[...].astype(F32) + mm_t(change, weight[...])).astype(BF)
+def grid_local(me, own_t, grad, lists, slope, weight, cotangent, base, table, slope_rows):
+    rows = own_t.shape[0]
+    size = lists.shape[2]
+    for k, wanted in enumerate(pair_order(lists, me[0])):
+        table[:, k * size : (k + 1) * size] = pick(rows, wanted)
+    slope_rows[...] = t_mm(table[...], slope[...])
+    change = (mm(own_t[...], grad[...]) * slope[...].astype(F32)).astype(BF)
+    base[...] = cotangent[...].astype(F32) + mm_t(change, weight[...])
+
+
+def grid_back(base, table, slope_rows, weight, outer_in, inner_in, output, staging, sems):
+    returned = jnp.concatenate([outer_in[...], inner_in[...]], axis=0).astype(F32)
+    change = mm_t((returned * slope_rows[...]).astype(BF), weight[...]).astype(BF)
+    copies = []
+    for i, part in enumerate(row_chunks(base.shape[0])):
+        staging[part] = (base[part] + mm(table[part], change)).astype(BF)
+        copies.append(pltpu.make_async_copy(staging.at[part], output.at[part], sems.at[i]))
+        copies[-1].start()
+    for copy in copies:
+        copy.wait()
 
 
 def toggle(value, bits):
@@ -296,28 +364,29 @@
     return lax.ppermute(value, "dom", pairs)
 
 
-def exchange(outs, cap):
-    width = outs[0].shape[1]
-    if len(outs) == 3:
-        outer, inner, far = outs
+def exchange(outer, outs, cap, after):
+    width = outer.shape[1]
+    if len(outs) == 2:
+        inner, far = outs
         peers = lax.axis_size("dom")
         blocks = far.reshape(peers, cap, width)
         blocks = lax.all_to_all(blocks, "dom", split_axis=0, concat_axis=0, tiled=True)
         return [across(outer), toggle(inner, 1), blocks.reshape(-1, width)]
-    outer, inner, own, second, third = outs
+    inner, own, second, third = outs
+    outer_in = across(outer)
+    inner_in = toggle(inner, 1)
+    second_in = toggle(second, 2)
     third_in = toggle(third, 3)
-    second_in = toggle(second, 2)
-    inner_in = toggle(inner, 1)
-    outer_in = across(outer)
     columns = STAGED // PLANE
     blocks = call(
         shuffle,
         [((PLANE * cap, width), BF)] * columns,
         2 * (STAGED * cap) ** 2 * width,
-        own, inner_in, second_in, third_in,
+        own, third_in, second_in, inner_in, after,
+        free=1,
     )
     moved = [toggle(blocks[m], m * PLANE) for m in reversed(range(1, columns))]
-    return [outer_in, inner_in, blocks[0]] + moved[::-1]
+    return [outer_in, inner_in, blocks[0]] + moved
 
 
 def on_device(
@@ -350,87 +419,100 @@
 
     def sends(per_side):
         if devices != STAGED:
-            return [((per_side, width), BF)] * 2 + [((slots, width), BF)]
+            return [((per_side, width), BF), ((slots, width), BF)]
         block = slots // PLANE
-        return [((per_side, width), BF), ((per_side + block, width), BF)] + [((block, width), BF)] * (PLANE - 1)
+        return [((per_side + block, width), BF)] + [((block, width), BF)] * (PLANE - 1)
 
     state = ((mesh_rows, width), BF)
     total = ((mesh_rows, width), F32)
+    rim = ((halo, width), BF)
+    wide = ((2 * halo, width), BF)
+    grid_rim = ((ghalo, width), BF)
     step = 3 * square(mesh_rows, width)
+    rim_flops = square(halo, mesh_rows)
+    forth = functools.partial(outer_forth, size=halo)
+    back = functools.partial(outer_back, size=halo)
 
     outer, inner = call(
-        grid_send, [((ghalo, width), BF)] * 2, square(2 * ghalo, grid_rows), me, grid_latent, grid_halo_rows,
-        scalars=1,
+        grid_send,
+        [grid_rim, grid_rim],
+        square(2 * ghalo, grid_rows),
+        me, grid_latent, grid_halo_rows,
+        scalars=1, hbm=2,
+        scratch=copies_of([grid_latent, grid_halo_rows]) + [pltpu.SemaphoreType.DMA((CHUNKS + 1,))],
     )
     outer_in, inner_in = across(outer), toggle(inner, 1)
 
-    near, grid_own_t, grid_rim_t, grid_slope = call(
+    sources = [
+        encoder_neighbours.T, mesh_neighbours.T, halo_rows, far_sources[0].T, encoder_weight, grid_latent, mesh_latent,
+    ]
+    near, grid_own_t, grid_rim_t, grid_slope, send, receive, own_t, forth_t, back_t = call(
         functools.partial(encoder_local, size=ghalo),
-        [total, ((grid_rows, mesh_rows), BF), ((2 * ghalo, mesh_rows), BF), ((grid_rows, width), BF)],
-        square(grid_rows, width) + square(mesh_rows, grid_rows),
-        me, grid_latent, encoder_weight, mesh_latent, encoder_neighbours.T,
-        scalars=1,
-    )
-    send, receive = call(
-        functools.partial(list_tables, rows=mesh_rows),
-        [((mesh_rows, listed), BF)] * 2,
-        16 * mesh_rows * listed,
-        me, halo_rows, far_sources[0].T,
-        scalars=1,
+        [
+            total,
+            ((grid_rows, mesh_rows), BF),
+            ((2 * ghalo, mesh_rows), BF),
+            ((grid_rows, width), BF),
+            ((mesh_rows, listed), BF),
+            ((mesh_rows, listed), BF),
+            ((mesh_rows, mesh_rows), BF),
+            ((listed, mesh_rows), BF),
+            ((listed, mesh_rows), BF),
+        ],
+        4 * square(grid_rows, width),
+        me, *sources,
+        scalars=1, hbm=len(sources),
+        scratch=copies_of(sources) + [pltpu.SemaphoreType.DMA((len(sources),))],
     )
 
     hidden, message, slope_0, *outs = call(
-        first_hidden,
+        functools.partial(first_hidden, size=halo),
         [state, state, total] + sends(halo),
         step,
         near, grid_rim_t, outer_in, inner_in, encoder_weight, processor_weights, send,
     )
-    ins = exchange(outs, cap)
-
-    own_t, forth_t, back_t = call(
-        functools.partial(mesh_tables, size=halo, devices=devices),
-        [((mesh_rows, mesh_rows), BF)] + [((listed, mesh_rows), BF)] * 2,
-        30 * mesh_rows * listed,
-        me, mesh_neighbours.T,
-        scalars=1,
-    )
+    (outer,) = call(forth, [rim], rim_flops, send, message)
     local = functools.partial(layer_local, scale=scale)
-    (near,) = call(local, [total], square(mesh_rows, mesh_rows), hidden, own_t, message)
-    decoder_own_t, decoder_rim_t, decoder_near, outer_back, inner_back = call(
+    (near,) = call(local, [total], 5 * square(mesh_rows, mesh_rows), hidden, own_t, message)
+    decoder_own_t, decoder_rim_t, decoder_near, outer_extra, inner_extra = call(
         decoder_back,
-        [((mesh_rows, grid_rows), BF), ((2 * halo, grid_rows), BF), total, ((halo, width), BF), ((halo, width), BF)],
+        [((mesh_rows, grid_rows), BF), ((2 * halo, grid_rows), BF), total, rim, rim],
         square(grid_rows, mesh_rows),
         me, decoder_neighbours.T, cotangent,
         scalars=1,
     )
+    ins = exchange(outer, outs, cap, decoder_near)
 
     hidden, message, slope_1, *outs = call(
-        functools.partial(next_hidden, ins=len(ins), layer=1, scale=scale),
+        functools.partial(next_hidden, ins=len(ins), layer=1, scale=scale, size=halo),
         [state, state, total] + sends(2 * halo),
         step,
-        near, forth_t, processor_weights, send, outer_back, inner_back, *ins,
-    )
-    ins = exchange(outs, cap)
-    (near,) = call(local, [total], square(mesh_rows, mesh_rows), hidden, own_t, message)
+        near, forth_t, processor_weights, send, inner_extra, *ins,
+    )
+    (outer,) = call(forth, [wide], rim_flops, send, message, outer_extra)
+    (near,) = call(local, [total], 5 * square(mesh_rows, mesh_rows), hidden, own_t, message)
+    ins = exchange(outer, outs, cap, near)
 
     message, grad, *outs = call(
-        functools.partial(turn, ins=len(ins), scale=scale),
+        functools.partial(turn, ins=len(ins), scale=scale, size=halo),
         [state, state] + sends(2 * halo),
         2 * step,
         near, forth_t, decoder_weight, send, receive, back_t, decoder_near, *ins,
     )
-    ins = exchange(outs, cap)
+    (outer,) = call(back, [wide], rim_flops, back_t, grad, send, message)
+    (near,) = call(back_local, [total], 5 * square(mesh_rows, mesh_rows), own_t, grad)
+    ins = exchange(outer, outs, cap, near)
     outer_decoder, inner_decoder = ins[:2]
-    (near,) = call(back_local, [total], square(mesh_rows, mesh_rows), own_t, grad)
 
     grad, *outs = call(
-        functools.partial(middle_back, ins=len(ins), layer=1, scale=scale),
+        functools.partial(middle_back, ins=len(ins), layer=1, scale=scale, size=halo),
         [state] + sends(halo),
         step,
         near, receive, slope_1, processor_weights, grad, back_t, *ins,
     )
-    ins = exchange(outs, cap)
+    (outer,) = call(back, [rim], rim_flops, back_t, grad)
     (near,) = call(back_local, [total], square(mesh_rows, mesh_rows), own_t, grad)
+    ins = exchange(outer, outs, cap, near)
     (output,) = call(
         decode,
         [((grid_rows, width), BF)],
@@ -440,20 +522,25 @@
 
     mesh_grad, outer, inner = call(
         functools.partial(last_back, ins=len(ins), scale=scale),
-        [state, ((ghalo, width), BF), ((ghalo, width), BF)],
+        [state, grid_rim, grid_rim],
         step,
         near, receive, slope_0, processor_weights, grad, grid_rim_t, *ins,
     )
     outer_in, inner_in = across(outer), toggle(inner, 1)
-    (near,) = call(
-        back_local, [((grid_rows, width), F32)], square(mesh_rows, grid_rows), grid_own_t, mesh_grad
+    base, table, slope_rows = call(
+        grid_local,
+        [((grid_rows, width), F32), ((grid_rows, 2 * ghalo), BF), ((2 * ghalo, width), F32)],
+        square(mesh_rows, grid_rows) + square(grid_rows, width),
+        me, grid_own_t, mesh_grad, grid_halo_rows, grid_slope, encoder_weight, cotangent,
+        scalars=1,
     )
     (grid_grad,) = call(
         grid_back,
         [((grid_rows, width), BF)],
-        square(grid_rows, width),
-        me, near, grid_halo_rows, outer_in, inner_in, grid_slope, encoder_weight, cotangent,
-        scalars=1,
+        square(grid_rows, 4 * ghalo),
+        base, table, slope_rows, encoder_weight, outer_in, inner_in,
+        hbm_out=1,
+        scratch=[pltpu.VMEM((grid_rows, width), BF), pltpu.SemaphoreType.DMA((CHUNKS,))],
     )
     return (output, grid_grad, mesh_grad)
 

time: 90.4 us -> 82.1 us (0.908)
  waiting for transfers between devices: 27.4 us -> 10.4 us
  starting transfers between devices: 35.2 us -> 39.7 us
  Pallas kernels: 19 us -> 21.4 us
  local copies, waits for them, and re-layouts: 7.3 us -> 9.05 us
    ppermute x26, waiting for transfers between devices: 24.6 us -> 5.67 us  [toggle(): return lax.ppermute(value, 'dom', [(i, i ^ bits) for i in range(peers)])]
    ppermute x26, starting transfers between devices: 21 us -> 27 us  [toggle(): return lax.ppermute(value, 'dom', [(i, i ^ bits) for i in range(peers)])]
    pallas_call x21 -> x23, Pallas kernels: 19 us -> 21.4 us  [call(): pl.pallas_call(body, out_shape=shapes, in_specs=[pl.BlockSpec(memory_spac...]
    ppermute x6, waiting for transfers between devices: 2.85 us -> 4.68 us  [across(): return lax.ppermute(value, 'dom', pairs)]
    unnamed x34, local copies, waits for them, and re-layouts: 7.3 us -> 9.05 us
    ppermute x6, starting transfers between devices: 14.1 us -> 12.7 us  [across(): return lax.ppermute(value, 'dom', pairs)]
  transfers between devices with their start and end apart: 32 -> 32, of which waited for: 9 -> 15; matrix products, arithmetic and copies ran while one was open for 0% -> 0% of each run, Pallas kernels for 12% -> 16%
where the time goes in v5:
time: 82.1 us; the launch traced here: 81.6 us
  starting transfers between devices  39.7 us (48%)
  Pallas kernels  21.4 us (26%)
  waiting for transfers between devices  10.4 us (13%)
  local copies, waits for them, and re-layouts  9.05 us (11%)
  between operations  1.11 us (1%)
    ppermute x26, starting transfers between devices, toggle(): return lax.ppermute(value, 'dom', [(i, i ^ bits) for i in range(peers)])  27 us
    pallas_call x23, Pallas kernels, call(): pl.pallas_call(body, out_shape=shapes, in_specs=[pl.BlockSpec(memory_spac...  21.4 us
    ppermute x6, starting transfers between devices, across(): return lax.ppermute(value, 'dom', pairs)  12.7 us
    unnamed x34, local copies, waits for them, and re-layouts  9.05 us
    ppermute x26, waiting for transfers between devices, toggle(): return lax.ppermute(value, 'dom', [(i, i ^ bits) for i in range(peers)])  5.67 us
    ppermute x6, waiting for transfers between devices, across(): return lax.ppermute(value, 'dom', pairs)  4.68 us
  transfers between devices with their start and end apart: 32, of which 15 were waited for; matrix products, arithmetic and copies ran while one was open for 0% of the time, Pallas kernels for 16%

profile of v5, /device:TPU:0, one launch (start us, length us, event | category | flops | bytes accessed | tf_op | source)
XLA Modules:
  0.0 81.6 jit_solution(10859897064446485751)
XLA Ops:
  0.6 1.2 %copy-done.3 = bf16[1024,512]{1,0:T(8,128)(2,1)S(1)} copy-done((bf16[1024,512]{1,0:T(8,128)(2,1)S(1)}, bf16[1024,512]{1,0:T(8,128)(2,1)}, u32[]{:S(2)}) %copy-start.3) | copy-done | bytes 1048600
  3.3 5.5 %collective-permute-start = (bf16[64,512]{1,0:T(8,128)(2,1)S(1)}, bf16[64,512]{1,0:T(8,128)(2,1)S(1)}, u32[]{:S(2)}, u32[]{:S(2)}) collective-permute-start(bf16[64,512]{1,0:T(8,128)(2,1)S(1)} %get-tuple-element.70), channel_id=1, source_target_pairs={{0,15},{1,2},{2,1},{3,4},{4,3},{5,6},{6,5},{7,8},{8,7},{9,10},{10,... | collective-permute-start | bytes 196616 | tf_op jit(solution)/shard_map/ppermute | solution.py:364
  9.9 1.2 %copy-done.4 = bf16[1024,512]{1,0:T(8,128)(2,1)S(1)} copy-done((bf16[1024,512]{1,0:T(8,128)(2,1)S(1)}, bf16[1024,512]{1,0:T(8,128)(2,1)}, u32[]{:S(2)}) %copy-start.4) | copy-done | bytes 1048600
  14.9 5.2 %shard_map.140 = (f32[512,512]{1,0:T(8,128)S(1)}, bf16[1024,512]{1,0:T(8,128)(2,1)S(1)}, bf16[128,512]{1,0:T(8,128)(2,1)S(1)}, bf16[1024,512]{1,0:T(8,128)(2,1)S...) custom-call(s32[1]{0:T(128)} %bitcast.me, ...), custom_call_target="tpu_custom_call" | custom-call | flops 2147483648 | bytes 6710020 | tf_op jit(solution)/shard_map/pallas_call | solution.py:73
  21.9 1.7 %collective-permute-start.5 = (bf16[16,512]{1,0:T(8,128)(2,1)S(1)}, bf16[16,512]{1,0:T(8,128)(2,1)S(1)}, u32[]{:S(2)}, u32[]{:S(2)}) collective-permute-start(bf16[16,512]{1,0:T(8,128)(2,1)S(1)} %get-tuple-element.81), channel_id=1, source_target_pairs={{0,2},{1,3},{2,0},{3,1},{4,6},{5,7},{6,4},{7,5},{8,10},{9,11},{10,... | collective-permute-start | bytes 49160 | tf_op jit(solution)/shard_map/ppermute | solution.py:358
  25.9 1.4 %collective-permute-start.6 = (bf16[16,512]{1,0:T(8,128)(2,1)S(1)}, bf16[16,512]{1,0:T(8,128)(2,1)S(1)}, u32[]{:S(2)}, u32[]{:S(2)}) collective-permute-start(bf16[16,512]{1,0:T(8,128)(2,1)S(1)} %get-tuple-element.84), channel_id=1, source_target_pairs={{0,12},{1,13},{2,14},{3,15},{4,8},{5,9},{6,10},{7,11},{8,4},{9,5},... | collective-permute-start | bytes 49160 | tf_op jit(solution)/shard_map/ppermute | solution.py:358
  28.2 2.1 %collective-permute-start.8 = (bf16[16,512]{1,0:T(8,128)(2,1)S(1)}, bf16[16,512]{1,0:T(8,128)(2,1)S(1)}, u32[]{:S(2)}, u32[]{:S(2)}) collective-permute-start(bf16[16,512]{1,0:T(8,128)(2,1)S(1)} %get-tuple-element.86), channel_id=1, source_target_pairs={{0,4},{1,5},{2,6},{3,7},{4,0},{5,1},{6,2},{7,3},{8,12},{9,13},{10,... | collective-permute-start | bytes 49160 | tf_op jit(solution)/shard_map/ppermute | solution.py:358
  33.2 1.7 %collective-permute-start.11 = (bf16[16,512]{1,0:T(8,128)(2,1)S(1)}, bf16[16,512]{1,0:T(8,128)(2,1)S(1)}, u32[]{:S(2)}, u32[]{:S(2)}) collective-permute-start(bf16[16,512]{1,0:T(8,128)(2,1)S(1)} %get-tuple-element.94), channel_id=1, source_target_pairs={{0,3},{1,2},{2,1},{3,0},{4,7},{5,6},{6,5},{7,4},{8,11},{9,10},{10,... | collective-permute-start | bytes 49160 | tf_op jit(solution)/shard_map/ppermute | solution.py:358
  35.5 2.9 %collective-permute-start.9 = (bf16[128,512]{1,0:T(8,128)(2,1)S(1)}, bf16[128,512]{1,0:T(8,128)(2,1)S(1)}, u32[]{:S(2)}, u32[]{:S(2)}) collective-permute-start(bf16[128,512]{1,0:T(8,128)(2,1)S(1)} %shard_map.148), channel_id=1, source_target_pairs={{0,15},{1,2},{2,1},{3,4},{4,3},{5,6},{6,5},{7,8},{8,7},{9,10},{10,... | collective-permute-start | bytes 393224 | tf_op jit(solution)/shard_map/ppermute | solution.py:364
  39.1 2.2 %collective-permute-start.13 = (bf16[16,512]{1,0:T(8,128)(2,1)S(1)}, bf16[16,512]{1,0:T(8,128)(2,1)S(1)}, u32[]{:S(2)}, u32[]{:S(2)}) collective-permute-start(bf16[16,512]{1,0:T(8,128)(2,1)S(1)} %get-tuple-element.97), channel_id=1, source_target_pairs={{0,12},{1,13},{2,14},{3,15},{4,8},{5,9},{6,10},{7,11},{8,4},{9,5},... | collective-permute-start | bytes 49160 | tf_op jit(solution)/shard_map/ppermute | solution.py:358
  44.7 1.2 %collective-permute-done.14.refs_4_ = bf16[16,512]{1,0:T(8,128)(2,1)S(1)} collective-permute-done((bf16[16,512]{1,0:T(8,128)(2,1)S(1)}, bf16[16,512]{1,0:T(8,128)(2,1)S(1)}, u32[]{:S(2)}, u32[]{:S(2)}) %collective-permute-start.14) | collective-permute-done | bytes 16416 | tf_op jit(solution)/shard_map/ppermute | solution.py:358
  46.1 1.5 %shard_map.150 = (bf16[512,512]{1,0:T(8,128)(2,1)S(1)}, bf16[512,512]{1,0:T(8,128)(2,1)S(1)}, bf16[144,512]{1,0:T(8,128)(2,1)S(1)}, bf16[16,512]{1,0:T(8,128)(2,...) custom-call(f32[512,512]{1,0:T(8,128)S(1)} %shard_map.147._after.near, ...), custom_call_target="tpu_custom_call" | custom-call | flops 1610612736 | bytes 4997120 | tf_op jit(solution)/shard_map/pallas_call | solution.py:73
  48.1 1.7 %collective-permute-start.19 = (bf16[16,512]{1,0:T(8,128)(2,1)S(1)}, bf16[16,512]{1,0:T(8,128)(2,1)S(1)}, u32[]{:S(2)}, u32[]{:S(2)}) collective-permute-start(bf16[16,512]{1,0:T(8,128)(2,1)S(1)} %get-tuple-element.107), channel_id=1, source_target_pairs={{0,2},{1,3},{2,0},{3,1},{4,6},{5,7},{6,4},{7,5},{8,10},{9,11},{10,... | collective-permute-start | bytes 49160 | tf_op jit(solution)/shard_map/ppermute | solution.py:358
  52.0 1.5 %collective-permute-start.20 = (bf16[16,512]{1,0:T(8,128)(2,1)S(1)}, bf16[16,512]{1,0:T(8,128)(2,1)S(1)}, u32[]{:S(2)}, u32[]{:S(2)}) collective-permute-start(bf16[16,512]{1,0:T(8,128)(2,1)S(1)} %get-tuple-element.109), channel_id=1, source_target_pairs={{0,12},{1,13},{2,14},{3,15},{4,8},{5,9},{6,10},{7,11},{8,4},{9,5},... | collective-permute-start | bytes 49160 | tf_op jit(solution)/shard_map/ppermute | solution.py:358
  54.5 1.9 %collective-permute-start.22 = (bf16[16,512]{1,0:T(8,128)(2,1)S(1)}, bf16[16,512]{1,0:T(8,128)(2,1)S(1)}, u32[]{:S(2)}, u32[]{:S(2)}) collective-permute-start(bf16[16,512]{1,0:T(8,128)(2,1)S(1)} %get-tuple-element.111), channel_id=1, source_target_pairs={{0,4},{1,5},{2,6},{3,7},{4,0},{5,1},{6,2},{7,3},{8,12},{9,13},{10,... | collective-permute-start | bytes 49160 | tf_op jit(solution)/shard_map/ppermute | solution.py:358
  59.2 2.1 %collective-permute-start.25 = (bf16[16,512]{1,0:T(8,128)(2,1)S(1)}, bf16[16,512]{1,0:T(8,128)(2,1)S(1)}, u32[]{:S(2)}, u32[]{:S(2)}) collective-permute-start(bf16[16,512]{1,0:T(8,128)(2,1)S(1)} %get-tuple-element.116), channel_id=1, source_target_pairs={{0,3},{1,2},{2,1},{3,0},{4,7},{5,6},{6,5},{7,4},{8,11},{9,10},{10,... | collective-permute-start | bytes 49160 | tf_op jit(solution)/shard_map/ppermute | solution.py:358
  61.6 2.8 %collective-permute-start.23 = (bf16[64,512]{1,0:T(8,128)(2,1)S(1)}, bf16[64,512]{1,0:T(8,128)(2,1)S(1)}, u32[]{:S(2)}, u32[]{:S(2)}) collective-permute-start(bf16[64,512]{1,0:T(8,128)(2,1)S(1)} %shard_map.157), channel_id=1, source_target_pairs={{0,15},{1,2},{2,1},{3,4},{4,3},{5,6},{6,5},{7,8},{8,7},{9,10},{10,... | collective-permute-start | bytes 196616 | tf_op jit(solution)/shard_map/ppermute | solution.py:364
  65.1 2.2 %collective-permute-start.27 = (bf16[16,512]{1,0:T(8,128)(2,1)S(1)}, bf16[16,512]{1,0:T(8,128)(2,1)S(1)}, u32[]{:S(2)}, u32[]{:S(2)}) collective-permute-start(bf16[16,512]{1,0:T(8,128)(2,1)S(1)} %get-tuple-element.119), channel_id=1, source_target_pairs={{0,12},{1,13},{2,14},{3,15},{4,8},{5,9},{6,10},{7,11},{8,4},{9,5},... | collective-permute-start | bytes 49160 | tf_op jit(solution)/shard_map/ppermute | solution.py:358
  68.2 1.3 %collective-permute-start.29 = (bf16[16,512]{1,0:T(8,128)(2,1)S(1)}, bf16[16,512]{1,0:T(8,128)(2,1)S(1)}, u32[]{:S(2)}, u32[]{:S(2)}) collective-permute-start(bf16[16,512]{1,0:T(8,128)(2,1)S(1)} %get-tuple-element.121), channel_id=1, source_target_pairs={{0,4},{1,5},{2,6},{3,7},{4,0},{5,1},{6,2},{7,3},{8,12},{9,13},{10,... | collective-permute-start | bytes 49160 | tf_op jit(solution)/shard_map/ppermute | solution.py:358
  69.6 2.0 %shard_map.152 = bf16[1024,512]{1,0:T(8,128)(2,1)} custom-call(bf16[1024,512]{1,0:T(8,128)(2,1)S(1)} %copy-done.5, bf16[512,1024]{1,0:T(8,128)(2,1)S(1)} %get-tuple-element.66.own_t, bf16[128,1024]{1,0:T(8,128)(2,1)S(1)} %get-tuple-element.67.rim_t, bf16[512,512]{1,0:T(8,128)(2,1)S(1)} %get-tuple-element.100.refs_1_.message, ...), custom_call_target="tpu_custom_call" | custom-call | flops 536870912 | bytes 4210688 | tf_op jit(solution)/shard_map/pallas_call | solution.py:73
  72.1 1.4 %shard_map.159 = (bf16[512,512]{1,0:T(8,128)(2,1)}, bf16[64,512]{1,0:T(8,128)(2,1)S(1)}, bf16[64,512]{1,0:T(8,128)(2,1)S(1)}) custom-call(f32[512,512]{1,0:T(8,128)S(1)} %shard_map.156._after.near, bf16[512,192]{1,0:T(8,128)(2,1)S(1)} %get-tuple-element.89.receive, f32[512,512]{1,0:T(8,128)S(1)} %get-tuple-element.113.slope, ...), custom_call_target="tpu_custom_call" | custom-call | flops 805306368 | bytes 4866048 | tf_op jit(solution)/shard_map/pallas_call | solution.py:73
  75.0 1.8 %shard_map.160 = (f32[1024,512]{1,0:T(8,128)S(1)}, bf16[1024,128]{1,0:T(8,128)(2,1)S(1)}, f32[128,512]{1,0:T(8,128)S(1)}) custom-call(s32[1]{0:T(128)} %bitcast.me, bf16[1024,512]{1,0:T(8,128)(2,1)S(1)} %get-tuple-element.103.own_t, bf16[512,512]{1,0:T(8,128)(2,1)S(1)} %copy-done.7, s32[1,2,64]{2,1,0:T(2,128)S(1)} %copy-done.9, ...), custom_call_target="tpu_custom_call" | custom-call | flops 1073741824 | bytes 6816260 | tf_op jit(solution)/shard_map/pallas_call | solution.py:73
  76.8 3.1 %collective-permute-done.30.outer_in = bf16[64,512]{1,0:T(8,128)(2,1)S(1)} collective-permute-done((bf16[64,512]{1,0:T(8,128)(2,1)S(1)}, bf16[64,512]{1,0:T(8,128)(2,1)S(1)}, u32[]{:S(2)}, u32[]{:S(2)}) %collective-permute-start.30) | collective-permute-done | bytes 65568 | tf_op jit(solution)/shard_map/ppermute | solution.py:364
  79.9 1.5 %shard_map.161 = bf16[1024,512]{1,0:T(8,128)(2,1)} custom-call(f32[1024,512]{1,0:T(8,128)S(1)} %get-tuple-element.124.base, bf16[1024,128]{1,0:T(8,128)(2,1)S(1)} %get-tuple-element.125.table, f32[128,512]{1,0:T(8,128)S(1)} %get-tuple-element.126.slope_rows, bf16[512,512]{1,0:T(8,128)(2,1)S(1)} %copy-done.2, ...), custom_call_target="tpu_custom_call" | custom-call | flops 268435456 | bytes 4325376 | tf_op jit(solution)/shard_map/pallas_call | solution.py:73
  (97 shorter events, 29.5 us)
Async XLA Ops:
  3.3 16.8 %collective-permute-start = (bf16[64,512]{1,0:T(8,128)(2,1)S(1)}, bf16[64,512]{1,0:T(8,128)(2,1)S(1)}, u32[]{:S(2)}, u32[]{:S(2)}) collective-permute-start(bf16[64,512]{1,0:T(8,128)(2,1)S(1)} %get-tuple-element.70), channel_id=1, source_target_pairs={{0,15},{1,2},{2,1},{3,4},{4,3},{5,6},{6,5},{7,8},{8,7},{9,10},{10,... | collective-permute-start | bytes 196616 | tf_op jit(solution)/shard_map/ppermute | solution.py:364
  8.8 11.3 %collective-permute-start.1 = (bf16[64,512]{1,0:T(8,128)(2,1)S(1)}, bf16[64,512]{1,0:T(8,128)(2,1)S(1)}, u32[]{:S(2)}, u32[]{:S(2)}) collective-permute-start(bf16[64,512]{1,0:T(8,128)(2,1)S(1)} %get-tuple-element.71), channel_id=1, source_target_pairs={{0,1},{1,0},{2,3},{3,2},{4,5},{5,4},{6,7},{7,6},{8,9},{9,8},{10,11... | collective-permute-start | bytes 196616 | tf_op jit(solution)/shard_map/ppermute | solution.py:358
  21.3 4.4 %collective-permute-start.3 = (bf16[80,512]{1,0:T(8,128)(2,1)S(1)}, bf16[80,512]{1,0:T(8,128)(2,1)S(1)}, u32[]{:S(2)}, u32[]{:S(2)}) collective-permute-start(bf16[80,512]{1,0:T(8,128)(2,1)S(1)} %get-tuple-element.78), channel_id=1, source_target_pairs={{0,1},{1,0},{2,3},{3,2},{4,5},{5,4},{6,7},{7,6},{8,9},{9,8},{10,11... | collective-permute-start | bytes 245768 | tf_op jit(solution)/shard_map/ppermute | solution.py:358
  25.0 6.5 %collective-permute-start.2 = (bf16[64,512]{1,0:T(8,128)(2,1)S(1)}, bf16[64,512]{1,0:T(8,128)(2,1)S(1)}, u32[]{:S(2)}, u32[]{:S(2)}) collective-permute-start(bf16[64,512]{1,0:T(8,128)(2,1)S(1)} %shard_map.144), channel_id=1, source_target_pairs={{0,15},{1,2},{2,1},{3,4},{4,3},{5,6},{6,5},{7,8},{8,7},{9,10},{10,... | collective-permute-start | bytes 196616 | tf_op jit(solution)/shard_map/ppermute | solution.py:364
  25.9 5.6 %collective-permute-start.6 = (bf16[16,512]{1,0:T(8,128)(2,1)S(1)}, bf16[16,512]{1,0:T(8,128)(2,1)S(1)}, u32[]{:S(2)}, u32[]{:S(2)}) collective-permute-start(bf16[16,512]{1,0:T(8,128)(2,1)S(1)} %get-tuple-element.84), channel_id=1, source_target_pairs={{0,12},{1,13},{2,14},{3,15},{4,8},{5,9},{6,10},{7,11},{8,4},{9,5},... | collective-permute-start | bytes 49160 | tf_op jit(solution)/shard_map/ppermute | solution.py:358
  27.2 4.9 %collective-permute-start.7 = (bf16[16,512]{1,0:T(8,128)(2,1)S(1)}, bf16[16,512]{1,0:T(8,128)(2,1)S(1)}, u32[]{:S(2)}, u32[]{:S(2)}) collective-permute-start(bf16[16,512]{1,0:T(8,128)(2,1)S(1)} %get-tuple-element.85), channel_id=1, source_target_pairs={{0,8},{1,9},{2,10},{3,11},{4,12},{5,13},{6,14},{7,15},{8,0},{9,1},... | collective-permute-start | bytes 49160 | tf_op jit(solution)/shard_map/ppermute | solution.py:358
  33.1 5.8 %collective-permute-start.10 = (bf16[144,512]{1,0:T(8,128)(2,1)S(1)}, bf16[144,512]{1,0:T(8,128)(2,1)S(1)}, u32[]{:S(2)}, u32[]{:S(2)}) collective-permute-start(bf16[144,512]{1,0:T(8,128)(2,1)S(1)} %get-tuple-element.92), channel_id=1, source_target_pairs={{0,1},{1,0},{2,3},{3,2},{4,5},{5,4},{6,7},{7,6},{8,9},{9,8},{10,11... | collective-permute-start | bytes 442376 | tf_op jit(solution)/shard_map/ppermute | solution.py:358
  33.2 5.7 %collective-permute-start.11 = (bf16[16,512]{1,0:T(8,128)(2,1)S(1)}, bf16[16,512]{1,0:T(8,128)(2,1)S(1)}, u32[]{:S(2)}, u32[]{:S(2)}) collective-permute-start(bf16[16,512]{1,0:T(8,128)(2,1)S(1)} %get-tuple-element.94), channel_id=1, source_target_pairs={{0,3},{1,2},{2,1},{3,0},{4,7},{5,6},{6,5},{7,4},{8,11},{9,10},{10,... | collective-permute-start | bytes 49160 | tf_op jit(solution)/shard_map/ppermute | solution.py:358
  34.9 4.0 %collective-permute-start.12 = (bf16[16,512]{1,0:T(8,128)(2,1)S(1)}, bf16[16,512]{1,0:T(8,128)(2,1)S(1)}, u32[]{:S(2)}, u32[]{:S(2)}) collective-permute-start(bf16[16,512]{1,0:T(8,128)(2,1)S(1)} %get-tuple-element.95), channel_id=1, source_target_pairs={{0,2},{1,3},{2,0},{3,1},{4,6},{5,7},{6,4},{7,5},{8,10},{9,11},{10,... | collective-permute-start | bytes 49160 | tf_op jit(solution)/shard_map/ppermute | solution.py:358
  35.5 8.0 %collective-permute-start.9 = (bf16[128,512]{1,0:T(8,128)(2,1)S(1)}, bf16[128,512]{1,0:T(8,128)(2,1)S(1)}, u32[]{:S(2)}, u32[]{:S(2)}) collective-permute-start(bf16[128,512]{1,0:T(8,128)(2,1)S(1)} %shard_map.148), channel_id=1, source_target_pairs={{0,15},{1,2},{2,1},{3,4},{4,3},{5,6},{6,5},{7,8},{8,7},{9,10},{10,... | collective-permute-start | bytes 393224 | tf_op jit(solution)/shard_map/ppermute | solution.py:364
  39.1 5.6 %collective-permute-start.13 = (bf16[16,512]{1,0:T(8,128)(2,1)S(1)}, bf16[16,512]{1,0:T(8,128)(2,1)S(1)}, u32[]{:S(2)}, u32[]{:S(2)}) collective-permute-start(bf16[16,512]{1,0:T(8,128)(2,1)S(1)} %get-tuple-element.97), channel_id=1, source_target_pairs={{0,12},{1,13},{2,14},{3,15},{4,8},{5,9},{6,10},{7,11},{8,4},{9,5},... | collective-permute-start | bytes 49160 | tf_op jit(solution)/shard_map/ppermute | solution.py:358
  41.2 4.6 %collective-permute-start.14 = (bf16[16,512]{1,0:T(8,128)(2,1)S(1)}, bf16[16,512]{1,0:T(8,128)(2,1)S(1)}, u32[]{:S(2)}, u32[]{:S(2)}) collective-permute-start(bf16[16,512]{1,0:T(8,128)(2,1)S(1)} %get-tuple-element.98), channel_id=1, source_target_pairs={{0,8},{1,9},{2,10},{3,11},{4,12},{5,13},{6,14},{7,15},{8,0},{9,1},... | collective-permute-start | bytes 49160 | tf_op jit(solution)/shard_map/ppermute | solution.py:358
  47.5 4.3 %collective-permute-start.17 = (bf16[144,512]{1,0:T(8,128)(2,1)S(1)}, bf16[144,512]{1,0:T(8,128)(2,1)S(1)}, u32[]{:S(2)}, u32[]{:S(2)}) collective-permute-start(bf16[144,512]{1,0:T(8,128)(2,1)S(1)} %get-tuple-element.102), channel_id=1, source_target_pairs={{0,1},{1,0},{2,3},{3,2},{4,5},{5,4},{6,7},{7,6},{8,9},{9,8},{10,11... | collective-permute-start | bytes 442376 | tf_op jit(solution)/shard_map/ppermute | solution.py:358
  50.1 7.3 %collective-permute-start.16 = (bf16[128,512]{1,0:T(8,128)(2,1)S(1)}, bf16[128,512]{1,0:T(8,128)(2,1)S(1)}, u32[]{:S(2)}, u32[]{:S(2)}) collective-permute-start(bf16[128,512]{1,0:T(8,128)(2,1)S(1)} %shard_map.151), channel_id=1, source_target_pairs={{0,15},{1,2},{2,1},{3,4},{4,3},{5,6},{6,5},{7,8},{8,7},{9,10},{10,... | collective-permute-start | bytes 393224 | tf_op jit(solution)/shard_map/ppermute | solution.py:364
  52.0 5.8 %collective-permute-start.20 = (bf16[16,512]{1,0:T(8,128)(2,1)S(1)}, bf16[16,512]{1,0:T(8,128)(2,1)S(1)}, u32[]{:S(2)}, u32[]{:S(2)}) collective-permute-start(bf16[16,512]{1,0:T(8,128)(2,1)S(1)} %get-tuple-element.109), channel_id=1, source_target_pairs={{0,12},{1,13},{2,14},{3,15},{4,8},{5,9},{6,10},{7,11},{8,4},{9,5},... | collective-permute-start | bytes 49160 | tf_op jit(solution)/shard_map/ppermute | solution.py:358
  53.5 4.6 %collective-permute-start.21 = (bf16[16,512]{1,0:T(8,128)(2,1)S(1)}, bf16[16,512]{1,0:T(8,128)(2,1)S(1)}, u32[]{:S(2)}, u32[]{:S(2)}) collective-permute-start(bf16[16,512]{1,0:T(8,128)(2,1)S(1)} %get-tuple-element.110), channel_id=1, source_target_pairs={{0,8},{1,9},{2,10},{3,11},{4,12},{5,13},{6,14},{7,15},{8,0},{9,1},... | collective-permute-start | bytes 49160 | tf_op jit(solution)/shard_map/ppermute | solution.py:358
  59.1 5.9 %collective-permute-start.24 = (bf16[80,512]{1,0:T(8,128)(2,1)S(1)}, bf16[80,512]{1,0:T(8,128)(2,1)S(1)}, u32[]{:S(2)}, u32[]{:S(2)}) collective-permute-start(bf16[80,512]{1,0:T(8,128)(2,1)S(1)} %get-tuple-element.114), channel_id=1, source_target_pairs={{0,1},{1,0},{2,3},{3,2},{4,5},{5,4},{6,7},{7,6},{8,9},{9,8},{10,11... | collective-permute-start | bytes 245768 | tf_op jit(solution)/shard_map/ppermute | solution.py:358
  59.2 5.7 %collective-permute-start.25 = (bf16[16,512]{1,0:T(8,128)(2,1)S(1)}, bf16[16,512]{1,0:T(8,128)(2,1)S(1)}, u32[]{:S(2)}, u32[]{:S(2)}) collective-permute-start(bf16[16,512]{1,0:T(8,128)(2,1)S(1)} %get-tuple-element.116), channel_id=1, source_target_pairs={{0,3},{1,2},{2,1},{3,0},{4,7},{5,6},{6,5},{7,4},{8,11},{9,10},{10,... | collective-permute-start | bytes 49160 | tf_op jit(solution)/shard_map/ppermute | solution.py:358
  61.6 9.9 %collective-permute-start.23 = (bf16[64,512]{1,0:T(8,128)(2,1)S(1)}, bf16[64,512]{1,0:T(8,128)(2,1)S(1)}, u32[]{:S(2)}, u32[]{:S(2)}) collective-permute-start(bf16[64,512]{1,0:T(8,128)(2,1)S(1)} %shard_map.157), channel_id=1, source_target_pairs={{0,15},{1,2},{2,1},{3,4},{4,3},{5,6},{6,5},{7,8},{8,7},{9,10},{10,... | collective-permute-start | bytes 196616 | tf_op jit(solution)/shard_map/ppermute | solution.py:364
  65.1 6.4 %collective-permute-start.27 = (bf16[16,512]{1,0:T(8,128)(2,1)S(1)}, bf16[16,512]{1,0:T(8,128)(2,1)S(1)}, u32[]{:S(2)}, u32[]{:S(2)}) collective-permute-start(bf16[16,512]{1,0:T(8,128)(2,1)S(1)} %get-tuple-element.119), channel_id=1, source_target_pairs={{0,12},{1,13},{2,14},{3,15},{4,8},{5,9},{6,10},{7,11},{8,4},{9,5},... | collective-permute-start | bytes 49160 | tf_op jit(solution)/shard_map/ppermute | solution.py:358
  67.3 4.6 %collective-permute-start.28 = (bf16[16,512]{1,0:T(8,128)(2,1)S(1)}, bf16[16,512]{1,0:T(8,128)(2,1)S(1)}, u32[]{:S(2)}, u32[]{:S(2)}) collective-permute-start(bf16[16,512]{1,0:T(8,128)(2,1)S(1)} %get-tuple-element.120), channel_id=1, source_target_pairs={{0,8},{1,9},{2,10},{3,11},{4,12},{5,13},{6,14},{7,15},{8,0},{9,1},... | collective-permute-start | bytes 49160 | tf_op jit(solution)/shard_map/ppermute | solution.py:358
  68.2 3.9 %collective-permute-start.29 = (bf16[16,512]{1,0:T(8,128)(2,1)S(1)}, bf16[16,512]{1,0:T(8,128)(2,1)S(1)}, u32[]{:S(2)}, u32[]{:S(2)}) collective-permute-start(bf16[16,512]{1,0:T(8,128)(2,1)S(1)} %get-tuple-element.121), channel_id=1, source_target_pairs={{0,4},{1,5},{2,6},{3,7},{4,0},{5,1},{6,2},{7,3},{8,12},{9,13},{10,... | collective-permute-start | bytes 49160 | tf_op jit(solution)/shard_map/ppermute | solution.py:358
  73.5 6.4 %collective-permute-start.30 = (bf16[64,512]{1,0:T(8,128)(2,1)S(1)}, bf16[64,512]{1,0:T(8,128)(2,1)S(1)}, u32[]{:S(2)}, u32[]{:S(2)}) collective-permute-start(bf16[64,512]{1,0:T(8,128)(2,1)S(1)} %get-tuple-element.127), channel_id=1, source_target_pairs={{0,15},{1,2},{2,1},{3,4},{4,3},{5,6},{6,5},{7,8},{8,7},{9,10},{10,... | collective-permute-start | bytes 196616 | tf_op jit(solution)/shard_map/ppermute | solution.py:364
  73.8 6.1 %collective-permute-start.31 = (bf16[64,512]{1,0:T(8,128)(2,1)S(1)}, bf16[64,512]{1,0:T(8,128)(2,1)S(1)}, u32[]{:S(2)}, u32[]{:S(2)}) collective-permute-start(bf16[64,512]{1,0:T(8,128)(2,1)S(1)} %get-tuple-element.128), channel_id=1, source_target_pairs={{0,1},{1,0},{2,3},{3,2},{4,5},{5,4},{6,7},{7,6},{8,9},{9,8},{10,11... | collective-permute-start | bytes 196616 | tf_op jit(solution)/shard_map/ppermute | solution.py:358
  (25 other events, 76.5 us)

commit v6 on v5

--- a/solution.py
+++ b/solution.py
@@ -63,20 +63,23 @@
     return (x % PLANE) * (devices // PLANE) + x // PLANE
 
 
-def call(body, out_shapes, flops, *args, scalars=0, hbm=0, free=0, hbm_out=0, scratch=()):
+def call(body, out_shapes, flops, *args, scalars=0, hbm=0, free=0, hbm_out=0, scratch=(), limit=VMEM_LIMIT):
     shapes = [jax.ShapeDtypeStruct(s, t) for s, t in out_shapes]
     size = sum(a.size * a.dtype.itemsize for a in args)
     size += sum(s.size * s.dtype.itemsize for s in shapes)
+    size *= hbm == 0
     places = [pltpu.SMEM] * scalars + [pltpu.HBM] * hbm + [pltpu.VMEM] * (len(args) - scalars - hbm - free)
     places += [pl.ANY] * free
     out_places = [pltpu.HBM] * hbm_out + [pltpu.VMEM] * (len(shapes) - hbm_out)
+    kept = len(args) - free
+    inner = body if free == 0 else lambda *refs: body(*refs[:kept], *refs[len(args) :])
     return pl.pallas_call(
-        body,
+        inner,
         out_shape=shapes,
         in_specs=[pl.BlockSpec(memory_space=place) for place in places],
         out_specs=[pl.BlockSpec(memory_space=place) for place in out_places],
         scratch_shapes=list(scratch),
-        compiler_params=pltpu.CompilerParams(vmem_limit_bytes=VMEM_LIMIT),
+        compiler_params=pltpu.CompilerParams(vmem_limit_bytes=limit),
         cost_estimate=pl.CostEstimate(flops=flops, bytes_accessed=size, transcendentals=0),
     )(*args)
 
@@ -114,29 +117,17 @@
     inner[...] = inner_rows.astype(BF)
 
 
-def encoder_local(me, entries, mesh_entries, lists, far_lists, weight, latent, mesh,
-                  near, grid_own_t, grid_rim_t, slope, send, receive, own_t, forth_t, back_t,
-                  entries_v, mesh_entries_v, lists_v, far_lists_v, weight_v, latent_v, mesh_v, sems, *, size):
-    sources = [entries, mesh_entries, lists, far_lists, weight, latent, mesh]
-    targets = [entries_v, mesh_entries_v, lists_v, far_lists_v, weight_v, latent_v, mesh_v]
-    copies = fetch(sources, targets, sems)
+def encoder_local(me, entries, lists, far_lists, weight, latent, mesh,
+                  near, grid_own_t, grid_rim_t, slope, send, receive, *, size):
     rows = latent.shape[0]
-    copies[0].wait()
-    columns = side_swap(entries_v[...], rows, size, me[0])
+    columns = side_swap(entries[...], rows, size, me[0])
     own = counts_t(rows, 0, columns)
     grid_own_t[...] = own
     grid_rim_t[...] = counts_t(2 * size, rows, columns)
-    copies[1].wait()
-    mesh_tables(me, mesh_entries_v, own_t, forth_t, back_t, lists.shape[2], far_lists.shape[1])
-    copies[2].wait()
-    copies[3].wait()
-    list_tables(me, lists_v, far_lists_v, send, receive)
-    copies[4].wait()
-    copies[5].wait()
-    message, gradient = silu_pair(mm(latent_v[...], weight_v[...]))
+    list_tables(me, lists, far_lists, send, receive)
+    message, gradient = silu_pair(mm(latent[...], weight[...]))
     slope[...] = gradient.astype(BF)
-    copies[6].wait()
-    near[...] = mesh_v[...].astype(F32) + t_mm(own, message.astype(BF))
+    near[...] = mesh[...].astype(F32) + t_mm(own, message.astype(BF))
 
 
 def list_tables(me, lists, far_lists, send, receive):
@@ -165,7 +156,7 @@
     receive[:, 2 * size :] = receive_far.astype(BF)
 
 
-def mesh_tables(me, entries, own_t, forth_t, back_t, size, devices):
+def mesh_tables(me, entries, own_t, forth_t, back_t, *, size, devices):
     rows = own_t.shape[0]
     slots = forth_t.shape[0] - 2 * size
     cap = slots // devices
@@ -240,7 +231,7 @@
     return jnp.concatenate([ins[0][:size], ins[1][:size]] + [ref[...] for ref in far], axis=0)
 
 
-def shuffle(own, third, second, first, _after, *outs):
+def shuffle(own, third, second, first, *outs):
     block = own.shape[0]
     parts = [own[...], first[first.shape[0] - block :], second[...], third[...]]
     rows = jnp.concatenate(parts, axis=0)
@@ -331,7 +322,8 @@
     output[...] = (latent[...].astype(F32) + total).astype(BF)
 
 
-def grid_local(me, own_t, grad, lists, slope, weight, cotangent, base, table, slope_rows):
+def grid_local(me, own_t, grad, lists, slope, weight, cotangent, base, table, slope_rows, mesh_grad):
+    mesh_grad[...] = grad[...]
     rows = own_t.shape[0]
     size = lists.shape[2]
     for k, wanted in enumerate(pair_order(lists, me[0])):
@@ -364,7 +356,7 @@
     return lax.ppermute(value, "dom", pairs)
 
 
-def exchange(outer, outs, cap, after):
+def exchange(outer, outs, cap):
     width = outer.shape[1]
     if len(outs) == 2:
         inner, far = outs
@@ -382,8 +374,7 @@
         shuffle,
         [((PLANE * cap, width), BF)] * columns,
         2 * (STAGED * cap) ** 2 * width,
-        own, third_in, second_in, inner_in, after,
-        free=1,
+        own, third_in, second_in, inner_in,
     )
     moved = [toggle(blocks[m], m * PLANE) for m in reversed(range(1, columns))]
     return [outer_in, inner_in, blocks[0]] + moved
@@ -436,17 +427,14 @@
     outer, inner = call(
         grid_send,
         [grid_rim, grid_rim],
-        square(2 * ghalo, grid_rows),
+        64 * square(grid_rows, width),
         me, grid_latent, grid_halo_rows,
-        scalars=1, hbm=2,
+        scalars=1, hbm=2, limit=60 * 1024 * 1024,
         scratch=copies_of([grid_latent, grid_halo_rows]) + [pltpu.SemaphoreType.DMA((CHUNKS + 1,))],
     )
     outer_in, inner_in = across(outer), toggle(inner, 1)
 
-    sources = [
-        encoder_neighbours.T, mesh_neighbours.T, halo_rows, far_sources[0].T, encoder_weight, grid_latent, mesh_latent,
-    ]
-    near, grid_own_t, grid_rim_t, grid_slope, send, receive, own_t, forth_t, back_t = call(
+    near, grid_own_t, grid_rim_t, grid_slope, send, receive = call(
         functools.partial(encoder_local, size=ghalo),
         [
             total,
@@ -455,33 +443,38 @@
             ((grid_rows, width), BF),
             ((mesh_rows, listed), BF),
             ((mesh_rows, listed), BF),
-            ((mesh_rows, mesh_rows), BF),
-            ((listed, mesh_rows), BF),
-            ((listed, mesh_rows), BF),
         ],
         4 * square(grid_rows, width),
-        me, *sources,
-        scalars=1, hbm=len(sources),
-        scratch=copies_of(sources) + [pltpu.SemaphoreType.DMA((len(sources),))],
+        me, encoder_neighbours.T, halo_rows, far_sources[0].T, encoder_weight, grid_latent, mesh_latent,
+        scalars=1,
+    )
+
+    own_t, forth_t, back_t = call(
+        functools.partial(mesh_tables, size=halo, devices=devices),
+        [((mesh_rows, mesh_rows), BF)] + [((listed, mesh_rows), BF)] * 2,
+        square(mesh_rows, mesh_rows),
+        me, mesh_neighbours.T,
+        scalars=1,
     )
 
     hidden, message, slope_0, *outs = call(
         functools.partial(first_hidden, size=halo),
         [state, state, total] + sends(halo),
         step,
-        near, grid_rim_t, outer_in, inner_in, encoder_weight, processor_weights, send,
+        near, grid_rim_t, outer_in, inner_in, encoder_weight, processor_weights, send, back_t,
+        free=1,
     )
     (outer,) = call(forth, [rim], rim_flops, send, message)
     local = functools.partial(layer_local, scale=scale)
-    (near,) = call(local, [total], 5 * square(mesh_rows, mesh_rows), hidden, own_t, message)
+    ins = exchange(outer, outs, cap)
+    (near,) = call(local, [total], square(mesh_rows, mesh_rows), hidden, own_t, message, ins[2], free=1)
     decoder_own_t, decoder_rim_t, decoder_near, outer_extra, inner_extra = call(
         decoder_back,
         [((mesh_rows, grid_rows), BF), ((2 * halo, grid_rows), BF), total, rim, rim],
         square(grid_rows, mesh_rows),
-        me, decoder_neighbours.T, cotangent,
-        scalars=1,
-    )
-    ins = exchange(outer, outs, cap, decoder_near)
+        me, decoder_neighbours.T, cotangent, ins[2],
+        scalars=1, free=1,
+    )
 
     hidden, message, slope_1, *outs = call(
         functools.partial(next_hidden, ins=len(ins), layer=1, scale=scale, size=halo),
@@ -490,8 +483,8 @@
         near, forth_t, processor_weights, send, inner_extra, *ins,
     )
     (outer,) = call(forth, [wide], rim_flops, send, message, outer_extra)
-    (near,) = call(local, [total], 5 * square(mesh_rows, mesh_rows), hidden, own_t, message)
-    ins = exchange(outer, outs, cap, near)
+    (near,) = call(local, [total], 6 * square(mesh_rows, mesh_rows), hidden, own_t, message)
+    ins = exchange(outer, outs, cap)
 
     message, grad, *outs = call(
         functools.partial(turn, ins=len(ins), scale=scale, size=halo),
@@ -500,8 +493,8 @@
         near, forth_t, decoder_weight, send, receive, back_t, decoder_near, *ins,
     )
     (outer,) = call(back, [wide], rim_flops, back_t, grad, send, message)
-    (near,) = call(back_local, [total], 5 * square(mesh_rows, mesh_rows), own_t, grad)
-    ins = exchange(outer, outs, cap, near)
+    (near,) = call(back_local, [total], 6 * square(mesh_rows, mesh_rows), own_t, grad)
+    ins = exchange(outer, outs, cap)
     outer_decoder, inner_decoder = ins[:2]
 
     grad, *outs = call(
@@ -511,27 +504,27 @@
         near, receive, slope_1, processor_weights, grad, back_t, *ins,
     )
     (outer,) = call(back, [rim], rim_flops, back_t, grad)
-    (near,) = call(back_local, [total], square(mesh_rows, mesh_rows), own_t, grad)
-    ins = exchange(outer, outs, cap, near)
+    (near,) = call(back_local, [total], 6 * square(mesh_rows, mesh_rows), own_t, grad)
+    ins = exchange(outer, outs, cap)
+    grad, outer, inner = call(
+        functools.partial(last_back, ins=len(ins), scale=scale),
+        [state, grid_rim, grid_rim],
+        step,
+        near, receive, slope_0, processor_weights, grad, grid_rim_t, *ins,
+    )
+    outer_in, inner_in = across(outer), toggle(inner, 1)
     (output,) = call(
         decode,
         [((grid_rows, width), BF)],
         square(grid_rows, mesh_rows),
-        grid_latent, decoder_own_t, decoder_rim_t, message, outer_decoder, inner_decoder,
-    )
-
-    mesh_grad, outer, inner = call(
-        functools.partial(last_back, ins=len(ins), scale=scale),
-        [state, grid_rim, grid_rim],
-        step,
-        near, receive, slope_0, processor_weights, grad, grid_rim_t, *ins,
-    )
-    outer_in, inner_in = across(outer), toggle(inner, 1)
-    base, table, slope_rows = call(
+        grid_latent, decoder_own_t, decoder_rim_t, message, outer_decoder, inner_decoder, grad,
+        free=1,
+    )
+    base, table, slope_rows, mesh_grad = call(
         grid_local,
-        [((grid_rows, width), F32), ((grid_rows, 2 * ghalo), BF), ((2 * ghalo, width), F32)],
+        [((grid_rows, width), F32), ((grid_rows, 2 * ghalo), BF), ((2 * ghalo, width), F32), state],
         square(mesh_rows, grid_rows) + square(grid_rows, width),
-        me, grid_own_t, mesh_grad, grid_halo_rows, grid_slope, encoder_weight, cotangent,
+        me, grid_own_t, grad, grid_halo_rows, grid_slope, encoder_weight, cotangent,
         scalars=1,
     )
     (grid_grad,) = call(

time: 82.1 us -> 74.3 us (0.905)
  local copies, waits for them, and re-layouts: 9.05 us -> 0.06 us
  Pallas kernels: 21.4 us -> 22.4 us
    unnamed x34 -> x24, local copies, waits for them, and re-layouts: 9.05 us -> 0.06 us
    ppermute x6, waiting for transfers between devices: 4.68 us -> 1.89 us  [across(): return lax.ppermute(value, 'dom', pairs)]
    ppermute x26, waiting for transfers between devices: 5.67 us -> 8.09 us  [toggle(): return lax.ppermute(value, 'dom', [(i, i ^ bits) for i in range(peers)])]
    pallas_call x23 -> x24, Pallas kernels: 21.4 us -> 22.4 us  [call(): pl.pallas_call(inner, out_shape=shapes, in_specs=[pl.BlockSpec(memory_spa...]
  transfers between devices with their start and end apart: 32 -> 32, of which waited for: 15 -> 15; matrix products, arithmetic and copies ran while one was open for 0% -> 0% of each run, Pallas kernels for 16% -> 18%
where the time goes in v6:
time: 74.3 us; the launch traced here: 74.1 us
  starting transfers between devices  40.5 us (55%)
  Pallas kernels  22.4 us (30%)
  waiting for transfers between devices  9.98 us (13%)
  between operations  1.2 us (2%)
    ppermute x26, starting transfers between devices, toggle(): return lax.ppermute(value, 'dom', [(i, i ^ bits) for i in range(peers)])  27.2 us
    pallas_call x24, Pallas kernels, call(): pl.pallas_call(inner, out_shape=shapes, in_specs=[pl.BlockSpec(memory_spa...  22.4 us
    ppermute x6, starting transfers between devices, across(): return lax.ppermute(value, 'dom', pairs)  13.3 us
    ppermute x26, waiting for transfers between devices, toggle(): return lax.ppermute(value, 'dom', [(i, i ^ bits) for i in range(peers)])  8.09 us
    ppermute x6, waiting for transfers between devices, across(): return lax.ppermute(value, 'dom', pairs)  1.89 us
  transfers between devices with their start and end apart: 32, of which 15 were waited for; matrix products, arithmetic and copies ran while one was open for 0% of the time, Pallas kernels for 18%

profile of v6, /device:TPU:0, one launch (start us, length us, event | category | flops | bytes accessed | tf_op | source)
XLA Modules:
  0.0 74.1 jit_solution(16506546480410683201)
XLA Ops:
  0.7 2.4 %shard_map.140 = (bf16[64,512]{1,0:T(8,128)(2,1)}, bf16[64,512]{1,0:T(8,128)(2,1)}) custom-call(s32[1]{0:T(128)} %bitcast.me.refs_0_, bf16[1024,512]{1,0:T(8,128)(2,1)} %refs_0_.1, s32[1,2,64]{2,1,0:T(2,128)} %lists.5), custom_call_target="tpu_custom_call" | custom-call | flops 34359738368 | tf_op jit(solution)/shard_map/pallas_call | solution.py:76
  3.1 5.5 %collective-permute-start = (bf16[64,512]{1,0:T(8,128)(2,1)}, bf16[64,512]{1,0:T(8,128)(2,1)S(1)}, u32[]{:S(2)}, u32[]{:S(2)}) collective-permute-start(bf16[64,512]{1,0:T(8,128)(2,1)} %get-tuple-element.69), channel_id=1, source_target_pairs={{0,15},{1,2},{2,1},{3,4},{4,3},{5,6},{6,5},{7,8},{8,7},{9,10},{10,... | collective-permute-start | bytes 196616 | tf_op jit(solution)/shard_map/ppermute | solution.py:356
  8.7 2.9 %shard_map.139 = (f32[512,512]{1,0:T(8,128)S(1)}, bf16[1024,512]{1,0:T(8,128)(2,1)S(1)}, bf16[128,512]{1,0:T(8,128)(2,1)S(1)}, bf16[1024,512]{1,0:T(8,128)(2,1)S...) custom-call(s32[1]{0:T(128)} %bitcast.me.refs_0_, s32[4,512]{1,0:T(4,128)S(1)} %bitcast.9, ...), custom_call_target="tpu_custom_call" | custom-call | flops 2147483648 | bytes 5776132 | tf_op jit(solution)/shard_map/pallas_call | solution.py:76
  11.7 1.3 %shard_map.141 = (bf16[512,512]{1,0:T(8,128)(2,1)S(1)}, bf16[192,512]{1,0:T(8,128)(2,1)S(1)}, bf16[192,512]{1,0:T(8,128)(2,1)S(1)}) custom-call(s32[1]{0:T(128)} %bitcast.me.refs_0_, s32[8,512]{1,0:T(8,128)S(1)} %bitcast.7), custom_call_target="tpu_custom_call" | custom-call | flops 268435456 | bytes 933892 | tf_op jit(solution)/shard_map/pallas_call | solution.py:76
  14.8 1.7 %collective-permute-start.3 = (bf16[16,512]{1,0:T(8,128)(2,1)S(1)}, bf16[16,512]{1,0:T(8,128)(2,1)S(1)}, u32[]{:S(2)}, u32[]{:S(2)}) collective-permute-start(bf16[16,512]{1,0:T(8,128)(2,1)S(1)} %get-tuple-element.75), channel_id=1, source_target_pairs={{0,2},{1,3},{2,0},{3,1},{4,6},{5,7},{6,4},{7,5},{8,10},{9,11},{10,... | collective-permute-start | bytes 49160 | tf_op jit(solution)/shard_map/ppermute | solution.py:350
  16.8 1.9 %collective-permute-start.5 = (bf16[64,512]{1,0:T(8,128)(2,1)S(1)}, bf16[64,512]{1,0:T(8,128)(2,1)S(1)}, u32[]{:S(2)}, u32[]{:S(2)}) collective-permute-start(bf16[64,512]{1,0:T(8,128)(2,1)S(1)} %shard_map.146), channel_id=1, source_target_pairs={{0,15},{1,2},{2,1},{3,4},{4,3},{5,6},{6,5},{7,8},{8,7},{9,10},{10,... | collective-permute-start | bytes 196616 | tf_op jit(solution)/shard_map/ppermute | solution.py:356
  18.9 2.3 %collective-permute-start.6 = (bf16[16,512]{1,0:T(8,128)(2,1)S(1)}, bf16[16,512]{1,0:T(8,128)(2,1)S(1)}, u32[]{:S(2)}, u32[]{:S(2)}) collective-permute-start(bf16[16,512]{1,0:T(8,128)(2,1)S(1)} %get-tuple-element.85), channel_id=1, source_target_pairs={{0,12},{1,13},{2,14},{3,15},{4,8},{5,9},{6,10},{7,11},{8,4},{9,5},... | collective-permute-start | bytes 49160 | tf_op jit(solution)/shard_map/ppermute | solution.py:350
  21.1 2.2 %collective-permute-start.8 = (bf16[16,512]{1,0:T(8,128)(2,1)S(1)}, bf16[16,512]{1,0:T(8,128)(2,1)S(1)}, u32[]{:S(2)}, u32[]{:S(2)}) collective-permute-start(bf16[16,512]{1,0:T(8,128)(2,1)S(1)} %get-tuple-element.87), channel_id=1, source_target_pairs={{0,4},{1,5},{2,6},{3,7},{4,0},{5,1},{6,2},{7,3},{8,12},{9,13},{10,... | collective-permute-start | bytes 49160 | tf_op jit(solution)/shard_map/ppermute | solution.py:350
  29.2 2.2 %collective-permute-start.9 = (bf16[128,512]{1,0:T(8,128)(2,1)S(1)}, bf16[128,512]{1,0:T(8,128)(2,1)S(1)}, u32[]{:S(2)}, u32[]{:S(2)}) collective-permute-start(bf16[128,512]{1,0:T(8,128)(2,1)S(1)} %shard_map.149), channel_id=1, source_target_pairs={{0,15},{1,2},{2,1},{3,4},{4,3},{5,6},{6,5},{7,8},{8,7},{9,10},{10,... | collective-permute-start | bytes 393224 | tf_op jit(solution)/shard_map/ppermute | solution.py:356
  31.8 2.4 %collective-permute-start.13 = (bf16[16,512]{1,0:T(8,128)(2,1)S(1)}, bf16[16,512]{1,0:T(8,128)(2,1)S(1)}, u32[]{:S(2)}, u32[]{:S(2)}) collective-permute-start(bf16[16,512]{1,0:T(8,128)(2,1)S(1)} %get-tuple-element.98), channel_id=1, source_target_pairs={{0,12},{1,13},{2,14},{3,15},{4,8},{5,9},{6,10},{7,11},{8,4},{9,5},... | collective-permute-start | bytes 49160 | tf_op jit(solution)/shard_map/ppermute | solution.py:350
  37.4 1.5 %collective-permute-done.14.refs_4_ = bf16[16,512]{1,0:T(8,128)(2,1)S(1)} collective-permute-done((bf16[16,512]{1,0:T(8,128)(2,1)S(1)}, bf16[16,512]{1,0:T(8,128)(2,1)S(1)}, u32[]{:S(2)}, u32[]{:S(2)}) %collective-permute-start.14) | collective-permute-done | bytes 16416 | tf_op jit(solution)/shard_map/ppermute | solution.py:350
  39.1 1.5 %shard_map.151 = (bf16[512,512]{1,0:T(8,128)(2,1)S(1)}, bf16[512,512]{1,0:T(8,128)(2,1)S(1)}, bf16[144,512]{1,0:T(8,128)(2,1)S(1)}, bf16[16,512]{1,0:T(8,128)(2,...) custom-call(f32[512,512]{1,0:T(8,128)S(1)} %shard_map.148.near, ...), custom_call_target="tpu_custom_call" | custom-call | flops 1610612736 | bytes 4997120 | tf_op jit(solution)/shard_map/pallas_call | solution.py:76
  41.1 1.7 %collective-permute-start.19 = (bf16[16,512]{1,0:T(8,128)(2,1)S(1)}, bf16[16,512]{1,0:T(8,128)(2,1)S(1)}, u32[]{:S(2)}, u32[]{:S(2)}) collective-permute-start(bf16[16,512]{1,0:T(8,128)(2,1)S(1)} %get-tuple-element.107), channel_id=1, source_target_pairs={{0,2},{1,3},{2,0},{3,1},{4,6},{5,7},{6,4},{7,5},{8,10},{9,11},{10,... | collective-permute-start | bytes 49160 | tf_op jit(solution)/shard_map/ppermute | solution.py:350
  43.1 1.4 %collective-permute-start.16 = (bf16[128,512]{1,0:T(8,128)(2,1)S(1)}, bf16[128,512]{1,0:T(8,128)(2,1)S(1)}, u32[]{:S(2)}, u32[]{:S(2)}) collective-permute-start(bf16[128,512]{1,0:T(8,128)(2,1)S(1)} %shard_map.152), channel_id=1, source_target_pairs={{0,15},{1,2},{2,1},{3,4},{4,3},{5,6},{6,5},{7,8},{8,7},{9,10},{10,... | collective-permute-start | bytes 393224 | tf_op jit(solution)/shard_map/ppermute | solution.py:356
  45.0 2.3 %collective-permute-start.20 = (bf16[16,512]{1,0:T(8,128)(2,1)S(1)}, bf16[16,512]{1,0:T(8,128)(2,1)S(1)}, u32[]{:S(2)}, u32[]{:S(2)}) collective-permute-start(bf16[16,512]{1,0:T(8,128)(2,1)S(1)} %get-tuple-element.109), channel_id=1, source_target_pairs={{0,12},{1,13},{2,14},{3,15},{4,8},{5,9},{6,10},{7,11},{8,4},{9,5},... | collective-permute-start | bytes 49160 | tf_op jit(solution)/shard_map/ppermute | solution.py:350
  48.2 1.3 %collective-permute-start.22 = (bf16[16,512]{1,0:T(8,128)(2,1)S(1)}, bf16[16,512]{1,0:T(8,128)(2,1)S(1)}, u32[]{:S(2)}, u32[]{:S(2)}) collective-permute-start(bf16[16,512]{1,0:T(8,128)(2,1)S(1)} %get-tuple-element.111), channel_id=1, source_target_pairs={{0,4},{1,5},{2,6},{3,7},{4,0},{5,1},{6,2},{7,3},{8,12},{9,13},{10,... | collective-permute-start | bytes 49160 | tf_op jit(solution)/shard_map/ppermute | solution.py:350
  50.6 1.3 %collective-permute-done.21.refs_4_ = bf16[16,512]{1,0:T(8,128)(2,1)S(1)} collective-permute-done((bf16[16,512]{1,0:T(8,128)(2,1)S(1)}, bf16[16,512]{1,0:T(8,128)(2,1)S(1)}, u32[]{:S(2)}, u32[]{:S(2)}) %collective-permute-start.21) | collective-permute-done | bytes 16416 | tf_op jit(solution)/shard_map/ppermute | solution.py:350
  55.3 2.2 %collective-permute-start.23 = (bf16[64,512]{1,0:T(8,128)(2,1)S(1)}, bf16[64,512]{1,0:T(8,128)(2,1)S(1)}, u32[]{:S(2)}, u32[]{:S(2)}) collective-permute-start(bf16[64,512]{1,0:T(8,128)(2,1)S(1)} %shard_map.157), channel_id=1, source_target_pairs={{0,15},{1,2},{2,1},{3,4},{4,3},{5,6},{6,5},{7,8},{8,7},{9,10},{10,... | collective-permute-start | bytes 196616 | tf_op jit(solution)/shard_map/ppermute | solution.py:356
  58.0 2.5 %collective-permute-start.27 = (bf16[16,512]{1,0:T(8,128)(2,1)S(1)}, bf16[16,512]{1,0:T(8,128)(2,1)S(1)}, u32[]{:S(2)}, u32[]{:S(2)}) collective-permute-start(bf16[16,512]{1,0:T(8,128)(2,1)S(1)} %get-tuple-element.119), channel_id=1, source_target_pairs={{0,12},{1,13},{2,14},{3,15},{4,8},{5,9},{6,10},{7,11},{8,4},{9,5},... | collective-permute-start | bytes 49160 | tf_op jit(solution)/shard_map/ppermute | solution.py:350
  63.6 1.5 %collective-permute-done.28.refs_4_ = bf16[16,512]{1,0:T(8,128)(2,1)S(1)} collective-permute-done((bf16[16,512]{1,0:T(8,128)(2,1)S(1)}, bf16[16,512]{1,0:T(8,128)(2,1)S(1)}, u32[]{:S(2)}, u32[]{:S(2)}) %collective-permute-start.28) | collective-permute-done | bytes 16416 | tf_op jit(solution)/shard_map/ppermute | solution.py:350
  66.5 2.5 %shard_map.161 = (f32[1024,512]{1,0:T(8,128)S(1)}, bf16[1024,128]{1,0:T(8,128)(2,1)S(1)}, f32[128,512]{1,0:T(8,128)S(1)}, bf16[512,512]{1,0:T(8,128)(2,1)}) custom-call(s32[1]{0:T(128)} %bitcast.me.refs_0_, bf16[1024,512]{1,0:T(8,128)(2,1)S(1)} %get-tuple-element.123.own_t, bf16[512,512]{1,0:T(8,128)(2,1)S(1)} %get-tuple-element.122.refs_6_.grad, ...), custom_call_target="tpu_custom_call" | custom-call | flops 1073741824 | bytes 7340548 | tf_op jit(solution)/shard_map/pallas_call | solution.py:76
  69.1 2.0 %shard_map.160 = bf16[1024,512]{1,0:T(8,128)(2,1)} custom-call(bf16[1024,512]{1,0:T(8,128)(2,1)S(1)} %copy-done.3, bf16[512,1024]{1,0:T(8,128)(2,1)S(1)} %get-tuple-element.78.refs_1_, bf16[128,1024]{1,0:T(8,128)(2,1)S(1)} %get-tuple-element.79.refs_2_, bf16[512,512]{1,0:T(8,128)(2,1)S(1)} %get-tuple-element.101.refs_1_.refs_3_, ...), custom_call_target="tpu_custom_call" | custom-call | flops 536870912 | bytes 4734976 | tf_op jit(solution)/shard_map/pallas_call | solution.py:76
  71.0 1.4 %collective-permute-done.30.outer_in = bf16[64,512]{1,0:T(8,128)(2,1)S(1)} collective-permute-done((bf16[64,512]{1,0:T(8,128)(2,1)S(1)}, bf16[64,512]{1,0:T(8,128)(2,1)S(1)}, u32[]{:S(2)}, u32[]{:S(2)}) %collective-permute-start.30) | collective-permute-done | bytes 65568 | tf_op jit(solution)/shard_map/ppermute | solution.py:356
  72.5 1.5 %shard_map.162 = bf16[1024,512]{1,0:T(8,128)(2,1)} custom-call(f32[1024,512]{1,0:T(8,128)S(1)} %get-tuple-element.125.base, bf16[1024,128]{1,0:T(8,128)(2,1)S(1)} %get-tuple-element.126.table, f32[128,512]{1,0:T(8,128)S(1)} %get-tuple-element.127.slope_rows, bf16[512,512]{1,0:T(8,128)(2,1)S(1)} %copy-done.1, ...), custom_call_target="tpu_custom_call" | custom-call | flops 268435456 | bytes 4325376 | tf_op jit(solution)/shard_map/pallas_call | solution.py:76
  (88 shorter events, 23.5 us)
Async XLA Ops:
  3.1 9.9 %collective-permute-start = (bf16[64,512]{1,0:T(8,128)(2,1)}, bf16[64,512]{1,0:T(8,128)(2,1)S(1)}, u32[]{:S(2)}, u32[]{:S(2)}) collective-permute-start(bf16[64,512]{1,0:T(8,128)(2,1)} %get-tuple-element.69), channel_id=1, source_target_pairs={{0,15},{1,2},{2,1},{3,4},{4,3},{5,6},{6,5},{7,8},{8,7},{9,10},{10,... | collective-permute-start | bytes 196616 | tf_op jit(solution)/shard_map/ppermute | solution.py:356
  8.6 4.4 %collective-permute-start.1 = (bf16[64,512]{1,0:T(8,128)(2,1)}, bf16[64,512]{1,0:T(8,128)(2,1)S(1)}, u32[]{:S(2)}, u32[]{:S(2)}) collective-permute-start(bf16[64,512]{1,0:T(8,128)(2,1)} %get-tuple-element.70), channel_id=1, source_target_pairs={{0,1},{1,0},{2,3},{3,2},{4,5},{5,4},{6,7},{7,6},{8,9},{9,8},{10,11... | collective-permute-start | bytes 196616 | tf_op jit(solution)/shard_map/ppermute | solution.py:350
  14.2 4.5 %collective-permute-start.4 = (bf16[80,512]{1,0:T(8,128)(2,1)S(1)}, bf16[80,512]{1,0:T(8,128)(2,1)S(1)}, u32[]{:S(2)}, u32[]{:S(2)}) collective-permute-start(bf16[80,512]{1,0:T(8,128)(2,1)S(1)} %get-tuple-element.76), channel_id=1, source_target_pairs={{0,1},{1,0},{2,3},{3,2},{4,5},{5,4},{6,7},{7,6},{8,9},{9,8},{10,11... | collective-permute-start | bytes 245768 | tf_op jit(solution)/shard_map/ppermute | solution.py:350
  16.8 8.1 %collective-permute-start.5 = (bf16[64,512]{1,0:T(8,128)(2,1)S(1)}, bf16[64,512]{1,0:T(8,128)(2,1)S(1)}, u32[]{:S(2)}, u32[]{:S(2)}) collective-permute-start(bf16[64,512]{1,0:T(8,128)(2,1)S(1)} %shard_map.146), channel_id=1, source_target_pairs={{0,15},{1,2},{2,1},{3,4},{4,3},{5,6},{6,5},{7,8},{8,7},{9,10},{10,... | collective-permute-start | bytes 196616 | tf_op jit(solution)/shard_map/ppermute | solution.py:356
  18.9 6.1 %collective-permute-start.6 = (bf16[16,512]{1,0:T(8,128)(2,1)S(1)}, bf16[16,512]{1,0:T(8,128)(2,1)S(1)}, u32[]{:S(2)}, u32[]{:S(2)}) collective-permute-start(bf16[16,512]{1,0:T(8,128)(2,1)S(1)} %get-tuple-element.85), channel_id=1, source_target_pairs={{0,12},{1,13},{2,14},{3,15},{4,8},{5,9},{6,10},{7,11},{8,4},{9,5},... | collective-permute-start | bytes 49160 | tf_op jit(solution)/shard_map/ppermute | solution.py:350
  21.1 4.6 %collective-permute-start.7 = (bf16[16,512]{1,0:T(8,128)(2,1)S(1)}, bf16[16,512]{1,0:T(8,128)(2,1)S(1)}, u32[]{:S(2)}, u32[]{:S(2)}) collective-permute-start(bf16[16,512]{1,0:T(8,128)(2,1)S(1)} %get-tuple-element.86), channel_id=1, source_target_pairs={{0,8},{1,9},{2,10},{3,11},{4,12},{5,13},{6,14},{7,15},{8,0},{9,1},... | collective-permute-start | bytes 49160 | tf_op jit(solution)/shard_map/ppermute | solution.py:350
  21.1 4.6 %collective-permute-start.8 = (bf16[16,512]{1,0:T(8,128)(2,1)S(1)}, bf16[16,512]{1,0:T(8,128)(2,1)S(1)}, u32[]{:S(2)}, u32[]{:S(2)}) collective-permute-start(bf16[16,512]{1,0:T(8,128)(2,1)S(1)} %get-tuple-element.87), channel_id=1, source_target_pairs={{0,4},{1,5},{2,6},{3,7},{4,0},{5,1},{6,2},{7,3},{8,12},{9,13},{10,... | collective-permute-start | bytes 49160 | tf_op jit(solution)/shard_map/ppermute | solution.py:350
  26.8 4.9 %collective-permute-start.10 = (bf16[144,512]{1,0:T(8,128)(2,1)S(1)}, bf16[144,512]{1,0:T(8,128)(2,1)S(1)}, u32[]{:S(2)}, u32[]{:S(2)}) collective-permute-start(bf16[144,512]{1,0:T(8,128)(2,1)S(1)} %get-tuple-element.93), channel_id=1, source_target_pairs={{0,1},{1,0},{2,3},{3,2},{4,5},{5,4},{6,7},{7,6},{8,9},{9,8},{10,11... | collective-permute-start | bytes 442376 | tf_op jit(solution)/shard_map/ppermute | solution.py:350
  26.8 4.5 %collective-permute-start.11 = (bf16[16,512]{1,0:T(8,128)(2,1)S(1)}, bf16[16,512]{1,0:T(8,128)(2,1)S(1)}, u32[]{:S(2)}, u32[]{:S(2)}) collective-permute-start(bf16[16,512]{1,0:T(8,128)(2,1)S(1)} %get-tuple-element.95), channel_id=1, source_target_pairs={{0,3},{1,2},{2,1},{3,0},{4,7},{5,6},{6,5},{7,4},{8,11},{9,10},{10,... | collective-permute-start | bytes 49160 | tf_op jit(solution)/shard_map/ppermute | solution.py:350
  29.2 7.5 %collective-permute-start.9 = (bf16[128,512]{1,0:T(8,128)(2,1)S(1)}, bf16[128,512]{1,0:T(8,128)(2,1)S(1)}, u32[]{:S(2)}, u32[]{:S(2)}) collective-permute-start(bf16[128,512]{1,0:T(8,128)(2,1)S(1)} %shard_map.149), channel_id=1, source_target_pairs={{0,15},{1,2},{2,1},{3,4},{4,3},{5,6},{6,5},{7,8},{8,7},{9,10},{10,... | collective-permute-start | bytes 393224 | tf_op jit(solution)/shard_map/ppermute | solution.py:356
  31.8 5.6 %collective-permute-start.13 = (bf16[16,512]{1,0:T(8,128)(2,1)S(1)}, bf16[16,512]{1,0:T(8,128)(2,1)S(1)}, u32[]{:S(2)}, u32[]{:S(2)}) collective-permute-start(bf16[16,512]{1,0:T(8,128)(2,1)S(1)} %get-tuple-element.98), channel_id=1, source_target_pairs={{0,12},{1,13},{2,14},{3,15},{4,8},{5,9},{6,10},{7,11},{8,4},{9,5},... | collective-permute-start | bytes 49160 | tf_op jit(solution)/shard_map/ppermute | solution.py:350
  34.2 4.6 %collective-permute-start.14 = (bf16[16,512]{1,0:T(8,128)(2,1)S(1)}, bf16[16,512]{1,0:T(8,128)(2,1)S(1)}, u32[]{:S(2)}, u32[]{:S(2)}) collective-permute-start(bf16[16,512]{1,0:T(8,128)(2,1)S(1)} %get-tuple-element.99), channel_id=1, source_target_pairs={{0,8},{1,9},{2,10},{3,11},{4,12},{5,13},{6,14},{7,15},{8,0},{9,1},... | collective-permute-start | bytes 49160 | tf_op jit(solution)/shard_map/ppermute | solution.py:350
  40.5 4.3 %collective-permute-start.17 = (bf16[144,512]{1,0:T(8,128)(2,1)S(1)}, bf16[144,512]{1,0:T(8,128)(2,1)S(1)}, u32[]{:S(2)}, u32[]{:S(2)}) collective-permute-start(bf16[144,512]{1,0:T(8,128)(2,1)S(1)} %get-tuple-element.103), channel_id=1, source_target_pairs={{0,1},{1,0},{2,3},{3,2},{4,5},{5,4},{6,7},{7,6},{8,9},{9,8},{10,11... | collective-permute-start | bytes 442376 | tf_op jit(solution)/shard_map/ppermute | solution.py:350
  43.1 7.3 %collective-permute-start.16 = (bf16[128,512]{1,0:T(8,128)(2,1)S(1)}, bf16[128,512]{1,0:T(8,128)(2,1)S(1)}, u32[]{:S(2)}, u32[]{:S(2)}) collective-permute-start(bf16[128,512]{1,0:T(8,128)(2,1)S(1)} %shard_map.152), channel_id=1, source_target_pairs={{0,15},{1,2},{2,1},{3,4},{4,3},{5,6},{6,5},{7,8},{8,7},{9,10},{10,... | collective-permute-start | bytes 393224 | tf_op jit(solution)/shard_map/ppermute | solution.py:356
  45.0 5.6 %collective-permute-start.20 = (bf16[16,512]{1,0:T(8,128)(2,1)S(1)}, bf16[16,512]{1,0:T(8,128)(2,1)S(1)}, u32[]{:S(2)}, u32[]{:S(2)}) collective-permute-start(bf16[16,512]{1,0:T(8,128)(2,1)S(1)} %get-tuple-element.109), channel_id=1, source_target_pairs={{0,12},{1,13},{2,14},{3,15},{4,8},{5,9},{6,10},{7,11},{8,4},{9,5},... | collective-permute-start | bytes 49160 | tf_op jit(solution)/shard_map/ppermute | solution.py:350
  47.2 4.7 %collective-permute-start.21 = (bf16[16,512]{1,0:T(8,128)(2,1)S(1)}, bf16[16,512]{1,0:T(8,128)(2,1)S(1)}, u32[]{:S(2)}, u32[]{:S(2)}) collective-permute-start(bf16[16,512]{1,0:T(8,128)(2,1)S(1)} %get-tuple-element.110), channel_id=1, source_target_pairs={{0,8},{1,9},{2,10},{3,11},{4,12},{5,13},{6,14},{7,15},{8,0},{9,1},... | collective-permute-start | bytes 49160 | tf_op jit(solution)/shard_map/ppermute | solution.py:350
  48.2 3.9 %collective-permute-start.22 = (bf16[16,512]{1,0:T(8,128)(2,1)S(1)}, bf16[16,512]{1,0:T(8,128)(2,1)S(1)}, u32[]{:S(2)}, u32[]{:S(2)}) collective-permute-start(bf16[16,512]{1,0:T(8,128)(2,1)S(1)} %get-tuple-element.111), channel_id=1, source_target_pairs={{0,4},{1,5},{2,6},{3,7},{4,0},{5,1},{6,2},{7,3},{8,12},{9,13},{10,... | collective-permute-start | bytes 49160 | tf_op jit(solution)/shard_map/ppermute | solution.py:350
  52.8 4.8 %collective-permute-start.24 = (bf16[80,512]{1,0:T(8,128)(2,1)S(1)}, bf16[80,512]{1,0:T(8,128)(2,1)S(1)}, u32[]{:S(2)}, u32[]{:S(2)}) collective-permute-start(bf16[80,512]{1,0:T(8,128)(2,1)S(1)} %get-tuple-element.114), channel_id=1, source_target_pairs={{0,1},{1,0},{2,3},{3,2},{4,5},{5,4},{6,7},{7,6},{8,9},{9,8},{10,11... | collective-permute-start | bytes 245768 | tf_op jit(solution)/shard_map/ppermute | solution.py:350
  52.9 4.5 %collective-permute-start.25 = (bf16[16,512]{1,0:T(8,128)(2,1)S(1)}, bf16[16,512]{1,0:T(8,128)(2,1)S(1)}, u32[]{:S(2)}, u32[]{:S(2)}) collective-permute-start(bf16[16,512]{1,0:T(8,128)(2,1)S(1)} %get-tuple-element.116), channel_id=1, source_target_pairs={{0,3},{1,2},{2,1},{3,0},{4,7},{5,6},{6,5},{7,4},{8,11},{9,10},{10,... | collective-permute-start | bytes 49160 | tf_op jit(solution)/shard_map/ppermute | solution.py:350
  55.3 7.6 %collective-permute-start.23 = (bf16[64,512]{1,0:T(8,128)(2,1)S(1)}, bf16[64,512]{1,0:T(8,128)(2,1)S(1)}, u32[]{:S(2)}, u32[]{:S(2)}) collective-permute-start(bf16[64,512]{1,0:T(8,128)(2,1)S(1)} %shard_map.157), channel_id=1, source_target_pairs={{0,15},{1,2},{2,1},{3,4},{4,3},{5,6},{6,5},{7,8},{8,7},{9,10},{10,... | collective-permute-start | bytes 196616 | tf_op jit(solution)/shard_map/ppermute | solution.py:356
  58.0 5.6 %collective-permute-start.27 = (bf16[16,512]{1,0:T(8,128)(2,1)S(1)}, bf16[16,512]{1,0:T(8,128)(2,1)S(1)}, u32[]{:S(2)}, u32[]{:S(2)}) collective-permute-start(bf16[16,512]{1,0:T(8,128)(2,1)S(1)} %get-tuple-element.119), channel_id=1, source_target_pairs={{0,12},{1,13},{2,14},{3,15},{4,8},{5,9},{6,10},{7,11},{8,4},{9,5},... | collective-permute-start | bytes 49160 | tf_op jit(solution)/shard_map/ppermute | solution.py:350
  60.5 4.6 %collective-permute-start.28 = (bf16[16,512]{1,0:T(8,128)(2,1)S(1)}, bf16[16,512]{1,0:T(8,128)(2,1)S(1)}, u32[]{:S(2)}, u32[]{:S(2)}) collective-permute-start(bf16[16,512]{1,0:T(8,128)(2,1)S(1)} %get-tuple-element.120), channel_id=1, source_target_pairs={{0,8},{1,9},{2,10},{3,11},{4,12},{5,13},{6,14},{7,15},{8,0},{9,1},... | collective-permute-start | bytes 49160 | tf_op jit(solution)/shard_map/ppermute | solution.py:350
  66.0 6.5 %collective-permute-start.30 = (bf16[64,512]{1,0:T(8,128)(2,1)S(1)}, bf16[64,512]{1,0:T(8,128)(2,1)S(1)}, u32[]{:S(2)}, u32[]{:S(2)}) collective-permute-start(bf16[64,512]{1,0:T(8,128)(2,1)S(1)} %get-tuple-element.128), channel_id=1, source_target_pairs={{0,15},{1,2},{2,1},{3,4},{4,3},{5,6},{6,5},{7,8},{8,7},{9,10},{10,... | collective-permute-start | bytes 196616 | tf_op jit(solution)/shard_map/ppermute | solution.py:356
  66.1 6.4 %collective-permute-start.31 = (bf16[64,512]{1,0:T(8,128)(2,1)S(1)}, bf16[64,512]{1,0:T(8,128)(2,1)S(1)}, u32[]{:S(2)}, u32[]{:S(2)}) collective-permute-start(bf16[64,512]{1,0:T(8,128)(2,1)S(1)} %get-tuple-element.129), channel_id=1, source_target_pairs={{0,1},{1,0},{2,3},{3,2},{4,5},{5,4},{6,7},{7,6},{8,9},{9,8},{10,11... | collective-permute-start | bytes 196616 | tf_op jit(solution)/shard_map/ppermute | solution.py:350
  (20 other events, 110.4 us)

commit v7 on v6

--- a/solution.py
+++ b/solution.py
@@ -143,7 +143,7 @@
     place = lax.broadcasted_iota(jnp.int32, (devices, devices * cap), 1)
     if devices == STAGED:
         x = partner ^ me[0]
-        send_place, receive_place = by_stage(x, devices) * cap, x * cap
+        send_place, receive_place = x * cap, by_stage(x, devices) * cap
     else:
         send_place, receive_place = partner * cap, partner * cap
     send_far = jnp.zeros((rows, devices * cap), F32)
@@ -169,7 +169,7 @@
     partner, slot = far // cap, far % cap
     if devices == STAGED:
         partner = partner ^ me[0]
-        send_place, receive_place = by_stage(partner, devices) * cap + slot, partner * cap + slot
+        send_place, receive_place = partner * cap + slot, by_stage(partner, devices) * cap + slot
     else:
         send_place, receive_place = far, far
     is_far = columns >= rows + 2 * size
@@ -196,19 +196,12 @@
     inner = outs[0]
     rows = rows.astype(BF)
     inner[:size] = rows[:size]
-    used = size
     if extra is not None:
-        inner[size : 2 * size] = extra
-        used = 2 * size
+        inner[size:] = extra
     far = rows[size:]
-    if len(outs) == 2:
-        outs[1][...] = far
-        return
-    block = far.shape[0] // PLANE
-    inner[used:] = far[block : 2 * block]
-    outs[1][...] = far[:block]
-    for k in range(2, PLANE):
-        outs[k][...] = far[k * block : (k + 1) * block]
+    block = far.shape[0] // (len(outs) - 1)
+    for m, out in enumerate(outs[1:]):
+        out[...] = far[m * block : (m + 1) * block]
 
 
 def outer_forth(send, message, *refs, size):
@@ -227,23 +220,34 @@
 
 
 def arrived(ins, size):
-    far = list(ins[2:3]) + list(ins[3:])[::-1]
-    return jnp.concatenate([ins[0][:size], ins[1][:size]] + [ref[...] for ref in far], axis=0)
-
-
-def shuffle(own, third, second, first, *outs):
-    block = own.shape[0]
-    parts = [own[...], first[first.shape[0] - block :], second[...], third[...]]
+    outer, inner = ins[:2]
+    parts = [outer[:size], inner[:size]]
+    if len(ins) > 3:
+        third, second, own = ins[2:]
+        parts += [own[...], inner[inner.shape[0] - own.shape[0] :], second[...], third[...]]
+    else:
+        parts += [ref[...] for ref in ins[2:]]
+    return jnp.concatenate(parts, axis=0)
+
+
+def shuffle(inner, own, *refs):
+    columns = STAGED // PLANE
+    parts = [own[...]] + [ref[...] for ref in refs[: columns - 1][::-1]]
     rows = jnp.concatenate(parts, axis=0)
+    outs = refs[columns - 1 :]
     count = rows.shape[0]
-    cap = count // (PLANE * len(outs))
+    cap = count // STAGED
     target = lax.broadcasted_iota(jnp.int32, (count, count), 0)
     source = lax.broadcasted_iota(jnp.int32, (count, count), 1)
     place, slot = target // cap, target % cap
-    wanted = ((place % PLANE) * len(outs) + place // PLANE) * cap + slot
+    wanted = ((place % columns) * PLANE + place // columns) * cap + slot
     moved = mm((source == wanted).astype(F32).astype(BF), rows).astype(BF)
-    for m, out in enumerate(outs):
-        out[...] = moved[m * PLANE * cap : (m + 1) * PLANE * cap]
+    block = columns * cap
+    used = inner.shape[0]
+    outs[1][:used] = inner[...]
+    outs[1][used:] = moved[block : 2 * block]
+    for k in (0, 2, 3):
+        outs[k][...] = moved[k * block : (k + 1) * block]
 
 
 def layer_local(hidden, own_t, message, near, *, scale):
@@ -364,20 +368,18 @@
         blocks = far.reshape(peers, cap, width)
         blocks = lax.all_to_all(blocks, "dom", split_axis=0, concat_axis=0, tiled=True)
         return [across(outer), toggle(inner, 1), blocks.reshape(-1, width)]
-    inner, own, second, third = outs
+    inner, own, *rest = outs
+    columns = STAGED // PLANE
+    moved = [toggle(rest[m - 1], m * PLANE) for m in reversed(range(1, columns))]
     outer_in = across(outer)
-    inner_in = toggle(inner, 1)
-    second_in = toggle(second, 2)
-    third_in = toggle(third, 3)
-    columns = STAGED // PLANE
+    block = columns * cap
     blocks = call(
         shuffle,
-        [((PLANE * cap, width), BF)] * columns,
+        [((block, width), BF), ((inner.shape[0] + block, width), BF), ((block, width), BF), ((block, width), BF)],
         2 * (STAGED * cap) ** 2 * width,
-        own, third_in, second_in, inner_in,
-    )
-    moved = [toggle(blocks[m], m * PLANE) for m in reversed(range(1, columns))]
-    return [outer_in, inner_in, blocks[0]] + moved
+        inner, own, *moved,
+    )
+    return [outer_in, toggle(blocks[1], 1), toggle(blocks[3], 3), toggle(blocks[2], 2), blocks[0]]
 
 
 def on_device(
@@ -409,10 +411,8 @@
         return 2 * rows * depth * width
 
     def sends(per_side):
-        if devices != STAGED:
-            return [((per_side, width), BF), ((slots, width), BF)]
-        block = slots // PLANE
-        return [((per_side + block, width), BF)] + [((block, width), BF)] * (PLANE - 1)
+        stages = STAGED // PLANE if devices == STAGED else 1
+        return [((per_side, width), BF)] + [((slots // stages, width), BF)] * stages
 
     state = ((mesh_rows, width), BF)
     total = ((mesh_rows, width), F32)
@@ -467,12 +467,12 @@
     (outer,) = call(forth, [rim], rim_flops, send, message)
     local = functools.partial(layer_local, scale=scale)
     ins = exchange(outer, outs, cap)
-    (near,) = call(local, [total], square(mesh_rows, mesh_rows), hidden, own_t, message, ins[2], free=1)
+    (near,) = call(local, [total], 6 * square(mesh_rows, mesh_rows), hidden, own_t, message, ins[-1], free=1)
     decoder_own_t, decoder_rim_t, decoder_near, outer_extra, inner_extra = call(
         decoder_back,
         [((mesh_rows, grid_rows), BF), ((2 * halo, grid_rows), BF), total, rim, rim],
         square(grid_rows, mesh_rows),
-        me, decoder_neighbours.T, cotangent, ins[2],
+        me, decoder_neighbours.T, cotangent, ins[-1],
         scalars=1, free=1,
     )
 

time: 74.3 us -> 73.4 us (0.988)
  starting transfers between devices: 40.5 us -> 38.2 us
    ppermute x26, starting transfers between devices: 27.2 us -> 25.5 us  [toggle(): return lax.ppermute(value, 'dom', [(i, i ^ bits) for i in range(peers)])]
    ppermute x6, waiting for transfers between devices: 1.89 us -> 2.64 us  [across(): return lax.ppermute(value, 'dom', pairs)]
    unnamed x24, local copies, waits for them, and re-layouts: 0.06 us -> 0.8 us
  transfers between devices with their start and end apart: 32 -> 32, of which waited for: 15 -> 13; matrix products, arithmetic and copies ran while one was open for 0% -> 0% of each run, Pallas kernels for 18% -> 18%
where the time goes in v7:
time: 73.4 us; the launch traced here: 73.2 us
  starting transfers between devices  38.2 us (52%)
  Pallas kernels  22.4 us (31%)
  waiting for transfers between devices  10.6 us (14%)
  between operations  1.17 us (2%)
  local copies, waits for them, and re-layouts  0.8 us (1%)
    ppermute x26, starting transfers between devices, toggle(): return lax.ppermute(value, 'dom', [(i, i ^ bits) for i in range(peers)])  25.5 us
    pallas_call x24, Pallas kernels, call(): pl.pallas_call(inner, out_shape=shapes, in_specs=[pl.BlockSpec(memory_spa...  22.4 us
    ppermute x6, starting transfers between devices, across(): return lax.ppermute(value, 'dom', pairs)  12.7 us
    ppermute x26, waiting for transfers between devices, toggle(): return lax.ppermute(value, 'dom', [(i, i ^ bits) for i in range(peers)])  7.98 us
    ppermute x6, waiting for transfers between devices, across(): return lax.ppermute(value, 'dom', pairs)  2.64 us
  transfers between devices with their start and end apart: 32, of which 13 were waited for; matrix products, arithmetic and copies ran while one was open for 0% of the time, Pallas kernels for 18%

profile of v7, /device:TPU:0, one launch (start us, length us, event | category | flops | bytes accessed | tf_op | source)
XLA Modules:
  0.0 73.2 jit_solution(13301563037325720907)
XLA Ops:
  0.7 2.4 %shard_map.140 = (bf16[64,512]{1,0:T(8,128)(2,1)}, bf16[64,512]{1,0:T(8,128)(2,1)}) custom-call(s32[1]{0:T(128)} %bitcast.me.refs_0_, bf16[1024,512]{1,0:T(8,128)(2,1)} %refs_0_.1, s32[1,2,64]{2,1,0:T(2,128)} %lists.5), custom_call_target="tpu_custom_call" | custom-call | flops 34359738368 | tf_op jit(solution)/shard_map/pallas_call | solution.py:76
  3.1 5.5 %collective-permute-start = (bf16[64,512]{1,0:T(8,128)(2,1)}, bf16[64,512]{1,0:T(8,128)(2,1)S(1)}, u32[]{:S(2)}, u32[]{:S(2)}) collective-permute-start(bf16[64,512]{1,0:T(8,128)(2,1)} %get-tuple-element.73), channel_id=1, source_target_pairs={{0,15},{1,2},{2,1},{3,4},{4,3},{5,6},{6,5},{7,8},{8,7},{9,10},{10,... | collective-permute-start | bytes 196616 | tf_op jit(solution)/shard_map/ppermute | solution.py:360
  8.7 2.9 %shard_map.139 = (f32[512,512]{1,0:T(8,128)S(1)}, bf16[1024,512]{1,0:T(8,128)(2,1)S(1)}, bf16[128,512]{1,0:T(8,128)(2,1)S(1)}, bf16[1024,512]{1,0:T(8,128)(2,1)S...) custom-call(s32[1]{0:T(128)} %bitcast.me.refs_0_, s32[4,512]{1,0:T(4,128)S(1)} %bitcast.9, ...), custom_call_target="tpu_custom_call" | custom-call | flops 2147483648 | bytes 5776132 | tf_op jit(solution)/shard_map/pallas_call | solution.py:76
  11.7 1.3 %shard_map.141 = (bf16[512,512]{1,0:T(8,128)(2,1)S(1)}, bf16[192,512]{1,0:T(8,128)(2,1)S(1)}, bf16[192,512]{1,0:T(8,128)(2,1)S(1)}) custom-call(s32[1]{0:T(128)} %bitcast.me.refs_0_, s32[8,512]{1,0:T(8,128)S(1)} %bitcast.7), custom_call_target="tpu_custom_call" | custom-call | flops 268435456 | bytes 933892 | tf_op jit(solution)/shard_map/pallas_call | solution.py:76
  14.2 1.3 %collective-permute-start.2 = (bf16[16,512]{1,0:T(8,128)(2,1)S(1)}, bf16[16,512]{1,0:T(8,128)(2,1)S(1)}, u32[]{:S(2)}, u32[]{:S(2)}) collective-permute-start(bf16[16,512]{1,0:T(8,128)(2,1)S(1)} %get-tuple-element.79), channel_id=1, source_target_pairs={{0,12},{1,13},{2,14},{3,15},{4,8},{5,9},{6,10},{7,11},{8,4},{9,5},... | collective-permute-start | bytes 49160 | tf_op jit(solution)/shard_map/ppermute | solution.py:354
  15.5 3.2 %collective-permute-start.4 = (bf16[16,512]{1,0:T(8,128)(2,1)S(1)}, bf16[16,512]{1,0:T(8,128)(2,1)S(1)}, u32[]{:S(2)}, u32[]{:S(2)}) collective-permute-start(bf16[16,512]{1,0:T(8,128)(2,1)S(1)} %get-tuple-element.81), channel_id=1, source_target_pairs={{0,4},{1,5},{2,6},{3,7},{4,0},{5,1},{6,2},{7,3},{8,12},{9,13},{10,... | collective-permute-start | bytes 49160 | tf_op jit(solution)/shard_map/ppermute | solution.py:354
  18.9 1.4 %collective-permute-start.5 = (bf16[64,512]{1,0:T(8,128)(2,1)S(1)}, bf16[64,512]{1,0:T(8,128)(2,1)S(1)}, u32[]{:S(2)}, u32[]{:S(2)}) collective-permute-start(bf16[64,512]{1,0:T(8,128)(2,1)S(1)} %shard_map.146), channel_id=1, source_target_pairs={{0,15},{1,2},{2,1},{3,4},{4,3},{5,6},{6,5},{7,8},{8,7},{9,10},{10,... | collective-permute-start | bytes 196616 | tf_op jit(solution)/shard_map/ppermute | solution.py:360
  26.3 2.7 %collective-permute-start.10 = (bf16[16,512]{1,0:T(8,128)(2,1)S(1)}, bf16[16,512]{1,0:T(8,128)(2,1)S(1)}, u32[]{:S(2)}, u32[]{:S(2)}) collective-permute-start(bf16[16,512]{1,0:T(8,128)(2,1)S(1)} %get-tuple-element.100), channel_id=1, source_target_pairs={{0,12},{1,13},{2,14},{3,15},{4,8},{5,9},{6,10},{7,11},{8,4},{9,5},... | collective-permute-start | bytes 49160 | tf_op jit(solution)/shard_map/ppermute | solution.py:354
  29.4 1.4 %collective-permute-start.12 = (bf16[16,512]{1,0:T(8,128)(2,1)S(1)}, bf16[16,512]{1,0:T(8,128)(2,1)S(1)}, u32[]{:S(2)}, u32[]{:S(2)}) collective-permute-start(bf16[16,512]{1,0:T(8,128)(2,1)S(1)} %get-tuple-element.102), channel_id=1, source_target_pairs={{0,4},{1,5},{2,6},{3,7},{4,0},{5,1},{6,2},{7,3},{8,12},{9,13},{10,... | collective-permute-start | bytes 49160 | tf_op jit(solution)/shard_map/ppermute | solution.py:354
  31.0 2.0 %collective-permute-start.9 = (bf16[128,512]{1,0:T(8,128)(2,1)S(1)}, bf16[128,512]{1,0:T(8,128)(2,1)S(1)}, u32[]{:S(2)}, u32[]{:S(2)}) collective-permute-start(bf16[128,512]{1,0:T(8,128)(2,1)S(1)} %shard_map.149), channel_id=1, source_target_pairs={{0,15},{1,2},{2,1},{3,4},{4,3},{5,6},{6,5},{7,8},{8,7},{9,10},{10,... | collective-permute-start | bytes 393224 | tf_op jit(solution)/shard_map/ppermute | solution.py:360
  36.3 2.2 %collective-permute-done.14.refs_2_ = bf16[16,512]{1,0:T(8,128)(2,1)S(1)} collective-permute-done((bf16[16,512]{1,0:T(8,128)(2,1)S(1)}, bf16[16,512]{1,0:T(8,128)(2,1)S(1)}, u32[]{:S(2)}, u32[]{:S(2)}) %collective-permute-start.14) | collective-permute-done | bytes 16416 | tf_op jit(solution)/shard_map/ppermute | solution.py:354
  38.6 1.4 %shard_map.151 = (bf16[512,512]{1,0:T(8,128)(2,1)S(1)}, bf16[512,512]{1,0:T(8,128)(2,1)S(1)}, bf16[128,512]{1,0:T(8,128)(2,1)S(1)}, bf16[16,512]{1,0:T(8,128)(2,...) custom-call(f32[512,512]{1,0:T(8,128)S(1)} %shard_map.148.near, ...), custom_call_target="tpu_custom_call" | custom-call | flops 1610612736 | bytes 4980736 | tf_op jit(solution)/shard_map/pallas_call | solution.py:76
  40.0 1.6 %collective-permute-start.17 = (bf16[16,512]{1,0:T(8,128)(2,1)S(1)}, bf16[16,512]{1,0:T(8,128)(2,1)S(1)}, u32[]{:S(2)}, u32[]{:S(2)}) collective-permute-start(bf16[16,512]{1,0:T(8,128)(2,1)S(1)} %get-tuple-element.111), channel_id=1, source_target_pairs={{0,12},{1,13},{2,14},{3,15},{4,8},{5,9},{6,10},{7,11},{8,4},{9,5},... | collective-permute-start | bytes 49160 | tf_op jit(solution)/shard_map/ppermute | solution.py:354
  41.6 2.9 %collective-permute-start.19 = (bf16[16,512]{1,0:T(8,128)(2,1)S(1)}, bf16[16,512]{1,0:T(8,128)(2,1)S(1)}, u32[]{:S(2)}, u32[]{:S(2)}) collective-permute-start(bf16[16,512]{1,0:T(8,128)(2,1)S(1)} %get-tuple-element.113), channel_id=1, source_target_pairs={{0,4},{1,5},{2,6},{3,7},{4,0},{5,1},{6,2},{7,3},{8,12},{9,13},{10,... | collective-permute-start | bytes 49160 | tf_op jit(solution)/shard_map/ppermute | solution.py:354
  44.8 1.4 %collective-permute-start.16 = (bf16[128,512]{1,0:T(8,128)(2,1)S(1)}, bf16[128,512]{1,0:T(8,128)(2,1)S(1)}, u32[]{:S(2)}, u32[]{:S(2)}) collective-permute-start(bf16[128,512]{1,0:T(8,128)(2,1)S(1)} %shard_map.152), channel_id=1, source_target_pairs={{0,15},{1,2},{2,1},{3,4},{4,3},{5,6},{6,5},{7,8},{8,7},{9,10},{10,... | collective-permute-start | bytes 393224 | tf_op jit(solution)/shard_map/ppermute | solution.py:360
  46.6 1.6 %collective-permute-start.22 = (bf16[16,512]{1,0:T(8,128)(2,1)S(1)}, bf16[16,512]{1,0:T(8,128)(2,1)S(1)}, u32[]{:S(2)}, u32[]{:S(2)}) collective-permute-start(bf16[16,512]{1,0:T(8,128)(2,1)S(1)} %get-tuple-element.117), channel_id=1, source_target_pairs={{0,2},{1,3},{2,0},{3,1},{4,6},{5,7},{6,4},{7,5},{8,10},{9,11},{10,... | collective-permute-start | bytes 49160 | tf_op jit(solution)/shard_map/ppermute | solution.py:354
  50.4 1.6 %collective-permute-done.16.refs_0_.refs_4_ = bf16[128,512]{1,0:T(8,128)(2,1)S(1)} collective-permute-done((bf16[128,512]{1,0:T(8,128)(2,1)S(1)}, bf16[128,512]{1,0:T(8,128)(2,1)S(1)}, u32[]{:S(2)}, u32[]{:S(2)}) %collective-permute-start.16) | collective-permute-done | bytes 131104 | tf_op jit(solution)/shard_map/ppermute | solution.py:360
  52.8 1.9 %collective-permute-start.24 = (bf16[16,512]{1,0:T(8,128)(2,1)S(1)}, bf16[16,512]{1,0:T(8,128)(2,1)S(1)}, u32[]{:S(2)}, u32[]{:S(2)}) collective-permute-start(bf16[16,512]{1,0:T(8,128)(2,1)S(1)} %get-tuple-element.123), channel_id=1, source_target_pairs={{0,12},{1,13},{2,14},{3,15},{4,8},{5,9},{6,10},{7,11},{8,4},{9,5},... | collective-permute-start | bytes 49160 | tf_op jit(solution)/shard_map/ppermute | solution.py:354
  54.7 2.6 %collective-permute-start.26 = (bf16[16,512]{1,0:T(8,128)(2,1)S(1)}, bf16[16,512]{1,0:T(8,128)(2,1)S(1)}, u32[]{:S(2)}, u32[]{:S(2)}) collective-permute-start(bf16[16,512]{1,0:T(8,128)(2,1)S(1)} %get-tuple-element.125), channel_id=1, source_target_pairs={{0,4},{1,5},{2,6},{3,7},{4,0},{5,1},{6,2},{7,3},{8,12},{9,13},{10,... | collective-permute-start | bytes 49160 | tf_op jit(solution)/shard_map/ppermute | solution.py:354
  63.0 1.3 %collective-permute-done.29.refs_3_ = bf16[16,512]{1,0:T(8,128)(2,1)S(1)} collective-permute-done((bf16[16,512]{1,0:T(8,128)(2,1)S(1)}, bf16[16,512]{1,0:T(8,128)(2,1)S(1)}, u32[]{:S(2)}, u32[]{:S(2)}) %collective-permute-start.29) | collective-permute-done | bytes 16416 | tf_op jit(solution)/shard_map/ppermute | solution.py:354
  65.1 1.5 %collective-permute-start.30 = (bf16[64,512]{1,0:T(8,128)(2,1)S(1)}, bf16[64,512]{1,0:T(8,128)(2,1)S(1)}, u32[]{:S(2)}, u32[]{:S(2)}) collective-permute-start(bf16[64,512]{1,0:T(8,128)(2,1)S(1)} %get-tuple-element.136), channel_id=1, source_target_pairs={{0,15},{1,2},{2,1},{3,4},{4,3},{5,6},{6,5},{7,8},{8,7},{9,10},{10,... | collective-permute-start | bytes 196616 | tf_op jit(solution)/shard_map/ppermute | solution.py:360
  66.5 2.5 %shard_map.161 = (f32[1024,512]{1,0:T(8,128)S(1)}, bf16[1024,128]{1,0:T(8,128)(2,1)S(1)}, f32[128,512]{1,0:T(8,128)S(1)}, bf16[512,512]{1,0:T(8,128)(2,1)}) custom-call(s32[1]{0:T(128)} %bitcast.me.refs_0_, bf16[1024,512]{1,0:T(8,128)(2,1)S(1)} %get-tuple-element.131.own_t, bf16[512,512]{1,0:T(8,128)(2,1)S(1)} %get-tuple-element.130.refs_6_.grad, ...), custom_call_target="tpu_custom_call" | custom-call | flops 1073741824 | bytes 7340548 | tf_op jit(solution)/shard_map/pallas_call | solution.py:76
  69.1 2.0 %shard_map.160 = bf16[1024,512]{1,0:T(8,128)(2,1)} custom-call(bf16[1024,512]{1,0:T(8,128)(2,1)S(1)} %copy-done.3, bf16[512,1024]{1,0:T(8,128)(2,1)S(1)} %get-tuple-element.83.refs_1_, bf16[128,1024]{1,0:T(8,128)(2,1)S(1)} %get-tuple-element.84.refs_2_, bf16[512,512]{1,0:T(8,128)(2,1)S(1)} %get-tuple-element.107.refs_1_.refs_3_, ...), custom_call_target="tpu_custom_call" | custom-call | flops 536870912 | bytes 4734976 | tf_op jit(solution)/shard_map/pallas_call | solution.py:76
  71.5 1.5 %shard_map.162 = bf16[1024,512]{1,0:T(8,128)(2,1)} custom-call(f32[1024,512]{1,0:T(8,128)S(1)} %get-tuple-element.133.base, bf16[1024,128]{1,0:T(8,128)(2,1)S(1)} %get-tuple-element.134.table, f32[128,512]{1,0:T(8,128)S(1)} %get-tuple-element.135.slope_rows, bf16[512,512]{1,0:T(8,128)(2,1)S(1)} %copy-done.1, ...), custom_call_target="tpu_custom_call" | custom-call | flops 268435456 | bytes 4325376 | tf_op jit(solution)/shard_map/pallas_call | solution.py:76
  (88 shorter events, 21.8 us)
Async XLA Ops:
  3.1 9.9 %collective-permute-start = (bf16[64,512]{1,0:T(8,128)(2,1)}, bf16[64,512]{1,0:T(8,128)(2,1)S(1)}, u32[]{:S(2)}, u32[]{:S(2)}) collective-permute-start(bf16[64,512]{1,0:T(8,128)(2,1)} %get-tuple-element.73), channel_id=1, source_target_pairs={{0,15},{1,2},{2,1},{3,4},{4,3},{5,6},{6,5},{7,8},{8,7},{9,10},{10,... | collective-permute-start | bytes 196616 | tf_op jit(solution)/shard_map/ppermute | solution.py:360
  8.6 4.4 %collective-permute-start.1 = (bf16[64,512]{1,0:T(8,128)(2,1)}, bf16[64,512]{1,0:T(8,128)(2,1)S(1)}, u32[]{:S(2)}, u32[]{:S(2)}) collective-permute-start(bf16[64,512]{1,0:T(8,128)(2,1)} %get-tuple-element.74), channel_id=1, source_target_pairs={{0,1},{1,0},{2,3},{3,2},{4,5},{5,4},{6,7},{7,6},{8,9},{9,8},{10,11... | collective-permute-start | bytes 196616 | tf_op jit(solution)/shard_map/ppermute | solution.py:354
  14.2 6.1 %collective-permute-start.2 = (bf16[16,512]{1,0:T(8,128)(2,1)S(1)}, bf16[16,512]{1,0:T(8,128)(2,1)S(1)}, u32[]{:S(2)}, u32[]{:S(2)}) collective-permute-start(bf16[16,512]{1,0:T(8,128)(2,1)S(1)} %get-tuple-element.79), channel_id=1, source_target_pairs={{0,12},{1,13},{2,14},{3,15},{4,8},{5,9},{6,10},{7,11},{8,4},{9,5},... | collective-permute-start | bytes 49160 | tf_op jit(solution)/shard_map/ppermute | solution.py:354
  15.5 4.8 %collective-permute-start.3 = (bf16[16,512]{1,0:T(8,128)(2,1)S(1)}, bf16[16,512]{1,0:T(8,128)(2,1)S(1)}, u32[]{:S(2)}, u32[]{:S(2)}) collective-permute-start(bf16[16,512]{1,0:T(8,128)(2,1)S(1)} %get-tuple-element.80), channel_id=1, source_target_pairs={{0,8},{1,9},{2,10},{3,11},{4,12},{5,13},{6,14},{7,15},{8,0},{9,1},... | collective-permute-start | bytes 49160 | tf_op jit(solution)/shard_map/ppermute | solution.py:354
  15.5 4.9 %collective-permute-start.4 = (bf16[16,512]{1,0:T(8,128)(2,1)S(1)}, bf16[16,512]{1,0:T(8,128)(2,1)S(1)}, u32[]{:S(2)}, u32[]{:S(2)}) collective-permute-start(bf16[16,512]{1,0:T(8,128)(2,1)S(1)} %get-tuple-element.81), channel_id=1, source_target_pairs={{0,4},{1,5},{2,6},{3,7},{4,0},{5,1},{6,2},{7,3},{8,12},{9,13},{10,... | collective-permute-start | bytes 49160 | tf_op jit(solution)/shard_map/ppermute | solution.py:354
  18.9 6.5 %collective-permute-start.5 = (bf16[64,512]{1,0:T(8,128)(2,1)S(1)}, bf16[64,512]{1,0:T(8,128)(2,1)S(1)}, u32[]{:S(2)}, u32[]{:S(2)}) collective-permute-start(bf16[64,512]{1,0:T(8,128)(2,1)S(1)} %shard_map.146), channel_id=1, source_target_pairs={{0,15},{1,2},{2,1},{3,4},{4,3},{5,6},{6,5},{7,8},{8,7},{9,10},{10,... | collective-permute-start | bytes 196616 | tf_op jit(solution)/shard_map/ppermute | solution.py:360
  20.5 4.3 %collective-permute-start.7 = (bf16[16,512]{1,0:T(8,128)(2,1)S(1)}, bf16[16,512]{1,0:T(8,128)(2,1)S(1)}, u32[]{:S(2)}, u32[]{:S(2)}) collective-permute-start(bf16[16,512]{1,0:T(8,128)(2,1)S(1)} %get-tuple-element.91), channel_id=1, source_target_pairs={{0,3},{1,2},{2,1},{3,0},{4,7},{5,6},{6,5},{7,4},{8,11},{9,10},{10,... | collective-permute-start | bytes 49160 | tf_op jit(solution)/shard_map/ppermute | solution.py:354
  26.3 6.7 %collective-permute-start.10 = (bf16[16,512]{1,0:T(8,128)(2,1)S(1)}, bf16[16,512]{1,0:T(8,128)(2,1)S(1)}, u32[]{:S(2)}, u32[]{:S(2)}) collective-permute-start(bf16[16,512]{1,0:T(8,128)(2,1)S(1)} %get-tuple-element.100), channel_id=1, source_target_pairs={{0,12},{1,13},{2,14},{3,15},{4,8},{5,9},{6,10},{7,11},{8,4},{9,5},... | collective-permute-start | bytes 49160 | tf_op jit(solution)/shard_map/ppermute | solution.py:354
  29.0 4.7 %collective-permute-start.11 = (bf16[16,512]{1,0:T(8,128)(2,1)S(1)}, bf16[16,512]{1,0:T(8,128)(2,1)S(1)}, u32[]{:S(2)}, u32[]{:S(2)}) collective-permute-start(bf16[16,512]{1,0:T(8,128)(2,1)S(1)} %get-tuple-element.101), channel_id=1, source_target_pairs={{0,8},{1,9},{2,10},{3,11},{4,12},{5,13},{6,14},{7,15},{8,0},{9,1},... | collective-permute-start | bytes 49160 | tf_op jit(solution)/shard_map/ppermute | solution.py:354
  29.4 4.4 %collective-permute-start.12 = (bf16[16,512]{1,0:T(8,128)(2,1)S(1)}, bf16[16,512]{1,0:T(8,128)(2,1)S(1)}, u32[]{:S(2)}, u32[]{:S(2)}) collective-permute-start(bf16[16,512]{1,0:T(8,128)(2,1)S(1)} %get-tuple-element.102), channel_id=1, source_target_pairs={{0,4},{1,5},{2,6},{3,7},{4,0},{5,1},{6,2},{7,3},{8,12},{9,13},{10,... | collective-permute-start | bytes 49160 | tf_op jit(solution)/shard_map/ppermute | solution.py:354
  31.0 7.6 %collective-permute-start.9 = (bf16[128,512]{1,0:T(8,128)(2,1)S(1)}, bf16[128,512]{1,0:T(8,128)(2,1)S(1)}, u32[]{:S(2)}, u32[]{:S(2)}) collective-permute-start(bf16[128,512]{1,0:T(8,128)(2,1)S(1)} %shard_map.149), channel_id=1, source_target_pairs={{0,15},{1,2},{2,1},{3,4},{4,3},{5,6},{6,5},{7,8},{8,7},{9,10},{10,... | collective-permute-start | bytes 393224 | tf_op jit(solution)/shard_map/ppermute | solution.py:360
  33.9 4.6 %collective-permute-start.14 = (bf16[16,512]{1,0:T(8,128)(2,1)S(1)}, bf16[16,512]{1,0:T(8,128)(2,1)S(1)}, u32[]{:S(2)}, u32[]{:S(2)}) collective-permute-start(bf16[16,512]{1,0:T(8,128)(2,1)S(1)} %get-tuple-element.104), channel_id=1, source_target_pairs={{0,3},{1,2},{2,1},{3,0},{4,7},{5,6},{6,5},{7,4},{8,11},{9,10},{10,... | collective-permute-start | bytes 49160 | tf_op jit(solution)/shard_map/ppermute | solution.py:354
  34.0 4.6 %collective-permute-start.15 = (bf16[16,512]{1,0:T(8,128)(2,1)S(1)}, bf16[16,512]{1,0:T(8,128)(2,1)S(1)}, u32[]{:S(2)}, u32[]{:S(2)}) collective-permute-start(bf16[16,512]{1,0:T(8,128)(2,1)S(1)} %get-tuple-element.105), channel_id=1, source_target_pairs={{0,2},{1,3},{2,0},{3,1},{4,6},{5,7},{6,4},{7,5},{8,10},{9,11},{10,... | collective-permute-start | bytes 49160 | tf_op jit(solution)/shard_map/ppermute | solution.py:354
  40.0 6.2 %collective-permute-start.17 = (bf16[16,512]{1,0:T(8,128)(2,1)S(1)}, bf16[16,512]{1,0:T(8,128)(2,1)S(1)}, u32[]{:S(2)}, u32[]{:S(2)}) collective-permute-start(bf16[16,512]{1,0:T(8,128)(2,1)S(1)} %get-tuple-element.111), channel_id=1, source_target_pairs={{0,12},{1,13},{2,14},{3,15},{4,8},{5,9},{6,10},{7,11},{8,4},{9,5},... | collective-permute-start | bytes 49160 | tf_op jit(solution)/shard_map/ppermute | solution.py:354
  41.6 4.7 %collective-permute-start.18 = (bf16[16,512]{1,0:T(8,128)(2,1)S(1)}, bf16[16,512]{1,0:T(8,128)(2,1)S(1)}, u32[]{:S(2)}, u32[]{:S(2)}) collective-permute-start(bf16[16,512]{1,0:T(8,128)(2,1)S(1)} %get-tuple-element.112), channel_id=1, source_target_pairs={{0,8},{1,9},{2,10},{3,11},{4,12},{5,13},{6,14},{7,15},{8,0},{9,1},... | collective-permute-start | bytes 49160 | tf_op jit(solution)/shard_map/ppermute | solution.py:354
  41.6 4.8 %collective-permute-start.19 = (bf16[16,512]{1,0:T(8,128)(2,1)S(1)}, bf16[16,512]{1,0:T(8,128)(2,1)S(1)}, u32[]{:S(2)}, u32[]{:S(2)}) collective-permute-start(bf16[16,512]{1,0:T(8,128)(2,1)S(1)} %get-tuple-element.113), channel_id=1, source_target_pairs={{0,4},{1,5},{2,6},{3,7},{4,0},{5,1},{6,2},{7,3},{8,12},{9,13},{10,... | collective-permute-start | bytes 49160 | tf_op jit(solution)/shard_map/ppermute | solution.py:354
  44.8 7.3 %collective-permute-start.16 = (bf16[128,512]{1,0:T(8,128)(2,1)S(1)}, bf16[128,512]{1,0:T(8,128)(2,1)S(1)}, u32[]{:S(2)}, u32[]{:S(2)}) collective-permute-start(bf16[128,512]{1,0:T(8,128)(2,1)S(1)} %shard_map.152), channel_id=1, source_target_pairs={{0,15},{1,2},{2,1},{3,4},{4,3},{5,6},{6,5},{7,8},{8,7},{9,10},{10,... | collective-permute-start | bytes 393224 | tf_op jit(solution)/shard_map/ppermute | solution.py:360
  52.8 5.6 %collective-permute-start.24 = (bf16[16,512]{1,0:T(8,128)(2,1)S(1)}, bf16[16,512]{1,0:T(8,128)(2,1)S(1)}, u32[]{:S(2)}, u32[]{:S(2)}) collective-permute-start(bf16[16,512]{1,0:T(8,128)(2,1)S(1)} %get-tuple-element.123), channel_id=1, source_target_pairs={{0,12},{1,13},{2,14},{3,15},{4,8},{5,9},{6,10},{7,11},{8,4},{9,5},... | collective-permute-start | bytes 49160 | tf_op jit(solution)/shard_map/ppermute | solution.py:354
  54.7 4.7 %collective-permute-start.25 = (bf16[16,512]{1,0:T(8,128)(2,1)S(1)}, bf16[16,512]{1,0:T(8,128)(2,1)S(1)}, u32[]{:S(2)}, u32[]{:S(2)}) collective-permute-start(bf16[16,512]{1,0:T(8,128)(2,1)S(1)} %get-tuple-element.124), channel_id=1, source_target_pairs={{0,8},{1,9},{2,10},{3,11},{4,12},{5,13},{6,14},{7,15},{8,0},{9,1},... | collective-permute-start | bytes 49160 | tf_op jit(solution)/shard_map/ppermute | solution.py:354
  54.7 4.7 %collective-permute-start.26 = (bf16[16,512]{1,0:T(8,128)(2,1)S(1)}, bf16[16,512]{1,0:T(8,128)(2,1)S(1)}, u32[]{:S(2)}, u32[]{:S(2)}) collective-permute-start(bf16[16,512]{1,0:T(8,128)(2,1)S(1)} %get-tuple-element.125), channel_id=1, source_target_pairs={{0,4},{1,5},{2,6},{3,7},{4,0},{5,1},{6,2},{7,3},{8,12},{9,13},{10,... | collective-permute-start | bytes 49160 | tf_op jit(solution)/shard_map/ppermute | solution.py:354
  57.5 6.8 %collective-permute-start.23 = (bf16[64,512]{1,0:T(8,128)(2,1)S(1)}, bf16[64,512]{1,0:T(8,128)(2,1)S(1)}, u32[]{:S(2)}, u32[]{:S(2)}) collective-permute-start(bf16[64,512]{1,0:T(8,128)(2,1)S(1)} %shard_map.157), channel_id=1, source_target_pairs={{0,15},{1,2},{2,1},{3,4},{4,3},{5,6},{6,5},{7,8},{8,7},{9,10},{10,... | collective-permute-start | bytes 196616 | tf_op jit(solution)/shard_map/ppermute | solution.py:360
  59.8 4.5 %collective-permute-start.29 = (bf16[16,512]{1,0:T(8,128)(2,1)S(1)}, bf16[16,512]{1,0:T(8,128)(2,1)S(1)}, u32[]{:S(2)}, u32[]{:S(2)}) collective-permute-start(bf16[16,512]{1,0:T(8,128)(2,1)S(1)} %get-tuple-element.128), channel_id=1, source_target_pairs={{0,2},{1,3},{2,0},{3,1},{4,6},{5,7},{6,4},{7,5},{8,10},{9,11},{10,... | collective-permute-start | bytes 49160 | tf_op jit(solution)/shard_map/ppermute | solution.py:354
  65.1 6.5 %collective-permute-start.30 = (bf16[64,512]{1,0:T(8,128)(2,1)S(1)}, bf16[64,512]{1,0:T(8,128)(2,1)S(1)}, u32[]{:S(2)}, u32[]{:S(2)}) collective-permute-start(bf16[64,512]{1,0:T(8,128)(2,1)S(1)} %get-tuple-element.136), channel_id=1, source_target_pairs={{0,15},{1,2},{2,1},{3,4},{4,3},{5,6},{6,5},{7,8},{8,7},{9,10},{10,... | collective-permute-start | bytes 196616 | tf_op jit(solution)/shard_map/ppermute | solution.py:360
  66.5 5.0 %collective-permute-start.31 = (bf16[64,512]{1,0:T(8,128)(2,1)S(1)}, bf16[64,512]{1,0:T(8,128)(2,1)S(1)}, u32[]{:S(2)}, u32[]{:S(2)}) collective-permute-start(bf16[64,512]{1,0:T(8,128)(2,1)S(1)} %get-tuple-element.137), channel_id=1, source_target_pairs={{0,1},{1,0},{2,3},{3,2},{4,5},{5,4},{6,7},{7,6},{8,9},{9,8},{10,11... | collective-permute-start | bytes 196616 | tf_op jit(solution)/shard_map/ppermute | solution.py:354
  (20 other events, 92.2 us)

commit v8 on v7

--- a/solution.py
+++ b/solution.py
@@ -193,30 +193,15 @@
 
 
 def emit(outs, rows, size, extra=None):
-    inner = outs[0]
     rows = rows.astype(BF)
-    inner[:size] = rows[:size]
-    if extra is not None:
-        inner[size:] = extra
-    far = rows[size:]
-    block = far.shape[0] // (len(outs) - 1)
-    for m, out in enumerate(outs[1:]):
+    for k in range(2):
+        outs[k][:size] = rows[k * size : (k + 1) * size]
+        if extra is not None:
+            outs[k][size:] = extra[k]
+    far = rows[2 * size :]
+    block = far.shape[0] // (len(outs) - 2)
+    for m, out in enumerate(outs[2:]):
         out[...] = far[m * block : (m + 1) * block]
-
-
-def outer_forth(send, message, *refs, size):
-    outer = refs[-1]
-    outer[:size] = t_mm(send[:, :size], message[...]).astype(BF)
-    if len(refs) == 2:
-        outer[size:] = refs[0][...]
-
-
-def outer_back(back_t, grad, *refs, size):
-    outer = refs[-1]
-    outer[:size] = mm(back_t[:size], grad[...]).astype(BF)
-    if len(refs) == 3:
-        send, message = refs[:2]
-        outer[size:] = t_mm(send[:, :size], message[...]).astype(BF)
 
 
 def arrived(ins, size):
@@ -266,10 +251,10 @@
     value = value.astype(BF)
     message[...] = value
     slope[...] = gradient
-    emit(outs, t_mm(send[:, size:], value), size)
-
-
-def next_hidden(near, forth_t, weight, send, inner_extra, *refs, ins, layer, scale, size):
+    emit(outs, t_mm(send[...], value), size)
+
+
+def next_hidden(near, forth_t, weight, send, outer_extra, inner_extra, *refs, ins, layer, scale, size):
     rows = arrived(refs[:ins], size)
     hidden, message, slope = refs[ins : ins + 3]
     state = (near[...] + scale * t_mm(forth_t[...], rows)).astype(BF)
@@ -278,7 +263,7 @@
     value = value.astype(BF)
     message[...] = value
     slope[...] = gradient
-    emit(refs[ins + 3 :], t_mm(send[:, size:], value), size, inner_extra[...])
+    emit(refs[ins + 3 :], t_mm(send[...], value), size, (outer_extra[...], inner_extra[...]))
 
 
 def turn(near, forth_t, weight, send, receive, back_t, back_near, *refs, ins, scale, size):
@@ -292,8 +277,8 @@
     back = back_near[...] + mm(receive[:, : 2 * size], returned)
     change = mm_t((back * gradient).astype(BF), weight[...]).astype(BF)
     grad[...] = change
-    rim = t_mm(send[:, size : 2 * size], value).astype(BF)
-    emit(refs[ins + 2 :], mm(back_t[size:], change), size, rim)
+    rim = t_mm(send[:, : 2 * size], value).astype(BF)
+    emit(refs[ins + 2 :], mm(back_t[...], change), size, (rim[:size], rim[size:]))
 
 
 def layer_back(near, receive, rows, slope, weight, grad, scale):
@@ -306,7 +291,7 @@
     rows = arrived(refs[:ins], size)
     change = layer_back(near, receive, rows, slope, weight[layer], grad, scale)
     refs[ins][...] = change
-    emit(refs[ins + 1 :], mm(back_t[size:], change), size)
+    emit(refs[ins + 1 :], mm(back_t[...], change), size)
 
 
 def last_back(near, receive, slope, weight, grad, grid_rim_t, *refs, ins, scale):
@@ -360,15 +345,15 @@
     return lax.ppermute(value, "dom", pairs)
 
 
-def exchange(outer, outs, cap):
-    width = outer.shape[1]
-    if len(outs) == 2:
-        inner, far = outs
+def exchange(outs, cap, after=()):
+    width = outs[0].shape[1]
+    if len(outs) == 3:
+        outer, inner, far = outs
         peers = lax.axis_size("dom")
         blocks = far.reshape(peers, cap, width)
         blocks = lax.all_to_all(blocks, "dom", split_axis=0, concat_axis=0, tiled=True)
         return [across(outer), toggle(inner, 1), blocks.reshape(-1, width)]
-    inner, own, *rest = outs
+    outer, inner, own, *rest = outs
     columns = STAGED // PLANE
     moved = [toggle(rest[m - 1], m * PLANE) for m in reversed(range(1, columns))]
     outer_in = across(outer)
@@ -377,7 +362,8 @@
         shuffle,
         [((block, width), BF), ((inner.shape[0] + block, width), BF), ((block, width), BF), ((block, width), BF)],
         2 * (STAGED * cap) ** 2 * width,
-        inner, own, *moved,
+        inner, own, *moved, outer_in, *after,
+        free=len(after) + 1,
     )
     return [outer_in, toggle(blocks[1], 1), toggle(blocks[3], 3), toggle(blocks[2], 2), blocks[0]]
 
@@ -412,17 +398,13 @@
 
     def sends(per_side):
         stages = STAGED // PLANE if devices == STAGED else 1
-        return [((per_side, width), BF)] + [((slots // stages, width), BF)] * stages
+        return [((per_side, width), BF)] * 2 + [((slots // stages, width), BF)] * stages
 
     state = ((mesh_rows, width), BF)
     total = ((mesh_rows, width), F32)
     rim = ((halo, width), BF)
-    wide = ((2 * halo, width), BF)
     grid_rim = ((ghalo, width), BF)
     step = 3 * square(mesh_rows, width)
-    rim_flops = square(halo, mesh_rows)
-    forth = functools.partial(outer_forth, size=halo)
-    back = functools.partial(outer_back, size=halo)
 
     outer, inner = call(
         grid_send,
@@ -464,10 +446,9 @@
         near, grid_rim_t, outer_in, inner_in, encoder_weight, processor_weights, send, back_t,
         free=1,
     )
-    (outer,) = call(forth, [rim], rim_flops, send, message)
     local = functools.partial(layer_local, scale=scale)
-    ins = exchange(outer, outs, cap)
-    (near,) = call(local, [total], 6 * square(mesh_rows, mesh_rows), hidden, own_t, message, ins[-1], free=1)
+    (near,) = call(local, [total], square(mesh_rows, mesh_rows), hidden, own_t, message)
+    ins = exchange(outs, cap, [near])
     decoder_own_t, decoder_rim_t, decoder_near, outer_extra, inner_extra = call(
         decoder_back,
         [((mesh_rows, grid_rows), BF), ((2 * halo, grid_rows), BF), total, rim, rim],
@@ -480,11 +461,10 @@
         functools.partial(next_hidden, ins=len(ins), layer=1, scale=scale, size=halo),
         [state, state, total] + sends(2 * halo),
         step,
-        near, forth_t, processor_weights, send, inner_extra, *ins,
-    )
-    (outer,) = call(forth, [wide], rim_flops, send, message, outer_extra)
-    (near,) = call(local, [total], 6 * square(mesh_rows, mesh_rows), hidden, own_t, message)
-    ins = exchange(outer, outs, cap)
+        near, forth_t, processor_weights, send, outer_extra, inner_extra, *ins,
+    )
+    (near,) = call(local, [total], square(mesh_rows, mesh_rows), hidden, own_t, message)
+    ins = exchange(outs, cap, [near])
 
     message, grad, *outs = call(
         functools.partial(turn, ins=len(ins), scale=scale, size=halo),
@@ -492,9 +472,8 @@
         2 * step,
         near, forth_t, decoder_weight, send, receive, back_t, decoder_near, *ins,
     )
-    (outer,) = call(back, [wide], rim_flops, back_t, grad, send, message)
-    (near,) = call(back_local, [total], 6 * square(mesh_rows, mesh_rows), own_t, grad)
-    ins = exchange(outer, outs, cap)
+    (near,) = call(back_local, [total], square(mesh_rows, mesh_rows), own_t, grad)
+    ins = exchange(outs, cap, [near])
     outer_decoder, inner_decoder = ins[:2]
 
     grad, *outs = call(
@@ -503,9 +482,8 @@
         step,
         near, receive, slope_1, processor_weights, grad, back_t, *ins,
     )
-    (outer,) = call(back, [rim], rim_flops, back_t, grad)
-    (near,) = call(back_local, [total], 6 * square(mesh_rows, mesh_rows), own_t, grad)
-    ins = exchange(outer, outs, cap)
+    (near,) = call(back_local, [total], square(mesh_rows, mesh_rows), own_t, grad)
+    ins = exchange(outs, cap, [near])
     grad, outer, inner = call(
         functools.partial(last_back, ins=len(ins), scale=scale),
         [state, grid_rim, grid_rim],

time: 73.4 us -> 78.1 us (1.064)
  waiting for transfers between devices: 10.6 us -> 15.2 us
  starting transfers between devices: 38.2 us -> 40.3 us
  Pallas kernels: 22.4 us -> 21.3 us
    ppermute x26, waiting for transfers between devices: 7.98 us -> 14.5 us  [toggle(): return lax.ppermute(value, 'dom', [(i, i ^ bits) for i in range(peers)])]
    ppermute x6, waiting for transfers between devices: 2.64 us -> 0.68 us  [across(): return lax.ppermute(value, 'dom', pairs)]
    ppermute x6, starting transfers between devices: 12.7 us -> 13.9 us  [across(): return lax.ppermute(value, 'dom', pairs)]
    pallas_call x24 -> x20, Pallas kernels: 22.4 us -> 21.3 us  [call(): pl.pallas_call(inner, out_shape=shapes, in_specs=[pl.BlockSpec(memory_spa...]
    ppermute x26, starting transfers between devices: 25.5 us -> 26.4 us  [toggle(): return lax.ppermute(value, 'dom', [(i, i ^ bits) for i in range(peers)])]
  transfers between devices with their start and end apart: 32 -> 32, of which waited for: 13 -> 16; matrix products, arithmetic and copies ran while one was open for 0% -> 0% of each run, Pallas kernels for 18% -> 15%
where the time goes in v8:
time: 78.1 us; the launch traced here: 78 us
  starting transfers between devices  40.3 us (52%)
  Pallas kernels  21.3 us (27%)
  waiting for transfers between devices  15.2 us (19%)
  between operations  1.15 us (1%)
    ppermute x26, starting transfers between devices, toggle(): return lax.ppermute(value, 'dom', [(i, i ^ bits) for i in range(peers)])  26.4 us
    pallas_call x20, Pallas kernels, call(): pl.pallas_call(inner, out_shape=shapes, in_specs=[pl.BlockSpec(memory_spa...  21.3 us
    ppermute x26, waiting for transfers between devices, toggle(): return lax.ppermute(value, 'dom', [(i, i ^ bits) for i in range(peers)])  14.5 us
    ppermute x6, starting transfers between devices, across(): return lax.ppermute(value, 'dom', pairs)  13.9 us
  transfers between devices with their start and end apart: 32, of which 16 were waited for; matrix products, arithmetic and copies ran while one was open for 0% of the time, Pallas kernels for 15%

profile of v8, /device:TPU:0, one launch (start us, length us, event | category | flops | bytes accessed | tf_op | source)
XLA Modules:
  0.0 78.0 jit_solution(12265900392525405321)
XLA Ops:
  0.7 2.4 %shard_map.140 = (bf16[64,512]{1,0:T(8,128)(2,1)}, bf16[64,512]{1,0:T(8,128)(2,1)}) custom-call(s32[1]{0:T(128)} %bitcast.me.refs_0_, bf16[1024,512]{1,0:T(8,128)(2,1)} %refs_0_.1, s32[1,2,64]{2,1,0:T(2,128)} %lists.5), custom_call_target="tpu_custom_call" | custom-call | flops 34359738368 | tf_op jit(solution)/shard_map/pallas_call | solution.py:76
  3.1 5.5 %collective-permute-start = (bf16[64,512]{1,0:T(8,128)(2,1)}, bf16[64,512]{1,0:T(8,128)(2,1)S(1)}, u32[]{:S(2)}, u32[]{:S(2)}) collective-permute-start(bf16[64,512]{1,0:T(8,128)(2,1)} %get-tuple-element.77), channel_id=1, source_target_pairs={{0,15},{1,2},{2,1},{3,4},{4,3},{5,6},{6,5},{7,8},{8,7},{9,10},{10,... | collective-permute-start | bytes 196616 | tf_op jit(solution)/shard_map/ppermute | solution.py:345
  8.7 2.9 %shard_map.139 = (f32[512,512]{1,0:T(8,128)S(1)}, bf16[1024,512]{1,0:T(8,128)(2,1)S(1)}, bf16[128,512]{1,0:T(8,128)(2,1)S(1)}, bf16[1024,512]{1,0:T(8,128)(2,1)S...) custom-call(s32[1]{0:T(128)} %bitcast.me.refs_0_, s32[4,512]{1,0:T(4,128)S(1)} %bitcast.9, ...), custom_call_target="tpu_custom_call" | custom-call | flops 2147483648 | bytes 5776132 | tf_op jit(solution)/shard_map/pallas_call | solution.py:76
  11.7 1.3 %shard_map.141 = (bf16[512,512]{1,0:T(8,128)(2,1)S(1)}, bf16[192,512]{1,0:T(8,128)(2,1)S(1)}, bf16[192,512]{1,0:T(8,128)(2,1)S(1)}) custom-call(s32[1]{0:T(128)} %bitcast.me.refs_0_, s32[8,512]{1,0:T(8,128)S(1)} %bitcast.7), custom_call_target="tpu_custom_call" | custom-call | flops 268435456 | bytes 933892 | tf_op jit(solution)/shard_map/pallas_call | solution.py:76
  13.0 1.2 %shard_map.142 = (bf16[512,512]{1,0:T(8,128)(2,1)S(1)}, bf16[512,512]{1,0:T(8,128)(2,1)S(1)}, f32[512,512]{1,0:T(8,128)S(1)}, bf16[64,512]{1,0:T(8,128)(2,1)S(1)...) custom-call(f32[512,512]{1,0:T(8,128)S(1)} %get-tuple-element.75.ref, ...), custom_call_target="tpu_custom_call" | custom-call | flops 805306368 | bytes 5570560 | tf_op jit(solution)/shard_map/pallas_call | solution.py:76
  14.3 2.3 %collective-permute-start.5 = (bf16[64,512]{1,0:T(8,128)(2,1)S(1)}, bf16[64,512]{1,0:T(8,128)(2,1)S(1)}, u32[]{:S(2)}, u32[]{:S(2)}) collective-permute-start(bf16[64,512]{1,0:T(8,128)(2,1)S(1)} %get-tuple-element.86), channel_id=1, source_target_pairs={{0,15},{1,2},{2,1},{3,4},{4,3},{5,6},{6,5},{7,8},{8,7},{9,10},{10,... | collective-permute-start | bytes 196616 | tf_op jit(solution)/shard_map/ppermute | solution.py:345
  16.6 4.4 %collective-permute-start.4 = (bf16[16,512]{1,0:T(8,128)(2,1)S(1)}, bf16[16,512]{1,0:T(8,128)(2,1)S(1)}, u32[]{:S(2)}, u32[]{:S(2)}) collective-permute-start(bf16[16,512]{1,0:T(8,128)(2,1)S(1)} %get-tuple-element.85), channel_id=1, source_target_pairs={{0,4},{1,5},{2,6},{3,7},{4,0},{5,1},{6,2},{7,3},{8,12},{9,13},{10,... | collective-permute-start | bytes 49160 | tf_op jit(solution)/shard_map/ppermute | solution.py:339
  23.0 2.1 %collective-permute-start.8 = (bf16[16,512]{1,0:T(8,128)(2,1)S(1)}, bf16[16,512]{1,0:T(8,128)(2,1)S(1)}, u32[]{:S(2)}, u32[]{:S(2)}) collective-permute-start(bf16[16,512]{1,0:T(8,128)(2,1)S(1)} %get-tuple-element.98), channel_id=1, source_target_pairs={{0,2},{1,3},{2,0},{3,1},{4,6},{5,7},{6,4},{7,5},{8,10},{9,11},{10,... | collective-permute-start | bytes 49160 | tf_op jit(solution)/shard_map/ppermute | solution.py:339
  28.0 2.2 %collective-permute-start.9 = (bf16[128,512]{1,0:T(8,128)(2,1)S(1)}, bf16[128,512]{1,0:T(8,128)(2,1)S(1)}, u32[]{:S(2)}, u32[]{:S(2)}) collective-permute-start(bf16[128,512]{1,0:T(8,128)(2,1)S(1)} %get-tuple-element.103), channel_id=1, source_target_pairs={{0,15},{1,2},{2,1},{3,4},{4,3},{5,6},{6,5},{7,8},{8,7},{9,10},{10,... | collective-permute-start | bytes 393224 | tf_op jit(solution)/shard_map/ppermute | solution.py:345
  31.6 3.0 %collective-permute-start.12 = (bf16[16,512]{1,0:T(8,128)(2,1)S(1)}, bf16[16,512]{1,0:T(8,128)(2,1)S(1)}, u32[]{:S(2)}, u32[]{:S(2)}) collective-permute-start(bf16[16,512]{1,0:T(8,128)(2,1)S(1)} %get-tuple-element.108), channel_id=1, source_target_pairs={{0,4},{1,5},{2,6},{3,7},{4,0},{5,1},{6,2},{7,3},{8,12},{9,13},{10,... | collective-permute-start | bytes 49160 | tf_op jit(solution)/shard_map/ppermute | solution.py:339
  39.8 1.5 %collective-permute-done.15.refs_3_ = bf16[16,512]{1,0:T(8,128)(2,1)S(1)} collective-permute-done((bf16[16,512]{1,0:T(8,128)(2,1)S(1)}, bf16[16,512]{1,0:T(8,128)(2,1)S(1)}, u32[]{:S(2)}, u32[]{:S(2)}) %collective-permute-start.15) | collective-permute-done | bytes 16416 | tf_op jit(solution)/shard_map/ppermute | solution.py:339
  41.3 1.4 %shard_map.149 = (bf16[512,512]{1,0:T(8,128)(2,1)S(1)}, bf16[512,512]{1,0:T(8,128)(2,1)S(1)}, bf16[128,512]{1,0:T(8,128)(2,1)S(1)}, bf16[128,512]{1,0:T(8,128)(2...) custom-call(f32[512,512]{1,0:T(8,128)S(1)} %shard_map.147.refs_6_.ne, ...), custom_call_target="tpu_custom_call" | custom-call | flops 1610612736 | bytes 5111808 | tf_op jit(solution)/shard_map/pallas_call | solution.py:76
  42.7 1.5 %collective-permute-start.16 = (bf16[128,512]{1,0:T(8,128)(2,1)S(1)}, bf16[128,512]{1,0:T(8,128)(2,1)S(1)}, u32[]{:S(2)}, u32[]{:S(2)}) collective-permute-start(bf16[128,512]{1,0:T(8,128)(2,1)S(1)} %get-tuple-element.114), channel_id=1, source_target_pairs={{0,15},{1,2},{2,1},{3,4},{4,3},{5,6},{6,5},{7,8},{8,7},{9,10},{10,... | collective-permute-start | bytes 393224 | tf_op jit(solution)/shard_map/ppermute | solution.py:345
  45.6 3.0 %collective-permute-start.19 = (bf16[16,512]{1,0:T(8,128)(2,1)S(1)}, bf16[16,512]{1,0:T(8,128)(2,1)S(1)}, u32[]{:S(2)}, u32[]{:S(2)}) collective-permute-start(bf16[16,512]{1,0:T(8,128)(2,1)S(1)} %get-tuple-element.119), channel_id=1, source_target_pairs={{0,4},{1,5},{2,6},{3,7},{4,0},{5,1},{6,2},{7,3},{8,12},{9,13},{10,... | collective-permute-start | bytes 49160 | tf_op jit(solution)/shard_map/ppermute | solution.py:339
  50.6 1.5 %collective-permute-start.21 = (bf16[16,512]{1,0:T(8,128)(2,1)S(1)}, bf16[16,512]{1,0:T(8,128)(2,1)S(1)}, u32[]{:S(2)}, u32[]{:S(2)}) collective-permute-start(bf16[16,512]{1,0:T(8,128)(2,1)S(1)} %get-tuple-element.123), channel_id=1, source_target_pairs={{0,3},{1,2},{2,1},{3,0},{4,7},{5,6},{6,5},{7,4},{8,11},{9,10},{10,... | collective-permute-start | bytes 49160 | tf_op jit(solution)/shard_map/ppermute | solution.py:339
  53.8 2.0 %collective-permute-done.22.refs_3_ = bf16[16,512]{1,0:T(8,128)(2,1)S(1)} collective-permute-done((bf16[16,512]{1,0:T(8,128)(2,1)S(1)}, bf16[16,512]{1,0:T(8,128)(2,1)S(1)}, u32[]{:S(2)}, u32[]{:S(2)}) %collective-permute-start.22) | collective-permute-done | bytes 16416 | tf_op jit(solution)/shard_map/ppermute | solution.py:339
  59.0 3.0 %collective-permute-start.26 = (bf16[16,512]{1,0:T(8,128)(2,1)S(1)}, bf16[16,512]{1,0:T(8,128)(2,1)S(1)}, u32[]{:S(2)}, u32[]{:S(2)}) collective-permute-start(bf16[16,512]{1,0:T(8,128)(2,1)S(1)} %get-tuple-element.133), channel_id=1, source_target_pairs={{0,4},{1,5},{2,6},{3,7},{4,0},{5,1},{6,2},{7,3},{8,12},{9,13},{10,... | collective-permute-start | bytes 49160 | tf_op jit(solution)/shard_map/ppermute | solution.py:339
  64.0 1.4 %collective-permute-start.28 = (bf16[16,512]{1,0:T(8,128)(2,1)S(1)}, bf16[16,512]{1,0:T(8,128)(2,1)S(1)}, u32[]{:S(2)}, u32[]{:S(2)}) collective-permute-start(bf16[16,512]{1,0:T(8,128)(2,1)S(1)} %get-tuple-element.135), channel_id=1, source_target_pairs={{0,3},{1,2},{2,1},{3,0},{4,7},{5,6},{6,5},{7,4},{8,11},{9,10},{10,... | collective-permute-start | bytes 49160 | tf_op jit(solution)/shard_map/ppermute | solution.py:339
  66.1 1.3 %collective-permute-done.28.refs_2_ = bf16[16,512]{1,0:T(8,128)(2,1)S(1)} collective-permute-done((bf16[16,512]{1,0:T(8,128)(2,1)S(1)}, bf16[16,512]{1,0:T(8,128)(2,1)S(1)}, u32[]{:S(2)}, u32[]{:S(2)}) %collective-permute-start.28) | collective-permute-done | bytes 16416 | tf_op jit(solution)/shard_map/ppermute | solution.py:339
  67.4 1.7 %collective-permute-done.29.refs_3_ = bf16[16,512]{1,0:T(8,128)(2,1)S(1)} collective-permute-done((bf16[16,512]{1,0:T(8,128)(2,1)S(1)}, bf16[16,512]{1,0:T(8,128)(2,1)S(1)}, u32[]{:S(2)}, u32[]{:S(2)}) %collective-permute-start.29) | collective-permute-done | bytes 16416 | tf_op jit(solution)/shard_map/ppermute | solution.py:339
  69.9 1.3 %collective-permute-start.30 = (bf16[64,512]{1,0:T(8,128)(2,1)S(1)}, bf16[64,512]{1,0:T(8,128)(2,1)S(1)}, u32[]{:S(2)}, u32[]{:S(2)}) collective-permute-start(bf16[64,512]{1,0:T(8,128)(2,1)S(1)} %get-tuple-element.144), channel_id=1, source_target_pairs={{0,15},{1,2},{2,1},{3,4},{4,3},{5,6},{6,5},{7,8},{8,7},{9,10},{10,... | collective-permute-start | bytes 196616 | tf_op jit(solution)/shard_map/ppermute | solution.py:345
  71.2 2.5 %shard_map.157 = (f32[1024,512]{1,0:T(8,128)S(1)}, bf16[1024,128]{1,0:T(8,128)(2,1)S(1)}, f32[128,512]{1,0:T(8,128)S(1)}, bf16[512,512]{1,0:T(8,128)(2,1)}) custom-call(s32[1]{0:T(128)} %bitcast.me.refs_0_, bf16[1024,512]{1,0:T(8,128)(2,1)S(1)} %get-tuple-element.139.own_t, bf16[512,512]{1,0:T(8,128)(2,1)S(1)} %get-tuple-element.138.refs_6_.grad, ...), custom_call_target="tpu_custom_call" | custom-call | flops 1073741824 | bytes 7340548 | tf_op jit(solution)/shard_map/pallas_call | solution.py:76
  73.7 2.0 %shard_map.156 = bf16[1024,512]{1,0:T(8,128)(2,1)} custom-call(bf16[1024,512]{1,0:T(8,128)(2,1)S(1)} %copy-done.3, bf16[512,1024]{1,0:T(8,128)(2,1)S(1)} %get-tuple-element.91.refs_1_, bf16[128,1024]{1,0:T(8,128)(2,1)S(1)} %get-tuple-element.92.refs_2_, bf16[512,512]{1,0:T(8,128)(2,1)S(1)} %get-tuple-element.113.refs_3_, ...), custom_call_target="tpu_custom_call" | custom-call | flops 536870912 | bytes 4734976 | tf_op jit(solution)/shard_map/pallas_call | solution.py:76
  76.3 1.5 %shard_map.158 = bf16[1024,512]{1,0:T(8,128)(2,1)} custom-call(f32[1024,512]{1,0:T(8,128)S(1)} %get-tuple-element.141.base, bf16[1024,128]{1,0:T(8,128)(2,1)S(1)} %get-tuple-element.142.table, f32[128,512]{1,0:T(8,128)S(1)} %get-tuple-element.143.slope_rows, bf16[512,512]{1,0:T(8,128)(2,1)S(1)} %copy-done.1, ...), custom_call_target="tpu_custom_call" | custom-call | flops 268435456 | bytes 4325376 | tf_op jit(solution)/shard_map/pallas_call | solution.py:76
  (84 shorter events, 23.8 us)
Async XLA Ops:
  3.1 9.9 %collective-permute-start = (bf16[64,512]{1,0:T(8,128)(2,1)}, bf16[64,512]{1,0:T(8,128)(2,1)S(1)}, u32[]{:S(2)}, u32[]{:S(2)}) collective-permute-start(bf16[64,512]{1,0:T(8,128)(2,1)} %get-tuple-element.77), channel_id=1, source_target_pairs={{0,15},{1,2},{2,1},{3,4},{4,3},{5,6},{6,5},{7,8},{8,7},{9,10},{10,... | collective-permute-start | bytes 196616 | tf_op jit(solution)/shard_map/ppermute | solution.py:345
  8.6 4.4 %collective-permute-start.1 = (bf16[64,512]{1,0:T(8,128)(2,1)}, bf16[64,512]{1,0:T(8,128)(2,1)S(1)}, u32[]{:S(2)}, u32[]{:S(2)}) collective-permute-start(bf16[64,512]{1,0:T(8,128)(2,1)} %get-tuple-element.78), channel_id=1, source_target_pairs={{0,1},{1,0},{2,3},{3,2},{4,5},{5,4},{6,7},{7,6},{8,9},{9,8},{10,11... | collective-permute-start | bytes 196616 | tf_op jit(solution)/shard_map/ppermute | solution.py:339
  14.3 8.4 %collective-permute-start.5 = (bf16[64,512]{1,0:T(8,128)(2,1)S(1)}, bf16[64,512]{1,0:T(8,128)(2,1)S(1)}, u32[]{:S(2)}, u32[]{:S(2)}) collective-permute-start(bf16[64,512]{1,0:T(8,128)(2,1)S(1)} %get-tuple-element.86), channel_id=1, source_target_pairs={{0,15},{1,2},{2,1},{3,4},{4,3},{5,6},{6,5},{7,8},{8,7},{9,10},{10,... | collective-permute-start | bytes 196616 | tf_op jit(solution)/shard_map/ppermute | solution.py:345
  16.6 5.5 %collective-permute-start.2 = (bf16[16,512]{1,0:T(8,128)(2,1)S(1)}, bf16[16,512]{1,0:T(8,128)(2,1)S(1)}, u32[]{:S(2)}, u32[]{:S(2)}) collective-permute-start(bf16[16,512]{1,0:T(8,128)(2,1)S(1)} %get-tuple-element.83), channel_id=1, source_target_pairs={{0,12},{1,13},{2,14},{3,15},{4,8},{5,9},{6,10},{7,11},{8,4},{9,5},... | collective-permute-start | bytes 49160 | tf_op jit(solution)/shard_map/ppermute | solution.py:339
  16.6 5.5 %collective-permute-start.3 = (bf16[16,512]{1,0:T(8,128)(2,1)S(1)}, bf16[16,512]{1,0:T(8,128)(2,1)S(1)}, u32[]{:S(2)}, u32[]{:S(2)}) collective-permute-start(bf16[16,512]{1,0:T(8,128)(2,1)S(1)} %get-tuple-element.84), channel_id=1, source_target_pairs={{0,8},{1,9},{2,10},{3,11},{4,12},{5,13},{6,14},{7,15},{8,0},{9,1},... | collective-permute-start | bytes 49160 | tf_op jit(solution)/shard_map/ppermute | solution.py:339
  16.6 6.1 %collective-permute-start.4 = (bf16[16,512]{1,0:T(8,128)(2,1)S(1)}, bf16[16,512]{1,0:T(8,128)(2,1)S(1)}, u32[]{:S(2)}, u32[]{:S(2)}) collective-permute-start(bf16[16,512]{1,0:T(8,128)(2,1)S(1)} %get-tuple-element.85), channel_id=1, source_target_pairs={{0,4},{1,5},{2,6},{3,7},{4,0},{5,1},{6,2},{7,3},{8,12},{9,13},{10,... | collective-permute-start | bytes 49160 | tf_op jit(solution)/shard_map/ppermute | solution.py:339
  22.8 4.1 %collective-permute-start.6 = (bf16[80,512]{1,0:T(8,128)(2,1)S(1)}, bf16[80,512]{1,0:T(8,128)(2,1)S(1)}, u32[]{:S(2)}, u32[]{:S(2)}) collective-permute-start(bf16[80,512]{1,0:T(8,128)(2,1)S(1)} %get-tuple-element.96), channel_id=1, source_target_pairs={{0,1},{1,0},{2,3},{3,2},{4,5},{5,4},{6,7},{7,6},{8,9},{9,8},{10,11... | collective-permute-start | bytes 245768 | tf_op jit(solution)/shard_map/ppermute | solution.py:339
  28.0 8.3 %collective-permute-start.9 = (bf16[128,512]{1,0:T(8,128)(2,1)S(1)}, bf16[128,512]{1,0:T(8,128)(2,1)S(1)}, u32[]{:S(2)}, u32[]{:S(2)}) collective-permute-start(bf16[128,512]{1,0:T(8,128)(2,1)S(1)} %get-tuple-element.103), channel_id=1, source_target_pairs={{0,15},{1,2},{2,1},{3,4},{4,3},{5,6},{6,5},{7,8},{8,7},{9,10},{10,... | collective-permute-start | bytes 393224 | tf_op jit(solution)/shard_map/ppermute | solution.py:345
  30.2 5.6 %collective-permute-start.10 = (bf16[16,512]{1,0:T(8,128)(2,1)S(1)}, bf16[16,512]{1,0:T(8,128)(2,1)S(1)}, u32[]{:S(2)}, u32[]{:S(2)}) collective-permute-start(bf16[16,512]{1,0:T(8,128)(2,1)S(1)} %get-tuple-element.106), channel_id=1, source_target_pairs={{0,12},{1,13},{2,14},{3,15},{4,8},{5,9},{6,10},{7,11},{8,4},{9,5},... | collective-permute-start | bytes 49160 | tf_op jit(solution)/shard_map/ppermute | solution.py:339
  30.5 5.4 %collective-permute-start.11 = (bf16[16,512]{1,0:T(8,128)(2,1)S(1)}, bf16[16,512]{1,0:T(8,128)(2,1)S(1)}, u32[]{:S(2)}, u32[]{:S(2)}) collective-permute-start(bf16[16,512]{1,0:T(8,128)(2,1)S(1)} %get-tuple-element.107), channel_id=1, source_target_pairs={{0,8},{1,9},{2,10},{3,11},{4,12},{5,13},{6,14},{7,15},{8,0},{9,1},... | collective-permute-start | bytes 49160 | tf_op jit(solution)/shard_map/ppermute | solution.py:339
  31.6 4.7 %collective-permute-start.12 = (bf16[16,512]{1,0:T(8,128)(2,1)S(1)}, bf16[16,512]{1,0:T(8,128)(2,1)S(1)}, u32[]{:S(2)}, u32[]{:S(2)}) collective-permute-start(bf16[16,512]{1,0:T(8,128)(2,1)S(1)} %get-tuple-element.108), channel_id=1, source_target_pairs={{0,4},{1,5},{2,6},{3,7},{4,0},{5,1},{6,2},{7,3},{8,12},{9,13},{10,... | collective-permute-start | bytes 49160 | tf_op jit(solution)/shard_map/ppermute | solution.py:339
  36.5 4.8 %collective-permute-start.13 = (bf16[144,512]{1,0:T(8,128)(2,1)S(1)}, bf16[144,512]{1,0:T(8,128)(2,1)S(1)}, u32[]{:S(2)}, u32[]{:S(2)}) collective-permute-start(bf16[144,512]{1,0:T(8,128)(2,1)S(1)} %get-tuple-element.109), channel_id=1, source_target_pairs={{0,1},{1,0},{2,3},{3,2},{4,5},{5,4},{6,7},{7,6},{8,9},{9,8},{10,11... | collective-permute-start | bytes 442376 | tf_op jit(solution)/shard_map/ppermute | solution.py:339
  42.7 7.6 %collective-permute-start.16 = (bf16[128,512]{1,0:T(8,128)(2,1)S(1)}, bf16[128,512]{1,0:T(8,128)(2,1)S(1)}, u32[]{:S(2)}, u32[]{:S(2)}) collective-permute-start(bf16[128,512]{1,0:T(8,128)(2,1)S(1)} %get-tuple-element.114), channel_id=1, source_target_pairs={{0,15},{1,2},{2,1},{3,4},{4,3},{5,6},{6,5},{7,8},{8,7},{9,10},{10,... | collective-permute-start | bytes 393224 | tf_op jit(solution)/shard_map/ppermute | solution.py:345
  44.2 5.6 %collective-permute-start.17 = (bf16[16,512]{1,0:T(8,128)(2,1)S(1)}, bf16[16,512]{1,0:T(8,128)(2,1)S(1)}, u32[]{:S(2)}, u32[]{:S(2)}) collective-permute-start(bf16[16,512]{1,0:T(8,128)(2,1)S(1)} %get-tuple-element.117), channel_id=1, source_target_pairs={{0,12},{1,13},{2,14},{3,15},{4,8},{5,9},{6,10},{7,11},{8,4},{9,5},... | collective-permute-start | bytes 49160 | tf_op jit(solution)/shard_map/ppermute | solution.py:339
  44.9 5.0 %collective-permute-start.18 = (bf16[16,512]{1,0:T(8,128)(2,1)S(1)}, bf16[16,512]{1,0:T(8,128)(2,1)S(1)}, u32[]{:S(2)}, u32[]{:S(2)}) collective-permute-start(bf16[16,512]{1,0:T(8,128)(2,1)S(1)} %get-tuple-element.118), channel_id=1, source_target_pairs={{0,8},{1,9},{2,10},{3,11},{4,12},{5,13},{6,14},{7,15},{8,0},{9,1},... | collective-permute-start | bytes 49160 | tf_op jit(solution)/shard_map/ppermute | solution.py:339
  45.6 4.7 %collective-permute-start.19 = (bf16[16,512]{1,0:T(8,128)(2,1)S(1)}, bf16[16,512]{1,0:T(8,128)(2,1)S(1)}, u32[]{:S(2)}, u32[]{:S(2)}) collective-permute-start(bf16[16,512]{1,0:T(8,128)(2,1)S(1)} %get-tuple-element.119), channel_id=1, source_target_pairs={{0,4},{1,5},{2,6},{3,7},{4,0},{5,1},{6,2},{7,3},{8,12},{9,13},{10,... | collective-permute-start | bytes 49160 | tf_op jit(solution)/shard_map/ppermute | solution.py:339
  50.5 5.3 %collective-permute-start.20 = (bf16[144,512]{1,0:T(8,128)(2,1)S(1)}, bf16[144,512]{1,0:T(8,128)(2,1)S(1)}, u32[]{:S(2)}, u32[]{:S(2)}) collective-permute-start(bf16[144,512]{1,0:T(8,128)(2,1)S(1)} %get-tuple-element.121), channel_id=1, source_target_pairs={{0,1},{1,0},{2,3},{3,2},{4,5},{5,4},{6,7},{7,6},{8,9},{9,8},{10,11... | collective-permute-start | bytes 442376 | tf_op jit(solution)/shard_map/ppermute | solution.py:339
  56.6 7.1 %collective-permute-start.23 = (bf16[64,512]{1,0:T(8,128)(2,1)S(1)}, bf16[64,512]{1,0:T(8,128)(2,1)S(1)}, u32[]{:S(2)}, u32[]{:S(2)}) collective-permute-start(bf16[64,512]{1,0:T(8,128)(2,1)S(1)} %get-tuple-element.128), channel_id=1, source_target_pairs={{0,15},{1,2},{2,1},{3,4},{4,3},{5,6},{6,5},{7,8},{8,7},{9,10},{10,... | collective-permute-start | bytes 196616 | tf_op jit(solution)/shard_map/ppermute | solution.py:345
  57.6 5.7 %collective-permute-start.24 = (bf16[16,512]{1,0:T(8,128)(2,1)S(1)}, bf16[16,512]{1,0:T(8,128)(2,1)S(1)}, u32[]{:S(2)}, u32[]{:S(2)}) collective-permute-start(bf16[16,512]{1,0:T(8,128)(2,1)S(1)} %get-tuple-element.131), channel_id=1, source_target_pairs={{0,12},{1,13},{2,14},{3,15},{4,8},{5,9},{6,10},{7,11},{8,4},{9,5},... | collective-permute-start | bytes 49160 | tf_op jit(solution)/shard_map/ppermute | solution.py:339
  58.3 5.0 %collective-permute-start.25 = (bf16[16,512]{1,0:T(8,128)(2,1)S(1)}, bf16[16,512]{1,0:T(8,128)(2,1)S(1)}, u32[]{:S(2)}, u32[]{:S(2)}) collective-permute-start(bf16[16,512]{1,0:T(8,128)(2,1)S(1)} %get-tuple-element.132), channel_id=1, source_target_pairs={{0,8},{1,9},{2,10},{3,11},{4,12},{5,13},{6,14},{7,15},{8,0},{9,1},... | collective-permute-start | bytes 49160 | tf_op jit(solution)/shard_map/ppermute | solution.py:339
  59.0 4.7 %collective-permute-start.26 = (bf16[16,512]{1,0:T(8,128)(2,1)S(1)}, bf16[16,512]{1,0:T(8,128)(2,1)S(1)}, u32[]{:S(2)}, u32[]{:S(2)}) collective-permute-start(bf16[16,512]{1,0:T(8,128)(2,1)S(1)} %get-tuple-element.133), channel_id=1, source_target_pairs={{0,4},{1,5},{2,6},{3,7},{4,0},{5,1},{6,2},{7,3},{8,12},{9,13},{10,... | collective-permute-start | bytes 49160 | tf_op jit(solution)/shard_map/ppermute | solution.py:339
  63.9 5.2 %collective-permute-start.27 = (bf16[80,512]{1,0:T(8,128)(2,1)S(1)}, bf16[80,512]{1,0:T(8,128)(2,1)S(1)}, u32[]{:S(2)}, u32[]{:S(2)}) collective-permute-start(bf16[80,512]{1,0:T(8,128)(2,1)S(1)} %get-tuple-element.134), channel_id=1, source_target_pairs={{0,1},{1,0},{2,3},{3,2},{4,5},{5,4},{6,7},{7,6},{8,9},{9,8},{10,11... | collective-permute-start | bytes 245768 | tf_op jit(solution)/shard_map/ppermute | solution.py:339
  69.9 6.5 %collective-permute-start.30 = (bf16[64,512]{1,0:T(8,128)(2,1)S(1)}, bf16[64,512]{1,0:T(8,128)(2,1)S(1)}, u32[]{:S(2)}, u32[]{:S(2)}) collective-permute-start(bf16[64,512]{1,0:T(8,128)(2,1)S(1)} %get-tuple-element.144), channel_id=1, source_target_pairs={{0,15},{1,2},{2,1},{3,4},{4,3},{5,6},{6,5},{7,8},{8,7},{9,10},{10,... | collective-permute-start | bytes 196616 | tf_op jit(solution)/shard_map/ppermute | solution.py:345
  71.1 5.2 %collective-permute-start.31 = (bf16[64,512]{1,0:T(8,128)(2,1)S(1)}, bf16[64,512]{1,0:T(8,128)(2,1)S(1)}, u32[]{:S(2)}, u32[]{:S(2)}) collective-permute-start(bf16[64,512]{1,0:T(8,128)(2,1)S(1)} %get-tuple-element.145), channel_id=1, source_target_pairs={{0,1},{1,0},{2,3},{3,2},{4,5},{5,4},{6,7},{7,6},{8,9},{9,8},{10,11... | collective-permute-start | bytes 196616 | tf_op jit(solution)/shard_map/ppermute | solution.py:339
  (20 other events, 120.6 us)

commit v9 on v8

--- a/solution.py
+++ b/solution.py
@@ -117,14 +117,12 @@
     inner[...] = inner_rows.astype(BF)
 
 
-def encoder_local(me, entries, lists, far_lists, weight, latent, mesh,
-                  near, grid_own_t, grid_rim_t, slope, send, receive, *, size):
+def encoder_local(me, entries, weight, latent, mesh, near, grid_own_t, grid_rim_t, slope, *, size):
     rows = latent.shape[0]
     columns = side_swap(entries[...], rows, size, me[0])
     own = counts_t(rows, 0, columns)
     grid_own_t[...] = own
     grid_rim_t[...] = counts_t(2 * size, rows, columns)
-    list_tables(me, lists, far_lists, send, receive)
     message, gradient = silu_pair(mm(latent[...], weight[...]))
     slope[...] = gradient.astype(BF)
     near[...] = mesh[...].astype(F32) + t_mm(own, message.astype(BF))
@@ -156,7 +154,7 @@
     receive[:, 2 * size :] = receive_far.astype(BF)
 
 
-def mesh_tables(me, entries, own_t, forth_t, back_t, *, size, devices):
+def mesh_tables(me, entries, own_t, forth_t, back_t, size, devices):
     rows = own_t.shape[0]
     slots = forth_t.shape[0] - 2 * size
     cap = slots // devices
@@ -235,6 +233,11 @@
         outs[k][...] = moved[k * block : (k + 1) * block]
 
 
+def tables(me, entries, lists, far_lists, own_t, forth_t, back_t, send, receive, *, size, devices):
+    mesh_tables(me, entries, own_t, forth_t, back_t, size, devices)
+    list_tables(me, lists, far_lists, send, receive)
+
+
 def layer_local(hidden, own_t, message, near, *, scale):
     near[...] = hidden[...].astype(F32) + scale * t_mm(own_t[...], message[...])
 
@@ -345,7 +348,7 @@
     return lax.ppermute(value, "dom", pairs)
 
 
-def exchange(outs, cap, after=()):
+def exchange(outs, cap):
     width = outs[0].shape[1]
     if len(outs) == 3:
         outer, inner, far = outs
@@ -362,8 +365,7 @@
         shuffle,
         [((block, width), BF), ((inner.shape[0] + block, width), BF), ((block, width), BF), ((block, width), BF)],
         2 * (STAGED * cap) ** 2 * width,
-        inner, own, *moved, outer_in, *after,
-        free=len(after) + 1,
+        inner, own, *moved,
     )
     return [outer_in, toggle(blocks[1], 1), toggle(blocks[3], 3), toggle(blocks[2], 2), blocks[0]]
 
@@ -416,26 +418,19 @@
     )
     outer_in, inner_in = across(outer), toggle(inner, 1)
 
-    near, grid_own_t, grid_rim_t, grid_slope, send, receive = call(
+    own_t, forth_t, back_t, send, receive = call(
+        functools.partial(tables, size=halo, devices=devices),
+        [((mesh_rows, mesh_rows), BF)] + [((listed, mesh_rows), BF)] * 2 + [((mesh_rows, listed), BF)] * 2,
+        64 * square(mesh_rows, mesh_rows),
+        me, mesh_neighbours.T, halo_rows, far_sources[0].T,
+        scalars=1,
+    )
+    _, latent, weight, mesh = lax.optimization_barrier((inner, grid_latent, encoder_weight, mesh_latent))
+    near, grid_own_t, grid_rim_t, grid_slope = call(
         functools.partial(encoder_local, size=ghalo),
-        [
-            total,
-            ((grid_rows, mesh_rows), BF),
-            ((2 * ghalo, mesh_rows), BF),
-            ((grid_rows, width), BF),
-            ((mesh_rows, listed), BF),
-            ((mesh_rows, listed), BF),
-        ],
+        [total, ((grid_rows, mesh_rows), BF), ((2 * ghalo, mesh_rows), BF), ((grid_rows, width), BF)],
         4 * square(grid_rows, width),
-        me, encoder_neighbours.T, halo_rows, far_sources[0].T, encoder_weight, grid_latent, mesh_latent,
-        scalars=1,
-    )
-
-    own_t, forth_t, back_t = call(
-        functools.partial(mesh_tables, size=halo, devices=devices),
-        [((mesh_rows, mesh_rows), BF)] + [((listed, mesh_rows), BF)] * 2,
-        square(mesh_rows, mesh_rows),
-        me, mesh_neighbours.T,
+        me, encoder_neighbours.T, weight, latent, mesh,
         scalars=1,
     )
 
@@ -443,12 +438,12 @@
         functools.partial(first_hidden, size=halo),
         [state, state, total] + sends(halo),
         step,
-        near, grid_rim_t, outer_in, inner_in, encoder_weight, processor_weights, send, back_t,
-        free=1,
+        near, grid_rim_t, outer_in, inner_in, encoder_weight, processor_weights, send,
     )
     local = functools.partial(layer_local, scale=scale)
-    (near,) = call(local, [total], square(mesh_rows, mesh_rows), hidden, own_t, message)
-    ins = exchange(outs, cap, [near])
+    ins = exchange(outs, cap)
+    (near,) = call(local, [total], 6 * square(mesh_rows, mesh_rows), hidden, own_t, message, ins[-1], free=1)
+
     decoder_own_t, decoder_rim_t, decoder_near, outer_extra, inner_extra = call(
         decoder_back,
         [((mesh_rows, grid_rows), BF), ((2 * halo, grid_rows), BF), total, rim, rim],
@@ -463,8 +458,9 @@
         step,
         near, forth_t, processor_weights, send, outer_extra, inner_extra, *ins,
     )
-    (near,) = call(local, [total], square(mesh_rows, mesh_rows), hidden, own_t, message)
-    ins = exchange(outs, cap, [near])
+    ins = exchange(outs, cap)
+    (near,) = call(local, [total], 6 * square(mesh_rows, mesh_rows), hidden, own_t, message)
+
 
     message, grad, *outs = call(
         functools.partial(turn, ins=len(ins), scale=scale, size=halo),
@@ -472,8 +468,9 @@
         2 * step,
         near, forth_t, decoder_weight, send, receive, back_t, decoder_near, *ins,
     )
-    (near,) = call(back_local, [total], square(mesh_rows, mesh_rows), own_t, grad)
-    ins = exchange(outs, cap, [near])
+    ins = exchange(outs, cap)
+    (near,) = call(back_local, [total], 6 * square(mesh_rows, mesh_rows), own_t, grad)
+
     outer_decoder, inner_decoder = ins[:2]
 
     grad, *outs = call(
@@ -482,8 +479,9 @@
         step,
         near, receive, slope_1, processor_weights, grad, back_t, *ins,
     )
-    (near,) = call(back_local, [total], square(mesh_rows, mesh_rows), own_t, grad)
-    ins = exchange(outs, cap, [near])
+    ins = exchange(outs, cap)
+    (near,) = call(back_local, [total], 6 * square(mesh_rows, mesh_rows), own_t, grad)
+
     grad, outer, inner = call(
         functools.partial(last_back, ins=len(ins), scale=scale),
         [state, grid_rim, grid_rim],

time: 78.1 us -> 72.7 us (0.931)
  waiting for transfers between devices: 15.2 us -> 11.1 us
  starting transfers between devices: 40.3 us -> 37.9 us
    ppermute x26, waiting for transfers between devices: 14.5 us -> 10.8 us  [toggle(): return lax.ppermute(value, 'dom', [(i, i ^ bits) for i in range(peers)])]
    ppermute x6, starting transfers between devices: 13.9 us -> 12.2 us  [across(): return lax.ppermute(value, 'dom', pairs)]
  transfers between devices with their start and end apart: 32 -> 32, of which waited for: 16 -> 14; matrix products, arithmetic and copies ran while one was open for 0% -> 0% of each run, Pallas kernels for 15% -> 17%
where the time goes in v9:
time: 72.7 us; the launch traced here: 72.5 us
  starting transfers between devices  37.9 us (52%)
  Pallas kernels  21.5 us (30%)
  waiting for transfers between devices  11.1 us (15%)
  between operations  1.13 us (2%)
  local copies, waits for them, and re-layouts  0.81 us (1%)
    ppermute x26, starting transfers between devices, toggle(): return lax.ppermute(value, 'dom', [(i, i ^ bits) for i in range(peers)])  25.7 us
    pallas_call x20, Pallas kernels, call(): pl.pallas_call(inner, out_shape=shapes, in_specs=[pl.BlockSpec(memory_spa...  21.5 us
    ppermute x6, starting transfers between devices, across(): return lax.ppermute(value, 'dom', pairs)  12.2 us
    ppermute x26, waiting for transfers between devices, toggle(): return lax.ppermute(value, 'dom', [(i, i ^ bits) for i in range(peers)])  10.8 us
  transfers between devices with their start and end apart: 32, of which 14 were waited for; matrix products, arithmetic and copies ran while one was open for 0% of the time, Pallas kernels for 17%

profile of v9, /device:TPU:0, one launch (start us, length us, event | category | flops | bytes accessed | tf_op | source)
XLA Modules:
  0.0 72.5 jit_solution(14717161614885116564)
XLA Ops:
  0.7 2.3 %shard_map.139 = (bf16[64,512]{1,0:T(8,128)(2,1)}, bf16[64,512]{1,0:T(8,128)(2,1)}) custom-call(s32[1]{0:T(128)} %bitcast.me.refs_0_, bf16[1024,512]{1,0:T(8,128)(2,1)} %refs_0_.1, s32[1,2,64]{2,1,0:T(2,128)} %lists.5), custom_call_target="tpu_custom_call" | custom-call | flops 34359738368 | tf_op jit(solution)/shard_map/pallas_call | solution.py:76
  3.0 5.5 %collective-permute-start = (bf16[64,512]{1,0:T(8,128)(2,1)}, bf16[64,512]{1,0:T(8,128)(2,1)S(1)}, u32[]{:S(2)}, u32[]{:S(2)}) collective-permute-start(bf16[64,512]{1,0:T(8,128)(2,1)} %get-tuple-element.84), channel_id=1, source_target_pairs={{0,15},{1,2},{2,1},{3,4},{4,3},{5,6},{6,5},{7,8},{8,7},{9,10},{10,... | collective-permute-start | bytes 196616 | tf_op jit(solution)/shard_map/ppermute | solution.py:348
  8.6 2.0 %shard_map.141 = (bf16[512,512]{1,0:T(8,128)(2,1)S(1)}, bf16[192,512]{1,0:T(8,128)(2,1)S(1)}, bf16[192,512]{1,0:T(8,128)(2,1)S(1)}, bf16[512,192]{1,0:T(8,128)(2,1)S(1)}, bf16[512,192]{1,0:T(8,128)(2,1)S(1)}) custom-call(s32[1]{0:T(128)} %bitcast.me.refs_0_, s32[8,512]{1,0:T(8,128)S(1)} %bitcast.7, s32[1,2,64]{2,1,0:T(2,128)S(1)} %copy-done.11, ...), custom_call_target="tpu_custom_call" | custom-call | flops 17179869184 | bytes 1327876 | tf_op jit(solution)/shard_map/pallas_call | solution.py:76
  10.6 2.6 %shard_map.140 = (f32[512,512]{1,0:T(8,128)S(1)}, bf16[1024,512]{1,0:T(8,128)(2,1)S(1)}, bf16[128,512]{1,0:T(8,128)(2,1)S(1)}, bf16[1024,512]{1,0:T(8,128)(2,1)S(1)}) custom-call(s32[1]{0:T(128)} %bitcast.me.refs_0_, s32[4,512]{1,0:T(4,128)S(1)} %bitcast.9, bf16[512,512]{1,0:T(8,128)(2,1)S(1)} %copy-done.1, bf16[1024,512]{1,0:T(8,128)(2,1)S(1)} %copy-done.3, ...), custom_call_target="tpu_custom_call" | custom-call | flops 2147483648 | bytes 5382148 | tf_op jit(solution)/shard_map/pallas_call | solution.py:76
  13.3 1.2 %shard_map.142 = (bf16[512,512]{1,0:T(8,128)(2,1)S(1)}, bf16[512,512]{1,0:T(8,128)(2,1)S(1)}, f32[512,512]{1,0:T(8,128)S(1)}, bf16[64,512]{1,0:T(8,128)(2,1)S(1)...) custom-call(f32[512,512]{1,0:T(8,128)S(1)} %get-tuple-element.82.nea, ...), custom_call_target="tpu_custom_call" | custom-call | flops 805306368 | bytes 5373952 | tf_op jit(solution)/shard_map/pallas_call | solution.py:76
  14.5 1.3 %collective-permute-start.2 = (bf16[16,512]{1,0:T(8,128)(2,1)S(1)}, bf16[16,512]{1,0:T(8,128)(2,1)S(1)}, u32[]{:S(2)}, u32[]{:S(2)}) collective-permute-start(bf16[16,512]{1,0:T(8,128)(2,1)S(1)} %get-tuple-element.88), channel_id=1, source_target_pairs={{0,12},{1,13},{2,14},{3,15},{4,8},{5,9},{6,10},{7,11},{8,4},{9,5},... | collective-permute-start | bytes 49160 | tf_op jit(solution)/shard_map/ppermute | solution.py:342
  15.8 3.2 %collective-permute-start.4 = (bf16[16,512]{1,0:T(8,128)(2,1)S(1)}, bf16[16,512]{1,0:T(8,128)(2,1)S(1)}, u32[]{:S(2)}, u32[]{:S(2)}) collective-permute-start(bf16[16,512]{1,0:T(8,128)(2,1)S(1)} %get-tuple-element.90), channel_id=1, source_target_pairs={{0,4},{1,5},{2,6},{3,7},{4,0},{5,1},{6,2},{7,3},{8,12},{9,13},{10,... | collective-permute-start | bytes 49160 | tf_op jit(solution)/shard_map/ppermute | solution.py:342
  26.4 2.6 %collective-permute-start.10 = (bf16[16,512]{1,0:T(8,128)(2,1)S(1)}, bf16[16,512]{1,0:T(8,128)(2,1)S(1)}, u32[]{:S(2)}, u32[]{:S(2)}) collective-permute-start(bf16[16,512]{1,0:T(8,128)(2,1)S(1)} %get-tuple-element.112), channel_id=1, source_target_pairs={{0,12},{1,13},{2,14},{3,15},{4,8},{5,9},{6,10},{7,11},{8,4},{9,5},... | collective-permute-start | bytes 49160 | tf_op jit(solution)/shard_map/ppermute | solution.py:342
  30.9 1.9 %collective-permute-start.9 = (bf16[128,512]{1,0:T(8,128)(2,1)S(1)}, bf16[128,512]{1,0:T(8,128)(2,1)S(1)}, u32[]{:S(2)}, u32[]{:S(2)}) collective-permute-start(bf16[128,512]{1,0:T(8,128)(2,1)S(1)} %get-tuple-element.109), channel_id=1, source_target_pairs={{0,15},{1,2},{2,1},{3,4},{4,3},{5,6},{6,5},{7,8},{8,7},{9,10},{10,... | collective-permute-start | bytes 393224 | tf_op jit(solution)/shard_map/ppermute | solution.py:348
  34.6 1.2 %collective-permute-start.13 = (bf16[144,512]{1,0:T(8,128)(2,1)S(1)}, bf16[144,512]{1,0:T(8,128)(2,1)S(1)}, u32[]{:S(2)}, u32[]{:S(2)}) collective-permute-start(bf16[144,512]{1,0:T(8,128)(2,1)S(1)} %get-tuple-element.115), channel_id=1, source_target_pairs={{0,1},{1,0},{2,3},{3,2},{4,5},{5,4},{6,7},{7,6},{8,9},{9,8},{10,11... | collective-permute-start | bytes 442376 | tf_op jit(solution)/shard_map/ppermute | solution.py:342
  36.3 1.9 %collective-permute-done.14.refs_2_ = bf16[16,512]{1,0:T(8,128)(2,1)S(1)} collective-permute-done((bf16[16,512]{1,0:T(8,128)(2,1)S(1)}, bf16[16,512]{1,0:T(8,128)(2,1)S(1)}, u32[]{:S(2)}, u32[]{:S(2)}) %collective-permute-start.14) | collective-permute-done | bytes 16416 | tf_op jit(solution)/shard_map/ppermute | solution.py:342
  38.4 1.4 %shard_map.149 = (bf16[512,512]{1,0:T(8,128)(2,1)S(1)}, bf16[512,512]{1,0:T(8,128)(2,1)S(1)}, bf16[128,512]{1,0:T(8,128)(2,1)S(1)}, bf16[128,512]{1,0:T(8,128)(2...) custom-call(f32[512,512]{1,0:T(8,128)S(1)} %shard_map.147.near, ...), custom_call_target="tpu_custom_call" | custom-call | flops 1610612736 | bytes 5111808 | tf_op jit(solution)/shard_map/pallas_call | solution.py:76
  39.8 1.6 %collective-permute-start.17 = (bf16[16,512]{1,0:T(8,128)(2,1)S(1)}, bf16[16,512]{1,0:T(8,128)(2,1)S(1)}, u32[]{:S(2)}, u32[]{:S(2)}) collective-permute-start(bf16[16,512]{1,0:T(8,128)(2,1)S(1)} %get-tuple-element.123), channel_id=1, source_target_pairs={{0,12},{1,13},{2,14},{3,15},{4,8},{5,9},{6,10},{7,11},{8,4},{9,5},... | collective-permute-start | bytes 49160 | tf_op jit(solution)/shard_map/ppermute | solution.py:342
  41.6 2.7 %collective-permute-start.19 = (bf16[16,512]{1,0:T(8,128)(2,1)S(1)}, bf16[16,512]{1,0:T(8,128)(2,1)S(1)}, u32[]{:S(2)}, u32[]{:S(2)}) collective-permute-start(bf16[16,512]{1,0:T(8,128)(2,1)S(1)} %get-tuple-element.125), channel_id=1, source_target_pairs={{0,4},{1,5},{2,6},{3,7},{4,0},{5,1},{6,2},{7,3},{8,12},{9,13},{10,... | collective-permute-start | bytes 49160 | tf_op jit(solution)/shard_map/ppermute | solution.py:342
  44.3 1.3 %collective-permute-start.16 = (bf16[128,512]{1,0:T(8,128)(2,1)S(1)}, bf16[128,512]{1,0:T(8,128)(2,1)S(1)}, u32[]{:S(2)}, u32[]{:S(2)}) collective-permute-start(bf16[128,512]{1,0:T(8,128)(2,1)S(1)} %get-tuple-element.120), channel_id=1, source_target_pairs={{0,15},{1,2},{2,1},{3,4},{4,3},{5,6},{6,5},{7,8},{8,7},{9,10},{10,... | collective-permute-start | bytes 393224 | tf_op jit(solution)/shard_map/ppermute | solution.py:348
  46.4 1.6 %collective-permute-start.22 = (bf16[16,512]{1,0:T(8,128)(2,1)S(1)}, bf16[16,512]{1,0:T(8,128)(2,1)S(1)}, u32[]{:S(2)}, u32[]{:S(2)}) collective-permute-start(bf16[16,512]{1,0:T(8,128)(2,1)S(1)} %get-tuple-element.130), channel_id=1, source_target_pairs={{0,2},{1,3},{2,0},{3,1},{4,6},{5,7},{6,4},{7,5},{8,10},{9,11},{10,... | collective-permute-start | bytes 49160 | tf_op jit(solution)/shard_map/ppermute | solution.py:342
  49.6 2.0 %collective-permute-done.22.refs_3_ = bf16[16,512]{1,0:T(8,128)(2,1)S(1)} collective-permute-done((bf16[16,512]{1,0:T(8,128)(2,1)S(1)}, bf16[16,512]{1,0:T(8,128)(2,1)S(1)}, u32[]{:S(2)}, u32[]{:S(2)}) %collective-permute-start.22) | collective-permute-done | bytes 16416 | tf_op jit(solution)/shard_map/ppermute | solution.py:342
  52.4 1.7 %collective-permute-start.24 = (bf16[16,512]{1,0:T(8,128)(2,1)S(1)}, bf16[16,512]{1,0:T(8,128)(2,1)S(1)}, u32[]{:S(2)}, u32[]{:S(2)}) collective-permute-start(bf16[16,512]{1,0:T(8,128)(2,1)S(1)} %get-tuple-element.137), channel_id=1, source_target_pairs={{0,12},{1,13},{2,14},{3,15},{4,8},{5,9},{6,10},{7,11},{8,4},{9,5},... | collective-permute-start | bytes 49160 | tf_op jit(solution)/shard_map/ppermute | solution.py:342
  54.3 2.5 %collective-permute-start.26 = (bf16[16,512]{1,0:T(8,128)(2,1)S(1)}, bf16[16,512]{1,0:T(8,128)(2,1)S(1)}, u32[]{:S(2)}, u32[]{:S(2)}) collective-permute-start(bf16[16,512]{1,0:T(8,128)(2,1)S(1)} %get-tuple-element.139), channel_id=1, source_target_pairs={{0,4},{1,5},{2,6},{3,7},{4,0},{5,1},{6,2},{7,3},{8,12},{9,13},{10,... | collective-permute-start | bytes 49160 | tf_op jit(solution)/shard_map/ppermute | solution.py:342
  62.4 1.2 %collective-permute-done.29.refs_3_ = bf16[16,512]{1,0:T(8,128)(2,1)S(1)} collective-permute-done((bf16[16,512]{1,0:T(8,128)(2,1)S(1)}, bf16[16,512]{1,0:T(8,128)(2,1)S(1)}, u32[]{:S(2)}, u32[]{:S(2)}) %collective-permute-start.29) | collective-permute-done | bytes 16416 | tf_op jit(solution)/shard_map/ppermute | solution.py:342
  64.4 1.9 %collective-permute-start.30 = (bf16[64,512]{1,0:T(8,128)(2,1)S(1)}, bf16[64,512]{1,0:T(8,128)(2,1)S(1)}, u32[]{:S(2)}, u32[]{:S(2)}) collective-permute-start(bf16[64,512]{1,0:T(8,128)(2,1)S(1)} %get-tuple-element.150), channel_id=1, source_target_pairs={{0,15},{1,2},{2,1},{3,4},{4,3},{5,6},{6,5},{7,8},{8,7},{9,10},{10,... | collective-permute-start | bytes 196616 | tf_op jit(solution)/shard_map/ppermute | solution.py:348
  66.3 2.5 %shard_map.157 = (f32[1024,512]{1,0:T(8,128)S(1)}, bf16[1024,128]{1,0:T(8,128)(2,1)S(1)}, f32[128,512]{1,0:T(8,128)S(1)}, bf16[512,512]{1,0:T(8,128)(2,1)}) custom-call(s32[1]{0:T(128)} %bitcast.me.refs_0_, bf16[1024,512]{1,0:T(8,128)(2,1)S(1)} %get-tuple-element.145.own_t, bf16[512,512]{1,0:T(8,128)(2,1)S(1)} %get-tuple-element.144.refs_6_.grad, ...), custom_call_target="tpu_custom_call" | custom-call | flops 1073741824 | bytes 7340548 | tf_op jit(solution)/shard_map/pallas_call | solution.py:76
  68.8 2.0 %shard_map.156 = bf16[1024,512]{1,0:T(8,128)(2,1)} custom-call(bf16[1024,512]{1,0:T(8,128)(2,1)S(1)} %copy-done.3, bf16[512,1024]{1,0:T(8,128)(2,1)S(1)} %get-tuple-element.92.refs_1_, bf16[128,1024]{1,0:T(8,128)(2,1)S(1)} %get-tuple-element.93.refs_2_, bf16[512,512]{1,0:T(8,128)(2,1)S(1)} %get-tuple-element.119.refs_3_, ...), custom_call_target="tpu_custom_call" | custom-call | flops 536870912 | bytes 4734976 | tf_op jit(solution)/shard_map/pallas_call | solution.py:76
  70.8 1.5 %shard_map.158 = bf16[1024,512]{1,0:T(8,128)(2,1)} custom-call(f32[1024,512]{1,0:T(8,128)S(1)} %get-tuple-element.147.base, bf16[1024,128]{1,0:T(8,128)(2,1)S(1)} %get-tuple-element.148.table, f32[128,512]{1,0:T(8,128)S(1)} %get-tuple-element.149.slope_rows, bf16[512,512]{1,0:T(8,128)(2,1)S(1)} %copy-done.1, ...), custom_call_target="tpu_custom_call" | custom-call | flops 268435456 | bytes 4325376 | tf_op jit(solution)/shard_map/pallas_call | solution.py:76
  (84 shorter events, 21.7 us)
Async XLA Ops:
  3.0 10.3 %collective-permute-start = (bf16[64,512]{1,0:T(8,128)(2,1)}, bf16[64,512]{1,0:T(8,128)(2,1)S(1)}, u32[]{:S(2)}, u32[]{:S(2)}) collective-permute-start(bf16[64,512]{1,0:T(8,128)(2,1)} %get-tuple-element.84), channel_id=1, source_target_pairs={{0,15},{1,2},{2,1},{3,4},{4,3},{5,6},{6,5},{7,8},{8,7},{9,10},{10,... | collective-permute-start | bytes 196616 | tf_op jit(solution)/shard_map/ppermute | solution.py:348
  8.5 4.8 %collective-permute-start.1 = (bf16[64,512]{1,0:T(8,128)(2,1)}, bf16[64,512]{1,0:T(8,128)(2,1)S(1)}, u32[]{:S(2)}, u32[]{:S(2)}) collective-permute-start(bf16[64,512]{1,0:T(8,128)(2,1)} %get-tuple-element.78), channel_id=1, source_target_pairs={{0,1},{1,0},{2,3},{3,2},{4,5},{5,4},{6,7},{7,6},{8,9},{9,8},{10,11... | collective-permute-start | bytes 196616 | tf_op jit(solution)/shard_map/ppermute | solution.py:342
  14.5 5.6 %collective-permute-start.2 = (bf16[16,512]{1,0:T(8,128)(2,1)S(1)}, bf16[16,512]{1,0:T(8,128)(2,1)S(1)}, u32[]{:S(2)}, u32[]{:S(2)}) collective-permute-start(bf16[16,512]{1,0:T(8,128)(2,1)S(1)} %get-tuple-element.88), channel_id=1, source_target_pairs={{0,12},{1,13},{2,14},{3,15},{4,8},{5,9},{6,10},{7,11},{8,4},{9,5},... | collective-permute-start | bytes 49160 | tf_op jit(solution)/shard_map/ppermute | solution.py:342
  15.8 4.7 %collective-permute-start.3 = (bf16[16,512]{1,0:T(8,128)(2,1)S(1)}, bf16[16,512]{1,0:T(8,128)(2,1)S(1)}, u32[]{:S(2)}, u32[]{:S(2)}) collective-permute-start(bf16[16,512]{1,0:T(8,128)(2,1)S(1)} %get-tuple-element.89), channel_id=1, source_target_pairs={{0,8},{1,9},{2,10},{3,11},{4,12},{5,13},{6,14},{7,15},{8,0},{9,1},... | collective-permute-start | bytes 49160 | tf_op jit(solution)/shard_map/ppermute | solution.py:342
  15.8 4.9 %collective-permute-start.4 = (bf16[16,512]{1,0:T(8,128)(2,1)S(1)}, bf16[16,512]{1,0:T(8,128)(2,1)S(1)}, u32[]{:S(2)}, u32[]{:S(2)}) collective-permute-start(bf16[16,512]{1,0:T(8,128)(2,1)S(1)} %get-tuple-element.90), channel_id=1, source_target_pairs={{0,4},{1,5},{2,6},{3,7},{4,0},{5,1},{6,2},{7,3},{8,12},{9,13},{10,... | collective-permute-start | bytes 49160 | tf_op jit(solution)/shard_map/ppermute | solution.py:342
  19.0 6.4 %collective-permute-start.5 = (bf16[64,512]{1,0:T(8,128)(2,1)S(1)}, bf16[64,512]{1,0:T(8,128)(2,1)S(1)}, u32[]{:S(2)}, u32[]{:S(2)}) collective-permute-start(bf16[64,512]{1,0:T(8,128)(2,1)S(1)} %get-tuple-element.100), channel_id=1, source_target_pairs={{0,15},{1,2},{2,1},{3,4},{4,3},{5,6},{6,5},{7,8},{8,7},{9,10},{10,... | collective-permute-start | bytes 196616 | tf_op jit(solution)/shard_map/ppermute | solution.py:348
  20.8 4.3 %collective-permute-start.7 = (bf16[16,512]{1,0:T(8,128)(2,1)S(1)}, bf16[16,512]{1,0:T(8,128)(2,1)S(1)}, u32[]{:S(2)}, u32[]{:S(2)}) collective-permute-start(bf16[16,512]{1,0:T(8,128)(2,1)S(1)} %get-tuple-element.102), channel_id=1, source_target_pairs={{0,3},{1,2},{2,1},{3,0},{4,7},{5,6},{6,5},{7,4},{8,11},{9,10},{10,... | collective-permute-start | bytes 49160 | tf_op jit(solution)/shard_map/ppermute | solution.py:342
  26.4 6.4 %collective-permute-start.10 = (bf16[16,512]{1,0:T(8,128)(2,1)S(1)}, bf16[16,512]{1,0:T(8,128)(2,1)S(1)}, u32[]{:S(2)}, u32[]{:S(2)}) collective-permute-start(bf16[16,512]{1,0:T(8,128)(2,1)S(1)} %get-tuple-element.112), channel_id=1, source_target_pairs={{0,12},{1,13},{2,14},{3,15},{4,8},{5,9},{6,10},{7,11},{8,4},{9,5},... | collective-permute-start | bytes 49160 | tf_op jit(solution)/shard_map/ppermute | solution.py:342
  29.0 4.7 %collective-permute-start.11 = (bf16[16,512]{1,0:T(8,128)(2,1)S(1)}, bf16[16,512]{1,0:T(8,128)(2,1)S(1)}, u32[]{:S(2)}, u32[]{:S(2)}) collective-permute-start(bf16[16,512]{1,0:T(8,128)(2,1)S(1)} %get-tuple-element.113), channel_id=1, source_target_pairs={{0,8},{1,9},{2,10},{3,11},{4,12},{5,13},{6,14},{7,15},{8,0},{9,1},... | collective-permute-start | bytes 49160 | tf_op jit(solution)/shard_map/ppermute | solution.py:342
  30.9 7.5 %collective-permute-start.9 = (bf16[128,512]{1,0:T(8,128)(2,1)S(1)}, bf16[128,512]{1,0:T(8,128)(2,1)S(1)}, u32[]{:S(2)}, u32[]{:S(2)}) collective-permute-start(bf16[128,512]{1,0:T(8,128)(2,1)S(1)} %get-tuple-element.109), channel_id=1, source_target_pairs={{0,15},{1,2},{2,1},{3,4},{4,3},{5,6},{6,5},{7,8},{8,7},{9,10},{10,... | collective-permute-start | bytes 393224 | tf_op jit(solution)/shard_map/ppermute | solution.py:348
  33.9 4.3 %collective-permute-start.14 = (bf16[16,512]{1,0:T(8,128)(2,1)S(1)}, bf16[16,512]{1,0:T(8,128)(2,1)S(1)}, u32[]{:S(2)}, u32[]{:S(2)}) collective-permute-start(bf16[16,512]{1,0:T(8,128)(2,1)S(1)} %get-tuple-element.116), channel_id=1, source_target_pairs={{0,3},{1,2},{2,1},{3,0},{4,7},{5,6},{6,5},{7,4},{8,11},{9,10},{10,... | collective-permute-start | bytes 49160 | tf_op jit(solution)/shard_map/ppermute | solution.py:342
  34.0 4.4 %collective-permute-start.15 = (bf16[16,512]{1,0:T(8,128)(2,1)S(1)}, bf16[16,512]{1,0:T(8,128)(2,1)S(1)}, u32[]{:S(2)}, u32[]{:S(2)}) collective-permute-start(bf16[16,512]{1,0:T(8,128)(2,1)S(1)} %get-tuple-element.117), channel_id=1, source_target_pairs={{0,2},{1,3},{2,0},{3,1},{4,6},{5,7},{6,4},{7,5},{8,10},{9,11},{10,... | collective-permute-start | bytes 49160 | tf_op jit(solution)/shard_map/ppermute | solution.py:342
  39.8 5.8 %collective-permute-start.17 = (bf16[16,512]{1,0:T(8,128)(2,1)S(1)}, bf16[16,512]{1,0:T(8,128)(2,1)S(1)}, u32[]{:S(2)}, u32[]{:S(2)}) collective-permute-start(bf16[16,512]{1,0:T(8,128)(2,1)S(1)} %get-tuple-element.123), channel_id=1, source_target_pairs={{0,12},{1,13},{2,14},{3,15},{4,8},{5,9},{6,10},{7,11},{8,4},{9,5},... | collective-permute-start | bytes 49160 | tf_op jit(solution)/shard_map/ppermute | solution.py:342
  41.4 4.8 %collective-permute-start.18 = (bf16[16,512]{1,0:T(8,128)(2,1)S(1)}, bf16[16,512]{1,0:T(8,128)(2,1)S(1)}, u32[]{:S(2)}, u32[]{:S(2)}) collective-permute-start(bf16[16,512]{1,0:T(8,128)(2,1)S(1)} %get-tuple-element.124), channel_id=1, source_target_pairs={{0,8},{1,9},{2,10},{3,11},{4,12},{5,13},{6,14},{7,15},{8,0},{9,1},... | collective-permute-start | bytes 49160 | tf_op jit(solution)/shard_map/ppermute | solution.py:342
  41.6 4.5 %collective-permute-start.19 = (bf16[16,512]{1,0:T(8,128)(2,1)S(1)}, bf16[16,512]{1,0:T(8,128)(2,1)S(1)}, u32[]{:S(2)}, u32[]{:S(2)}) collective-permute-start(bf16[16,512]{1,0:T(8,128)(2,1)S(1)} %get-tuple-element.125), channel_id=1, source_target_pairs={{0,4},{1,5},{2,6},{3,7},{4,0},{5,1},{6,2},{7,3},{8,12},{9,13},{10,... | collective-permute-start | bytes 49160 | tf_op jit(solution)/shard_map/ppermute | solution.py:342
  44.3 7.4 %collective-permute-start.16 = (bf16[128,512]{1,0:T(8,128)(2,1)S(1)}, bf16[128,512]{1,0:T(8,128)(2,1)S(1)}, u32[]{:S(2)}, u32[]{:S(2)}) collective-permute-start(bf16[128,512]{1,0:T(8,128)(2,1)S(1)} %get-tuple-element.120), channel_id=1, source_target_pairs={{0,15},{1,2},{2,1},{3,4},{4,3},{5,6},{6,5},{7,8},{8,7},{9,10},{10,... | collective-permute-start | bytes 393224 | tf_op jit(solution)/shard_map/ppermute | solution.py:348
  46.4 5.3 %collective-permute-start.22 = (bf16[16,512]{1,0:T(8,128)(2,1)S(1)}, bf16[16,512]{1,0:T(8,128)(2,1)S(1)}, u32[]{:S(2)}, u32[]{:S(2)}) collective-permute-start(bf16[16,512]{1,0:T(8,128)(2,1)S(1)} %get-tuple-element.130), channel_id=1, source_target_pairs={{0,2},{1,3},{2,0},{3,1},{4,6},{5,7},{6,4},{7,5},{8,10},{9,11},{10,... | collective-permute-start | bytes 49160 | tf_op jit(solution)/shard_map/ppermute | solution.py:342
  52.4 5.6 %collective-permute-start.24 = (bf16[16,512]{1,0:T(8,128)(2,1)S(1)}, bf16[16,512]{1,0:T(8,128)(2,1)S(1)}, u32[]{:S(2)}, u32[]{:S(2)}) collective-permute-start(bf16[16,512]{1,0:T(8,128)(2,1)S(1)} %get-tuple-element.137), channel_id=1, source_target_pairs={{0,12},{1,13},{2,14},{3,15},{4,8},{5,9},{6,10},{7,11},{8,4},{9,5},... | collective-permute-start | bytes 49160 | tf_op jit(solution)/shard_map/ppermute | solution.py:342
  54.1 4.7 %collective-permute-start.25 = (bf16[16,512]{1,0:T(8,128)(2,1)S(1)}, bf16[16,512]{1,0:T(8,128)(2,1)S(1)}, u32[]{:S(2)}, u32[]{:S(2)}) collective-permute-start(bf16[16,512]{1,0:T(8,128)(2,1)S(1)} %get-tuple-element.138), channel_id=1, source_target_pairs={{0,8},{1,9},{2,10},{3,11},{4,12},{5,13},{6,14},{7,15},{8,0},{9,1},... | collective-permute-start | bytes 49160 | tf_op jit(solution)/shard_map/ppermute | solution.py:342
  54.3 4.5 %collective-permute-start.26 = (bf16[16,512]{1,0:T(8,128)(2,1)S(1)}, bf16[16,512]{1,0:T(8,128)(2,1)S(1)}, u32[]{:S(2)}, u32[]{:S(2)}) collective-permute-start(bf16[16,512]{1,0:T(8,128)(2,1)S(1)} %get-tuple-element.139), channel_id=1, source_target_pairs={{0,4},{1,5},{2,6},{3,7},{4,0},{5,1},{6,2},{7,3},{8,12},{9,13},{10,... | collective-permute-start | bytes 49160 | tf_op jit(solution)/shard_map/ppermute | solution.py:342
  56.9 6.7 %collective-permute-start.23 = (bf16[64,512]{1,0:T(8,128)(2,1)S(1)}, bf16[64,512]{1,0:T(8,128)(2,1)S(1)}, u32[]{:S(2)}, u32[]{:S(2)}) collective-permute-start(bf16[64,512]{1,0:T(8,128)(2,1)S(1)} %get-tuple-element.134), channel_id=1, source_target_pairs={{0,15},{1,2},{2,1},{3,4},{4,3},{5,6},{6,5},{7,8},{8,7},{9,10},{10,... | collective-permute-start | bytes 196616 | tf_op jit(solution)/shard_map/ppermute | solution.py:348
  59.2 4.4 %collective-permute-start.29 = (bf16[16,512]{1,0:T(8,128)(2,1)S(1)}, bf16[16,512]{1,0:T(8,128)(2,1)S(1)}, u32[]{:S(2)}, u32[]{:S(2)}) collective-permute-start(bf16[16,512]{1,0:T(8,128)(2,1)S(1)} %get-tuple-element.142), channel_id=1, source_target_pairs={{0,2},{1,3},{2,0},{3,1},{4,6},{5,7},{6,4},{7,5},{8,10},{9,11},{10,... | collective-permute-start | bytes 49160 | tf_op jit(solution)/shard_map/ppermute | solution.py:342
  64.4 6.5 %collective-permute-start.30 = (bf16[64,512]{1,0:T(8,128)(2,1)S(1)}, bf16[64,512]{1,0:T(8,128)(2,1)S(1)}, u32[]{:S(2)}, u32[]{:S(2)}) collective-permute-start(bf16[64,512]{1,0:T(8,128)(2,1)S(1)} %get-tuple-element.150), channel_id=1, source_target_pairs={{0,15},{1,2},{2,1},{3,4},{4,3},{5,6},{6,5},{7,8},{8,7},{9,10},{10,... | collective-permute-start | bytes 196616 | tf_op jit(solution)/shard_map/ppermute | solution.py:348
  66.3 4.5 %collective-permute-start.31 = (bf16[64,512]{1,0:T(8,128)(2,1)S(1)}, bf16[64,512]{1,0:T(8,128)(2,1)S(1)}, u32[]{:S(2)}, u32[]{:S(2)}) collective-permute-start(bf16[64,512]{1,0:T(8,128)(2,1)S(1)} %get-tuple-element.151), channel_id=1, source_target_pairs={{0,1},{1,0},{2,3},{3,2},{4,5},{5,4},{6,7},{7,6},{8,9},{9,8},{10,11... | collective-permute-start | bytes 196616 | tf_op jit(solution)/shard_map/ppermute | solution.py:342
  (20 other events, 71.4 us)

commit v10 on v9

--- a/solution.py
+++ b/solution.py
@@ -33,18 +33,24 @@
     return message, sigma + message * (1.0 - sigma)
 
 
+def match(places, wanted):
+    shape = places.shape
+    wanted = jnp.broadcast_to(wanted, shape).astype(jnp.int16)
+    return jnp.where(places == wanted, jnp.ones(shape, BF), jnp.zeros(shape, BF))
+
+
 def pick(rows, wanted):
-    places = lax.broadcasted_iota(jnp.int32, (rows, wanted.shape[1]), 0)
-    return (places == wanted).astype(F32).astype(BF)
+    places = lax.broadcasted_iota(jnp.int32, (rows, wanted.shape[1]), 0).astype(jnp.int16)
+    return match(places, wanted)
 
 
 def counts_t(columns, first, entries):
     degree, rows = entries.shape
-    places = lax.broadcasted_iota(jnp.int32, (columns, rows), 0) + first
-    total = jnp.zeros((columns, rows), F32)
-    for k in range(degree):
-        total = total + (places == entries[k : k + 1]).astype(F32)
-    return total.astype(BF)
+    places = (lax.broadcasted_iota(jnp.int32, (columns, rows), 0) + first).astype(jnp.int16)
+    total = match(places, entries[0:1])
+    for k in range(1, degree):
+        total = total + match(places, entries[k : k + 1])
+    return total
 
 
 def side_swap(entries, rows, size, me):
@@ -238,35 +244,33 @@
     list_tables(me, lists, far_lists, send, receive)
 
 
-def layer_local(hidden, own_t, message, near, *, scale):
-    near[...] = hidden[...].astype(F32) + scale * t_mm(own_t[...], message[...])
+def layer_local(hidden, own_t, weight, near, slope, *, layer, scale):
+    state = hidden[...]
+    value, gradient = silu_pair(mm(state, weight[layer]))
+    slope[...] = gradient
+    near[...] = state.astype(F32) + scale * t_mm(own_t[...], value.astype(BF))
 
 
 def back_local(own_t, grad, near):
     near[...] = mm(own_t[...], grad[...])
 
 
-def first_hidden(near, rim_t, outer_in, inner_in, encoder, weight, send, hidden, message, slope, *outs, size):
+def chosen_messages(send, state, weight):
+    return silu_pair(mm(t_mm(send[...], state).astype(BF), weight))[0]
+
+
+def first_hidden(near, rim_t, outer_in, inner_in, encoder, weight, send, hidden, *outs, size):
     incoming = silu_pair(mm(arrived([outer_in, inner_in], outer_in.shape[0]), encoder[...]))[0].astype(BF)
     state = (near[...] + t_mm(rim_t[...], incoming)).astype(BF)
     hidden[...] = state
-    value, gradient = silu_pair(mm(state, weight[0]))
-    value = value.astype(BF)
-    message[...] = value
-    slope[...] = gradient
-    emit(outs, t_mm(send[...], value), size)
+    emit(outs, chosen_messages(send, state, weight[0]), size)
 
 
 def next_hidden(near, forth_t, weight, send, outer_extra, inner_extra, *refs, ins, layer, scale, size):
     rows = arrived(refs[:ins], size)
-    hidden, message, slope = refs[ins : ins + 3]
     state = (near[...] + scale * t_mm(forth_t[...], rows)).astype(BF)
-    hidden[...] = state
-    value, gradient = silu_pair(mm(state, weight[layer]))
-    value = value.astype(BF)
-    message[...] = value
-    slope[...] = gradient
-    emit(refs[ins + 3 :], t_mm(send[...], value), size, (outer_extra[...], inner_extra[...]))
+    refs[ins][...] = state
+    emit(refs[ins + 1 :], chosen_messages(send, state, weight[layer]), size, (outer_extra[...], inner_extra[...]))
 
 
 def turn(near, forth_t, weight, send, receive, back_t, back_near, *refs, ins, scale, size):
@@ -307,11 +311,15 @@
     inner[...] = back[outer.shape[0] :]
 
 
-def decode(latent, own_t, rim_t, message, outer_in, inner_in, output):
+def decode_own(latent, own_t, message, base):
+    base[...] = latent[...].astype(F32) + t_mm(own_t[...], message[...])
+
+
+def decode_rim(base, rim_t, outer_in, inner_in, output, token):
     size = outer_in.shape[0] // 2
     incoming = jnp.concatenate([outer_in[size:], inner_in[size : 2 * size]], axis=0)
-    total = t_mm(own_t[...], message[...]) + t_mm(rim_t[...], incoming)
-    output[...] = (latent[...].astype(F32) + total).astype(BF)
+    output[...] = (base[...] + t_mm(rim_t[...], incoming)).astype(BF)
+    token[...] = jnp.zeros(token.shape, F32)
 
 
 def grid_local(me, own_t, grad, lists, slope, weight, cotangent, base, table, slope_rows, mesh_grad):
@@ -434,16 +442,20 @@
         scalars=1,
     )
 
-    hidden, message, slope_0, *outs = call(
+    hidden, *outs = call(
         functools.partial(first_hidden, size=halo),
-        [state, state, total] + sends(halo),
+        [state] + sends(halo),
         step,
         near, grid_rim_t, outer_in, inner_in, encoder_weight, processor_weights, send,
     )
-    local = functools.partial(layer_local, scale=scale)
     ins = exchange(outs, cap)
-    (near,) = call(local, [total], 6 * square(mesh_rows, mesh_rows), hidden, own_t, message, ins[-1], free=1)
-
+    near, slope_0 = call(
+        functools.partial(layer_local, layer=0, scale=scale),
+        [total, total],
+        6 * square(mesh_rows, mesh_rows),
+        hidden, own_t, processor_weights, ins[-1],
+        free=1,
+    )
     decoder_own_t, decoder_rim_t, decoder_near, outer_extra, inner_extra = call(
         decoder_back,
         [((mesh_rows, grid_rows), BF), ((2 * halo, grid_rows), BF), total, rim, rim],
@@ -452,15 +464,20 @@
         scalars=1, free=1,
     )
 
-    hidden, message, slope_1, *outs = call(
+    hidden, *outs = call(
         functools.partial(next_hidden, ins=len(ins), layer=1, scale=scale, size=halo),
-        [state, state, total] + sends(2 * halo),
+        [state] + sends(2 * halo),
         step,
         near, forth_t, processor_weights, send, outer_extra, inner_extra, *ins,
     )
     ins = exchange(outs, cap)
-    (near,) = call(local, [total], 6 * square(mesh_rows, mesh_rows), hidden, own_t, message)
-
+    near, slope_1 = call(
+        functools.partial(layer_local, layer=1, scale=scale),
+        [total, total],
+        6 * square(mesh_rows, mesh_rows),
+        hidden, own_t, processor_weights, ins[-1],
+        free=1,
+    )
 
     message, grad, *outs = call(
         functools.partial(turn, ins=len(ins), scale=scale, size=halo),
@@ -472,30 +489,40 @@
     (near,) = call(back_local, [total], 6 * square(mesh_rows, mesh_rows), own_t, grad)
 
     outer_decoder, inner_decoder = ins[:2]
+    (near,) = call(back_local, [total], 6 * square(mesh_rows, mesh_rows), own_t, grad, ins[-1], free=1)
+    (base,) = call(
+        decode_own,
+        [((grid_rows, width), F32)],
+        square(grid_rows, mesh_rows),
+        grid_latent, decoder_own_t, message, ins[-1],
+        free=1,
+    )
 
     grad, *outs = call(
         functools.partial(middle_back, ins=len(ins), layer=1, scale=scale, size=halo),
         [state] + sends(halo),
         step,
-        near, receive, slope_1, processor_weights, grad, back_t, *ins,
+        near, receive, slope_1, processor_weights, grad, back_t, *ins, base,
+        free=1,
     )
     ins = exchange(outs, cap)
-    (near,) = call(back_local, [total], 6 * square(mesh_rows, mesh_rows), own_t, grad)
+    (near,) = call(back_local, [total], 6 * square(mesh_rows, mesh_rows), own_t, grad, ins[-1], free=1)
+    output, token = call(
+        decode_rim,
+        [((grid_rows, width), BF), ((8, 128), F32)],
+        square(grid_rows, 2 * halo),
+        base, decoder_rim_t, outer_decoder, inner_decoder, ins[-1],
+        free=1,
+    )
 
     grad, outer, inner = call(
         functools.partial(last_back, ins=len(ins), scale=scale),
         [state, grid_rim, grid_rim],
         step,
-        near, receive, slope_0, processor_weights, grad, grid_rim_t, *ins,
+        near, receive, slope_0, processor_weights, grad, grid_rim_t, *ins, token,
+        free=1,
     )
     outer_in, inner_in = across(outer), toggle(inner, 1)
-    (output,) = call(
-        decode,
-        [((grid_rows, width), BF)],
-        square(grid_rows, mesh_rows),
-        grid_latent, decoder_own_t, decoder_rim_t, message, outer_decoder, inner_decoder, grad,
-        free=1,
-    )
     base, table, slope_rows, mesh_grad = call(
         grid_local,
         [((grid_rows, width), F32), ((grid_rows, 2 * ghalo), BF), ((2 * ghalo, width), F32), state],

time: 72.7 us -> 70.9 us (0.975)
  Pallas kernels: 21.5 us -> 20.1 us
  waiting for transfers between devices: 11.1 us -> 10.3 us
    ppermute x26, waiting for transfers between devices: 10.8 us -> 8.48 us  [toggle(): return lax.ppermute(value, 'dom', [(i, i ^ bits) for i in range(peers)])]
    ppermute x6, waiting for transfers between devices: 0.33 us -> 1.85 us  [across(): return lax.ppermute(value, 'dom', pairs)]
    pallas_call x20 -> x21, Pallas kernels: 21.5 us -> 20.1 us  [call(): pl.pallas_call(inner, out_shape=shapes, in_specs=[pl.BlockSpec(memory_spa...]
    ppermute x6, starting transfers between devices: 12.2 us -> 13 us  [across(): return lax.ppermute(value, 'dom', pairs)]
  transfers between devices with their start and end apart: 32 -> 32, of which waited for: 14 -> 13; matrix products, arithmetic and copies ran while one was open for 0% -> 0% of each run, Pallas kernels for 17% -> 17%
where the time goes in v10:
time: 70.9 us; the launch traced here: 70.7 us
  starting transfers between devices  38.5 us (54%)
  Pallas kernels  20.1 us (28%)
  waiting for transfers between devices  10.3 us (15%)
  between operations  0.94 us (1%)
  local copies, waits for them, and re-layouts  0.76 us (1%)
    ppermute x26, starting transfers between devices, toggle(): return lax.ppermute(value, 'dom', [(i, i ^ bits) for i in range(peers)])  25.5 us
    pallas_call x21, Pallas kernels, call(): pl.pallas_call(inner, out_shape=shapes, in_specs=[pl.BlockSpec(memory_spa...  20.1 us
    ppermute x6, starting transfers between devices, across(): return lax.ppermute(value, 'dom', pairs)  13 us
    ppermute x26, waiting for transfers between devices, toggle(): return lax.ppermute(value, 'dom', [(i, i ^ bits) for i in range(peers)])  8.48 us
    ppermute x6, waiting for transfers between devices, across(): return lax.ppermute(value, 'dom', pairs)  1.85 us
  transfers between devices with their start and end apart: 32, of which 13 were waited for; matrix products, arithmetic and copies ran while one was open for 0% of the time, Pallas kernels for 17%

profile of v10, /device:TPU:0, one launch (start us, length us, event | category | flops | bytes accessed | tf_op | source)
XLA Modules:
  0.0 70.7 jit_solution(9022309654802136323)
XLA Ops:
  0.7 2.3 %shard_map.139 = (bf16[64,512]{1,0:T(8,128)(2,1)}, bf16[64,512]{1,0:T(8,128)(2,1)}) custom-call(s32[1]{0:T(128)} %bitcast.me.refs_0_, bf16[1024,512]{1,0:T(8,128)(2,1)} %refs_0_.1, s32[1,2,64]{2,1,0:T(2,128)} %lists.5), custom_call_target="tpu_custom_call" | custom-call | flops 34359738368 | tf_op jit(solution)/shard_map/pallas_call | solution.py:82
  3.0 5.5 %collective-permute-start = (bf16[64,512]{1,0:T(8,128)(2,1)}, bf16[64,512]{1,0:T(8,128)(2,1)S(1)}, u32[]{:S(2)}, u32[]{:S(2)}) collective-permute-start(bf16[64,512]{1,0:T(8,128)(2,1)} %get-tuple-element.86), channel_id=1, source_target_pairs={{0,15},{1,2},{2,1},{3,4},{4,3},{5,6},{6,5},{7,8},{8,7},{9,10},{10,... | collective-permute-start | bytes 196616 | tf_op jit(solution)/shard_map/ppermute | solution.py:356
  10.0 1.9 %shard_map.140 = (f32[512,512]{1,0:T(8,128)S(1)}, bf16[1024,512]{1,0:T(8,128)(2,1)S(1)}, bf16[128,512]{1,0:T(8,128)(2,1)S(1)}, bf16[1024,512]{1,0:T(8,128)(2,1)S(1)}) custom-call(s32[1]{0:T(128)} %bitcast.me.refs_0_, s32[4,512]{1,0:T(4,128)S(1)} %bitcast.9, bf16[512,512]{1,0:T(8,128)(2,1)S(1)} %copy-done.1, bf16[1024,512]{1,0:T(8,128)(2,1)S(1)} %copy-done.3, ...), custom_call_target="tpu_custom_call" | custom-call | flops 2147483648 | bytes 5382148 | tf_op jit(solution)/shard_map/pallas_call | solution.py:82
  12.9 1.3 %collective-permute-start.2 = (bf16[16,512]{1,0:T(8,128)(2,1)S(1)}, bf16[16,512]{1,0:T(8,128)(2,1)S(1)}, u32[]{:S(2)}, u32[]{:S(2)}) collective-permute-start(bf16[16,512]{1,0:T(8,128)(2,1)S(1)} %get-tuple-element.90), channel_id=1, source_target_pairs={{0,12},{1,13},{2,14},{3,15},{4,8},{5,9},{6,10},{7,11},{8,4},{9,5},... | collective-permute-start | bytes 49160 | tf_op jit(solution)/shard_map/ppermute | solution.py:350
  14.2 3.2 %collective-permute-start.4 = (bf16[16,512]{1,0:T(8,128)(2,1)S(1)}, bf16[16,512]{1,0:T(8,128)(2,1)S(1)}, u32[]{:S(2)}, u32[]{:S(2)}) collective-permute-start(bf16[16,512]{1,0:T(8,128)(2,1)S(1)} %get-tuple-element.92), channel_id=1, source_target_pairs={{0,4},{1,5},{2,6},{3,7},{4,0},{5,1},{6,2},{7,3},{8,12},{9,13},{10,... | collective-permute-start | bytes 49160 | tf_op jit(solution)/shard_map/ppermute | solution.py:350
  17.4 2.3 %collective-permute-start.5 = (bf16[64,512]{1,0:T(8,128)(2,1)S(1)}, bf16[64,512]{1,0:T(8,128)(2,1)S(1)}, u32[]{:S(2)}, u32[]{:S(2)}) collective-permute-start(bf16[64,512]{1,0:T(8,128)(2,1)S(1)} %get-tuple-element.101), channel_id=1, source_target_pairs={{0,15},{1,2},{2,1},{3,4},{4,3},{5,6},{6,5},{7,8},{8,7},{9,10},{10,... | collective-permute-start | bytes 196616 | tf_op jit(solution)/shard_map/ppermute | solution.py:356
  20.3 1.5 %collective-permute-start.6 = (bf16[80,512]{1,0:T(8,128)(2,1)S(1)}, bf16[80,512]{1,0:T(8,128)(2,1)S(1)}, u32[]{:S(2)}, u32[]{:S(2)}) collective-permute-start(bf16[80,512]{1,0:T(8,128)(2,1)S(1)} %get-tuple-element.102), channel_id=1, source_target_pairs={{0,1},{1,0},{2,3},{3,2},{4,5},{5,4},{6,7},{7,6},{8,9},{9,8},{10,11... | collective-permute-start | bytes 245768 | tf_op jit(solution)/shard_map/ppermute | solution.py:350
  24.9 2.3 %collective-permute-start.9 = (bf16[16,512]{1,0:T(8,128)(2,1)S(1)}, bf16[16,512]{1,0:T(8,128)(2,1)S(1)}, u32[]{:S(2)}, u32[]{:S(2)}) collective-permute-start(bf16[16,512]{1,0:T(8,128)(2,1)S(1)} %get-tuple-element.108), channel_id=1, source_target_pairs={{0,12},{1,13},{2,14},{3,15},{4,8},{5,9},{6,10},{7,11},{8,4},{9,5},... | collective-permute-start | bytes 49160 | tf_op jit(solution)/shard_map/ppermute | solution.py:350
  27.6 1.7 %collective-permute-start.11 = (bf16[16,512]{1,0:T(8,128)(2,1)S(1)}, bf16[16,512]{1,0:T(8,128)(2,1)S(1)}, u32[]{:S(2)}, u32[]{:S(2)}) collective-permute-start(bf16[16,512]{1,0:T(8,128)(2,1)S(1)} %get-tuple-element.110), channel_id=1, source_target_pairs={{0,4},{1,5},{2,6},{3,7},{4,0},{5,1},{6,2},{7,3},{8,12},{9,13},{10,... | collective-permute-start | bytes 49160 | tf_op jit(solution)/shard_map/ppermute | solution.py:350
  29.3 1.6 %collective-permute-start.12 = (bf16[128,512]{1,0:T(8,128)(2,1)S(1)}, bf16[128,512]{1,0:T(8,128)(2,1)S(1)}, u32[]{:S(2)}, u32[]{:S(2)}) collective-permute-start(bf16[128,512]{1,0:T(8,128)(2,1)S(1)} %get-tuple-element.116), channel_id=1, source_target_pairs={{0,15},{1,2},{2,1},{3,4},{4,3},{5,6},{6,5},{7,8},{8,7},{9,10},{10,... | collective-permute-start | bytes 393224 | tf_op jit(solution)/shard_map/ppermute | solution.py:356
  32.1 1.1 %collective-permute-start.15 = (bf16[16,512]{1,0:T(8,128)(2,1)S(1)}, bf16[16,512]{1,0:T(8,128)(2,1)S(1)}, u32[]{:S(2)}, u32[]{:S(2)}) collective-permute-start(bf16[16,512]{1,0:T(8,128)(2,1)S(1)} %get-tuple-element.119), channel_id=1, source_target_pairs={{0,2},{1,3},{2,0},{3,1},{4,6},{5,7},{6,4},{7,5},{8,10},{9,11},{10,... | collective-permute-start | bytes 49160 | tf_op jit(solution)/shard_map/ppermute | solution.py:350
  34.8 1.9 %collective-permute-done.14.refs_2_ = bf16[16,512]{1,0:T(8,128)(2,1)S(1)} collective-permute-done((bf16[16,512]{1,0:T(8,128)(2,1)S(1)}, bf16[16,512]{1,0:T(8,128)(2,1)S(1)}, u32[]{:S(2)}, u32[]{:S(2)}) %collective-permute-start.14) | collective-permute-done | bytes 16416 | tf_op jit(solution)/shard_map/ppermute | solution.py:350
  36.8 1.4 %shard_map.149 = (bf16[512,512]{1,0:T(8,128)(2,1)S(1)}, bf16[512,512]{1,0:T(8,128)(2,1)S(1)}, bf16[128,512]{1,0:T(8,128)(2,1)S(1)}, bf16[128,512]{1,0:T(8,128)(2...) custom-call(f32[512,512]{1,0:T(8,128)S(1)} %get-tuple-element.112.ne, ...), custom_call_target="tpu_custom_call" | custom-call | flops 1610612736 | bytes 5111808 | tf_op jit(solution)/shard_map/pallas_call | solution.py:82
  38.2 1.5 %collective-permute-start.16 = (bf16[16,512]{1,0:T(8,128)(2,1)S(1)}, bf16[16,512]{1,0:T(8,128)(2,1)S(1)}, u32[]{:S(2)}, u32[]{:S(2)}) collective-permute-start(bf16[16,512]{1,0:T(8,128)(2,1)S(1)} %get-tuple-element.123), channel_id=1, source_target_pairs={{0,12},{1,13},{2,14},{3,15},{4,8},{5,9},{6,10},{7,11},{8,4},{9,5},... | collective-permute-start | bytes 49160 | tf_op jit(solution)/shard_map/ppermute | solution.py:350
  40.0 2.6 %collective-permute-start.18 = (bf16[16,512]{1,0:T(8,128)(2,1)S(1)}, bf16[16,512]{1,0:T(8,128)(2,1)S(1)}, u32[]{:S(2)}, u32[]{:S(2)}) collective-permute-start(bf16[16,512]{1,0:T(8,128)(2,1)S(1)} %get-tuple-element.125), channel_id=1, source_target_pairs={{0,4},{1,5},{2,6},{3,7},{4,0},{5,1},{6,2},{7,3},{8,12},{9,13},{10,... | collective-permute-start | bytes 49160 | tf_op jit(solution)/shard_map/ppermute | solution.py:350
  44.8 1.3 %collective-permute-start.22 = (bf16[16,512]{1,0:T(8,128)(2,1)S(1)}, bf16[16,512]{1,0:T(8,128)(2,1)S(1)}, u32[]{:S(2)}, u32[]{:S(2)}) collective-permute-start(bf16[16,512]{1,0:T(8,128)(2,1)S(1)} %get-tuple-element.133), channel_id=1, source_target_pairs={{0,2},{1,3},{2,0},{3,1},{4,6},{5,7},{6,4},{7,5},{8,10},{9,11},{10,... | collective-permute-start | bytes 49160 | tf_op jit(solution)/shard_map/ppermute | solution.py:350
  47.9 2.1 %collective-permute-done.22.refs_9_ = bf16[16,512]{1,0:T(8,128)(2,1)S(1)} collective-permute-done((bf16[16,512]{1,0:T(8,128)(2,1)S(1)}, bf16[16,512]{1,0:T(8,128)(2,1)S(1)}, u32[]{:S(2)}, u32[]{:S(2)}) %collective-permute-start.22) | collective-permute-done | bytes 16416 | tf_op jit(solution)/shard_map/ppermute | solution.py:350
  50.8 1.6 %collective-permute-start.23 = (bf16[16,512]{1,0:T(8,128)(2,1)S(1)}, bf16[16,512]{1,0:T(8,128)(2,1)S(1)}, u32[]{:S(2)}, u32[]{:S(2)}) collective-permute-start(bf16[16,512]{1,0:T(8,128)(2,1)S(1)} %get-tuple-element.136), channel_id=1, source_target_pairs={{0,12},{1,13},{2,14},{3,15},{4,8},{5,9},{6,10},{7,11},{8,4},{9,5},... | collective-permute-start | bytes 49160 | tf_op jit(solution)/shard_map/ppermute | solution.py:350
  52.7 2.6 %collective-permute-start.25 = (bf16[16,512]{1,0:T(8,128)(2,1)S(1)}, bf16[16,512]{1,0:T(8,128)(2,1)S(1)}, u32[]{:S(2)}, u32[]{:S(2)}) collective-permute-start(bf16[16,512]{1,0:T(8,128)(2,1)S(1)} %get-tuple-element.138), channel_id=1, source_target_pairs={{0,4},{1,5},{2,6},{3,7},{4,0},{5,1},{6,2},{7,3},{8,12},{9,13},{10,... | collective-permute-start | bytes 49160 | tf_op jit(solution)/shard_map/ppermute | solution.py:350
  59.7 1.4 %shard_map.155 = (bf16[1024,512]{1,0:T(8,128)(2,1)}, f32[8,128]{1,0:T(8,128)S(1)}) custom-call(f32[1024,512]{1,0:T(8,128)S(1)} %shard_map.151.refs_11_.refs_0_, bf16[128,1024]{1,0:T(8,128)(2,1)S(1)} %get-tuple-element.127.refs_1_, bf16[128,512]{1,0:T(8,128)(2,1)S(1)} %collective-permute-done.19.refs_6_.refs_2_, ...), custom_call_target="tpu_custom_call" | custom-call | flops 134217728 | bytes 3706880 | tf_op jit(solution)/shard_map/pallas_call | solution.py:82
  62.7 2.1 %collective-permute-start.30 = (bf16[64,512]{1,0:T(8,128)(2,1)S(1)}, bf16[64,512]{1,0:T(8,128)(2,1)S(1)}, u32[]{:S(2)}, u32[]{:S(2)}) collective-permute-start(bf16[64,512]{1,0:T(8,128)(2,1)S(1)} %get-tuple-element.154), channel_id=1, source_target_pairs={{0,15},{1,2},{2,1},{3,4},{4,3},{5,6},{6,5},{7,8},{8,7},{9,10},{10,... | collective-permute-start | bytes 196616 | tf_op jit(solution)/shard_map/ppermute | solution.py:356
  64.8 2.5 %shard_map.158 = (f32[1024,512]{1,0:T(8,128)S(1)}, bf16[1024,128]{1,0:T(8,128)(2,1)S(1)}, f32[128,512]{1,0:T(8,128)S(1)}, bf16[512,512]{1,0:T(8,128)(2,1)}) custom-call(s32[1]{0:T(128)} %bitcast.me.refs_0_, bf16[1024,512]{1,0:T(8,128)(2,1)S(1)} %get-tuple-element.141.own_t, bf16[512,512]{1,0:T(8,128)(2,1)S(1)} %get-tuple-element.149.grad, ...), custom_call_target="tpu_custom_call" | custom-call | flops 1073741824 | bytes 7340548 | tf_op jit(solution)/shard_map/pallas_call | solution.py:82
  67.3 1.8 %collective-permute-done.30.outer_in = bf16[64,512]{1,0:T(8,128)(2,1)S(1)} collective-permute-done((bf16[64,512]{1,0:T(8,128)(2,1)S(1)}, bf16[64,512]{1,0:T(8,128)(2,1)S(1)}, u32[]{:S(2)}, u32[]{:S(2)}) %collective-permute-start.30) | collective-permute-done | bytes 65568 | tf_op jit(solution)/shard_map/ppermute | solution.py:356
  69.2 1.5 %shard_map.159 = bf16[1024,512]{1,0:T(8,128)(2,1)} custom-call(f32[1024,512]{1,0:T(8,128)S(1)} %get-tuple-element.151.base, bf16[1024,128]{1,0:T(8,128)(2,1)S(1)} %get-tuple-element.152.table, f32[128,512]{1,0:T(8,128)S(1)} %get-tuple-element.153.slope_rows, bf16[512,512]{1,0:T(8,128)(2,1)S(1)} %copy-done.1, ...), custom_call_target="tpu_custom_call" | custom-call | flops 268435456 | bytes 4325376 | tf_op jit(solution)/shard_map/pallas_call | solution.py:82
  (85 shorter events, 20.8 us)
Async XLA Ops:
  3.0 9.0 %collective-permute-start = (bf16[64,512]{1,0:T(8,128)(2,1)}, bf16[64,512]{1,0:T(8,128)(2,1)S(1)}, u32[]{:S(2)}, u32[]{:S(2)}) collective-permute-start(bf16[64,512]{1,0:T(8,128)(2,1)} %get-tuple-element.86), channel_id=1, source_target_pairs={{0,15},{1,2},{2,1},{3,4},{4,3},{5,6},{6,5},{7,8},{8,7},{9,10},{10,... | collective-permute-start | bytes 196616 | tf_op jit(solution)/shard_map/ppermute | solution.py:356
  12.9 6.7 %collective-permute-start.2 = (bf16[16,512]{1,0:T(8,128)(2,1)S(1)}, bf16[16,512]{1,0:T(8,128)(2,1)S(1)}, u32[]{:S(2)}, u32[]{:S(2)}) collective-permute-start(bf16[16,512]{1,0:T(8,128)(2,1)S(1)} %get-tuple-element.90), channel_id=1, source_target_pairs={{0,12},{1,13},{2,14},{3,15},{4,8},{5,9},{6,10},{7,11},{8,4},{9,5},... | collective-permute-start | bytes 49160 | tf_op jit(solution)/shard_map/ppermute | solution.py:350
  14.2 5.5 %collective-permute-start.3 = (bf16[16,512]{1,0:T(8,128)(2,1)S(1)}, bf16[16,512]{1,0:T(8,128)(2,1)S(1)}, u32[]{:S(2)}, u32[]{:S(2)}) collective-permute-start(bf16[16,512]{1,0:T(8,128)(2,1)S(1)} %get-tuple-element.91), channel_id=1, source_target_pairs={{0,8},{1,9},{2,10},{3,11},{4,12},{5,13},{6,14},{7,15},{8,0},{9,1},... | collective-permute-start | bytes 49160 | tf_op jit(solution)/shard_map/ppermute | solution.py:350
  14.2 5.5 %collective-permute-start.4 = (bf16[16,512]{1,0:T(8,128)(2,1)S(1)}, bf16[16,512]{1,0:T(8,128)(2,1)S(1)}, u32[]{:S(2)}, u32[]{:S(2)}) collective-permute-start(bf16[16,512]{1,0:T(8,128)(2,1)S(1)} %get-tuple-element.92), channel_id=1, source_target_pairs={{0,4},{1,5},{2,6},{3,7},{4,0},{5,1},{6,2},{7,3},{8,12},{9,13},{10,... | collective-permute-start | bytes 49160 | tf_op jit(solution)/shard_map/ppermute | solution.py:350
  17.4 6.7 %collective-permute-start.5 = (bf16[64,512]{1,0:T(8,128)(2,1)S(1)}, bf16[64,512]{1,0:T(8,128)(2,1)S(1)}, u32[]{:S(2)}, u32[]{:S(2)}) collective-permute-start(bf16[64,512]{1,0:T(8,128)(2,1)S(1)} %get-tuple-element.101), channel_id=1, source_target_pairs={{0,15},{1,2},{2,1},{3,4},{4,3},{5,6},{6,5},{7,8},{8,7},{9,10},{10,... | collective-permute-start | bytes 196616 | tf_op jit(solution)/shard_map/ppermute | solution.py:356
  24.9 6.0 %collective-permute-start.9 = (bf16[16,512]{1,0:T(8,128)(2,1)S(1)}, bf16[16,512]{1,0:T(8,128)(2,1)S(1)}, u32[]{:S(2)}, u32[]{:S(2)}) collective-permute-start(bf16[16,512]{1,0:T(8,128)(2,1)S(1)} %get-tuple-element.108), channel_id=1, source_target_pairs={{0,12},{1,13},{2,14},{3,15},{4,8},{5,9},{6,10},{7,11},{8,4},{9,5},... | collective-permute-start | bytes 49160 | tf_op jit(solution)/shard_map/ppermute | solution.py:350
  27.2 4.6 %collective-permute-start.10 = (bf16[16,512]{1,0:T(8,128)(2,1)S(1)}, bf16[16,512]{1,0:T(8,128)(2,1)S(1)}, u32[]{:S(2)}, u32[]{:S(2)}) collective-permute-start(bf16[16,512]{1,0:T(8,128)(2,1)S(1)} %get-tuple-element.109), channel_id=1, source_target_pairs={{0,8},{1,9},{2,10},{3,11},{4,12},{5,13},{6,14},{7,15},{8,0},{9,1},... | collective-permute-start | bytes 49160 | tf_op jit(solution)/shard_map/ppermute | solution.py:350
  27.6 4.2 %collective-permute-start.11 = (bf16[16,512]{1,0:T(8,128)(2,1)S(1)}, bf16[16,512]{1,0:T(8,128)(2,1)S(1)}, u32[]{:S(2)}, u32[]{:S(2)}) collective-permute-start(bf16[16,512]{1,0:T(8,128)(2,1)S(1)} %get-tuple-element.110), channel_id=1, source_target_pairs={{0,4},{1,5},{2,6},{3,7},{4,0},{5,1},{6,2},{7,3},{8,12},{9,13},{10,... | collective-permute-start | bytes 49160 | tf_op jit(solution)/shard_map/ppermute | solution.py:350
  29.3 7.5 %collective-permute-start.12 = (bf16[128,512]{1,0:T(8,128)(2,1)S(1)}, bf16[128,512]{1,0:T(8,128)(2,1)S(1)}, u32[]{:S(2)}, u32[]{:S(2)}) collective-permute-start(bf16[128,512]{1,0:T(8,128)(2,1)S(1)} %get-tuple-element.116), channel_id=1, source_target_pairs={{0,15},{1,2},{2,1},{3,4},{4,3},{5,6},{6,5},{7,8},{8,7},{9,10},{10,... | collective-permute-start | bytes 393224 | tf_op jit(solution)/shard_map/ppermute | solution.py:356
  32.0 4.7 %collective-permute-start.14 = (bf16[16,512]{1,0:T(8,128)(2,1)S(1)}, bf16[16,512]{1,0:T(8,128)(2,1)S(1)}, u32[]{:S(2)}, u32[]{:S(2)}) collective-permute-start(bf16[16,512]{1,0:T(8,128)(2,1)S(1)} %get-tuple-element.118), channel_id=1, source_target_pairs={{0,3},{1,2},{2,1},{3,0},{4,7},{5,6},{6,5},{7,4},{8,11},{9,10},{10,... | collective-permute-start | bytes 49160 | tf_op jit(solution)/shard_map/ppermute | solution.py:350
  32.1 4.8 %collective-permute-start.15 = (bf16[16,512]{1,0:T(8,128)(2,1)S(1)}, bf16[16,512]{1,0:T(8,128)(2,1)S(1)}, u32[]{:S(2)}, u32[]{:S(2)}) collective-permute-start(bf16[16,512]{1,0:T(8,128)(2,1)S(1)} %get-tuple-element.119), channel_id=1, source_target_pairs={{0,2},{1,3},{2,0},{3,1},{4,6},{5,7},{6,4},{7,5},{8,10},{9,11},{10,... | collective-permute-start | bytes 49160 | tf_op jit(solution)/shard_map/ppermute | solution.py:350
  38.2 5.6 %collective-permute-start.16 = (bf16[16,512]{1,0:T(8,128)(2,1)S(1)}, bf16[16,512]{1,0:T(8,128)(2,1)S(1)}, u32[]{:S(2)}, u32[]{:S(2)}) collective-permute-start(bf16[16,512]{1,0:T(8,128)(2,1)S(1)} %get-tuple-element.123), channel_id=1, source_target_pairs={{0,12},{1,13},{2,14},{3,15},{4,8},{5,9},{6,10},{7,11},{8,4},{9,5},... | collective-permute-start | bytes 49160 | tf_op jit(solution)/shard_map/ppermute | solution.py:350
  39.7 4.7 %collective-permute-start.17 = (bf16[16,512]{1,0:T(8,128)(2,1)S(1)}, bf16[16,512]{1,0:T(8,128)(2,1)S(1)}, u32[]{:S(2)}, u32[]{:S(2)}) collective-permute-start(bf16[16,512]{1,0:T(8,128)(2,1)S(1)} %get-tuple-element.124), channel_id=1, source_target_pairs={{0,8},{1,9},{2,10},{3,11},{4,12},{5,13},{6,14},{7,15},{8,0},{9,1},... | collective-permute-start | bytes 49160 | tf_op jit(solution)/shard_map/ppermute | solution.py:350
  40.0 4.5 %collective-permute-start.18 = (bf16[16,512]{1,0:T(8,128)(2,1)S(1)}, bf16[16,512]{1,0:T(8,128)(2,1)S(1)}, u32[]{:S(2)}, u32[]{:S(2)}) collective-permute-start(bf16[16,512]{1,0:T(8,128)(2,1)S(1)} %get-tuple-element.125), channel_id=1, source_target_pairs={{0,4},{1,5},{2,6},{3,7},{4,0},{5,1},{6,2},{7,3},{8,12},{9,13},{10,... | collective-permute-start | bytes 49160 | tf_op jit(solution)/shard_map/ppermute | solution.py:350
  42.6 7.4 %collective-permute-start.19 = (bf16[128,512]{1,0:T(8,128)(2,1)S(1)}, bf16[128,512]{1,0:T(8,128)(2,1)S(1)}, u32[]{:S(2)}, u32[]{:S(2)}) collective-permute-start(bf16[128,512]{1,0:T(8,128)(2,1)S(1)} %get-tuple-element.128), channel_id=1, source_target_pairs={{0,15},{1,2},{2,1},{3,4},{4,3},{5,6},{6,5},{7,8},{8,7},{9,10},{10,... | collective-permute-start | bytes 393224 | tf_op jit(solution)/shard_map/ppermute | solution.py:356
  44.8 5.3 %collective-permute-start.22 = (bf16[16,512]{1,0:T(8,128)(2,1)S(1)}, bf16[16,512]{1,0:T(8,128)(2,1)S(1)}, u32[]{:S(2)}, u32[]{:S(2)}) collective-permute-start(bf16[16,512]{1,0:T(8,128)(2,1)S(1)} %get-tuple-element.133), channel_id=1, source_target_pairs={{0,2},{1,3},{2,0},{3,1},{4,6},{5,7},{6,4},{7,5},{8,10},{9,11},{10,... | collective-permute-start | bytes 49160 | tf_op jit(solution)/shard_map/ppermute | solution.py:350
  46.0 4.0 %collective-permute-start.20 = (bf16[144,512]{1,0:T(8,128)(2,1)S(1)}, bf16[144,512]{1,0:T(8,128)(2,1)S(1)}, u32[]{:S(2)}, u32[]{:S(2)}) collective-permute-start(bf16[144,512]{1,0:T(8,128)(2,1)S(1)} %get-tuple-element.129), channel_id=1, source_target_pairs={{0,1},{1,0},{2,3},{3,2},{4,5},{5,4},{6,7},{7,6},{8,9},{9,8},{10,11... | collective-permute-start | bytes 442376 | tf_op jit(solution)/shard_map/ppermute | solution.py:350
  50.8 5.6 %collective-permute-start.23 = (bf16[16,512]{1,0:T(8,128)(2,1)S(1)}, bf16[16,512]{1,0:T(8,128)(2,1)S(1)}, u32[]{:S(2)}, u32[]{:S(2)}) collective-permute-start(bf16[16,512]{1,0:T(8,128)(2,1)S(1)} %get-tuple-element.136), channel_id=1, source_target_pairs={{0,12},{1,13},{2,14},{3,15},{4,8},{5,9},{6,10},{7,11},{8,4},{9,5},... | collective-permute-start | bytes 49160 | tf_op jit(solution)/shard_map/ppermute | solution.py:350
  52.5 4.7 %collective-permute-start.24 = (bf16[16,512]{1,0:T(8,128)(2,1)S(1)}, bf16[16,512]{1,0:T(8,128)(2,1)S(1)}, u32[]{:S(2)}, u32[]{:S(2)}) collective-permute-start(bf16[16,512]{1,0:T(8,128)(2,1)S(1)} %get-tuple-element.137), channel_id=1, source_target_pairs={{0,8},{1,9},{2,10},{3,11},{4,12},{5,13},{6,14},{7,15},{8,0},{9,1},... | collective-permute-start | bytes 49160 | tf_op jit(solution)/shard_map/ppermute | solution.py:350
  52.7 4.5 %collective-permute-start.25 = (bf16[16,512]{1,0:T(8,128)(2,1)S(1)}, bf16[16,512]{1,0:T(8,128)(2,1)S(1)}, u32[]{:S(2)}, u32[]{:S(2)}) collective-permute-start(bf16[16,512]{1,0:T(8,128)(2,1)S(1)} %get-tuple-element.138), channel_id=1, source_target_pairs={{0,4},{1,5},{2,6},{3,7},{4,0},{5,1},{6,2},{7,3},{8,12},{9,13},{10,... | collective-permute-start | bytes 49160 | tf_op jit(solution)/shard_map/ppermute | solution.py:350
  55.3 6.7 %collective-permute-start.26 = (bf16[64,512]{1,0:T(8,128)(2,1)S(1)}, bf16[64,512]{1,0:T(8,128)(2,1)S(1)}, u32[]{:S(2)}, u32[]{:S(2)}) collective-permute-start(bf16[64,512]{1,0:T(8,128)(2,1)S(1)} %get-tuple-element.144), channel_id=1, source_target_pairs={{0,15},{1,2},{2,1},{3,4},{4,3},{5,6},{6,5},{7,8},{8,7},{9,10},{10,... | collective-permute-start | bytes 196616 | tf_op jit(solution)/shard_map/ppermute | solution.py:356
  57.4 4.5 %collective-permute-start.29 = (bf16[16,512]{1,0:T(8,128)(2,1)S(1)}, bf16[16,512]{1,0:T(8,128)(2,1)S(1)}, u32[]{:S(2)}, u32[]{:S(2)}) collective-permute-start(bf16[16,512]{1,0:T(8,128)(2,1)S(1)} %get-tuple-element.147), channel_id=1, source_target_pairs={{0,2},{1,3},{2,0},{3,1},{4,6},{5,7},{6,4},{7,5},{8,10},{9,11},{10,... | collective-permute-start | bytes 49160 | tf_op jit(solution)/shard_map/ppermute | solution.py:350
  62.7 6.5 %collective-permute-start.30 = (bf16[64,512]{1,0:T(8,128)(2,1)S(1)}, bf16[64,512]{1,0:T(8,128)(2,1)S(1)}, u32[]{:S(2)}, u32[]{:S(2)}) collective-permute-start(bf16[64,512]{1,0:T(8,128)(2,1)S(1)} %get-tuple-element.154), channel_id=1, source_target_pairs={{0,15},{1,2},{2,1},{3,4},{4,3},{5,6},{6,5},{7,8},{8,7},{9,10},{10,... | collective-permute-start | bytes 196616 | tf_op jit(solution)/shard_map/ppermute | solution.py:356
  64.8 4.4 %collective-permute-start.31 = (bf16[64,512]{1,0:T(8,128)(2,1)S(1)}, bf16[64,512]{1,0:T(8,128)(2,1)S(1)}, u32[]{:S(2)}, u32[]{:S(2)}) collective-permute-start(bf16[64,512]{1,0:T(8,128)(2,1)S(1)} %get-tuple-element.155), channel_id=1, source_target_pairs={{0,1},{1,0},{2,3},{3,2},{4,5},{5,4},{6,7},{7,6},{8,9},{9,8},{10,11... | collective-permute-start | bytes 196616 | tf_op jit(solution)/shard_map/ppermute | solution.py:350
  (20 other events, 68.9 us)

commit v11 on v10

--- a/solution.py
+++ b/solution.py
@@ -69,12 +69,12 @@
     return (x % PLANE) * (devices // PLANE) + x // PLANE
 
 
-def call(body, out_shapes, flops, *args, scalars=0, hbm=0, free=0, hbm_out=0, scratch=(), limit=VMEM_LIMIT):
+def call(body, out_shapes, flops, *args, hbm=0, free=0, hbm_out=0, scratch=(), limit=VMEM_LIMIT):
     shapes = [jax.ShapeDtypeStruct(s, t) for s, t in out_shapes]
     size = sum(a.size * a.dtype.itemsize for a in args)
     size += sum(s.size * s.dtype.itemsize for s in shapes)
     size *= hbm == 0
-    places = [pltpu.SMEM] * scalars + [pltpu.HBM] * hbm + [pltpu.VMEM] * (len(args) - scalars - hbm - free)
+    places = [pltpu.HBM] * hbm + [pltpu.VMEM] * (len(args) - hbm - free)
     places += [pl.ANY] * free
     out_places = [pltpu.HBM] * hbm_out + [pltpu.VMEM] * (len(shapes) - hbm_out)
     kept = len(args) - free
@@ -106,12 +106,13 @@
     return [pl.ds(i * step, step) for i in range(CHUNKS)]
 
 
-def grid_send(me, latent, lists, outer, inner, values, wanted, sems):
+def grid_send(latent, lists, outer, inner, values, wanted, sems):
+    me = lax.axis_index("dom")
     parts = row_chunks(latent.shape[0])
     sources = [lists] + [latent.at[part] for part in parts]
     copies = fetch(sources, [wanted] + [values.at[part] for part in parts], sems)
     copies[0].wait()
-    wanted_outer, wanted_inner = pair_order(wanted, me[0])
+    wanted_outer, wanted_inner = pair_order(wanted, me)
     step = latent.shape[0] // CHUNKS
     outer_rows = inner_rows = 0.0
     for i, part in enumerate(parts):
@@ -123,9 +124,10 @@
     inner[...] = inner_rows.astype(BF)
 
 
-def encoder_local(me, entries, weight, latent, mesh, near, grid_own_t, grid_rim_t, slope, *, size):
+def encoder_local(entries, weight, latent, mesh, near, grid_own_t, grid_rim_t, slope, *, size):
+    me = lax.axis_index("dom")
     rows = latent.shape[0]
-    columns = side_swap(entries[...], rows, size, me[0])
+    columns = side_swap(entries[...], rows, size, me)
     own = counts_t(rows, 0, columns)
     grid_own_t[...] = own
     grid_rim_t[...] = counts_t(2 * size, rows, columns)
@@ -138,7 +140,7 @@
     rows = send.shape[0]
     size = lists.shape[2]
     cap, devices = far_lists.shape
-    outer, inner = pair_order(lists, me[0])
+    outer, inner = pair_order(lists, me)
     rim = [pick(rows, outer), pick(rows, inner)]
     for k in range(2):
         send[:, k * size : (k + 1) * size] = rim[k]
@@ -146,7 +148,7 @@
     partner = lax.broadcasted_iota(jnp.int32, (devices, devices * cap), 0)
     place = lax.broadcasted_iota(jnp.int32, (devices, devices * cap), 1)
     if devices == STAGED:
-        x = partner ^ me[0]
+        x = partner ^ me
         send_place, receive_place = x * cap, by_stage(x, devices) * cap
     else:
         send_place, receive_place = partner * cap, partner * cap
@@ -164,7 +166,7 @@
     rows = own_t.shape[0]
     slots = forth_t.shape[0] - 2 * size
     cap = slots // devices
-    columns = side_swap(entries[...], rows, size, me[0])
+    columns = side_swap(entries[...], rows, size, me)
     own_t[...] = counts_t(rows, 0, columns)
     rim = counts_t(2 * size, rows, columns)
     forth_t[: 2 * size] = rim
@@ -172,7 +174,7 @@
     far = jnp.maximum(columns - rows - 2 * size, 0)
     partner, slot = far // cap, far % cap
     if devices == STAGED:
-        partner = partner ^ me[0]
+        partner = partner ^ me
         send_place, receive_place = partner * cap + slot, by_stage(partner, devices) * cap + slot
     else:
         send_place, receive_place = far, far
@@ -181,10 +183,11 @@
     back_t[2 * size :] = counts_t(slots, 0, jnp.where(is_far, send_place, -1))
 
 
-def decoder_back(me, entries, cotangent, own_t, rim_t, near, outer, inner):
+def decoder_back(entries, cotangent, own_t, rim_t, near, outer, inner):
+    me = lax.axis_index("dom")
     rows = near.shape[0]
     size = outer.shape[0]
-    columns = side_swap(entries[...], rows, size, me[0])
+    columns = side_swap(entries[...], rows, size, me)
     own = counts_t(rows, 0, columns)
     side = counts_t(2 * size, rows, columns)
     own_t[...] = own
@@ -239,7 +242,8 @@
         outs[k][...] = moved[k * block : (k + 1) * block]
 
 
-def tables(me, entries, lists, far_lists, own_t, forth_t, back_t, send, receive, *, size, devices):
+def tables(entries, lists, far_lists, own_t, forth_t, back_t, send, receive, *, size, devices):
+    me = lax.axis_index("dom")
     mesh_tables(me, entries, own_t, forth_t, back_t, size, devices)
     list_tables(me, lists, far_lists, send, receive)
 
@@ -273,7 +277,7 @@
     emit(refs[ins + 1 :], chosen_messages(send, state, weight[layer]), size, (outer_extra[...], inner_extra[...]))
 
 
-def turn(near, forth_t, weight, send, receive, back_t, back_near, *refs, ins, scale, size):
+def turn(near, forth_t, weight, receive, back_t, back_near, *refs, ins, scale, size):
     rows = arrived(refs[:ins], size)
     message, grad = refs[ins : ins + 2]
     state = (near[...] + scale * t_mm(forth_t[...], rows)).astype(BF)
@@ -284,8 +288,14 @@
     back = back_near[...] + mm(receive[:, : 2 * size], returned)
     change = mm_t((back * gradient).astype(BF), weight[...]).astype(BF)
     grad[...] = change
-    rim = t_mm(send[:, : 2 * size], value).astype(BF)
-    emit(refs[ins + 2 :], mm(back_t[...], change), size, (rim[:size], rim[size:]))
+    emit(refs[ins + 2 :], mm(back_t[...], change), size)
+
+
+def rim_messages(send, message, outer, inner):
+    size = outer.shape[0]
+    rows = t_mm(send[:, : 2 * size], message[...]).astype(BF)
+    outer[...] = rows[:size]
+    inner[...] = rows[size:]
 
 
 def layer_back(near, receive, rows, slope, weight, grad, scale):
@@ -315,18 +325,17 @@
     base[...] = latent[...].astype(F32) + t_mm(own_t[...], message[...])
 
 
-def decode_rim(base, rim_t, outer_in, inner_in, output, token):
-    size = outer_in.shape[0] // 2
-    incoming = jnp.concatenate([outer_in[size:], inner_in[size : 2 * size]], axis=0)
+def decode_rim(base, rim_t, outer_in, inner_in, output):
+    incoming = jnp.concatenate([outer_in[...], inner_in[...]], axis=0)
     output[...] = (base[...] + t_mm(rim_t[...], incoming)).astype(BF)
-    token[...] = jnp.zeros(token.shape, F32)
-
-
-def grid_local(me, own_t, grad, lists, slope, weight, cotangent, base, table, slope_rows, mesh_grad):
+
+
+def grid_local(own_t, grad, lists, slope, weight, cotangent, base, table, slope_rows, mesh_grad):
+    me = lax.axis_index("dom")
     mesh_grad[...] = grad[...]
     rows = own_t.shape[0]
     size = lists.shape[2]
-    for k, wanted in enumerate(pair_order(lists, me[0])):
+    for k, wanted in enumerate(pair_order(lists, me)):
         table[:, k * size : (k + 1) * size] = pick(rows, wanted)
     slope_rows[...] = t_mm(table[...], slope[...])
     change = (mm(own_t[...], grad[...]) * slope[...].astype(F32)).astype(BF)
@@ -356,7 +365,7 @@
     return lax.ppermute(value, "dom", pairs)
 
 
-def exchange(outs, cap):
+def exchange(outs, cap, after=()):
     width = outs[0].shape[1]
     if len(outs) == 3:
         outer, inner, far = outs
@@ -373,7 +382,8 @@
         shuffle,
         [((block, width), BF), ((inner.shape[0] + block, width), BF), ((block, width), BF), ((block, width), BF)],
         2 * (STAGED * cap) ** 2 * width,
-        inner, own, *moved,
+        inner, own, *moved, *after,
+        free=len(after),
     )
     return [outer_in, toggle(blocks[1], 1), toggle(blocks[3], 3), toggle(blocks[2], 2), blocks[0]]
 
@@ -401,7 +411,6 @@
     slots = devices * cap
     listed = 2 * halo + slots
     scale = 1.0 / mesh_neighbours.shape[1]
-    me = lax.axis_index("dom").astype(jnp.int32).reshape(1)
 
     def square(rows, depth):
         return 2 * rows * depth * width
@@ -420,8 +429,8 @@
         grid_send,
         [grid_rim, grid_rim],
         64 * square(grid_rows, width),
-        me, grid_latent, grid_halo_rows,
-        scalars=1, hbm=2, limit=60 * 1024 * 1024,
+        grid_latent, grid_halo_rows,
+        hbm=2, limit=60 * 1024 * 1024,
         scratch=copies_of([grid_latent, grid_halo_rows]) + [pltpu.SemaphoreType.DMA((CHUNKS + 1,))],
     )
     outer_in, inner_in = across(outer), toggle(inner, 1)
@@ -430,16 +439,14 @@
         functools.partial(tables, size=halo, devices=devices),
         [((mesh_rows, mesh_rows), BF)] + [((listed, mesh_rows), BF)] * 2 + [((mesh_rows, listed), BF)] * 2,
         64 * square(mesh_rows, mesh_rows),
-        me, mesh_neighbours.T, halo_rows, far_sources[0].T,
-        scalars=1,
+        mesh_neighbours.T, halo_rows, far_sources[0].T,
     )
     _, latent, weight, mesh = lax.optimization_barrier((inner, grid_latent, encoder_weight, mesh_latent))
     near, grid_own_t, grid_rim_t, grid_slope = call(
         functools.partial(encoder_local, size=ghalo),
         [total, ((grid_rows, mesh_rows), BF), ((2 * ghalo, mesh_rows), BF), ((grid_rows, width), BF)],
         4 * square(grid_rows, width),
-        me, encoder_neighbours.T, weight, latent, mesh,
-        scalars=1,
+        encoder_neighbours.T, weight, latent, mesh,
     )
 
     hidden, *outs = call(
@@ -460,8 +467,8 @@
         decoder_back,
         [((mesh_rows, grid_rows), BF), ((2 * halo, grid_rows), BF), total, rim, rim],
         square(grid_rows, mesh_rows),
-        me, decoder_neighbours.T, cotangent, ins[-1],
-        scalars=1, free=1,
+        decoder_neighbours.T, cotangent, ins[-1],
+        free=1,
     )
 
     hidden, *outs = call(
@@ -481,16 +488,26 @@
 
     message, grad, *outs = call(
         functools.partial(turn, ins=len(ins), scale=scale, size=halo),
-        [state, state] + sends(2 * halo),
+        [state, state] + sends(halo),
         2 * step,
-        near, forth_t, decoder_weight, send, receive, back_t, decoder_near, *ins,
+        near, forth_t, decoder_weight, receive, back_t, decoder_near, *ins,
     )
     ins = exchange(outs, cap)
     (near,) = call(back_local, [total], 6 * square(mesh_rows, mesh_rows), own_t, grad)
 
-    outer_decoder, inner_decoder = ins[:2]
+    outer, inner = call(rim_messages, [rim, rim], square(2 * halo, mesh_rows), send, message, ins[-1], free=1)
+    outer_decoder, inner_decoder = across(outer), toggle(inner, 1)
+    (near,) = call(back_local, [total], 3 * square(mesh_rows, mesh_rows), own_t, grad, ins[-1], free=1)
+
+    grad, *outs = call(
+        functools.partial(middle_back, ins=len(ins), layer=1, scale=scale, size=halo),
+        [state] + sends(halo),
+        step,
+        near, receive, slope_1, processor_weights, grad, back_t, *ins,
+    )
+    ins = exchange(outs, cap, [outer_decoder, inner_decoder])
     (near,) = call(back_local, [total], 6 * square(mesh_rows, mesh_rows), own_t, grad, ins[-1], free=1)
-    (base,) = call(
+    (decoded,) = call(
         decode_own,
         [((grid_rows, width), F32)],
         square(grid_rows, mesh_rows),
@@ -498,37 +515,26 @@
         free=1,
     )
 
-    grad, *outs = call(
-        functools.partial(middle_back, ins=len(ins), layer=1, scale=scale, size=halo),
-        [state] + sends(halo),
-        step,
-        near, receive, slope_1, processor_weights, grad, back_t, *ins, base,
-        free=1,
-    )
-    ins = exchange(outs, cap)
-    (near,) = call(back_local, [total], 6 * square(mesh_rows, mesh_rows), own_t, grad, ins[-1], free=1)
-    output, token = call(
-        decode_rim,
-        [((grid_rows, width), BF), ((8, 128), F32)],
-        square(grid_rows, 2 * halo),
-        base, decoder_rim_t, outer_decoder, inner_decoder, ins[-1],
-        free=1,
-    )
-
     grad, outer, inner = call(
         functools.partial(last_back, ins=len(ins), scale=scale),
         [state, grid_rim, grid_rim],
         step,
-        near, receive, slope_0, processor_weights, grad, grid_rim_t, *ins, token,
+        near, receive, slope_0, processor_weights, grad, grid_rim_t, *ins, decoded,
         free=1,
     )
     outer_in, inner_in = across(outer), toggle(inner, 1)
+    (output,) = call(
+        decode_rim,
+        [((grid_rows, width), BF)],
+        square(grid_rows, 2 * halo),
+        decoded, decoder_rim_t, outer_decoder, inner_decoder, grad,
+        free=1,
+    )
     base, table, slope_rows, mesh_grad = call(
         grid_local,
         [((grid_rows, width), F32), ((grid_rows, 2 * ghalo), BF), ((2 * ghalo, width), F32), state],
         square(mesh_rows, grid_rows) + square(grid_rows, width),
-        me, grid_own_t, grad, grid_halo_rows, grid_slope, encoder_weight, cotangent,
-        scalars=1,
+        grid_own_t, grad, grid_halo_rows, grid_slope, encoder_weight, cotangent,
     )
     (grid_grad,) = call(
         grid_back,

time: 70.9 us -> 71 us (level)
  waiting for transfers between devices: 10.3 us -> 7.1 us
  starting transfers between devices: 38.5 us -> 41.6 us
    ppermute x6 -> x7, starting transfers between devices: 13 us -> 16 us  [across(): return lax.ppermute(value, 'dom', pairs)]
    ppermute x26 -> x27, waiting for transfers between devices: 8.48 us -> 6.59 us  [toggle(): return lax.ppermute(value, 'dom', [(i, i ^ bits) for i in range(peers)])]
    ppermute x6 -> x7, waiting for transfers between devices: 1.85 us -> 0.5 us  [across(): return lax.ppermute(value, 'dom', pairs)]
    pallas_call x21 -> x22, Pallas kernels: 20.1 us -> 20.4 us  [call(): pl.pallas_call(inner, out_shape=shapes, in_specs=[pl.BlockSpec(memory_spa...]
    ppermute x26 -> x27, starting transfers between devices: 25.5 us -> 25.6 us  [toggle(): return lax.ppermute(value, 'dom', [(i, i ^ bits) for i in range(peers)])]
  transfers between devices with their start and end apart: 32 -> 34, of which waited for: 13 -> 12; matrix products, arithmetic and copies ran while one was open for 0% -> 0% of each run, Pallas kernels for 17% -> 18%
where the time goes in v11:
time: 71 us; the launch traced here: 70.8 us
  starting transfers between devices  41.6 us (59%)
  Pallas kernels  20.4 us (29%)
  waiting for transfers between devices  7.1 us (10%)
  between operations  0.99 us (1%)
  local copies, waits for them, and re-layouts  0.74 us (1%)
    ppermute x27, starting transfers between devices, toggle(): return lax.ppermute(value, 'dom', [(i, i ^ bits) for i in range(peers)])  25.6 us
    pallas_call x22, Pallas kernels, call(): pl.pallas_call(inner, out_shape=shapes, in_specs=[pl.BlockSpec(memory_spa...  20.4 us
    ppermute x7, starting transfers between devices, across(): return lax.ppermute(value, 'dom', pairs)  16 us
    ppermute x27, waiting for transfers between devices, toggle(): return lax.ppermute(value, 'dom', [(i, i ^ bits) for i in range(peers)])  6.59 us
  transfers between devices with their start and end apart: 34, of which 12 were waited for; matrix products, arithmetic and copies ran while one was open for 0% of the time, Pallas kernels for 18%

profile of v11, /device:TPU:0, one launch (start us, length us, event | category | flops | bytes accessed | tf_op | source)
XLA Modules:
  0.0 70.8 jit_solution(6940293754680762115)
XLA Ops:
  0.7 2.3 %shard_map.139 = (bf16[64,512]{1,0:T(8,128)(2,1)}, bf16[64,512]{1,0:T(8,128)(2,1)}) custom-call(bf16[1024,512]{1,0:T(8,128)(2,1)} %refs_0_.1, s32[1,2,64]{2,1,0:T(2,128)} %lists.5), custom_call_target="tpu_custom_call" | custom-call | flops 34359738368 | tf_op jit(solution)/shard_map/pallas_call | solution.py:82
  3.0 5.5 %collective-permute-start = (bf16[64,512]{1,0:T(8,128)(2,1)}, bf16[64,512]{1,0:T(8,128)(2,1)S(1)}, u32[]{:S(2)}, u32[]{:S(2)}) collective-permute-start(bf16[64,512]{1,0:T(8,128)(2,1)} %get-tuple-element.86), channel_id=1, source_target_pairs={{0,15},{1,2},{2,1},{3,4},{4,3},{5,6},{6,5},{7,8},{8,7},{9,10},{10,... | collective-permute-start | bytes 196616 | tf_op jit(solution)/shard_map/ppermute | solution.py:365
  10.0 1.9 %shard_map.140 = (f32[512,512]{1,0:T(8,128)S(1)}, bf16[1024,512]{1,0:T(8,128)(2,1)S(1)}, bf16[128,512]{1,0:T(8,128)(2,1)S(1)}, bf16[1024,512]{1,0:T(8,128)(2,1)S(1)}) custom-call(s32[4,512]{1,0:T(4,128)S(1)} %bitcast.8, bf16[512,512]{1,0:T(8,128)(2,1)S(1)} %copy-done.1, bf16[1024,512]{1,0:T(8,128)(2,1)S(1)} %copy-done.3, bf16[512,512]{1,0:T(8,128)(2,1)S(1)} %copy-done.5), custom_call_target="tpu_custom_call" | custom-call | flops 2147483648 | bytes 5382144 | tf_op jit(solution)/shard_map/pallas_call | solution.py:82
  12.9 1.3 %collective-permute-start.2 = (bf16[16,512]{1,0:T(8,128)(2,1)S(1)}, bf16[16,512]{1,0:T(8,128)(2,1)S(1)}, u32[]{:S(2)}, u32[]{:S(2)}) collective-permute-start(bf16[16,512]{1,0:T(8,128)(2,1)S(1)} %get-tuple-element.90), channel_id=1, source_target_pairs={{0,12},{1,13},{2,14},{3,15},{4,8},{5,9},{6,10},{7,11},{8,4},{9,5},... | collective-permute-start | bytes 49160 | tf_op jit(solution)/shard_map/ppermute | solution.py:359
  14.2 3.2 %collective-permute-start.4 = (bf16[16,512]{1,0:T(8,128)(2,1)S(1)}, bf16[16,512]{1,0:T(8,128)(2,1)S(1)}, u32[]{:S(2)}, u32[]{:S(2)}) collective-permute-start(bf16[16,512]{1,0:T(8,128)(2,1)S(1)} %get-tuple-element.92), channel_id=1, source_target_pairs={{0,4},{1,5},{2,6},{3,7},{4,0},{5,1},{6,2},{7,3},{8,12},{9,13},{10,... | collective-permute-start | bytes 49160 | tf_op jit(solution)/shard_map/ppermute | solution.py:359
  17.4 2.3 %collective-permute-start.5 = (bf16[64,512]{1,0:T(8,128)(2,1)S(1)}, bf16[64,512]{1,0:T(8,128)(2,1)S(1)}, u32[]{:S(2)}, u32[]{:S(2)}) collective-permute-start(bf16[64,512]{1,0:T(8,128)(2,1)S(1)} %get-tuple-element.101), channel_id=1, source_target_pairs={{0,15},{1,2},{2,1},{3,4},{4,3},{5,6},{6,5},{7,8},{8,7},{9,10},{10,... | collective-permute-start | bytes 196616 | tf_op jit(solution)/shard_map/ppermute | solution.py:365
  20.3 1.4 %collective-permute-start.6 = (bf16[80,512]{1,0:T(8,128)(2,1)S(1)}, bf16[80,512]{1,0:T(8,128)(2,1)S(1)}, u32[]{:S(2)}, u32[]{:S(2)}) collective-permute-start(bf16[80,512]{1,0:T(8,128)(2,1)S(1)} %get-tuple-element.102), channel_id=1, source_target_pairs={{0,1},{1,0},{2,3},{3,2},{4,5},{5,4},{6,7},{7,6},{8,9},{9,8},{10,11... | collective-permute-start | bytes 245768 | tf_op jit(solution)/shard_map/ppermute | solution.py:359
  24.9 2.3 %collective-permute-start.9 = (bf16[16,512]{1,0:T(8,128)(2,1)S(1)}, bf16[16,512]{1,0:T(8,128)(2,1)S(1)}, u32[]{:S(2)}, u32[]{:S(2)}) collective-permute-start(bf16[16,512]{1,0:T(8,128)(2,1)S(1)} %get-tuple-element.108), channel_id=1, source_target_pairs={{0,12},{1,13},{2,14},{3,15},{4,8},{5,9},{6,10},{7,11},{8,4},{9,5},... | collective-permute-start | bytes 49160 | tf_op jit(solution)/shard_map/ppermute | solution.py:359
  27.6 1.7 %collective-permute-start.11 = (bf16[16,512]{1,0:T(8,128)(2,1)S(1)}, bf16[16,512]{1,0:T(8,128)(2,1)S(1)}, u32[]{:S(2)}, u32[]{:S(2)}) collective-permute-start(bf16[16,512]{1,0:T(8,128)(2,1)S(1)} %get-tuple-element.110), channel_id=1, source_target_pairs={{0,4},{1,5},{2,6},{3,7},{4,0},{5,1},{6,2},{7,3},{8,12},{9,13},{10,... | collective-permute-start | bytes 49160 | tf_op jit(solution)/shard_map/ppermute | solution.py:359
  29.3 1.6 %collective-permute-start.12 = (bf16[128,512]{1,0:T(8,128)(2,1)S(1)}, bf16[128,512]{1,0:T(8,128)(2,1)S(1)}, u32[]{:S(2)}, u32[]{:S(2)}) collective-permute-start(bf16[128,512]{1,0:T(8,128)(2,1)S(1)} %get-tuple-element.116), channel_id=1, source_target_pairs={{0,15},{1,2},{2,1},{3,4},{4,3},{5,6},{6,5},{7,8},{8,7},{9,10},{10,... | collective-permute-start | bytes 393224 | tf_op jit(solution)/shard_map/ppermute | solution.py:365
  34.8 1.9 %collective-permute-done.14.refs_2_ = bf16[16,512]{1,0:T(8,128)(2,1)S(1)} collective-permute-done((bf16[16,512]{1,0:T(8,128)(2,1)S(1)}, bf16[16,512]{1,0:T(8,128)(2,1)S(1)}, u32[]{:S(2)}, u32[]{:S(2)}) %collective-permute-start.14) | collective-permute-done | bytes 16416 | tf_op jit(solution)/shard_map/ppermute | solution.py:359
  36.8 1.4 %shard_map.149 = (bf16[512,512]{1,0:T(8,128)(2,1)S(1)}, bf16[512,512]{1,0:T(8,128)(2,1)S(1)}, bf16[64,512]{1,0:T(8,128)(2,1)S(1)}, bf16[64,512]{1,0:T(8,128)(2,1...) custom-call(f32[512,512]{1,0:T(8,128)S(1)} %get-tuple-element.112.ne, ...), custom_call_target="tpu_custom_call" | custom-call | flops 1610612736 | bytes 4784128 | tf_op jit(solution)/shard_map/pallas_call | solution.py:82
  38.2 1.5 %collective-permute-start.16 = (bf16[16,512]{1,0:T(8,128)(2,1)S(1)}, bf16[16,512]{1,0:T(8,128)(2,1)S(1)}, u32[]{:S(2)}, u32[]{:S(2)}) collective-permute-start(bf16[16,512]{1,0:T(8,128)(2,1)S(1)} %get-tuple-element.124), channel_id=1, source_target_pairs={{0,12},{1,13},{2,14},{3,15},{4,8},{5,9},{6,10},{7,11},{8,4},{9,5},... | collective-permute-start | bytes 49160 | tf_op jit(solution)/shard_map/ppermute | solution.py:359
  40.0 2.7 %collective-permute-start.18 = (bf16[16,512]{1,0:T(8,128)(2,1)S(1)}, bf16[16,512]{1,0:T(8,128)(2,1)S(1)}, u32[]{:S(2)}, u32[]{:S(2)}) collective-permute-start(bf16[16,512]{1,0:T(8,128)(2,1)S(1)} %get-tuple-element.126), channel_id=1, source_target_pairs={{0,4},{1,5},{2,6},{3,7},{4,0},{5,1},{6,2},{7,3},{8,12},{9,13},{10,... | collective-permute-start | bytes 49160 | tf_op jit(solution)/shard_map/ppermute | solution.py:359
  44.8 1.2 %collective-permute-start.22 = (bf16[16,512]{1,0:T(8,128)(2,1)S(1)}, bf16[16,512]{1,0:T(8,128)(2,1)S(1)}, u32[]{:S(2)}, u32[]{:S(2)}) collective-permute-start(bf16[16,512]{1,0:T(8,128)(2,1)S(1)} %get-tuple-element.132), channel_id=1, source_target_pairs={{0,2},{1,3},{2,0},{3,1},{4,6},{5,7},{6,4},{7,5},{8,10},{9,11},{10,... | collective-permute-start | bytes 49160 | tf_op jit(solution)/shard_map/ppermute | solution.py:359
  46.9 2.9 %collective-permute-start.26 = (bf16[64,512]{1,0:T(8,128)(2,1)S(1)}, bf16[64,512]{1,0:T(8,128)(2,1)S(1)}, u32[]{:S(2)}, u32[]{:S(2)}) collective-permute-start(bf16[64,512]{1,0:T(8,128)(2,1)S(1)} %get-tuple-element.138), channel_id=1, source_target_pairs={{0,15},{1,2},{2,1},{3,4},{4,3},{5,6},{6,5},{7,8},{8,7},{9,10},{10,... | collective-permute-start | bytes 196616 | tf_op jit(solution)/shard_map/ppermute | solution.py:365
  51.1 1.4 %collective-permute-start.23 = (bf16[16,512]{1,0:T(8,128)(2,1)S(1)}, bf16[16,512]{1,0:T(8,128)(2,1)S(1)}, u32[]{:S(2)}, u32[]{:S(2)}) collective-permute-start(bf16[16,512]{1,0:T(8,128)(2,1)S(1)} %get-tuple-element.135), channel_id=1, source_target_pairs={{0,12},{1,13},{2,14},{3,15},{4,8},{5,9},{6,10},{7,11},{8,4},{9,5},... | collective-permute-start | bytes 49160 | tf_op jit(solution)/shard_map/ppermute | solution.py:359
  52.7 2.8 %collective-permute-start.25 = (bf16[16,512]{1,0:T(8,128)(2,1)S(1)}, bf16[16,512]{1,0:T(8,128)(2,1)S(1)}, u32[]{:S(2)}, u32[]{:S(2)}) collective-permute-start(bf16[16,512]{1,0:T(8,128)(2,1)S(1)} %get-tuple-element.137), channel_id=1, source_target_pairs={{0,4},{1,5},{2,6},{3,7},{4,0},{5,1},{6,2},{7,3},{8,12},{9,13},{10,... | collective-permute-start | bytes 49160 | tf_op jit(solution)/shard_map/ppermute | solution.py:359
  57.5 1.1 %collective-permute-start.31 = (bf16[16,512]{1,0:T(8,128)(2,1)S(1)}, bf16[16,512]{1,0:T(8,128)(2,1)S(1)}, u32[]{:S(2)}, u32[]{:S(2)}) collective-permute-start(bf16[16,512]{1,0:T(8,128)(2,1)S(1)} %get-tuple-element.147), channel_id=1, source_target_pairs={{0,2},{1,3},{2,0},{3,1},{4,6},{5,7},{6,4},{7,5},{8,10},{9,11},{10,... | collective-permute-start | bytes 49160 | tf_op jit(solution)/shard_map/ppermute | solution.py:359
  60.7 1.4 %collective-permute-done.31.refs_9_ = bf16[16,512]{1,0:T(8,128)(2,1)S(1)} collective-permute-done((bf16[16,512]{1,0:T(8,128)(2,1)S(1)}, bf16[16,512]{1,0:T(8,128)(2,1)S(1)}, u32[]{:S(2)}, u32[]{:S(2)}) %collective-permute-start.31) | collective-permute-done | bytes 16416 | tf_op jit(solution)/shard_map/ppermute | solution.py:359
  62.8 2.0 %collective-permute-start.32 = (bf16[64,512]{1,0:T(8,128)(2,1)S(1)}, bf16[64,512]{1,0:T(8,128)(2,1)S(1)}, u32[]{:S(2)}, u32[]{:S(2)}) collective-permute-start(bf16[64,512]{1,0:T(8,128)(2,1)S(1)} %get-tuple-element.154), channel_id=1, source_target_pairs={{0,15},{1,2},{2,1},{3,4},{4,3},{5,6},{6,5},{7,8},{8,7},{9,10},{10,... | collective-permute-start | bytes 196616 | tf_op jit(solution)/shard_map/ppermute | solution.py:365
  64.9 1.4 %shard_map.158 = bf16[1024,512]{1,0:T(8,128)(2,1)} custom-call(f32[1024,512]{1,0:T(8,128)S(1)} %shard_map.155.refs_11_.refs_0_, bf16[128,1024]{1,0:T(8,128)(2,1)S(1)} %get-tuple-element.141.refs_1_, bf16[64,512]{1,0:T(8,128)(2,1)S(1)} %collective-permute-done.26.refs_5_.refs_2_, bf16[64,512]{1,0:T(8,128)(2,1)S(1)} %collective-permute-done.27.refs_6_.refs_3_, ...), custom_call_target="tpu_custom_call" | custom-call | flops 134217728 | bytes 4063232 | tf_op jit(solution)/shard_map/pallas_call | solution.py:82
  66.3 2.5 %shard_map.159 = (f32[1024,512]{1,0:T(8,128)S(1)}, bf16[1024,128]{1,0:T(8,128)(2,1)S(1)}, f32[128,512]{1,0:T(8,128)S(1)}, bf16[512,512]{1,0:T(8,128)(2,1)}) custom-call(bf16[1024,512]{1,0:T(8,128)(2,1)S(1)} %get-tuple-element.149.own_t, bf16[512,512]{1,0:T(8,128)(2,1)S(1)} %get-tuple-element.148.refs_4_.grad, s32[1,2,64]{2,1,0:T(2,128)S(1)} %copy-done.4, ...), custom_call_target="tpu_custom_call" | custom-call | flops 1073741824 | bytes 7340544 | tf_op jit(solution)/shard_map/pallas_call | solution.py:82
  69.3 1.5 %shard_map.160 = bf16[1024,512]{1,0:T(8,128)(2,1)} custom-call(f32[1024,512]{1,0:T(8,128)S(1)} %get-tuple-element.151.base, bf16[1024,128]{1,0:T(8,128)(2,1)S(1)} %get-tuple-element.152.table, f32[128,512]{1,0:T(8,128)S(1)} %get-tuple-element.153.slope_rows, bf16[512,512]{1,0:T(8,128)(2,1)S(1)} %copy-done.1, ...), custom_call_target="tpu_custom_call" | custom-call | flops 268435456 | bytes 4325376 | tf_op jit(solution)/shard_map/pallas_call | solution.py:82
  (90 shorter events, 20.5 us)
Async XLA Ops:
  3.0 9.0 %collective-permute-start = (bf16[64,512]{1,0:T(8,128)(2,1)}, bf16[64,512]{1,0:T(8,128)(2,1)S(1)}, u32[]{:S(2)}, u32[]{:S(2)}) collective-permute-start(bf16[64,512]{1,0:T(8,128)(2,1)} %get-tuple-element.86), channel_id=1, source_target_pairs={{0,15},{1,2},{2,1},{3,4},{4,3},{5,6},{6,5},{7,8},{8,7},{9,10},{10,... | collective-permute-start | bytes 196616 | tf_op jit(solution)/shard_map/ppermute | solution.py:365
  12.9 6.7 %collective-permute-start.2 = (bf16[16,512]{1,0:T(8,128)(2,1)S(1)}, bf16[16,512]{1,0:T(8,128)(2,1)S(1)}, u32[]{:S(2)}, u32[]{:S(2)}) collective-permute-start(bf16[16,512]{1,0:T(8,128)(2,1)S(1)} %get-tuple-element.90), channel_id=1, source_target_pairs={{0,12},{1,13},{2,14},{3,15},{4,8},{5,9},{6,10},{7,11},{8,4},{9,5},... | collective-permute-start | bytes 49160 | tf_op jit(solution)/shard_map/ppermute | solution.py:359
  14.2 5.4 %collective-permute-start.3 = (bf16[16,512]{1,0:T(8,128)(2,1)S(1)}, bf16[16,512]{1,0:T(8,128)(2,1)S(1)}, u32[]{:S(2)}, u32[]{:S(2)}) collective-permute-start(bf16[16,512]{1,0:T(8,128)(2,1)S(1)} %get-tuple-element.91), channel_id=1, source_target_pairs={{0,8},{1,9},{2,10},{3,11},{4,12},{5,13},{6,14},{7,15},{8,0},{9,1},... | collective-permute-start | bytes 49160 | tf_op jit(solution)/shard_map/ppermute | solution.py:359
  14.2 5.4 %collective-permute-start.4 = (bf16[16,512]{1,0:T(8,128)(2,1)S(1)}, bf16[16,512]{1,0:T(8,128)(2,1)S(1)}, u32[]{:S(2)}, u32[]{:S(2)}) collective-permute-start(bf16[16,512]{1,0:T(8,128)(2,1)S(1)} %get-tuple-element.92), channel_id=1, source_target_pairs={{0,4},{1,5},{2,6},{3,7},{4,0},{5,1},{6,2},{7,3},{8,12},{9,13},{10,... | collective-permute-start | bytes 49160 | tf_op jit(solution)/shard_map/ppermute | solution.py:359
  17.4 6.7 %collective-permute-start.5 = (bf16[64,512]{1,0:T(8,128)(2,1)S(1)}, bf16[64,512]{1,0:T(8,128)(2,1)S(1)}, u32[]{:S(2)}, u32[]{:S(2)}) collective-permute-start(bf16[64,512]{1,0:T(8,128)(2,1)S(1)} %get-tuple-element.101), channel_id=1, source_target_pairs={{0,15},{1,2},{2,1},{3,4},{4,3},{5,6},{6,5},{7,8},{8,7},{9,10},{10,... | collective-permute-start | bytes 196616 | tf_op jit(solution)/shard_map/ppermute | solution.py:365
  24.9 6.0 %collective-permute-start.9 = (bf16[16,512]{1,0:T(8,128)(2,1)S(1)}, bf16[16,512]{1,0:T(8,128)(2,1)S(1)}, u32[]{:S(2)}, u32[]{:S(2)}) collective-permute-start(bf16[16,512]{1,0:T(8,128)(2,1)S(1)} %get-tuple-element.108), channel_id=1, source_target_pairs={{0,12},{1,13},{2,14},{3,15},{4,8},{5,9},{6,10},{7,11},{8,4},{9,5},... | collective-permute-start | bytes 49160 | tf_op jit(solution)/shard_map/ppermute | solution.py:359
  27.2 4.6 %collective-permute-start.10 = (bf16[16,512]{1,0:T(8,128)(2,1)S(1)}, bf16[16,512]{1,0:T(8,128)(2,1)S(1)}, u32[]{:S(2)}, u32[]{:S(2)}) collective-permute-start(bf16[16,512]{1,0:T(8,128)(2,1)S(1)} %get-tuple-element.109), channel_id=1, source_target_pairs={{0,8},{1,9},{2,10},{3,11},{4,12},{5,13},{6,14},{7,15},{8,0},{9,1},... | collective-permute-start | bytes 49160 | tf_op jit(solution)/shard_map/ppermute | solution.py:359
  29.3 7.5 %collective-permute-start.12 = (bf16[128,512]{1,0:T(8,128)(2,1)S(1)}, bf16[128,512]{1,0:T(8,128)(2,1)S(1)}, u32[]{:S(2)}, u32[]{:S(2)}) collective-permute-start(bf16[128,512]{1,0:T(8,128)(2,1)S(1)} %get-tuple-element.116), channel_id=1, source_target_pairs={{0,15},{1,2},{2,1},{3,4},{4,3},{5,6},{6,5},{7,8},{8,7},{9,10},{10,... | collective-permute-start | bytes 393224 | tf_op jit(solution)/shard_map/ppermute | solution.py:365
  32.0 4.7 %collective-permute-start.14 = (bf16[16,512]{1,0:T(8,128)(2,1)S(1)}, bf16[16,512]{1,0:T(8,128)(2,1)S(1)}, u32[]{:S(2)}, u32[]{:S(2)}) collective-permute-start(bf16[16,512]{1,0:T(8,128)(2,1)S(1)} %get-tuple-element.118), channel_id=1, source_target_pairs={{0,3},{1,2},{2,1},{3,0},{4,7},{5,6},{6,5},{7,4},{8,11},{9,10},{10,... | collective-permute-start | bytes 49160 | tf_op jit(solution)/shard_map/ppermute | solution.py:359
  32.0 4.8 %collective-permute-start.15 = (bf16[16,512]{1,0:T(8,128)(2,1)S(1)}, bf16[16,512]{1,0:T(8,128)(2,1)S(1)}, u32[]{:S(2)}, u32[]{:S(2)}) collective-permute-start(bf16[16,512]{1,0:T(8,128)(2,1)S(1)} %get-tuple-element.119), channel_id=1, source_target_pairs={{0,2},{1,3},{2,0},{3,1},{4,6},{5,7},{6,4},{7,5},{8,10},{9,11},{10,... | collective-permute-start | bytes 49160 | tf_op jit(solution)/shard_map/ppermute | solution.py:359
  38.2 5.6 %collective-permute-start.16 = (bf16[16,512]{1,0:T(8,128)(2,1)S(1)}, bf16[16,512]{1,0:T(8,128)(2,1)S(1)}, u32[]{:S(2)}, u32[]{:S(2)}) collective-permute-start(bf16[16,512]{1,0:T(8,128)(2,1)S(1)} %get-tuple-element.124), channel_id=1, source_target_pairs={{0,12},{1,13},{2,14},{3,15},{4,8},{5,9},{6,10},{7,11},{8,4},{9,5},... | collective-permute-start | bytes 49160 | tf_op jit(solution)/shard_map/ppermute | solution.py:359
  39.7 4.7 %collective-permute-start.17 = (bf16[16,512]{1,0:T(8,128)(2,1)S(1)}, bf16[16,512]{1,0:T(8,128)(2,1)S(1)}, u32[]{:S(2)}, u32[]{:S(2)}) collective-permute-start(bf16[16,512]{1,0:T(8,128)(2,1)S(1)} %get-tuple-element.125), channel_id=1, source_target_pairs={{0,8},{1,9},{2,10},{3,11},{4,12},{5,13},{6,14},{7,15},{8,0},{9,1},... | collective-permute-start | bytes 49160 | tf_op jit(solution)/shard_map/ppermute | solution.py:359
  40.0 4.5 %collective-permute-start.18 = (bf16[16,512]{1,0:T(8,128)(2,1)S(1)}, bf16[16,512]{1,0:T(8,128)(2,1)S(1)}, u32[]{:S(2)}, u32[]{:S(2)}) collective-permute-start(bf16[16,512]{1,0:T(8,128)(2,1)S(1)} %get-tuple-element.126), channel_id=1, source_target_pairs={{0,4},{1,5},{2,6},{3,7},{4,0},{5,1},{6,2},{7,3},{8,12},{9,13},{10,... | collective-permute-start | bytes 49160 | tf_op jit(solution)/shard_map/ppermute | solution.py:359
  42.6 7.7 %collective-permute-start.19 = (bf16[64,512]{1,0:T(8,128)(2,1)S(1)}, bf16[64,512]{1,0:T(8,128)(2,1)S(1)}, u32[]{:S(2)}, u32[]{:S(2)}) collective-permute-start(bf16[64,512]{1,0:T(8,128)(2,1)S(1)} %get-tuple-element.129), channel_id=1, source_target_pairs={{0,15},{1,2},{2,1},{3,4},{4,3},{5,6},{6,5},{7,8},{8,7},{9,10},{10,... | collective-permute-start | bytes 196616 | tf_op jit(solution)/shard_map/ppermute | solution.py:365
  44.7 5.5 %collective-permute-start.21 = (bf16[16,512]{1,0:T(8,128)(2,1)S(1)}, bf16[16,512]{1,0:T(8,128)(2,1)S(1)}, u32[]{:S(2)}, u32[]{:S(2)}) collective-permute-start(bf16[16,512]{1,0:T(8,128)(2,1)S(1)} %get-tuple-element.131), channel_id=1, source_target_pairs={{0,3},{1,2},{2,1},{3,0},{4,7},{5,6},{6,5},{7,4},{8,11},{9,10},{10,... | collective-permute-start | bytes 49160 | tf_op jit(solution)/shard_map/ppermute | solution.py:359
  44.8 5.5 %collective-permute-start.22 = (bf16[16,512]{1,0:T(8,128)(2,1)S(1)}, bf16[16,512]{1,0:T(8,128)(2,1)S(1)}, u32[]{:S(2)}, u32[]{:S(2)}) collective-permute-start(bf16[16,512]{1,0:T(8,128)(2,1)S(1)} %get-tuple-element.132), channel_id=1, source_target_pairs={{0,2},{1,3},{2,0},{3,1},{4,6},{5,7},{6,4},{7,5},{8,10},{9,11},{10,... | collective-permute-start | bytes 49160 | tf_op jit(solution)/shard_map/ppermute | solution.py:359
  46.9 8.7 %collective-permute-start.26 = (bf16[64,512]{1,0:T(8,128)(2,1)S(1)}, bf16[64,512]{1,0:T(8,128)(2,1)S(1)}, u32[]{:S(2)}, u32[]{:S(2)}) collective-permute-start(bf16[64,512]{1,0:T(8,128)(2,1)S(1)} %get-tuple-element.138), channel_id=1, source_target_pairs={{0,15},{1,2},{2,1},{3,4},{4,3},{5,6},{6,5},{7,8},{8,7},{9,10},{10,... | collective-permute-start | bytes 196616 | tf_op jit(solution)/shard_map/ppermute | solution.py:365
  50.2 6.1 %collective-permute-start.27 = (bf16[64,512]{1,0:T(8,128)(2,1)S(1)}, bf16[64,512]{1,0:T(8,128)(2,1)S(1)}, u32[]{:S(2)}, u32[]{:S(2)}) collective-permute-start(bf16[64,512]{1,0:T(8,128)(2,1)S(1)} %get-tuple-element.139), channel_id=1, source_target_pairs={{0,1},{1,0},{2,3},{3,2},{4,5},{5,4},{6,7},{7,6},{8,9},{9,8},{10,11... | collective-permute-start | bytes 196616 | tf_op jit(solution)/shard_map/ppermute | solution.py:359
  51.1 5.6 %collective-permute-start.23 = (bf16[16,512]{1,0:T(8,128)(2,1)S(1)}, bf16[16,512]{1,0:T(8,128)(2,1)S(1)}, u32[]{:S(2)}, u32[]{:S(2)}) collective-permute-start(bf16[16,512]{1,0:T(8,128)(2,1)S(1)} %get-tuple-element.135), channel_id=1, source_target_pairs={{0,12},{1,13},{2,14},{3,15},{4,8},{5,9},{6,10},{7,11},{8,4},{9,5},... | collective-permute-start | bytes 49160 | tf_op jit(solution)/shard_map/ppermute | solution.py:359
  52.5 4.6 %collective-permute-start.24 = (bf16[16,512]{1,0:T(8,128)(2,1)S(1)}, bf16[16,512]{1,0:T(8,128)(2,1)S(1)}, u32[]{:S(2)}, u32[]{:S(2)}) collective-permute-start(bf16[16,512]{1,0:T(8,128)(2,1)S(1)} %get-tuple-element.136), channel_id=1, source_target_pairs={{0,8},{1,9},{2,10},{3,11},{4,12},{5,13},{6,14},{7,15},{8,0},{9,1},... | collective-permute-start | bytes 49160 | tf_op jit(solution)/shard_map/ppermute | solution.py:359
  52.7 4.6 %collective-permute-start.25 = (bf16[16,512]{1,0:T(8,128)(2,1)S(1)}, bf16[16,512]{1,0:T(8,128)(2,1)S(1)}, u32[]{:S(2)}, u32[]{:S(2)}) collective-permute-start(bf16[16,512]{1,0:T(8,128)(2,1)S(1)} %get-tuple-element.137), channel_id=1, source_target_pairs={{0,4},{1,5},{2,6},{3,7},{4,0},{5,1},{6,2},{7,3},{8,12},{9,13},{10,... | collective-permute-start | bytes 49160 | tf_op jit(solution)/shard_map/ppermute | solution.py:359
  55.6 6.5 %collective-permute-start.28 = (bf16[64,512]{1,0:T(8,128)(2,1)S(1)}, bf16[64,512]{1,0:T(8,128)(2,1)S(1)}, u32[]{:S(2)}, u32[]{:S(2)}) collective-permute-start(bf16[64,512]{1,0:T(8,128)(2,1)S(1)} %get-tuple-element.144), channel_id=1, source_target_pairs={{0,15},{1,2},{2,1},{3,4},{4,3},{5,6},{6,5},{7,8},{8,7},{9,10},{10,... | collective-permute-start | bytes 196616 | tf_op jit(solution)/shard_map/ppermute | solution.py:365
  57.5 4.6 %collective-permute-start.31 = (bf16[16,512]{1,0:T(8,128)(2,1)S(1)}, bf16[16,512]{1,0:T(8,128)(2,1)S(1)}, u32[]{:S(2)}, u32[]{:S(2)}) collective-permute-start(bf16[16,512]{1,0:T(8,128)(2,1)S(1)} %get-tuple-element.147), channel_id=1, source_target_pairs={{0,2},{1,3},{2,0},{3,1},{4,6},{5,7},{6,4},{7,5},{8,10},{9,11},{10,... | collective-permute-start | bytes 49160 | tf_op jit(solution)/shard_map/ppermute | solution.py:359
  62.8 6.5 %collective-permute-start.32 = (bf16[64,512]{1,0:T(8,128)(2,1)S(1)}, bf16[64,512]{1,0:T(8,128)(2,1)S(1)}, u32[]{:S(2)}, u32[]{:S(2)}) collective-permute-start(bf16[64,512]{1,0:T(8,128)(2,1)S(1)} %get-tuple-element.154), channel_id=1, source_target_pairs={{0,15},{1,2},{2,1},{3,4},{4,3},{5,6},{6,5},{7,8},{8,7},{9,10},{10,... | collective-permute-start | bytes 196616 | tf_op jit(solution)/shard_map/ppermute | solution.py:365
  (22 other events, 78.4 us)

commit v12 on v10

--- a/solution.py
+++ b/solution.py
@@ -10,6 +10,7 @@
 BF = jnp.bfloat16
 F32 = jnp.float32
 VMEM_LIMIT = 24 * 1024 * 1024
+FIRST_LIMIT = 60 * 1024 * 1024
 PLANE = 4
 STAGED = 16
 CHUNKS = 4
@@ -69,12 +70,12 @@
     return (x % PLANE) * (devices // PLANE) + x // PLANE
 
 
-def call(body, out_shapes, flops, *args, scalars=0, hbm=0, free=0, hbm_out=0, scratch=(), limit=VMEM_LIMIT):
+def call(body, out_shapes, flops, *args, hbm=0, free=0, hbm_out=0, scratch=(), limit=VMEM_LIMIT):
     shapes = [jax.ShapeDtypeStruct(s, t) for s, t in out_shapes]
     size = sum(a.size * a.dtype.itemsize for a in args)
     size += sum(s.size * s.dtype.itemsize for s in shapes)
     size *= hbm == 0
-    places = [pltpu.SMEM] * scalars + [pltpu.HBM] * hbm + [pltpu.VMEM] * (len(args) - scalars - hbm - free)
+    places = [pltpu.HBM] * hbm + [pltpu.VMEM] * (len(args) - hbm - free)
     places += [pl.ANY] * free
     out_places = [pltpu.HBM] * hbm_out + [pltpu.VMEM] * (len(shapes) - hbm_out)
     kept = len(args) - free
@@ -106,26 +107,28 @@
     return [pl.ds(i * step, step) for i in range(CHUNKS)]
 
 
-def grid_send(me, latent, lists, outer, inner, values, wanted, sems):
+def grid_send(latent, lists, outer, inner, values, wanted, rows, sems):
     parts = row_chunks(latent.shape[0])
-    sources = [lists] + [latent.at[part] for part in parts]
-    copies = fetch(sources, [wanted] + [values.at[part] for part in parts], sems)
+    copies = fetch([lists] + [latent.at[part] for part in parts], [wanted] + [values.at[part] for part in parts], sems)
+    size = outer.shape[0]
+    step = latent.shape[0] // CHUNKS
     copies[0].wait()
-    wanted_outer, wanted_inner = pair_order(wanted, me[0])
-    step = latent.shape[0] // CHUNKS
-    outer_rows = inner_rows = 0.0
+    listed = jnp.concatenate(pair_order(wanted, lax.axis_index("dom")), axis=1)
+    chosen = pick(latent.shape[0], listed)
+    total = 0.0
     for i, part in enumerate(parts):
         copies[i + 1].wait()
-        chunk = values[part]
-        outer_rows += t_mm(pick(step, wanted_outer - i * step), chunk)
-        inner_rows += t_mm(pick(step, wanted_inner - i * step), chunk)
-    outer[...] = outer_rows.astype(BF)
-    inner[...] = inner_rows.astype(BF)
-
-
-def encoder_local(me, entries, weight, latent, mesh, near, grid_own_t, grid_rim_t, slope, *, size):
+        total += t_mm(chosen[i * step : (i + 1) * step], values[part])
+    rows[...] = total.astype(BF)
+    sides = [rows.at[pl.ds(0, size)], rows.at[pl.ds(size, size)]]
+    for copy in fetch(sides, [outer, inner], sems):
+        copy.wait()
+
+
+def encoder_local(entries, weight, latent, mesh, near, grid_own_t, grid_rim_t, slope, *, size):
+    me = lax.axis_index("dom")
     rows = latent.shape[0]
-    columns = side_swap(entries[...], rows, size, me[0])
+    columns = side_swap(entries[...], rows, size, me)
     own = counts_t(rows, 0, columns)
     grid_own_t[...] = own
     grid_rim_t[...] = counts_t(2 * size, rows, columns)
@@ -138,7 +141,7 @@
     rows = send.shape[0]
     size = lists.shape[2]
     cap, devices = far_lists.shape
-    outer, inner = pair_order(lists, me[0])
+    outer, inner = pair_order(lists, me)
     rim = [pick(rows, outer), pick(rows, inner)]
     for k in range(2):
         send[:, k * size : (k + 1) * size] = rim[k]
@@ -146,7 +149,7 @@
     partner = lax.broadcasted_iota(jnp.int32, (devices, devices * cap), 0)
     place = lax.broadcasted_iota(jnp.int32, (devices, devices * cap), 1)
     if devices == STAGED:
-        x = partner ^ me[0]
+        x = partner ^ me
         send_place, receive_place = x * cap, by_stage(x, devices) * cap
     else:
         send_place, receive_place = partner * cap, partner * cap
@@ -164,7 +167,7 @@
     rows = own_t.shape[0]
     slots = forth_t.shape[0] - 2 * size
     cap = slots // devices
-    columns = side_swap(entries[...], rows, size, me[0])
+    columns = side_swap(entries[...], rows, size, me)
     own_t[...] = counts_t(rows, 0, columns)
     rim = counts_t(2 * size, rows, columns)
     forth_t[: 2 * size] = rim
@@ -172,7 +175,7 @@
     far = jnp.maximum(columns - rows - 2 * size, 0)
     partner, slot = far // cap, far % cap
     if devices == STAGED:
-        partner = partner ^ me[0]
+        partner = partner ^ me
         send_place, receive_place = partner * cap + slot, by_stage(partner, devices) * cap + slot
     else:
         send_place, receive_place = far, far
@@ -181,10 +184,11 @@
     back_t[2 * size :] = counts_t(slots, 0, jnp.where(is_far, send_place, -1))
 
 
-def decoder_back(me, entries, cotangent, own_t, rim_t, near, outer, inner):
+def decoder_back(entries, cotangent, own_t, rim_t, near, outer, inner):
+    me = lax.axis_index("dom")
     rows = near.shape[0]
     size = outer.shape[0]
-    columns = side_swap(entries[...], rows, size, me[0])
+    columns = side_swap(entries[...], rows, size, me)
     own = counts_t(rows, 0, columns)
     side = counts_t(2 * size, rows, columns)
     own_t[...] = own
@@ -239,7 +243,8 @@
         outs[k][...] = moved[k * block : (k + 1) * block]
 
 
-def tables(me, entries, lists, far_lists, own_t, forth_t, back_t, send, receive, *, size, devices):
+def tables(entries, lists, far_lists, own_t, forth_t, back_t, send, receive, *, size, devices):
+    me = lax.axis_index("dom")
     mesh_tables(me, entries, own_t, forth_t, back_t, size, devices)
     list_tables(me, lists, far_lists, send, receive)
 
@@ -322,11 +327,12 @@
     token[...] = jnp.zeros(token.shape, F32)
 
 
-def grid_local(me, own_t, grad, lists, slope, weight, cotangent, base, table, slope_rows, mesh_grad):
+def grid_local(own_t, grad, lists, slope, weight, cotangent, base, table, slope_rows, mesh_grad):
+    me = lax.axis_index("dom")
     mesh_grad[...] = grad[...]
     rows = own_t.shape[0]
     size = lists.shape[2]
-    for k, wanted in enumerate(pair_order(lists, me[0])):
+    for k, wanted in enumerate(pair_order(lists, me)):
         table[:, k * size : (k + 1) * size] = pick(rows, wanted)
     slope_rows[...] = t_mm(table[...], slope[...])
     change = (mm(own_t[...], grad[...]) * slope[...].astype(F32)).astype(BF)
@@ -401,7 +407,6 @@
     slots = devices * cap
     listed = 2 * halo + slots
     scale = 1.0 / mesh_neighbours.shape[1]
-    me = lax.axis_index("dom").astype(jnp.int32).reshape(1)
 
     def square(rows, depth):
         return 2 * rows * depth * width
@@ -420,9 +425,10 @@
         grid_send,
         [grid_rim, grid_rim],
         64 * square(grid_rows, width),
-        me, grid_latent, grid_halo_rows,
-        scalars=1, hbm=2, limit=60 * 1024 * 1024,
-        scratch=copies_of([grid_latent, grid_halo_rows]) + [pltpu.SemaphoreType.DMA((CHUNKS + 1,))],
+        grid_latent, grid_halo_rows,
+        hbm=2, hbm_out=2, limit=FIRST_LIMIT,
+        scratch=copies_of([grid_latent, grid_halo_rows])
+        + [pltpu.VMEM((2 * ghalo, width), BF), pltpu.SemaphoreType.DMA((CHUNKS + 1,))],
     )
     outer_in, inner_in = across(outer), toggle(inner, 1)
 
@@ -430,16 +436,14 @@
         functools.partial(tables, size=halo, devices=devices),
         [((mesh_rows, mesh_rows), BF)] + [((listed, mesh_rows), BF)] * 2 + [((mesh_rows, listed), BF)] * 2,
         64 * square(mesh_rows, mesh_rows),
-        me, mesh_neighbours.T, halo_rows, far_sources[0].T,
-        scalars=1,
+        mesh_neighbours.T, halo_rows, far_sources[0].T,
     )
     _, latent, weight, mesh = lax.optimization_barrier((inner, grid_latent, encoder_weight, mesh_latent))
     near, grid_own_t, grid_rim_t, grid_slope = call(
         functools.partial(encoder_local, size=ghalo),
         [total, ((grid_rows, mesh_rows), BF), ((2 * ghalo, mesh_rows), BF), ((grid_rows, width), BF)],
         4 * square(grid_rows, width),
-        me, encoder_neighbours.T, weight, latent, mesh,
-        scalars=1,
+        encoder_neighbours.T, weight, latent, mesh,
     )
 
     hidden, *outs = call(
@@ -460,8 +464,8 @@
         decoder_back,
         [((mesh_rows, grid_rows), BF), ((2 * halo, grid_rows), BF), total, rim, rim],
         square(grid_rows, mesh_rows),
-        me, decoder_neighbours.T, cotangent, ins[-1],
-        scalars=1, free=1,
+        decoder_neighbours.T, cotangent, ins[-1],
+        free=1,
     )
 
     hidden, *outs = call(
@@ -527,8 +531,7 @@
         grid_local,
         [((grid_rows, width), F32), ((grid_rows, 2 * ghalo), BF), ((2 * ghalo, width), F32), state],
         square(mesh_rows, grid_rows) + square(grid_rows, width),
-        me, grid_own_t, grad, grid_halo_rows, grid_slope, encoder_weight, cotangent,
-        scalars=1,
+        grid_own_t, grad, grid_halo_rows, grid_slope, encoder_weight, cotangent,
     )
     (grid_grad,) = call(
         grid_back,

time: 70.9 us -> 70.8 us (level)
  no operation moved by 1% of the time
where the time goes in v12:
time: 70.8 us; the launch traced here: 70.5 us
  starting transfers between devices  38.5 us (54%)
  Pallas kernels  20 us (28%)
  waiting for transfers between devices  10.3 us (15%)
  between operations  0.94 us (1%)
  local copies, waits for them, and re-layouts  0.74 us (1%)
    ppermute x26, starting transfers between devices, toggle(): return lax.ppermute(value, 'dom', [(i, i ^ bits) for i in range(peers)])  25.5 us
    pallas_call x21, Pallas kernels, call(): pl.pallas_call(inner, out_shape=shapes, in_specs=[pl.BlockSpec(memory_spa...  20 us
    ppermute x6, starting transfers between devices, across(): return lax.ppermute(value, 'dom', pairs)  13 us
    ppermute x26, waiting for transfers between devices, toggle(): return lax.ppermute(value, 'dom', [(i, i ^ bits) for i in range(peers)])  8.5 us
    ppermute x6, waiting for transfers between devices, across(): return lax.ppermute(value, 'dom', pairs)  1.83 us
  transfers between devices with their start and end apart: 32, of which 13 were waited for; matrix products, arithmetic and copies ran while one was open for 0% of the time, Pallas kernels for 17%

profile of v12, /device:TPU:0, one launch (start us, length us, event | category | flops | bytes accessed | tf_op | source)
XLA Modules:
  0.0 70.5 jit_solution(17612501929721321724)
XLA Ops:
  0.7 2.2 %shard_map.139 = (bf16[64,512]{1,0:T(8,128)(2,1)}, bf16[64,512]{1,0:T(8,128)(2,1)}) custom-call(bf16[1024,512]{1,0:T(8,128)(2,1)} %refs_0_.1, s32[1,2,64]{2,1,0:T(2,128)} %lists.5), custom_call_target="tpu_custom_call" | custom-call | flops 34359738368 | tf_op jit(solution)/shard_map/pallas_call | solution.py:83
  2.9 5.5 %collective-permute-start = (bf16[64,512]{1,0:T(8,128)(2,1)}, bf16[64,512]{1,0:T(8,128)(2,1)S(1)}, u32[]{:S(2)}, u32[]{:S(2)}) collective-permute-start(bf16[64,512]{1,0:T(8,128)(2,1)} %get-tuple-element.86), channel_id=1, source_target_pairs={{0,15},{1,2},{2,1},{3,4},{4,3},{5,6},{6,5},{7,8},{8,7},{9,10},{10,... | collective-permute-start | bytes 196616 | tf_op jit(solution)/shard_map/ppermute | solution.py:362
  8.5 1.1 %shard_map.141 = (bf16[512,512]{1,0:T(8,128)(2,1)S(1)}, bf16[192,512]{1,0:T(8,128)(2,1)S(1)}, bf16[192,512]{1,0:T(8,128)(2,1)S(1)}, bf16[512,192]{1,0:T(8,128)(2,1)S(1)}, bf16[512,192]{1,0:T(8,128)(2,1)S(1)}) custom-call(s32[8,512]{1,0:T(8,128)S(1)} %bitcast.6, s32[1,2,64]{2,1,0:T(2,128)S(1)} %copy-done.11, s32[4,16]{1,0:T(4,128)S(1)} %bitcast.9), custom_call_target="tpu_custom_call" | custom-call | flops 17179869184 | bytes 1327872 | tf_op jit(solution)/shard_map/pallas_call | solution.py:83
  9.9 1.9 %shard_map.140 = (f32[512,512]{1,0:T(8,128)S(1)}, bf16[1024,512]{1,0:T(8,128)(2,1)S(1)}, bf16[128,512]{1,0:T(8,128)(2,1)S(1)}, bf16[1024,512]{1,0:T(8,128)(2,1)S(1)}) custom-call(s32[4,512]{1,0:T(4,128)S(1)} %bitcast.8, bf16[512,512]{1,0:T(8,128)(2,1)S(1)} %copy-done.1, bf16[1024,512]{1,0:T(8,128)(2,1)S(1)} %copy-done.3, bf16[512,512]{1,0:T(8,128)(2,1)S(1)} %copy-done.5), custom_call_target="tpu_custom_call" | custom-call | flops 2147483648 | bytes 5382144 | tf_op jit(solution)/shard_map/pallas_call | solution.py:83
  12.8 1.3 %collective-permute-start.2 = (bf16[16,512]{1,0:T(8,128)(2,1)S(1)}, bf16[16,512]{1,0:T(8,128)(2,1)S(1)}, u32[]{:S(2)}, u32[]{:S(2)}) collective-permute-start(bf16[16,512]{1,0:T(8,128)(2,1)S(1)} %get-tuple-element.90), channel_id=1, source_target_pairs={{0,12},{1,13},{2,14},{3,15},{4,8},{5,9},{6,10},{7,11},{8,4},{9,5},... | collective-permute-start | bytes 49160 | tf_op jit(solution)/shard_map/ppermute | solution.py:356
  14.1 3.2 %collective-permute-start.4 = (bf16[16,512]{1,0:T(8,128)(2,1)S(1)}, bf16[16,512]{1,0:T(8,128)(2,1)S(1)}, u32[]{:S(2)}, u32[]{:S(2)}) collective-permute-start(bf16[16,512]{1,0:T(8,128)(2,1)S(1)} %get-tuple-element.92), channel_id=1, source_target_pairs={{0,4},{1,5},{2,6},{3,7},{4,0},{5,1},{6,2},{7,3},{8,12},{9,13},{10,... | collective-permute-start | bytes 49160 | tf_op jit(solution)/shard_map/ppermute | solution.py:356
  17.3 2.3 %collective-permute-start.5 = (bf16[64,512]{1,0:T(8,128)(2,1)S(1)}, bf16[64,512]{1,0:T(8,128)(2,1)S(1)}, u32[]{:S(2)}, u32[]{:S(2)}) collective-permute-start(bf16[64,512]{1,0:T(8,128)(2,1)S(1)} %get-tuple-element.101), channel_id=1, source_target_pairs={{0,15},{1,2},{2,1},{3,4},{4,3},{5,6},{6,5},{7,8},{8,7},{9,10},{10,... | collective-permute-start | bytes 196616 | tf_op jit(solution)/shard_map/ppermute | solution.py:362
  20.2 1.4 %collective-permute-start.6 = (bf16[80,512]{1,0:T(8,128)(2,1)S(1)}, bf16[80,512]{1,0:T(8,128)(2,1)S(1)}, u32[]{:S(2)}, u32[]{:S(2)}) collective-permute-start(bf16[80,512]{1,0:T(8,128)(2,1)S(1)} %get-tuple-element.102), channel_id=1, source_target_pairs={{0,1},{1,0},{2,3},{3,2},{4,5},{5,4},{6,7},{7,6},{8,9},{9,8},{10,11... | collective-permute-start | bytes 245768 | tf_op jit(solution)/shard_map/ppermute | solution.py:356
  24.7 2.3 %collective-permute-start.9 = (bf16[16,512]{1,0:T(8,128)(2,1)S(1)}, bf16[16,512]{1,0:T(8,128)(2,1)S(1)}, u32[]{:S(2)}, u32[]{:S(2)}) collective-permute-start(bf16[16,512]{1,0:T(8,128)(2,1)S(1)} %get-tuple-element.108), channel_id=1, source_target_pairs={{0,12},{1,13},{2,14},{3,15},{4,8},{5,9},{6,10},{7,11},{8,4},{9,5},... | collective-permute-start | bytes 49160 | tf_op jit(solution)/shard_map/ppermute | solution.py:356
  27.5 1.7 %collective-permute-start.11 = (bf16[16,512]{1,0:T(8,128)(2,1)S(1)}, bf16[16,512]{1,0:T(8,128)(2,1)S(1)}, u32[]{:S(2)}, u32[]{:S(2)}) collective-permute-start(bf16[16,512]{1,0:T(8,128)(2,1)S(1)} %get-tuple-element.110), channel_id=1, source_target_pairs={{0,4},{1,5},{2,6},{3,7},{4,0},{5,1},{6,2},{7,3},{8,12},{9,13},{10,... | collective-permute-start | bytes 49160 | tf_op jit(solution)/shard_map/ppermute | solution.py:356
  29.2 1.6 %collective-permute-start.12 = (bf16[128,512]{1,0:T(8,128)(2,1)S(1)}, bf16[128,512]{1,0:T(8,128)(2,1)S(1)}, u32[]{:S(2)}, u32[]{:S(2)}) collective-permute-start(bf16[128,512]{1,0:T(8,128)(2,1)S(1)} %get-tuple-element.116), channel_id=1, source_target_pairs={{0,15},{1,2},{2,1},{3,4},{4,3},{5,6},{6,5},{7,8},{8,7},{9,10},{10,... | collective-permute-start | bytes 393224 | tf_op jit(solution)/shard_map/ppermute | solution.py:362
  34.7 1.9 %collective-permute-done.14.refs_2_ = bf16[16,512]{1,0:T(8,128)(2,1)S(1)} collective-permute-done((bf16[16,512]{1,0:T(8,128)(2,1)S(1)}, bf16[16,512]{1,0:T(8,128)(2,1)S(1)}, u32[]{:S(2)}, u32[]{:S(2)}) %collective-permute-start.14) | collective-permute-done | bytes 16416 | tf_op jit(solution)/shard_map/ppermute | solution.py:356
  36.7 1.3 %shard_map.149 = (bf16[512,512]{1,0:T(8,128)(2,1)S(1)}, bf16[512,512]{1,0:T(8,128)(2,1)S(1)}, bf16[128,512]{1,0:T(8,128)(2,1)S(1)}, bf16[128,512]{1,0:T(8,128)(2...) custom-call(f32[512,512]{1,0:T(8,128)S(1)} %get-tuple-element.112.ne, ...), custom_call_target="tpu_custom_call" | custom-call | flops 1610612736 | bytes 5111808 | tf_op jit(solution)/shard_map/pallas_call | solution.py:83
  38.1 1.5 %collective-permute-start.16 = (bf16[16,512]{1,0:T(8,128)(2,1)S(1)}, bf16[16,512]{1,0:T(8,128)(2,1)S(1)}, u32[]{:S(2)}, u32[]{:S(2)}) collective-permute-start(bf16[16,512]{1,0:T(8,128)(2,1)S(1)} %get-tuple-element.123), channel_id=1, source_target_pairs={{0,12},{1,13},{2,14},{3,15},{4,8},{5,9},{6,10},{7,11},{8,4},{9,5},... | collective-permute-start | bytes 49160 | tf_op jit(solution)/shard_map/ppermute | solution.py:356
  39.9 2.6 %collective-permute-start.18 = (bf16[16,512]{1,0:T(8,128)(2,1)S(1)}, bf16[16,512]{1,0:T(8,128)(2,1)S(1)}, u32[]{:S(2)}, u32[]{:S(2)}) collective-permute-start(bf16[16,512]{1,0:T(8,128)(2,1)S(1)} %get-tuple-element.125), channel_id=1, source_target_pairs={{0,4},{1,5},{2,6},{3,7},{4,0},{5,1},{6,2},{7,3},{8,12},{9,13},{10,... | collective-permute-start | bytes 49160 | tf_op jit(solution)/shard_map/ppermute | solution.py:356
  44.6 1.3 %collective-permute-start.22 = (bf16[16,512]{1,0:T(8,128)(2,1)S(1)}, bf16[16,512]{1,0:T(8,128)(2,1)S(1)}, u32[]{:S(2)}, u32[]{:S(2)}) collective-permute-start(bf16[16,512]{1,0:T(8,128)(2,1)S(1)} %get-tuple-element.133), channel_id=1, source_target_pairs={{0,2},{1,3},{2,0},{3,1},{4,6},{5,7},{6,4},{7,5},{8,10},{9,11},{10,... | collective-permute-start | bytes 49160 | tf_op jit(solution)/shard_map/ppermute | solution.py:356
  47.8 2.1 %collective-permute-done.22.refs_9_ = bf16[16,512]{1,0:T(8,128)(2,1)S(1)} collective-permute-done((bf16[16,512]{1,0:T(8,128)(2,1)S(1)}, bf16[16,512]{1,0:T(8,128)(2,1)S(1)}, u32[]{:S(2)}, u32[]{:S(2)}) %collective-permute-start.22) | collective-permute-done | bytes 16416 | tf_op jit(solution)/shard_map/ppermute | solution.py:356
  50.7 1.6 %collective-permute-start.23 = (bf16[16,512]{1,0:T(8,128)(2,1)S(1)}, bf16[16,512]{1,0:T(8,128)(2,1)S(1)}, u32[]{:S(2)}, u32[]{:S(2)}) collective-permute-start(bf16[16,512]{1,0:T(8,128)(2,1)S(1)} %get-tuple-element.136), channel_id=1, source_target_pairs={{0,12},{1,13},{2,14},{3,15},{4,8},{5,9},{6,10},{7,11},{8,4},{9,5},... | collective-permute-start | bytes 49160 | tf_op jit(solution)/shard_map/ppermute | solution.py:356
  52.6 2.6 %collective-permute-start.25 = (bf16[16,512]{1,0:T(8,128)(2,1)S(1)}, bf16[16,512]{1,0:T(8,128)(2,1)S(1)}, u32[]{:S(2)}, u32[]{:S(2)}) collective-permute-start(bf16[16,512]{1,0:T(8,128)(2,1)S(1)} %get-tuple-element.138), channel_id=1, source_target_pairs={{0,4},{1,5},{2,6},{3,7},{4,0},{5,1},{6,2},{7,3},{8,12},{9,13},{10,... | collective-permute-start | bytes 49160 | tf_op jit(solution)/shard_map/ppermute | solution.py:356
  59.6 1.4 %shard_map.155 = (bf16[1024,512]{1,0:T(8,128)(2,1)}, f32[8,128]{1,0:T(8,128)S(1)}) custom-call(f32[1024,512]{1,0:T(8,128)S(1)} %shard_map.151.refs_11_.refs_0_, bf16[128,1024]{1,0:T(8,128)(2,1)S(1)} %get-tuple-element.127.refs_1_, bf16[128,512]{1,0:T(8,128)(2,1)S(1)} %collective-permute-done.19.refs_6_.refs_2_, ...), custom_call_target="tpu_custom_call" | custom-call | flops 134217728 | bytes 3706880 | tf_op jit(solution)/shard_map/pallas_call | solution.py:83
  62.6 2.1 %collective-permute-start.30 = (bf16[64,512]{1,0:T(8,128)(2,1)S(1)}, bf16[64,512]{1,0:T(8,128)(2,1)S(1)}, u32[]{:S(2)}, u32[]{:S(2)}) collective-permute-start(bf16[64,512]{1,0:T(8,128)(2,1)S(1)} %get-tuple-element.154), channel_id=1, source_target_pairs={{0,15},{1,2},{2,1},{3,4},{4,3},{5,6},{6,5},{7,8},{8,7},{9,10},{10,... | collective-permute-start | bytes 196616 | tf_op jit(solution)/shard_map/ppermute | solution.py:362
  64.7 2.5 %shard_map.158 = (f32[1024,512]{1,0:T(8,128)S(1)}, bf16[1024,128]{1,0:T(8,128)(2,1)S(1)}, f32[128,512]{1,0:T(8,128)S(1)}, bf16[512,512]{1,0:T(8,128)(2,1)}) custom-call(bf16[1024,512]{1,0:T(8,128)(2,1)S(1)} %get-tuple-element.141.own_t, bf16[512,512]{1,0:T(8,128)(2,1)S(1)} %get-tuple-element.149.grad, s32[1,2,64]{2,1,0:T(2,128)S(1)} %copy-done.4, ...), custom_call_target="tpu_custom_call" | custom-call | flops 1073741824 | bytes 7340544 | tf_op jit(solution)/shard_map/pallas_call | solution.py:83
  67.2 1.8 %collective-permute-done.30.outer_in = bf16[64,512]{1,0:T(8,128)(2,1)S(1)} collective-permute-done((bf16[64,512]{1,0:T(8,128)(2,1)S(1)}, bf16[64,512]{1,0:T(8,128)(2,1)S(1)}, u32[]{:S(2)}, u32[]{:S(2)}) %collective-permute-start.30) | collective-permute-done | bytes 65568 | tf_op jit(solution)/shard_map/ppermute | solution.py:362
  69.0 1.5 %shard_map.159 = bf16[1024,512]{1,0:T(8,128)(2,1)} custom-call(f32[1024,512]{1,0:T(8,128)S(1)} %get-tuple-element.151.base, bf16[1024,128]{1,0:T(8,128)(2,1)S(1)} %get-tuple-element.152.table, f32[128,512]{1,0:T(8,128)S(1)} %get-tuple-element.153.slope_rows, bf16[512,512]{1,0:T(8,128)(2,1)S(1)} %copy-done.1, ...), custom_call_target="tpu_custom_call" | custom-call | flops 268435456 | bytes 4325376 | tf_op jit(solution)/shard_map/pallas_call | solution.py:83
  (85 shorter events, 20.8 us)
Async XLA Ops:
  2.9 9.0 %collective-permute-start = (bf16[64,512]{1,0:T(8,128)(2,1)}, bf16[64,512]{1,0:T(8,128)(2,1)S(1)}, u32[]{:S(2)}, u32[]{:S(2)}) collective-permute-start(bf16[64,512]{1,0:T(8,128)(2,1)} %get-tuple-element.86), channel_id=1, source_target_pairs={{0,15},{1,2},{2,1},{3,4},{4,3},{5,6},{6,5},{7,8},{8,7},{9,10},{10,... | collective-permute-start | bytes 196616 | tf_op jit(solution)/shard_map/ppermute | solution.py:362
  12.8 6.7 %collective-permute-start.2 = (bf16[16,512]{1,0:T(8,128)(2,1)S(1)}, bf16[16,512]{1,0:T(8,128)(2,1)S(1)}, u32[]{:S(2)}, u32[]{:S(2)}) collective-permute-start(bf16[16,512]{1,0:T(8,128)(2,1)S(1)} %get-tuple-element.90), channel_id=1, source_target_pairs={{0,12},{1,13},{2,14},{3,15},{4,8},{5,9},{6,10},{7,11},{8,4},{9,5},... | collective-permute-start | bytes 49160 | tf_op jit(solution)/shard_map/ppermute | solution.py:356
  14.1 5.4 %collective-permute-start.3 = (bf16[16,512]{1,0:T(8,128)(2,1)S(1)}, bf16[16,512]{1,0:T(8,128)(2,1)S(1)}, u32[]{:S(2)}, u32[]{:S(2)}) collective-permute-start(bf16[16,512]{1,0:T(8,128)(2,1)S(1)} %get-tuple-element.91), channel_id=1, source_target_pairs={{0,8},{1,9},{2,10},{3,11},{4,12},{5,13},{6,14},{7,15},{8,0},{9,1},... | collective-permute-start | bytes 49160 | tf_op jit(solution)/shard_map/ppermute | solution.py:356
  14.1 5.4 %collective-permute-start.4 = (bf16[16,512]{1,0:T(8,128)(2,1)S(1)}, bf16[16,512]{1,0:T(8,128)(2,1)S(1)}, u32[]{:S(2)}, u32[]{:S(2)}) collective-permute-start(bf16[16,512]{1,0:T(8,128)(2,1)S(1)} %get-tuple-element.92), channel_id=1, source_target_pairs={{0,4},{1,5},{2,6},{3,7},{4,0},{5,1},{6,2},{7,3},{8,12},{9,13},{10,... | collective-permute-start | bytes 49160 | tf_op jit(solution)/shard_map/ppermute | solution.py:356
  17.3 6.7 %collective-permute-start.5 = (bf16[64,512]{1,0:T(8,128)(2,1)S(1)}, bf16[64,512]{1,0:T(8,128)(2,1)S(1)}, u32[]{:S(2)}, u32[]{:S(2)}) collective-permute-start(bf16[64,512]{1,0:T(8,128)(2,1)S(1)} %get-tuple-element.101), channel_id=1, source_target_pairs={{0,15},{1,2},{2,1},{3,4},{4,3},{5,6},{6,5},{7,8},{8,7},{9,10},{10,... | collective-permute-start | bytes 196616 | tf_op jit(solution)/shard_map/ppermute | solution.py:362
  24.7 6.0 %collective-permute-start.9 = (bf16[16,512]{1,0:T(8,128)(2,1)S(1)}, bf16[16,512]{1,0:T(8,128)(2,1)S(1)}, u32[]{:S(2)}, u32[]{:S(2)}) collective-permute-start(bf16[16,512]{1,0:T(8,128)(2,1)S(1)} %get-tuple-element.108), channel_id=1, source_target_pairs={{0,12},{1,13},{2,14},{3,15},{4,8},{5,9},{6,10},{7,11},{8,4},{9,5},... | collective-permute-start | bytes 49160 | tf_op jit(solution)/shard_map/ppermute | solution.py:356
  27.1 4.6 %collective-permute-start.10 = (bf16[16,512]{1,0:T(8,128)(2,1)S(1)}, bf16[16,512]{1,0:T(8,128)(2,1)S(1)}, u32[]{:S(2)}, u32[]{:S(2)}) collective-permute-start(bf16[16,512]{1,0:T(8,128)(2,1)S(1)} %get-tuple-element.109), channel_id=1, source_target_pairs={{0,8},{1,9},{2,10},{3,11},{4,12},{5,13},{6,14},{7,15},{8,0},{9,1},... | collective-permute-start | bytes 49160 | tf_op jit(solution)/shard_map/ppermute | solution.py:356
  27.5 4.2 %collective-permute-start.11 = (bf16[16,512]{1,0:T(8,128)(2,1)S(1)}, bf16[16,512]{1,0:T(8,128)(2,1)S(1)}, u32[]{:S(2)}, u32[]{:S(2)}) collective-permute-start(bf16[16,512]{1,0:T(8,128)(2,1)S(1)} %get-tuple-element.110), channel_id=1, source_target_pairs={{0,4},{1,5},{2,6},{3,7},{4,0},{5,1},{6,2},{7,3},{8,12},{9,13},{10,... | collective-permute-start | bytes 49160 | tf_op jit(solution)/shard_map/ppermute | solution.py:356
  29.2 7.5 %collective-permute-start.12 = (bf16[128,512]{1,0:T(8,128)(2,1)S(1)}, bf16[128,512]{1,0:T(8,128)(2,1)S(1)}, u32[]{:S(2)}, u32[]{:S(2)}) collective-permute-start(bf16[128,512]{1,0:T(8,128)(2,1)S(1)} %get-tuple-element.116), channel_id=1, source_target_pairs={{0,15},{1,2},{2,1},{3,4},{4,3},{5,6},{6,5},{7,8},{8,7},{9,10},{10,... | collective-permute-start | bytes 393224 | tf_op jit(solution)/shard_map/ppermute | solution.py:362
  31.9 4.7 %collective-permute-start.14 = (bf16[16,512]{1,0:T(8,128)(2,1)S(1)}, bf16[16,512]{1,0:T(8,128)(2,1)S(1)}, u32[]{:S(2)}, u32[]{:S(2)}) collective-permute-start(bf16[16,512]{1,0:T(8,128)(2,1)S(1)} %get-tuple-element.118), channel_id=1, source_target_pairs={{0,3},{1,2},{2,1},{3,0},{4,7},{5,6},{6,5},{7,4},{8,11},{9,10},{10,... | collective-permute-start | bytes 49160 | tf_op jit(solution)/shard_map/ppermute | solution.py:356
  31.9 4.7 %collective-permute-start.15 = (bf16[16,512]{1,0:T(8,128)(2,1)S(1)}, bf16[16,512]{1,0:T(8,128)(2,1)S(1)}, u32[]{:S(2)}, u32[]{:S(2)}) collective-permute-start(bf16[16,512]{1,0:T(8,128)(2,1)S(1)} %get-tuple-element.119), channel_id=1, source_target_pairs={{0,2},{1,3},{2,0},{3,1},{4,6},{5,7},{6,4},{7,5},{8,10},{9,11},{10,... | collective-permute-start | bytes 49160 | tf_op jit(solution)/shard_map/ppermute | solution.py:356
  38.1 5.6 %collective-permute-start.16 = (bf16[16,512]{1,0:T(8,128)(2,1)S(1)}, bf16[16,512]{1,0:T(8,128)(2,1)S(1)}, u32[]{:S(2)}, u32[]{:S(2)}) collective-permute-start(bf16[16,512]{1,0:T(8,128)(2,1)S(1)} %get-tuple-element.123), channel_id=1, source_target_pairs={{0,12},{1,13},{2,14},{3,15},{4,8},{5,9},{6,10},{7,11},{8,4},{9,5},... | collective-permute-start | bytes 49160 | tf_op jit(solution)/shard_map/ppermute | solution.py:356
  39.6 4.7 %collective-permute-start.17 = (bf16[16,512]{1,0:T(8,128)(2,1)S(1)}, bf16[16,512]{1,0:T(8,128)(2,1)S(1)}, u32[]{:S(2)}, u32[]{:S(2)}) collective-permute-start(bf16[16,512]{1,0:T(8,128)(2,1)S(1)} %get-tuple-element.124), channel_id=1, source_target_pairs={{0,8},{1,9},{2,10},{3,11},{4,12},{5,13},{6,14},{7,15},{8,0},{9,1},... | collective-permute-start | bytes 49160 | tf_op jit(solution)/shard_map/ppermute | solution.py:356
  39.9 4.5 %collective-permute-start.18 = (bf16[16,512]{1,0:T(8,128)(2,1)S(1)}, bf16[16,512]{1,0:T(8,128)(2,1)S(1)}, u32[]{:S(2)}, u32[]{:S(2)}) collective-permute-start(bf16[16,512]{1,0:T(8,128)(2,1)S(1)} %get-tuple-element.125), channel_id=1, source_target_pairs={{0,4},{1,5},{2,6},{3,7},{4,0},{5,1},{6,2},{7,3},{8,12},{9,13},{10,... | collective-permute-start | bytes 49160 | tf_op jit(solution)/shard_map/ppermute | solution.py:356
  42.5 7.4 %collective-permute-start.19 = (bf16[128,512]{1,0:T(8,128)(2,1)S(1)}, bf16[128,512]{1,0:T(8,128)(2,1)S(1)}, u32[]{:S(2)}, u32[]{:S(2)}) collective-permute-start(bf16[128,512]{1,0:T(8,128)(2,1)S(1)} %get-tuple-element.128), channel_id=1, source_target_pairs={{0,15},{1,2},{2,1},{3,4},{4,3},{5,6},{6,5},{7,8},{8,7},{9,10},{10,... | collective-permute-start | bytes 393224 | tf_op jit(solution)/shard_map/ppermute | solution.py:362
  44.6 5.3 %collective-permute-start.22 = (bf16[16,512]{1,0:T(8,128)(2,1)S(1)}, bf16[16,512]{1,0:T(8,128)(2,1)S(1)}, u32[]{:S(2)}, u32[]{:S(2)}) collective-permute-start(bf16[16,512]{1,0:T(8,128)(2,1)S(1)} %get-tuple-element.133), channel_id=1, source_target_pairs={{0,2},{1,3},{2,0},{3,1},{4,6},{5,7},{6,4},{7,5},{8,10},{9,11},{10,... | collective-permute-start | bytes 49160 | tf_op jit(solution)/shard_map/ppermute | solution.py:356
  45.9 4.0 %collective-permute-start.20 = (bf16[144,512]{1,0:T(8,128)(2,1)S(1)}, bf16[144,512]{1,0:T(8,128)(2,1)S(1)}, u32[]{:S(2)}, u32[]{:S(2)}) collective-permute-start(bf16[144,512]{1,0:T(8,128)(2,1)S(1)} %get-tuple-element.129), channel_id=1, source_target_pairs={{0,1},{1,0},{2,3},{3,2},{4,5},{5,4},{6,7},{7,6},{8,9},{9,8},{10,11... | collective-permute-start | bytes 442376 | tf_op jit(solution)/shard_map/ppermute | solution.py:356
  50.7 5.6 %collective-permute-start.23 = (bf16[16,512]{1,0:T(8,128)(2,1)S(1)}, bf16[16,512]{1,0:T(8,128)(2,1)S(1)}, u32[]{:S(2)}, u32[]{:S(2)}) collective-permute-start(bf16[16,512]{1,0:T(8,128)(2,1)S(1)} %get-tuple-element.136), channel_id=1, source_target_pairs={{0,12},{1,13},{2,14},{3,15},{4,8},{5,9},{6,10},{7,11},{8,4},{9,5},... | collective-permute-start | bytes 49160 | tf_op jit(solution)/shard_map/ppermute | solution.py:356
  52.3 4.7 %collective-permute-start.24 = (bf16[16,512]{1,0:T(8,128)(2,1)S(1)}, bf16[16,512]{1,0:T(8,128)(2,1)S(1)}, u32[]{:S(2)}, u32[]{:S(2)}) collective-permute-start(bf16[16,512]{1,0:T(8,128)(2,1)S(1)} %get-tuple-element.137), channel_id=1, source_target_pairs={{0,8},{1,9},{2,10},{3,11},{4,12},{5,13},{6,14},{7,15},{8,0},{9,1},... | collective-permute-start | bytes 49160 | tf_op jit(solution)/shard_map/ppermute | solution.py:356
  52.6 4.5 %collective-permute-start.25 = (bf16[16,512]{1,0:T(8,128)(2,1)S(1)}, bf16[16,512]{1,0:T(8,128)(2,1)S(1)}, u32[]{:S(2)}, u32[]{:S(2)}) collective-permute-start(bf16[16,512]{1,0:T(8,128)(2,1)S(1)} %get-tuple-element.138), channel_id=1, source_target_pairs={{0,4},{1,5},{2,6},{3,7},{4,0},{5,1},{6,2},{7,3},{8,12},{9,13},{10,... | collective-permute-start | bytes 49160 | tf_op jit(solution)/shard_map/ppermute | solution.py:356
  55.2 6.7 %collective-permute-start.26 = (bf16[64,512]{1,0:T(8,128)(2,1)S(1)}, bf16[64,512]{1,0:T(8,128)(2,1)S(1)}, u32[]{:S(2)}, u32[]{:S(2)}) collective-permute-start(bf16[64,512]{1,0:T(8,128)(2,1)S(1)} %get-tuple-element.144), channel_id=1, source_target_pairs={{0,15},{1,2},{2,1},{3,4},{4,3},{5,6},{6,5},{7,8},{8,7},{9,10},{10,... | collective-permute-start | bytes 196616 | tf_op jit(solution)/shard_map/ppermute | solution.py:362
  57.3 4.5 %collective-permute-start.29 = (bf16[16,512]{1,0:T(8,128)(2,1)S(1)}, bf16[16,512]{1,0:T(8,128)(2,1)S(1)}, u32[]{:S(2)}, u32[]{:S(2)}) collective-permute-start(bf16[16,512]{1,0:T(8,128)(2,1)S(1)} %get-tuple-element.147), channel_id=1, source_target_pairs={{0,2},{1,3},{2,0},{3,1},{4,6},{5,7},{6,4},{7,5},{8,10},{9,11},{10,... | collective-permute-start | bytes 49160 | tf_op jit(solution)/shard_map/ppermute | solution.py:356
  62.6 6.5 %collective-permute-start.30 = (bf16[64,512]{1,0:T(8,128)(2,1)S(1)}, bf16[64,512]{1,0:T(8,128)(2,1)S(1)}, u32[]{:S(2)}, u32[]{:S(2)}) collective-permute-start(bf16[64,512]{1,0:T(8,128)(2,1)S(1)} %get-tuple-element.154), channel_id=1, source_target_pairs={{0,15},{1,2},{2,1},{3,4},{4,3},{5,6},{6,5},{7,8},{8,7},{9,10},{10,... | collective-permute-start | bytes 196616 | tf_op jit(solution)/shard_map/ppermute | solution.py:362
  64.7 4.4 %collective-permute-start.31 = (bf16[64,512]{1,0:T(8,128)(2,1)S(1)}, bf16[64,512]{1,0:T(8,128)(2,1)S(1)}, u32[]{:S(2)}, u32[]{:S(2)}) collective-permute-start(bf16[64,512]{1,0:T(8,128)(2,1)S(1)} %get-tuple-element.155), channel_id=1, source_target_pairs={{0,1},{1,0},{2,3},{3,2},{4,5},{5,4},{6,7},{7,6},{8,9},{9,8},{10,11... | collective-permute-start | bytes 196616 | tf_op jit(solution)/shard_map/ppermute | solution.py:356
  (20 other events, 68.6 us)

commit v13 on v12

--- a/solution.py
+++ b/solution.py
@@ -306,14 +306,39 @@
     emit(refs[ins + 1 :], mm(back_t[...], change), size)
 
 
-def last_back(near, receive, slope, weight, grad, grid_rim_t, *refs, ins, scale):
-    new_grad, outer, inner = refs[ins:]
-    rows = arrived(refs[:ins], refs[0].shape[0])
-    change = layer_back(near, receive, rows, slope, weight[0], grad, scale)
-    new_grad[...] = change
-    back = mm(grid_rim_t[...], change).astype(BF)
-    outer[...] = back[: outer.shape[0]]
-    inner[...] = back[outer.shape[0] :]
+def grid_base(own_t, grad, slope, weight, cotangent, base):
+    change = (mm(own_t[...], grad[...]) * slope[...].astype(F32)).astype(BF)
+    base[...] = cotangent[...].astype(F32) + mm_t(change, weight[...])
+
+
+def last_even(near, receive, slope, weight, grad, grid_rim_t, own_t, grid_slope, grid_weight, cotangent, *refs, ins, scale):
+    new_grad, outer, inner, base = refs[-4:]
+    last_back(near, receive, slope, weight, grad, grid_rim_t, *refs[:-1], ins=ins, scale=scale, parity=0)
+
+    @pl.when(lax.axis_index("dom") % 2 == 0)
+    def _():
+        grid_base(own_t, new_grad, grid_slope, grid_weight, cotangent, base)
+
+
+def last_back(near, receive, slope, weight, grad, grid_rim_t, *refs, ins, scale, parity):
+    new_grad, outer, inner = refs[-3:]
+    mine = lax.axis_index("dom") % 2 == parity
+
+    @pl.when(mine)
+    def _():
+        rows = arrived(refs[:ins], refs[0].shape[0])
+        change = layer_back(near, receive, rows, slope, weight[0], grad, scale)
+        new_grad[...] = change
+        back = mm(grid_rim_t[...], change).astype(BF)
+        outer[...] = back[: outer.shape[0]]
+        inner[...] = back[outer.shape[0] :]
+
+    if len(refs) > ins + 3:
+
+        @pl.when(jnp.logical_not(mine))
+        def _():
+            new_grad[...] = refs[ins][...]
+            inner[...] = refs[ins + 1][...]
 
 
 def decode_own(latent, own_t, message, base):
@@ -327,30 +352,40 @@
     token[...] = jnp.zeros(token.shape, F32)
 
 
-def grid_local(own_t, grad, lists, slope, weight, cotangent, base, table, slope_rows, mesh_grad):
-    me = lax.axis_index("dom")
+def halo_tables(lists, slope, table, slope_rows):
+    size = lists.shape[2]
+    for k, wanted in enumerate(pair_order(lists, lax.axis_index("dom"))):
+        table[:, k * size : (k + 1) * size] = pick(table.shape[0], wanted)
+    slope_rows[...] = t_mm(table[...], slope[...])
+
+
+def grid_local(own_t, grad, slope, weight, cotangent, base, mesh_grad):
     mesh_grad[...] = grad[...]
-    rows = own_t.shape[0]
-    size = lists.shape[2]
-    for k, wanted in enumerate(pair_order(lists, me)):
-        table[:, k * size : (k + 1) * size] = pick(rows, wanted)
-    slope_rows[...] = t_mm(table[...], slope[...])
-    change = (mm(own_t[...], grad[...]) * slope[...].astype(F32)).astype(BF)
-    base[...] = cotangent[...].astype(F32) + mm_t(change, weight[...])
-
-
-def grid_back(base, table, slope_rows, weight, outer_in, inner_in, output, staging, sems):
-    returned = jnp.concatenate([outer_in[...], inner_in[...]], axis=0).astype(F32)
+
+    @pl.when(lax.axis_index("dom") % 2 == 1)
+    def _():
+        grid_base(own_t, grad, slope, weight, cotangent, base)
+
+
+def grid_back(even_base, odd_base, table, slope_rows, weight, even_in, odd_in, inner_in, output, staging, sems):
+    even = lax.axis_index("dom") % 2 == 0
+    outer_in = jnp.where(even, even_in[...], odd_in[...])
+    returned = jnp.concatenate([outer_in, inner_in[...]], axis=0).astype(F32)
     change = mm_t((returned * slope_rows[...]).astype(BF), weight[...]).astype(BF)
     copies = []
-    for i, part in enumerate(row_chunks(base.shape[0])):
-        staging[part] = (base[part] + mm(table[part], change)).astype(BF)
+    for i, part in enumerate(row_chunks(table.shape[0])):
+        base = jnp.where(even, even_base[part], odd_base[part])
+        staging[part] = (base + mm(table[part], change)).astype(BF)
         copies.append(pltpu.make_async_copy(staging.at[part], output.at[part], sems.at[i]))
         copies[-1].start()
     for copy in copies:
         copy.wait()
 
 
+def touch(_, token):
+    token[...] = jnp.zeros(token.shape, F32)
+
+
 def toggle(value, bits):
     peers = lax.axis_size("dom")
     return lax.ppermute(value, "dom", [(i, i ^ bits) for i in range(peers)])
@@ -360,6 +395,12 @@
     peers = lax.axis_size("dom")
     pairs = [(i, (i + 1) % peers if i % 2 else (i - 1) % peers) for i in range(peers)]
     return lax.ppermute(value, "dom", pairs)
+
+
+def across_one_way(value, parity):
+    peers = lax.axis_size("dom")
+    step = 1 if parity else -1
+    return lax.ppermute(value, "dom", [(i, (i + step) % peers) for i in range(peers) if i % 2 == parity])
 
 
 def exchange(outs, cap):
@@ -502,12 +543,20 @@
         free=1,
     )
 
+    table, slope_rows = call(
+        halo_tables,
+        [((grid_rows, 2 * ghalo), BF), ((2 * ghalo, width), F32)],
+        square(grid_rows, 2 * ghalo),
+        grid_halo_rows, grid_slope, ins[-1],
+        free=1,
+    )
+
     grad, *outs = call(
         functools.partial(middle_back, ins=len(ins), layer=1, scale=scale, size=halo),
         [state] + sends(halo),
         step,
-        near, receive, slope_1, processor_weights, grad, back_t, *ins, base,
-        free=1,
+        near, receive, slope_1, processor_weights, grad, back_t, *ins, base, slope_rows,
+        free=2,
     )
     ins = exchange(outs, cap)
     (near,) = call(back_local, [total], 6 * square(mesh_rows, mesh_rows), own_t, grad, ins[-1], free=1)
@@ -519,26 +568,35 @@
         free=1,
     )
 
-    grad, outer, inner = call(
-        functools.partial(last_back, ins=len(ins), scale=scale),
-        [state, grid_rim, grid_rim],
-        step,
-        near, receive, slope_0, processor_weights, grad, grid_rim_t, *ins, token,
-        free=1,
-    )
-    outer_in, inner_in = across(outer), toggle(inner, 1)
-    base, table, slope_rows, mesh_grad = call(
+    sides = [state, grid_rim, grid_rim]
+    last = functools.partial(last_back, ins=len(ins), scale=scale)
+    operands = (near, receive, slope_0, processor_weights, grad, grid_rim_t, *ins)
+    odd_grad, outer, odd_inner = call(
+        functools.partial(last, parity=1), sides, step, *operands, token, free=1
+    )
+    even_in = across_one_way(outer, 1)
+    grid_shape = ((grid_rows, width), F32)
+    grid_operands = (grid_slope, encoder_weight, cotangent)
+    grad, outer, inner, even_base = call(
+        functools.partial(last_even, ins=len(ins), scale=scale),
+        sides + [grid_shape],
+        step + 2 * square(grid_rows, width),
+        *operands[:6], grid_own_t, *grid_operands, *ins, odd_grad, odd_inner,
+    )
+    odd_in, inner_in = across_one_way(outer, 0), toggle(inner, 1)
+    odd_base, mesh_grad = call(
         grid_local,
-        [((grid_rows, width), F32), ((grid_rows, 2 * ghalo), BF), ((2 * ghalo, width), F32), state],
-        square(mesh_rows, grid_rows) + square(grid_rows, width),
-        grid_own_t, grad, grid_halo_rows, grid_slope, encoder_weight, cotangent,
-    )
+        [grid_shape, state],
+        square(grid_rows, width),
+        grid_own_t, grad, *grid_operands,
+    )
+    (token,) = call(touch, [((8, 128), F32)], 1 * step, even_in)
     (grid_grad,) = call(
         grid_back,
         [((grid_rows, width), BF)],
         square(grid_rows, 4 * ghalo),
-        base, table, slope_rows, encoder_weight, outer_in, inner_in,
-        hbm_out=1,
+        even_base, odd_base, table, slope_rows, encoder_weight, even_in, odd_in, inner_in, token,
+        free=1, hbm_out=1,
         scratch=[pltpu.VMEM((grid_rows, width), BF), pltpu.SemaphoreType.DMA((CHUNKS,))],
     )
     return (output, grid_grad, mesh_grad)

time: 70.8 us -> 74.3 us (1.049)
  starting transfers between devices: 38.5 us -> 42.7 us
  waiting for transfers between devices: 10.3 us -> 8.91 us
    ppermute x0 -> x2, starting transfers between devices: none -> 6.32 us  [across_one_way(): lax.ppermute(value, 'dom', [(i, (i + step) % peers) for i in range(peers)...]
    ppermute x6 -> x5, starting transfers between devices: 13 us -> 10.8 us  [across(): return lax.ppermute(value, 'dom', pairs)]
    ppermute x6 -> x5, waiting for transfers between devices: 1.83 us -> 0.01 us  [across(): return lax.ppermute(value, 'dom', pairs)]
    ppermute x0 -> x2, waiting for transfers between devices: none -> 0.97 us  [across_one_way(): lax.ppermute(value, 'dom', [(i, (i + step) % peers) for i in range(peers)...]
    pallas_call x21 -> x24, Pallas kernels: 20 us -> 20.2 us  [call(): pl.pallas_call(inner, out_shape=shapes, in_specs=[pl.BlockSpec(memory_spa...]
  transfers between devices with their start and end apart: 32 -> 33, of which waited for: 13 -> 12; matrix products, arithmetic and copies ran while one was open for 0% -> 0% of each run, Pallas kernels for 17% -> 17%
where the time goes in v13:
time: 74.3 us; the launch traced here: 73.7 us
  starting transfers between devices  42.7 us (57%)
  Pallas kernels  20.2 us (27%)
  waiting for transfers between devices  8.91 us (12%)
  between operations  1.15 us (2%)
    ppermute x26, starting transfers between devices, toggle(): return lax.ppermute(value, 'dom', [(i, i ^ bits) for i in range(peers)])  25.6 us
    pallas_call x24, Pallas kernels, call(): pl.pallas_call(inner, out_shape=shapes, in_specs=[pl.BlockSpec(memory_spa...  20.2 us
    ppermute x5, starting transfers between devices, across(): return lax.ppermute(value, 'dom', pairs)  10.8 us
    ppermute x26, waiting for transfers between devices, toggle(): return lax.ppermute(value, 'dom', [(i, i ^ bits) for i in range(peers)])  7.92 us
    ppermute x2, starting transfers between devices, across_one_way(): lax.ppermute(value, 'dom', [(i, (i + step) % peers) for i in range(peers)...  6.32 us
  transfers between devices with their start and end apart: 33, of which 12 were waited for; matrix products, arithmetic and copies ran while one was open for 0% of the time, Pallas kernels for 17%

profile of v13, /device:TPU:0, one launch (start us, length us, event | category | flops | bytes accessed | tf_op | source)
XLA Modules:
  0.0 73.7 jit_solution(12792989226791843084)
XLA Ops:
  0.7 2.2 %shard_map.139 = (bf16[64,512]{1,0:T(8,128)(2,1)}, bf16[64,512]{1,0:T(8,128)(2,1)}) custom-call(bf16[1024,512]{1,0:T(8,128)(2,1)} %refs_0_.2, s32[1,2,64]{2,1,0:T(2,128)} %refs_0_.3), custom_call_target="tpu_custom_call" | custom-call | flops 34359738368 | tf_op jit(solution)/shard_map/pallas_call | solution.py:83
  2.9 5.5 %collective-permute-start = (bf16[64,512]{1,0:T(8,128)(2,1)}, bf16[64,512]{1,0:T(8,128)(2,1)S(1)}, u32[]{:S(2)}, u32[]{:S(2)}) collective-permute-start(bf16[64,512]{1,0:T(8,128)(2,1)} %get-tuple-element.90), channel_id=1, source_target_pairs={{0,15},{1,2},{2,1},{3,4},{4,3},{5,6},{6,5},{7,8},{8,7},{9,10},{10,... | collective-permute-start | bytes 196616 | tf_op jit(solution)/shard_map/ppermute | solution.py:397
  8.4 1.1 %shard_map.141 = (bf16[512,512]{1,0:T(8,128)(2,1)S(1)}, bf16[192,512]{1,0:T(8,128)(2,1)S(1)}, bf16[192,512]{1,0:T(8,128)(2,1)S(1)}, bf16[512,192]{1,0:T(8,128)(2,1)S(1)}, bf16[512,192]{1,0:T(8,128)(2,1)S(1)}) custom-call(s32[8,512]{1,0:T(8,128)S(1)} %bitcast.6, s32[1,2,64]{2,1,0:T(2,128)S(1)} %copy-done.11, s32[4,16]{1,0:T(4,128)S(1)} %bitcast.9), custom_call_target="tpu_custom_call" | custom-call | flops 17179869184 | bytes 1327872 | tf_op jit(solution)/shard_map/pallas_call | solution.py:83
  9.9 1.9 %shard_map.140 = (f32[512,512]{1,0:T(8,128)S(1)}, bf16[1024,512]{1,0:T(8,128)(2,1)S(1)}, bf16[128,512]{1,0:T(8,128)(2,1)S(1)}, bf16[1024,512]{1,0:T(8,128)(2,1)S(1)}) custom-call(s32[4,512]{1,0:T(4,128)S(1)} %bitcast.8, bf16[512,512]{1,0:T(8,128)(2,1)S(1)} %copy-done.1, bf16[1024,512]{1,0:T(8,128)(2,1)S(1)} %copy-done.3, bf16[512,512]{1,0:T(8,128)(2,1)S(1)} %copy-done.5), custom_call_target="tpu_custom_call" | custom-call | flops 2147483648 | bytes 5382144 | tf_op jit(solution)/shard_map/pallas_call | solution.py:83
  12.8 1.3 %collective-permute-start.2 = (bf16[16,512]{1,0:T(8,128)(2,1)S(1)}, bf16[16,512]{1,0:T(8,128)(2,1)S(1)}, u32[]{:S(2)}, u32[]{:S(2)}) collective-permute-start(bf16[16,512]{1,0:T(8,128)(2,1)S(1)} %get-tuple-element.94), channel_id=1, source_target_pairs={{0,12},{1,13},{2,14},{3,15},{4,8},{5,9},{6,10},{7,11},{8,4},{9,5},... | collective-permute-start | bytes 49160 | tf_op jit(solution)/shard_map/ppermute | solution.py:391
  14.1 3.2 %collective-permute-start.4 = (bf16[16,512]{1,0:T(8,128)(2,1)S(1)}, bf16[16,512]{1,0:T(8,128)(2,1)S(1)}, u32[]{:S(2)}, u32[]{:S(2)}) collective-permute-start(bf16[16,512]{1,0:T(8,128)(2,1)S(1)} %get-tuple-element.96), channel_id=1, source_target_pairs={{0,4},{1,5},{2,6},{3,7},{4,0},{5,1},{6,2},{7,3},{8,12},{9,13},{10,... | collective-permute-start | bytes 49160 | tf_op jit(solution)/shard_map/ppermute | solution.py:391
  17.3 2.3 %collective-permute-start.5 = (bf16[64,512]{1,0:T(8,128)(2,1)S(1)}, bf16[64,512]{1,0:T(8,128)(2,1)S(1)}, u32[]{:S(2)}, u32[]{:S(2)}) collective-permute-start(bf16[64,512]{1,0:T(8,128)(2,1)S(1)} %get-tuple-element.105), channel_id=1, source_target_pairs={{0,15},{1,2},{2,1},{3,4},{4,3},{5,6},{6,5},{7,8},{8,7},{9,10},{10,... | collective-permute-start | bytes 196616 | tf_op jit(solution)/shard_map/ppermute | solution.py:397
  20.2 1.4 %collective-permute-start.6 = (bf16[80,512]{1,0:T(8,128)(2,1)S(1)}, bf16[80,512]{1,0:T(8,128)(2,1)S(1)}, u32[]{:S(2)}, u32[]{:S(2)}) collective-permute-start(bf16[80,512]{1,0:T(8,128)(2,1)S(1)} %get-tuple-element.106), channel_id=1, source_target_pairs={{0,1},{1,0},{2,3},{3,2},{4,5},{5,4},{6,7},{7,6},{8,9},{9,8},{10,11... | collective-permute-start | bytes 245768 | tf_op jit(solution)/shard_map/ppermute | solution.py:391
  24.7 2.3 %collective-permute-start.9 = (bf16[16,512]{1,0:T(8,128)(2,1)S(1)}, bf16[16,512]{1,0:T(8,128)(2,1)S(1)}, u32[]{:S(2)}, u32[]{:S(2)}) collective-permute-start(bf16[16,512]{1,0:T(8,128)(2,1)S(1)} %get-tuple-element.112), channel_id=1, source_target_pairs={{0,12},{1,13},{2,14},{3,15},{4,8},{5,9},{6,10},{7,11},{8,4},{9,5},... | collective-permute-start | bytes 49160 | tf_op jit(solution)/shard_map/ppermute | solution.py:391
  27.5 1.7 %collective-permute-start.11 = (bf16[16,512]{1,0:T(8,128)(2,1)S(1)}, bf16[16,512]{1,0:T(8,128)(2,1)S(1)}, u32[]{:S(2)}, u32[]{:S(2)}) collective-permute-start(bf16[16,512]{1,0:T(8,128)(2,1)S(1)} %get-tuple-element.114), channel_id=1, source_target_pairs={{0,4},{1,5},{2,6},{3,7},{4,0},{5,1},{6,2},{7,3},{8,12},{9,13},{10,... | collective-permute-start | bytes 49160 | tf_op jit(solution)/shard_map/ppermute | solution.py:391
  29.2 1.6 %collective-permute-start.12 = (bf16[128,512]{1,0:T(8,128)(2,1)S(1)}, bf16[128,512]{1,0:T(8,128)(2,1)S(1)}, u32[]{:S(2)}, u32[]{:S(2)}) collective-permute-start(bf16[128,512]{1,0:T(8,128)(2,1)S(1)} %get-tuple-element.120), channel_id=1, source_target_pairs={{0,15},{1,2},{2,1},{3,4},{4,3},{5,6},{6,5},{7,8},{8,7},{9,10},{10,... | collective-permute-start | bytes 393224 | tf_op jit(solution)/shard_map/ppermute | solution.py:397
  34.7 1.9 %collective-permute-done.14.refs_2_ = bf16[16,512]{1,0:T(8,128)(2,1)S(1)} collective-permute-done((bf16[16,512]{1,0:T(8,128)(2,1)S(1)}, bf16[16,512]{1,0:T(8,128)(2,1)S(1)}, u32[]{:S(2)}, u32[]{:S(2)}) %collective-permute-start.14) | collective-permute-done | bytes 16416 | tf_op jit(solution)/shard_map/ppermute | solution.py:391
  36.7 1.3 %shard_map.149 = (bf16[512,512]{1,0:T(8,128)(2,1)S(1)}, bf16[512,512]{1,0:T(8,128)(2,1)S(1)}, bf16[128,512]{1,0:T(8,128)(2,1)S(1)}, bf16[128,512]{1,0:T(8,128)(2...) custom-call(f32[512,512]{1,0:T(8,128)S(1)} %get-tuple-element.116.ne, ...), custom_call_target="tpu_custom_call" | custom-call | flops 1610612736 | bytes 5111808 | tf_op jit(solution)/shard_map/pallas_call | solution.py:83
  38.1 1.5 %collective-permute-start.16 = (bf16[16,512]{1,0:T(8,128)(2,1)S(1)}, bf16[16,512]{1,0:T(8,128)(2,1)S(1)}, u32[]{:S(2)}, u32[]{:S(2)}) collective-permute-start(bf16[16,512]{1,0:T(8,128)(2,1)S(1)} %get-tuple-element.127), channel_id=1, source_target_pairs={{0,12},{1,13},{2,14},{3,15},{4,8},{5,9},{6,10},{7,11},{8,4},{9,5},... | collective-permute-start | bytes 49160 | tf_op jit(solution)/shard_map/ppermute | solution.py:391
  39.9 2.6 %collective-permute-start.18 = (bf16[16,512]{1,0:T(8,128)(2,1)S(1)}, bf16[16,512]{1,0:T(8,128)(2,1)S(1)}, u32[]{:S(2)}, u32[]{:S(2)}) collective-permute-start(bf16[16,512]{1,0:T(8,128)(2,1)S(1)} %get-tuple-element.129), channel_id=1, source_target_pairs={{0,4},{1,5},{2,6},{3,7},{4,0},{5,1},{6,2},{7,3},{8,12},{9,13},{10,... | collective-permute-start | bytes 49160 | tf_op jit(solution)/shard_map/ppermute | solution.py:391
  44.6 1.3 %collective-permute-start.22 = (bf16[16,512]{1,0:T(8,128)(2,1)S(1)}, bf16[16,512]{1,0:T(8,128)(2,1)S(1)}, u32[]{:S(2)}, u32[]{:S(2)}) collective-permute-start(bf16[16,512]{1,0:T(8,128)(2,1)S(1)} %get-tuple-element.137), channel_id=1, source_target_pairs={{0,2},{1,3},{2,0},{3,1},{4,6},{5,7},{6,4},{7,5},{8,10},{9,11},{10,... | collective-permute-start | bytes 49160 | tf_op jit(solution)/shard_map/ppermute | solution.py:391
  48.4 1.6 %collective-permute-done.22.refs_9_ = bf16[16,512]{1,0:T(8,128)(2,1)S(1)} collective-permute-done((bf16[16,512]{1,0:T(8,128)(2,1)S(1)}, bf16[16,512]{1,0:T(8,128)(2,1)S(1)}, u32[]{:S(2)}, u32[]{:S(2)}) %collective-permute-start.22) | collective-permute-done | bytes 16416 | tf_op jit(solution)/shard_map/ppermute | solution.py:391
  50.7 1.6 %collective-permute-start.23 = (bf16[16,512]{1,0:T(8,128)(2,1)S(1)}, bf16[16,512]{1,0:T(8,128)(2,1)S(1)}, u32[]{:S(2)}, u32[]{:S(2)}) collective-permute-start(bf16[16,512]{1,0:T(8,128)(2,1)S(1)} %get-tuple-element.142), channel_id=1, source_target_pairs={{0,12},{1,13},{2,14},{3,15},{4,8},{5,9},{6,10},{7,11},{8,4},{9,5},... | collective-permute-start | bytes 49160 | tf_op jit(solution)/shard_map/ppermute | solution.py:391
  52.6 2.6 %collective-permute-start.25 = (bf16[16,512]{1,0:T(8,128)(2,1)S(1)}, bf16[16,512]{1,0:T(8,128)(2,1)S(1)}, u32[]{:S(2)}, u32[]{:S(2)}) collective-permute-start(bf16[16,512]{1,0:T(8,128)(2,1)S(1)} %get-tuple-element.144), channel_id=1, source_target_pairs={{0,4},{1,5},{2,6},{3,7},{4,0},{5,1},{6,2},{7,3},{8,12},{9,13},{10,... | collective-permute-start | bytes 49160 | tf_op jit(solution)/shard_map/ppermute | solution.py:391
  59.6 1.4 %shard_map.156 = (bf16[1024,512]{1,0:T(8,128)(2,1)}, f32[8,128]{1,0:T(8,128)S(1)}) custom-call(f32[1024,512]{1,0:T(8,128)S(1)} %shard_map.151.refs_11_.refs_0_, bf16[128,1024]{1,0:T(8,128)(2,1)S(1)} %get-tuple-element.131.refs_1_, bf16[128,512]{1,0:T(8,128)(2,1)S(1)} %collective-permute-done.19.refs_6_.refs_2_, ...), custom_call_target="tpu_custom_call" | custom-call | flops 134217728 | bytes 3706880 | tf_op jit(solution)/shard_map/pallas_call | solution.py:83
  61.8 1.3 %collective-permute-start.30 = (bf16[64,512]{1,0:T(8,128)(2,1)S(1)}, bf16[64,512]{1,0:T(8,128)(2,1)S(1)}, u32[]{:S(2)}, u32[]{:S(2)}) collective-permute-start(bf16[64,512]{1,0:T(8,128)(2,1)S(1)} %get-tuple-element.161), channel_id=1, source_target_pairs={{1,2},{3,4},{5,6},{7,8},{9,10},{11,12},{13,14},{15,0},{17,18},{19,... | collective-permute-start | bytes 196616 | tf_op jit(solution)/shard_map/ppermute | solution.py:403
  63.1 2.0 %shard_map.159 = (bf16[512,512]{1,0:T(8,128)(2,1)S(1)}, bf16[64,512]{1,0:T(8,128)(2,1)S(1)}, bf16[64,512]{1,0:T(8,128)(2,1)S(1)}, f32[1024,512]{1,0:T(8,128)S(1)}) custom-call(f32[512,512]{1,0:T(8,128)S(1)} %shard_map.157.refs_0_.near, bf16[512,192]{1,0:T(8,128)(2,1)S(1)} %get-tuple-element.117.receive.refs_1_, ...), custom_call_target="tpu_custom_call" | custom-call | flops 1879048192 | bytes 11206656 | tf_op jit(solution)/shard_map/pallas_call | solution.py:83
  65.1 5.0 %collective-permute-start.31 = (bf16[64,512]{1,0:T(8,128)(2,1)S(1)}, bf16[64,512]{1,0:T(8,128)(2,1)S(1)}, u32[]{:S(2)}, u32[]{:S(2)}) collective-permute-start(bf16[64,512]{1,0:T(8,128)(2,1)S(1)} %get-tuple-element.162), channel_id=1, source_target_pairs={{0,15},{2,1},{4,3},{6,5},{8,7},{10,9},{12,11},{14,13},{16,31},{18,... | collective-permute-start | bytes 196616 | tf_op jit(solution)/shard_map/ppermute | solution.py:403
  72.1 1.5 %shard_map.162 = bf16[1024,512]{1,0:T(8,128)(2,1)} custom-call(f32[1024,512]{1,0:T(8,128)S(1)} %get-tuple-element.157.refs_0_, f32[1024,512]{1,0:T(8,128)S(1)} %get-tuple-element.159.refs_1_, bf16[1024,128]{1,0:T(8,128)(2,1)S(1)} %get-tuple-element.160.refs_2_, f32[128,512]{1,0:T(8,128)S(1)} %get-tuple-element.139.refs_12_.refs_3_, ...), custom_call_target="tpu_custom_call" | custom-call | flops 268435456 | bytes 6492160 | tf_op jit(solution)/shard_map/pallas_call | solution.py:83
  (90 shorter events, 22.5 us)
Async XLA Ops:
  2.9 9.0 %collective-permute-start = (bf16[64,512]{1,0:T(8,128)(2,1)}, bf16[64,512]{1,0:T(8,128)(2,1)S(1)}, u32[]{:S(2)}, u32[]{:S(2)}) collective-permute-start(bf16[64,512]{1,0:T(8,128)(2,1)} %get-tuple-element.90), channel_id=1, source_target_pairs={{0,15},{1,2},{2,1},{3,4},{4,3},{5,6},{6,5},{7,8},{8,7},{9,10},{10,... | collective-permute-start | bytes 196616 | tf_op jit(solution)/shard_map/ppermute | solution.py:397
  12.8 6.7 %collective-permute-start.2 = (bf16[16,512]{1,0:T(8,128)(2,1)S(1)}, bf16[16,512]{1,0:T(8,128)(2,1)S(1)}, u32[]{:S(2)}, u32[]{:S(2)}) collective-permute-start(bf16[16,512]{1,0:T(8,128)(2,1)S(1)} %get-tuple-element.94), channel_id=1, source_target_pairs={{0,12},{1,13},{2,14},{3,15},{4,8},{5,9},{6,10},{7,11},{8,4},{9,5},... | collective-permute-start | bytes 49160 | tf_op jit(solution)/shard_map/ppermute | solution.py:391
  14.1 5.4 %collective-permute-start.3 = (bf16[16,512]{1,0:T(8,128)(2,1)S(1)}, bf16[16,512]{1,0:T(8,128)(2,1)S(1)}, u32[]{:S(2)}, u32[]{:S(2)}) collective-permute-start(bf16[16,512]{1,0:T(8,128)(2,1)S(1)} %get-tuple-element.95), channel_id=1, source_target_pairs={{0,8},{1,9},{2,10},{3,11},{4,12},{5,13},{6,14},{7,15},{8,0},{9,1},... | collective-permute-start | bytes 49160 | tf_op jit(solution)/shard_map/ppermute | solution.py:391
  14.1 5.4 %collective-permute-start.4 = (bf16[16,512]{1,0:T(8,128)(2,1)S(1)}, bf16[16,512]{1,0:T(8,128)(2,1)S(1)}, u32[]{:S(2)}, u32[]{:S(2)}) collective-permute-start(bf16[16,512]{1,0:T(8,128)(2,1)S(1)} %get-tuple-element.96), channel_id=1, source_target_pairs={{0,4},{1,5},{2,6},{3,7},{4,0},{5,1},{6,2},{7,3},{8,12},{9,13},{10,... | collective-permute-start | bytes 49160 | tf_op jit(solution)/shard_map/ppermute | solution.py:391
  17.3 6.7 %collective-permute-start.5 = (bf16[64,512]{1,0:T(8,128)(2,1)S(1)}, bf16[64,512]{1,0:T(8,128)(2,1)S(1)}, u32[]{:S(2)}, u32[]{:S(2)}) collective-permute-start(bf16[64,512]{1,0:T(8,128)(2,1)S(1)} %get-tuple-element.105), channel_id=1, source_target_pairs={{0,15},{1,2},{2,1},{3,4},{4,3},{5,6},{6,5},{7,8},{8,7},{9,10},{10,... | collective-permute-start | bytes 196616 | tf_op jit(solution)/shard_map/ppermute | solution.py:397
  24.7 6.0 %collective-permute-start.9 = (bf16[16,512]{1,0:T(8,128)(2,1)S(1)}, bf16[16,512]{1,0:T(8,128)(2,1)S(1)}, u32[]{:S(2)}, u32[]{:S(2)}) collective-permute-start(bf16[16,512]{1,0:T(8,128)(2,1)S(1)} %get-tuple-element.112), channel_id=1, source_target_pairs={{0,12},{1,13},{2,14},{3,15},{4,8},{5,9},{6,10},{7,11},{8,4},{9,5},... | collective-permute-start | bytes 49160 | tf_op jit(solution)/shard_map/ppermute | solution.py:391
  27.1 4.6 %collective-permute-start.10 = (bf16[16,512]{1,0:T(8,128)(2,1)S(1)}, bf16[16,512]{1,0:T(8,128)(2,1)S(1)}, u32[]{:S(2)}, u32[]{:S(2)}) collective-permute-start(bf16[16,512]{1,0:T(8,128)(2,1)S(1)} %get-tuple-element.113), channel_id=1, source_target_pairs={{0,8},{1,9},{2,10},{3,11},{4,12},{5,13},{6,14},{7,15},{8,0},{9,1},... | collective-permute-start | bytes 49160 | tf_op jit(solution)/shard_map/ppermute | solution.py:391
  27.5 4.2 %collective-permute-start.11 = (bf16[16,512]{1,0:T(8,128)(2,1)S(1)}, bf16[16,512]{1,0:T(8,128)(2,1)S(1)}, u32[]{:S(2)}, u32[]{:S(2)}) collective-permute-start(bf16[16,512]{1,0:T(8,128)(2,1)S(1)} %get-tuple-element.114), channel_id=1, source_target_pairs={{0,4},{1,5},{2,6},{3,7},{4,0},{5,1},{6,2},{7,3},{8,12},{9,13},{10,... | collective-permute-start | bytes 49160 | tf_op jit(solution)/shard_map/ppermute | solution.py:391
  29.2 7.5 %collective-permute-start.12 = (bf16[128,512]{1,0:T(8,128)(2,1)S(1)}, bf16[128,512]{1,0:T(8,128)(2,1)S(1)}, u32[]{:S(2)}, u32[]{:S(2)}) collective-permute-start(bf16[128,512]{1,0:T(8,128)(2,1)S(1)} %get-tuple-element.120), channel_id=1, source_target_pairs={{0,15},{1,2},{2,1},{3,4},{4,3},{5,6},{6,5},{7,8},{8,7},{9,10},{10,... | collective-permute-start | bytes 393224 | tf_op jit(solution)/shard_map/ppermute | solution.py:397
  31.9 4.7 %collective-permute-start.14 = (bf16[16,512]{1,0:T(8,128)(2,1)S(1)}, bf16[16,512]{1,0:T(8,128)(2,1)S(1)}, u32[]{:S(2)}, u32[]{:S(2)}) collective-permute-start(bf16[16,512]{1,0:T(8,128)(2,1)S(1)} %get-tuple-element.122), channel_id=1, source_target_pairs={{0,3},{1,2},{2,1},{3,0},{4,7},{5,6},{6,5},{7,4},{8,11},{9,10},{10,... | collective-permute-start | bytes 49160 | tf_op jit(solution)/shard_map/ppermute | solution.py:391
  31.9 4.8 %collective-permute-start.15 = (bf16[16,512]{1,0:T(8,128)(2,1)S(1)}, bf16[16,512]{1,0:T(8,128)(2,1)S(1)}, u32[]{:S(2)}, u32[]{:S(2)}) collective-permute-start(bf16[16,512]{1,0:T(8,128)(2,1)S(1)} %get-tuple-element.123), channel_id=1, source_target_pairs={{0,2},{1,3},{2,0},{3,1},{4,6},{5,7},{6,4},{7,5},{8,10},{9,11},{10,... | collective-permute-start | bytes 49160 | tf_op jit(solution)/shard_map/ppermute | solution.py:391
  38.1 5.6 %collective-permute-start.16 = (bf16[16,512]{1,0:T(8,128)(2,1)S(1)}, bf16[16,512]{1,0:T(8,128)(2,1)S(1)}, u32[]{:S(2)}, u32[]{:S(2)}) collective-permute-start(bf16[16,512]{1,0:T(8,128)(2,1)S(1)} %get-tuple-element.127), channel_id=1, source_target_pairs={{0,12},{1,13},{2,14},{3,15},{4,8},{5,9},{6,10},{7,11},{8,4},{9,5},... | collective-permute-start | bytes 49160 | tf_op jit(solution)/shard_map/ppermute | solution.py:391
  39.6 4.7 %collective-permute-start.17 = (bf16[16,512]{1,0:T(8,128)(2,1)S(1)}, bf16[16,512]{1,0:T(8,128)(2,1)S(1)}, u32[]{:S(2)}, u32[]{:S(2)}) collective-permute-start(bf16[16,512]{1,0:T(8,128)(2,1)S(1)} %get-tuple-element.128), channel_id=1, source_target_pairs={{0,8},{1,9},{2,10},{3,11},{4,12},{5,13},{6,14},{7,15},{8,0},{9,1},... | collective-permute-start | bytes 49160 | tf_op jit(solution)/shard_map/ppermute | solution.py:391
  39.9 4.5 %collective-permute-start.18 = (bf16[16,512]{1,0:T(8,128)(2,1)S(1)}, bf16[16,512]{1,0:T(8,128)(2,1)S(1)}, u32[]{:S(2)}, u32[]{:S(2)}) collective-permute-start(bf16[16,512]{1,0:T(8,128)(2,1)S(1)} %get-tuple-element.129), channel_id=1, source_target_pairs={{0,4},{1,5},{2,6},{3,7},{4,0},{5,1},{6,2},{7,3},{8,12},{9,13},{10,... | collective-permute-start | bytes 49160 | tf_op jit(solution)/shard_map/ppermute | solution.py:391
  42.5 7.4 %collective-permute-start.19 = (bf16[128,512]{1,0:T(8,128)(2,1)S(1)}, bf16[128,512]{1,0:T(8,128)(2,1)S(1)}, u32[]{:S(2)}, u32[]{:S(2)}) collective-permute-start(bf16[128,512]{1,0:T(8,128)(2,1)S(1)} %get-tuple-element.132), channel_id=1, source_target_pairs={{0,15},{1,2},{2,1},{3,4},{4,3},{5,6},{6,5},{7,8},{8,7},{9,10},{10,... | collective-permute-start | bytes 393224 | tf_op jit(solution)/shard_map/ppermute | solution.py:397
  44.6 5.3 %collective-permute-start.22 = (bf16[16,512]{1,0:T(8,128)(2,1)S(1)}, bf16[16,512]{1,0:T(8,128)(2,1)S(1)}, u32[]{:S(2)}, u32[]{:S(2)}) collective-permute-start(bf16[16,512]{1,0:T(8,128)(2,1)S(1)} %get-tuple-element.137), channel_id=1, source_target_pairs={{0,2},{1,3},{2,0},{3,1},{4,6},{5,7},{6,4},{7,5},{8,10},{9,11},{10,... | collective-permute-start | bytes 49160 | tf_op jit(solution)/shard_map/ppermute | solution.py:391
  45.9 4.1 %collective-permute-start.20 = (bf16[144,512]{1,0:T(8,128)(2,1)S(1)}, bf16[144,512]{1,0:T(8,128)(2,1)S(1)}, u32[]{:S(2)}, u32[]{:S(2)}) collective-permute-start(bf16[144,512]{1,0:T(8,128)(2,1)S(1)} %get-tuple-element.133), channel_id=1, source_target_pairs={{0,1},{1,0},{2,3},{3,2},{4,5},{5,4},{6,7},{7,6},{8,9},{9,8},{10,11... | collective-permute-start | bytes 442376 | tf_op jit(solution)/shard_map/ppermute | solution.py:391
  50.7 5.6 %collective-permute-start.23 = (bf16[16,512]{1,0:T(8,128)(2,1)S(1)}, bf16[16,512]{1,0:T(8,128)(2,1)S(1)}, u32[]{:S(2)}, u32[]{:S(2)}) collective-permute-start(bf16[16,512]{1,0:T(8,128)(2,1)S(1)} %get-tuple-element.142), channel_id=1, source_target_pairs={{0,12},{1,13},{2,14},{3,15},{4,8},{5,9},{6,10},{7,11},{8,4},{9,5},... | collective-permute-start | bytes 49160 | tf_op jit(solution)/shard_map/ppermute | solution.py:391
  52.3 4.7 %collective-permute-start.24 = (bf16[16,512]{1,0:T(8,128)(2,1)S(1)}, bf16[16,512]{1,0:T(8,128)(2,1)S(1)}, u32[]{:S(2)}, u32[]{:S(2)}) collective-permute-start(bf16[16,512]{1,0:T(8,128)(2,1)S(1)} %get-tuple-element.143), channel_id=1, source_target_pairs={{0,8},{1,9},{2,10},{3,11},{4,12},{5,13},{6,14},{7,15},{8,0},{9,1},... | collective-permute-start | bytes 49160 | tf_op jit(solution)/shard_map/ppermute | solution.py:391
  52.6 4.5 %collective-permute-start.25 = (bf16[16,512]{1,0:T(8,128)(2,1)S(1)}, bf16[16,512]{1,0:T(8,128)(2,1)S(1)}, u32[]{:S(2)}, u32[]{:S(2)}) collective-permute-start(bf16[16,512]{1,0:T(8,128)(2,1)S(1)} %get-tuple-element.144), channel_id=1, source_target_pairs={{0,4},{1,5},{2,6},{3,7},{4,0},{5,1},{6,2},{7,3},{8,12},{9,13},{10,... | collective-permute-start | bytes 49160 | tf_op jit(solution)/shard_map/ppermute | solution.py:391
  55.1 6.7 %collective-permute-start.26 = (bf16[64,512]{1,0:T(8,128)(2,1)S(1)}, bf16[64,512]{1,0:T(8,128)(2,1)S(1)}, u32[]{:S(2)}, u32[]{:S(2)}) collective-permute-start(bf16[64,512]{1,0:T(8,128)(2,1)S(1)} %get-tuple-element.150), channel_id=1, source_target_pairs={{0,15},{1,2},{2,1},{3,4},{4,3},{5,6},{6,5},{7,8},{8,7},{9,10},{10,... | collective-permute-start | bytes 196616 | tf_op jit(solution)/shard_map/ppermute | solution.py:397
  57.3 4.5 %collective-permute-start.29 = (bf16[16,512]{1,0:T(8,128)(2,1)S(1)}, bf16[16,512]{1,0:T(8,128)(2,1)S(1)}, u32[]{:S(2)}, u32[]{:S(2)}) collective-permute-start(bf16[16,512]{1,0:T(8,128)(2,1)S(1)} %get-tuple-element.153), channel_id=1, source_target_pairs={{0,2},{1,3},{2,0},{3,1},{4,6},{5,7},{6,4},{7,5},{8,10},{9,11},{10,... | collective-permute-start | bytes 49160 | tf_op jit(solution)/shard_map/ppermute | solution.py:391
  61.8 9.3 %collective-permute-start.30 = (bf16[64,512]{1,0:T(8,128)(2,1)S(1)}, bf16[64,512]{1,0:T(8,128)(2,1)S(1)}, u32[]{:S(2)}, u32[]{:S(2)}) collective-permute-start(bf16[64,512]{1,0:T(8,128)(2,1)S(1)} %get-tuple-element.161), channel_id=1, source_target_pairs={{1,2},{3,4},{5,6},{7,8},{9,10},{11,12},{13,14},{15,0},{17,18},{19,... | collective-permute-start | bytes 196616 | tf_op jit(solution)/shard_map/ppermute | solution.py:403
  65.1 6.9 %collective-permute-start.31 = (bf16[64,512]{1,0:T(8,128)(2,1)S(1)}, bf16[64,512]{1,0:T(8,128)(2,1)S(1)}, u32[]{:S(2)}, u32[]{:S(2)}) collective-permute-start(bf16[64,512]{1,0:T(8,128)(2,1)S(1)} %get-tuple-element.162), channel_id=1, source_target_pairs={{0,15},{2,1},{4,3},{6,5},{8,7},{10,9},{12,11},{14,13},{16,31},{18,... | collective-permute-start | bytes 196616 | tf_op jit(solution)/shard_map/ppermute | solution.py:403
  (21 other events, 68.9 us)

commit v14 on v12

--- a/solution.py
+++ b/solution.py
@@ -256,10 +256,6 @@
     near[...] = state.astype(F32) + scale * t_mm(own_t[...], value.astype(BF))
 
 
-def back_local(own_t, grad, near):
-    near[...] = mm(own_t[...], grad[...])
-
-
 def chosen_messages(send, state, weight):
     return silu_pair(mm(t_mm(send[...], state).astype(BF), weight))[0]
 
@@ -287,31 +283,44 @@
     message[...] = value
     returned = jnp.concatenate([refs[0][size : 2 * size], refs[1][size : 2 * size]], axis=0)
     back = back_near[...] + mm(receive[:, : 2 * size], returned)
-    change = mm_t((back * gradient).astype(BF), weight[...]).astype(BF)
+    change = (back * gradient).astype(BF)
     grad[...] = change
     rim = t_mm(send[:, : 2 * size], value).astype(BF)
-    emit(refs[ins + 2 :], mm(back_t[...], change), size, (rim[:size], rim[size:]))
-
-
-def layer_back(near, receive, rows, slope, weight, grad, scale):
+    rows = mm_t(mm(back_t[...], change).astype(BF), weight[...])
+    emit(refs[ins + 2 :], rows, size, (rim[:size], rim[size:]))
+
+
+def turn_local(own_t, change, weight, near, grad):
+    whole = mm_t(change[...], weight[...]).astype(BF)
+    grad[...] = whole
+    near[...] = mm(own_t[...], whole)
+
+
+def layer_change(near, receive, rows, slope, scale):
     total = near[...] + mm(receive[...], rows)
-    change = (total * scale * slope[...]).astype(BF)
-    return (grad[...].astype(F32) + mm_t(change, weight)).astype(BF)
+    return (total * scale * slope[...]).astype(BF)
 
 
 def middle_back(near, receive, slope, weight, grad, back_t, *refs, ins, layer, scale, size):
     rows = arrived(refs[:ins], size)
-    change = layer_back(near, receive, rows, slope, weight[layer], grad, scale)
+    change = mm_t(layer_change(near, receive, rows, slope, scale), weight[layer])
+    change = (grad[...].astype(F32) + change).astype(BF)
     refs[ins][...] = change
     emit(refs[ins + 1 :], mm(back_t[...], change), size)
 
 
-def last_back(near, receive, slope, weight, grad, grid_rim_t, *refs, ins, scale):
-    new_grad, outer, inner = refs[ins:]
+def last_local(own_t, grad, grid_rim_t, near, rim_near):
+    near[...] = mm(own_t[...], grad[...])
+    rim_near[...] = mm(grid_rim_t[...], grad[...])
+
+
+def last_back(near, rim_near, receive, slope, weight, grid_rim_t, *refs, ins, scale):
+    kept, outer, inner = refs[ins:]
     rows = arrived(refs[:ins], refs[0].shape[0])
-    change = layer_back(near, receive, rows, slope, weight[0], grad, scale)
-    new_grad[...] = change
-    back = mm(grid_rim_t[...], change).astype(BF)
+    change = layer_change(near, receive, rows, slope, scale)
+    kept[...] = change
+    back = rim_near[...] + mm_t(mm(grid_rim_t[...], change).astype(BF), weight[0])
+    back = back.astype(BF)
     outer[...] = back[: outer.shape[0]]
     inner[...] = back[outer.shape[0] :]
 
@@ -327,26 +336,33 @@
     token[...] = jnp.zeros(token.shape, F32)
 
 
-def grid_local(own_t, grad, lists, slope, weight, cotangent, base, table, slope_rows, mesh_grad):
-    me = lax.axis_index("dom")
-    mesh_grad[...] = grad[...]
-    rows = own_t.shape[0]
+def halo_tables(lists, slope, table, slope_rows):
     size = lists.shape[2]
-    for k, wanted in enumerate(pair_order(lists, me)):
-        table[:, k * size : (k + 1) * size] = pick(rows, wanted)
+    for k, wanted in enumerate(pair_order(lists, lax.axis_index("dom"))):
+        table[:, k * size : (k + 1) * size] = pick(table.shape[0], wanted)
     slope_rows[...] = t_mm(table[...], slope[...])
-    change = (mm(own_t[...], grad[...]) * slope[...].astype(F32)).astype(BF)
-    base[...] = cotangent[...].astype(F32) + mm_t(change, weight[...])
+
+
+def grid_local(own_t, grad, change, mesh_weight, slope, weight, cotangent, base, mesh_grad):
+    whole = (grad[...].astype(F32) + mm_t(change[...], mesh_weight[0])).astype(BF)
+    mesh_grad[...] = whole
+    spread = (mm(own_t[...], whole) * slope[...].astype(F32)).astype(BF)
+    base[...] = cotangent[...].astype(F32) + mm_t(spread, weight[...])
 
 
 def grid_back(base, table, slope_rows, weight, outer_in, inner_in, output, staging, sems):
     returned = jnp.concatenate([outer_in[...], inner_in[...]], axis=0).astype(F32)
-    change = mm_t((returned * slope_rows[...]).astype(BF), weight[...]).astype(BF)
+    returned = (returned * slope_rows[...]).astype(BF)
+    half = weight.shape[0] // 2
     copies = []
-    for i, part in enumerate(row_chunks(base.shape[0])):
-        staging[part] = (base[part] + mm(table[part], change)).astype(BF)
-        copies.append(pltpu.make_async_copy(staging.at[part], output.at[part], sems.at[i]))
-        copies[-1].start()
+    for columns in (pl.ds(0, half), pl.ds(half, half)):
+        change = mm_t(returned, weight[columns]).astype(BF)
+        for rows in row_chunks(base.shape[0])[:: CHUNKS // 2]:
+            rows = pl.ds(rows.start, base.shape[0] // 2)
+            staging[rows, columns] = (base[rows, columns] + mm(table[rows], change)).astype(BF)
+            place = (rows, columns)
+            copies.append(pltpu.make_async_copy(staging.at[place], output.at[place], sems.at[len(copies)]))
+            copies[-1].start()
     for copy in copies:
         copy.wait()
 
@@ -483,17 +499,28 @@
         free=1,
     )
 
-    message, grad, *outs = call(
+    message, change, *outs = call(
         functools.partial(turn, ins=len(ins), scale=scale, size=halo),
         [state, state] + sends(2 * halo),
         2 * step,
         near, forth_t, decoder_weight, send, receive, back_t, decoder_near, *ins,
     )
     ins = exchange(outs, cap)
-    (near,) = call(back_local, [total], 6 * square(mesh_rows, mesh_rows), own_t, grad)
-
     outer_decoder, inner_decoder = ins[:2]
-    (near,) = call(back_local, [total], 6 * square(mesh_rows, mesh_rows), own_t, grad, ins[-1], free=1)
+    near, grad = call(
+        turn_local,
+        [total, state],
+        6 * square(mesh_rows, mesh_rows),
+        own_t, change, decoder_weight, ins[-1],
+        free=1,
+    )
+    table, slope_rows = call(
+        halo_tables,
+        [((grid_rows, 2 * ghalo), BF), ((2 * ghalo, width), F32)],
+        square(grid_rows, 2 * ghalo),
+        grid_halo_rows, grid_slope, ins[-1],
+        free=1,
+    )
     (base,) = call(
         decode_own,
         [((grid_rows, width), F32)],
@@ -506,11 +533,17 @@
         functools.partial(middle_back, ins=len(ins), layer=1, scale=scale, size=halo),
         [state] + sends(halo),
         step,
-        near, receive, slope_1, processor_weights, grad, back_t, *ins, base,
-        free=1,
+        near, receive, slope_1, processor_weights, grad, back_t, *ins, base, slope_rows,
+        free=2,
     )
     ins = exchange(outs, cap)
-    (near,) = call(back_local, [total], 6 * square(mesh_rows, mesh_rows), own_t, grad, ins[-1], free=1)
+    near, rim_near = call(
+        last_local,
+        [total, ((2 * ghalo, width), F32)],
+        6 * square(mesh_rows, mesh_rows),
+        own_t, grad, grid_rim_t, ins[-1],
+        free=1,
+    )
     output, token = call(
         decode_rim,
         [((grid_rows, width), BF), ((8, 128), F32)],
@@ -519,19 +552,19 @@
         free=1,
     )
 
-    grad, outer, inner = call(
+    change, outer, inner = call(
         functools.partial(last_back, ins=len(ins), scale=scale),
         [state, grid_rim, grid_rim],
         step,
-        near, receive, slope_0, processor_weights, grad, grid_rim_t, *ins, token,
+        near, rim_near, receive, slope_0, processor_weights, grid_rim_t, *ins, token,
         free=1,
     )
     outer_in, inner_in = across(outer), toggle(inner, 1)
-    base, table, slope_rows, mesh_grad = call(
+    base, mesh_grad = call(
         grid_local,
-        [((grid_rows, width), F32), ((grid_rows, 2 * ghalo), BF), ((2 * ghalo, width), F32), state],
+        [((grid_rows, width), F32), state],
         square(mesh_rows, grid_rows) + square(grid_rows, width),
-        grid_own_t, grad, grid_halo_rows, grid_slope, encoder_weight, cotangent,
+        grid_own_t, grad, change, processor_weights, grid_slope, encoder_weight, cotangent,
     )
     (grid_grad,) = call(
         grid_back,

time: 70.8 us -> 71 us (level)
  waiting for transfers between devices: 10.3 us -> 9.34 us
    ppermute x26, waiting for transfers between devices: 8.5 us -> 6.9 us  [toggle(): return lax.ppermute(value, 'dom', [(i, i ^ bits) for i in range(peers)])]
    pallas_call x21 -> x22, Pallas kernels: 20 us -> 20.6 us  [call(): pl.pallas_call(inner, out_shape=shapes, in_specs=[pl.BlockSpec(memory_spa...]
  transfers between devices with their start and end apart: 32 -> 32, of which waited for: 13 -> 12; matrix products, arithmetic and copies ran while one was open for 0% -> 0% of each run, Pallas kernels for 17% -> 17%
where the time goes in v14:
time: 71 us; the launch traced here: 70.8 us
  starting transfers between devices  39.1 us (55%)
  Pallas kernels  20.6 us (29%)
  waiting for transfers between devices  9.34 us (13%)
  between operations  1.13 us (2%)
  local copies, waits for them, and re-layouts  0.74 us (1%)
    ppermute x26, starting transfers between devices, toggle(): return lax.ppermute(value, 'dom', [(i, i ^ bits) for i in range(peers)])  25.5 us
    pallas_call x22, Pallas kernels, call(): pl.pallas_call(inner, out_shape=shapes, in_specs=[pl.BlockSpec(memory_spa...  20.6 us
    ppermute x6, starting transfers between devices, across(): return lax.ppermute(value, 'dom', pairs)  13.6 us
    ppermute x26, waiting for transfers between devices, toggle(): return lax.ppermute(value, 'dom', [(i, i ^ bits) for i in range(peers)])  6.9 us
    ppermute x6, waiting for transfers between devices, across(): return lax.ppermute(value, 'dom', pairs)  2.44 us
  transfers between devices with their start and end apart: 32, of which 12 were waited for; matrix products, arithmetic and copies ran while one was open for 0% of the time, Pallas kernels for 17%

profile of v14, /device:TPU:0, one launch (start us, length us, event | category | flops | bytes accessed | tf_op | source)
XLA Modules:
  0.0 70.8 jit_solution(10644309239312241864)
XLA Ops:
  0.7 2.2 %shard_map.139 = (bf16[64,512]{1,0:T(8,128)(2,1)}, bf16[64,512]{1,0:T(8,128)(2,1)}) custom-call(bf16[1024,512]{1,0:T(8,128)(2,1)} %refs_0_.2, s32[1,2,64]{2,1,0:T(2,128)} %refs_0_.3), custom_call_target="tpu_custom_call" | custom-call | flops 34359738368 | tf_op jit(solution)/shard_map/pallas_call | solution.py:83
  2.9 5.5 %collective-permute-start = (bf16[64,512]{1,0:T(8,128)(2,1)}, bf16[64,512]{1,0:T(8,128)(2,1)S(1)}, u32[]{:S(2)}, u32[]{:S(2)}) collective-permute-start(bf16[64,512]{1,0:T(8,128)(2,1)} %get-tuple-element.90), channel_id=1, source_target_pairs={{0,15},{1,2},{2,1},{3,4},{4,3},{5,6},{6,5},{7,8},{8,7},{9,10},{10,... | collective-permute-start | bytes 196616 | tf_op jit(solution)/shard_map/ppermute | solution.py:378
  9.9 1.9 %shard_map.140 = (f32[512,512]{1,0:T(8,128)S(1)}, bf16[1024,512]{1,0:T(8,128)(2,1)S(1)}, bf16[128,512]{1,0:T(8,128)(2,1)S(1)}, bf16[1024,512]{1,0:T(8,128)(2,1)S(1)}) custom-call(s32[4,512]{1,0:T(4,128)S(1)} %bitcast.8, bf16[512,512]{1,0:T(8,128)(2,1)S(1)} %copy-done.1, bf16[1024,512]{1,0:T(8,128)(2,1)S(1)} %copy-done.2, bf16[512,512]{1,0:T(8,128)(2,1)S(1)} %copy-done.5), custom_call_target="tpu_custom_call" | custom-call | flops 2147483648 | bytes 5382144 | tf_op jit(solution)/shard_map/pallas_call | solution.py:83
  12.8 1.3 %collective-permute-start.2 = (bf16[16,512]{1,0:T(8,128)(2,1)S(1)}, bf16[16,512]{1,0:T(8,128)(2,1)S(1)}, u32[]{:S(2)}, u32[]{:S(2)}) collective-permute-start(bf16[16,512]{1,0:T(8,128)(2,1)S(1)} %get-tuple-element.94), channel_id=1, source_target_pairs={{0,12},{1,13},{2,14},{3,15},{4,8},{5,9},{6,10},{7,11},{8,4},{9,5},... | collective-permute-start | bytes 49160 | tf_op jit(solution)/shard_map/ppermute | solution.py:372
  14.1 3.2 %collective-permute-start.4 = (bf16[16,512]{1,0:T(8,128)(2,1)S(1)}, bf16[16,512]{1,0:T(8,128)(2,1)S(1)}, u32[]{:S(2)}, u32[]{:S(2)}) collective-permute-start(bf16[16,512]{1,0:T(8,128)(2,1)S(1)} %get-tuple-element.96), channel_id=1, source_target_pairs={{0,4},{1,5},{2,6},{3,7},{4,0},{5,1},{6,2},{7,3},{8,12},{9,13},{10,... | collective-permute-start | bytes 49160 | tf_op jit(solution)/shard_map/ppermute | solution.py:372
  17.3 2.3 %collective-permute-start.5 = (bf16[64,512]{1,0:T(8,128)(2,1)S(1)}, bf16[64,512]{1,0:T(8,128)(2,1)S(1)}, u32[]{:S(2)}, u32[]{:S(2)}) collective-permute-start(bf16[64,512]{1,0:T(8,128)(2,1)S(1)} %get-tuple-element.105), channel_id=1, source_target_pairs={{0,15},{1,2},{2,1},{3,4},{4,3},{5,6},{6,5},{7,8},{8,7},{9,10},{10,... | collective-permute-start | bytes 196616 | tf_op jit(solution)/shard_map/ppermute | solution.py:378
  20.2 1.4 %collective-permute-start.6 = (bf16[80,512]{1,0:T(8,128)(2,1)S(1)}, bf16[80,512]{1,0:T(8,128)(2,1)S(1)}, u32[]{:S(2)}, u32[]{:S(2)}) collective-permute-start(bf16[80,512]{1,0:T(8,128)(2,1)S(1)} %get-tuple-element.106), channel_id=1, source_target_pairs={{0,1},{1,0},{2,3},{3,2},{4,5},{5,4},{6,7},{7,6},{8,9},{9,8},{10,11... | collective-permute-start | bytes 245768 | tf_op jit(solution)/shard_map/ppermute | solution.py:372
  24.7 2.3 %collective-permute-start.9 = (bf16[16,512]{1,0:T(8,128)(2,1)S(1)}, bf16[16,512]{1,0:T(8,128)(2,1)S(1)}, u32[]{:S(2)}, u32[]{:S(2)}) collective-permute-start(bf16[16,512]{1,0:T(8,128)(2,1)S(1)} %get-tuple-element.112), channel_id=1, source_target_pairs={{0,12},{1,13},{2,14},{3,15},{4,8},{5,9},{6,10},{7,11},{8,4},{9,5},... | collective-permute-start | bytes 49160 | tf_op jit(solution)/shard_map/ppermute | solution.py:372
  27.5 1.7 %collective-permute-start.11 = (bf16[16,512]{1,0:T(8,128)(2,1)S(1)}, bf16[16,512]{1,0:T(8,128)(2,1)S(1)}, u32[]{:S(2)}, u32[]{:S(2)}) collective-permute-start(bf16[16,512]{1,0:T(8,128)(2,1)S(1)} %get-tuple-element.114), channel_id=1, source_target_pairs={{0,4},{1,5},{2,6},{3,7},{4,0},{5,1},{6,2},{7,3},{8,12},{9,13},{10,... | collective-permute-start | bytes 49160 | tf_op jit(solution)/shard_map/ppermute | solution.py:372
  29.2 1.6 %collective-permute-start.12 = (bf16[128,512]{1,0:T(8,128)(2,1)S(1)}, bf16[128,512]{1,0:T(8,128)(2,1)S(1)}, u32[]{:S(2)}, u32[]{:S(2)}) collective-permute-start(bf16[128,512]{1,0:T(8,128)(2,1)S(1)} %get-tuple-element.120), channel_id=1, source_target_pairs={{0,15},{1,2},{2,1},{3,4},{4,3},{5,6},{6,5},{7,8},{8,7},{9,10},{10,... | collective-permute-start | bytes 393224 | tf_op jit(solution)/shard_map/ppermute | solution.py:378
  31.9 1.1 %collective-permute-start.15 = (bf16[16,512]{1,0:T(8,128)(2,1)S(1)}, bf16[16,512]{1,0:T(8,128)(2,1)S(1)}, u32[]{:S(2)}, u32[]{:S(2)}) collective-permute-start(bf16[16,512]{1,0:T(8,128)(2,1)S(1)} %get-tuple-element.123), channel_id=1, source_target_pairs={{0,2},{1,3},{2,0},{3,1},{4,6},{5,7},{6,4},{7,5},{8,10},{9,11},{10,... | collective-permute-start | bytes 49160 | tf_op jit(solution)/shard_map/ppermute | solution.py:372
  34.7 1.9 %collective-permute-done.14.refs_2_ = bf16[16,512]{1,0:T(8,128)(2,1)S(1)} collective-permute-done((bf16[16,512]{1,0:T(8,128)(2,1)S(1)}, bf16[16,512]{1,0:T(8,128)(2,1)S(1)}, u32[]{:S(2)}, u32[]{:S(2)}) %collective-permute-start.14) | collective-permute-done | bytes 16416 | tf_op jit(solution)/shard_map/ppermute | solution.py:372
  36.7 1.4 %shard_map.149 = (bf16[512,512]{1,0:T(8,128)(2,1)S(1)}, bf16[512,512]{1,0:T(8,128)(2,1)S(1)}, bf16[128,512]{1,0:T(8,128)(2,1)S(1)}, bf16[128,512]{1,0:T(8,128)(2...) custom-call(f32[512,512]{1,0:T(8,128)S(1)} %get-tuple-element.116.ne, ...), custom_call_target="tpu_custom_call" | custom-call | flops 1610612736 | bytes 5111808 | tf_op jit(solution)/shard_map/pallas_call | solution.py:83
  38.1 1.5 %collective-permute-start.16 = (bf16[16,512]{1,0:T(8,128)(2,1)S(1)}, bf16[16,512]{1,0:T(8,128)(2,1)S(1)}, u32[]{:S(2)}, u32[]{:S(2)}) collective-permute-start(bf16[16,512]{1,0:T(8,128)(2,1)S(1)} %get-tuple-element.127), channel_id=1, source_target_pairs={{0,12},{1,13},{2,14},{3,15},{4,8},{5,9},{6,10},{7,11},{8,4},{9,5},... | collective-permute-start | bytes 49160 | tf_op jit(solution)/shard_map/ppermute | solution.py:372
  39.9 2.7 %collective-permute-start.18 = (bf16[16,512]{1,0:T(8,128)(2,1)S(1)}, bf16[16,512]{1,0:T(8,128)(2,1)S(1)}, u32[]{:S(2)}, u32[]{:S(2)}) collective-permute-start(bf16[16,512]{1,0:T(8,128)(2,1)S(1)} %get-tuple-element.129), channel_id=1, source_target_pairs={{0,4},{1,5},{2,6},{3,7},{4,0},{5,1},{6,2},{7,3},{8,12},{9,13},{10,... | collective-permute-start | bytes 49160 | tf_op jit(solution)/shard_map/ppermute | solution.py:372
  44.7 1.2 %collective-permute-start.22 = (bf16[16,512]{1,0:T(8,128)(2,1)S(1)}, bf16[16,512]{1,0:T(8,128)(2,1)S(1)}, u32[]{:S(2)}, u32[]{:S(2)}) collective-permute-start(bf16[16,512]{1,0:T(8,128)(2,1)S(1)} %get-tuple-element.139), channel_id=1, source_target_pairs={{0,2},{1,3},{2,0},{3,1},{4,6},{5,7},{6,4},{7,5},{8,10},{9,11},{10,... | collective-permute-start | bytes 49160 | tf_op jit(solution)/shard_map/ppermute | solution.py:372
  48.8 1.2 %collective-permute-done.22.refs_9_ = bf16[16,512]{1,0:T(8,128)(2,1)S(1)} collective-permute-done((bf16[16,512]{1,0:T(8,128)(2,1)S(1)}, bf16[16,512]{1,0:T(8,128)(2,1)S(1)}, u32[]{:S(2)}, u32[]{:S(2)}) %collective-permute-start.22) | collective-permute-done | bytes 16416 | tf_op jit(solution)/shard_map/ppermute | solution.py:372
  50.8 1.6 %collective-permute-start.23 = (bf16[16,512]{1,0:T(8,128)(2,1)S(1)}, bf16[16,512]{1,0:T(8,128)(2,1)S(1)}, u32[]{:S(2)}, u32[]{:S(2)}) collective-permute-start(bf16[16,512]{1,0:T(8,128)(2,1)S(1)} %get-tuple-element.144), channel_id=1, source_target_pairs={{0,12},{1,13},{2,14},{3,15},{4,8},{5,9},{6,10},{7,11},{8,4},{9,5},... | collective-permute-start | bytes 49160 | tf_op jit(solution)/shard_map/ppermute | solution.py:372
  53.0 2.2 %collective-permute-start.25 = (bf16[16,512]{1,0:T(8,128)(2,1)S(1)}, bf16[16,512]{1,0:T(8,128)(2,1)S(1)}, u32[]{:S(2)}, u32[]{:S(2)}) collective-permute-start(bf16[16,512]{1,0:T(8,128)(2,1)S(1)} %get-tuple-element.146), channel_id=1, source_target_pairs={{0,4},{1,5},{2,6},{3,7},{4,0},{5,1},{6,2},{7,3},{8,12},{9,13},{10,... | collective-permute-start | bytes 49160 | tf_op jit(solution)/shard_map/ppermute | solution.py:372
  59.7 1.6 %shard_map.156 = (bf16[1024,512]{1,0:T(8,128)(2,1)}, f32[8,128]{1,0:T(8,128)S(1)}) custom-call(f32[1024,512]{1,0:T(8,128)S(1)} %shard_map.151.refs_11_.refs_0_, bf16[128,1024]{1,0:T(8,128)(2,1)S(1)} %get-tuple-element.131.refs_1_, bf16[128,512]{1,0:T(8,128)(2,1)S(1)} %collective-permute-done.19.refs_6_.refs_2_, ...), custom_call_target="tpu_custom_call" | custom-call | flops 134217728 | bytes 3706880 | tf_op jit(solution)/shard_map/pallas_call | solution.py:83
  62.6 2.4 %collective-permute-start.30 = (bf16[64,512]{1,0:T(8,128)(2,1)S(1)}, bf16[64,512]{1,0:T(8,128)(2,1)S(1)}, u32[]{:S(2)}, u32[]{:S(2)}) collective-permute-start(bf16[64,512]{1,0:T(8,128)(2,1)S(1)} %get-tuple-element.162), channel_id=1, source_target_pairs={{0,15},{1,2},{2,1},{3,4},{4,3},{5,6},{6,5},{7,8},{8,7},{9,10},{10,... | collective-permute-start | bytes 196616 | tf_op jit(solution)/shard_map/ppermute | solution.py:378
  65.0 1.6 %shard_map.159 = (f32[1024,512]{1,0:T(8,128)S(1)}, bf16[512,512]{1,0:T(8,128)(2,1)}) custom-call(bf16[1024,512]{1,0:T(8,128)(2,1)S(1)} %get-tuple-element.149.own_t, bf16[512,512]{1,0:T(8,128)(2,1)S(1)} %get-tuple-element.150.refs_1_.grad, bf16[512,512]{1,0:T(8,128)(2,1)S(1)} %get-tuple-element.159.change, bf16[2,512,512]{2,1,0:T(8,128)(2,1)S(1)} %copy-done, ...), custom_call_target="tpu_custom_call" | custom-call | flops 1073741824 | bytes 8388608 | tf_op jit(solution)/shard_map/pallas_call | solution.py:83
  66.6 2.4 %collective-permute-done.30.outer_in = bf16[64,512]{1,0:T(8,128)(2,1)S(1)} collective-permute-done((bf16[64,512]{1,0:T(8,128)(2,1)S(1)}, bf16[64,512]{1,0:T(8,128)(2,1)S(1)}, u32[]{:S(2)}, u32[]{:S(2)}) %collective-permute-start.30) | collective-permute-done | bytes 65568 | tf_op jit(solution)/shard_map/ppermute | solution.py:378
  69.0 1.7 %shard_map.160 = bf16[1024,512]{1,0:T(8,128)(2,1)} custom-call(f32[1024,512]{1,0:T(8,128)S(1)} %get-tuple-element.160.base, bf16[1024,128]{1,0:T(8,128)(2,1)S(1)} %get-tuple-element.161.table, f32[128,512]{1,0:T(8,128)S(1)} %get-tuple-element.141.refs_12_.slope_rows, bf16[512,512]{1,0:T(8,128)(2,1)S(1)} %copy-done.1, ...), custom_call_target="tpu_custom_call" | custom-call | flops 268435456 | bytes 4325376 | tf_op jit(solution)/shard_map/pallas_call | solution.py:83
  (86 shorter events, 21.7 us)
Async XLA Ops:
  2.9 9.0 %collective-permute-start = (bf16[64,512]{1,0:T(8,128)(2,1)}, bf16[64,512]{1,0:T(8,128)(2,1)S(1)}, u32[]{:S(2)}, u32[]{:S(2)}) collective-permute-start(bf16[64,512]{1,0:T(8,128)(2,1)} %get-tuple-element.90), channel_id=1, source_target_pairs={{0,15},{1,2},{2,1},{3,4},{4,3},{5,6},{6,5},{7,8},{8,7},{9,10},{10,... | collective-permute-start | bytes 196616 | tf_op jit(solution)/shard_map/ppermute | solution.py:378
  12.8 6.7 %collective-permute-start.2 = (bf16[16,512]{1,0:T(8,128)(2,1)S(1)}, bf16[16,512]{1,0:T(8,128)(2,1)S(1)}, u32[]{:S(2)}, u32[]{:S(2)}) collective-permute-start(bf16[16,512]{1,0:T(8,128)(2,1)S(1)} %get-tuple-element.94), channel_id=1, source_target_pairs={{0,12},{1,13},{2,14},{3,15},{4,8},{5,9},{6,10},{7,11},{8,4},{9,5},... | collective-permute-start | bytes 49160 | tf_op jit(solution)/shard_map/ppermute | solution.py:372
  14.1 5.4 %collective-permute-start.3 = (bf16[16,512]{1,0:T(8,128)(2,1)S(1)}, bf16[16,512]{1,0:T(8,128)(2,1)S(1)}, u32[]{:S(2)}, u32[]{:S(2)}) collective-permute-start(bf16[16,512]{1,0:T(8,128)(2,1)S(1)} %get-tuple-element.95), channel_id=1, source_target_pairs={{0,8},{1,9},{2,10},{3,11},{4,12},{5,13},{6,14},{7,15},{8,0},{9,1},... | collective-permute-start | bytes 49160 | tf_op jit(solution)/shard_map/ppermute | solution.py:372
  14.1 5.4 %collective-permute-start.4 = (bf16[16,512]{1,0:T(8,128)(2,1)S(1)}, bf16[16,512]{1,0:T(8,128)(2,1)S(1)}, u32[]{:S(2)}, u32[]{:S(2)}) collective-permute-start(bf16[16,512]{1,0:T(8,128)(2,1)S(1)} %get-tuple-element.96), channel_id=1, source_target_pairs={{0,4},{1,5},{2,6},{3,7},{4,0},{5,1},{6,2},{7,3},{8,12},{9,13},{10,... | collective-permute-start | bytes 49160 | tf_op jit(solution)/shard_map/ppermute | solution.py:372
  17.3 6.7 %collective-permute-start.5 = (bf16[64,512]{1,0:T(8,128)(2,1)S(1)}, bf16[64,512]{1,0:T(8,128)(2,1)S(1)}, u32[]{:S(2)}, u32[]{:S(2)}) collective-permute-start(bf16[64,512]{1,0:T(8,128)(2,1)S(1)} %get-tuple-element.105), channel_id=1, source_target_pairs={{0,15},{1,2},{2,1},{3,4},{4,3},{5,6},{6,5},{7,8},{8,7},{9,10},{10,... | collective-permute-start | bytes 196616 | tf_op jit(solution)/shard_map/ppermute | solution.py:378
  24.7 6.0 %collective-permute-start.9 = (bf16[16,512]{1,0:T(8,128)(2,1)S(1)}, bf16[16,512]{1,0:T(8,128)(2,1)S(1)}, u32[]{:S(2)}, u32[]{:S(2)}) collective-permute-start(bf16[16,512]{1,0:T(8,128)(2,1)S(1)} %get-tuple-element.112), channel_id=1, source_target_pairs={{0,12},{1,13},{2,14},{3,15},{4,8},{5,9},{6,10},{7,11},{8,4},{9,5},... | collective-permute-start | bytes 49160 | tf_op jit(solution)/shard_map/ppermute | solution.py:372
  27.1 4.6 %collective-permute-start.10 = (bf16[16,512]{1,0:T(8,128)(2,1)S(1)}, bf16[16,512]{1,0:T(8,128)(2,1)S(1)}, u32[]{:S(2)}, u32[]{:S(2)}) collective-permute-start(bf16[16,512]{1,0:T(8,128)(2,1)S(1)} %get-tuple-element.113), channel_id=1, source_target_pairs={{0,8},{1,9},{2,10},{3,11},{4,12},{5,13},{6,14},{7,15},{8,0},{9,1},... | collective-permute-start | bytes 49160 | tf_op jit(solution)/shard_map/ppermute | solution.py:372
  27.5 4.2 %collective-permute-start.11 = (bf16[16,512]{1,0:T(8,128)(2,1)S(1)}, bf16[16,512]{1,0:T(8,128)(2,1)S(1)}, u32[]{:S(2)}, u32[]{:S(2)}) collective-permute-start(bf16[16,512]{1,0:T(8,128)(2,1)S(1)} %get-tuple-element.114), channel_id=1, source_target_pairs={{0,4},{1,5},{2,6},{3,7},{4,0},{5,1},{6,2},{7,3},{8,12},{9,13},{10,... | collective-permute-start | bytes 49160 | tf_op jit(solution)/shard_map/ppermute | solution.py:372
  29.2 7.5 %collective-permute-start.12 = (bf16[128,512]{1,0:T(8,128)(2,1)S(1)}, bf16[128,512]{1,0:T(8,128)(2,1)S(1)}, u32[]{:S(2)}, u32[]{:S(2)}) collective-permute-start(bf16[128,512]{1,0:T(8,128)(2,1)S(1)} %get-tuple-element.120), channel_id=1, source_target_pairs={{0,15},{1,2},{2,1},{3,4},{4,3},{5,6},{6,5},{7,8},{8,7},{9,10},{10,... | collective-permute-start | bytes 393224 | tf_op jit(solution)/shard_map/ppermute | solution.py:378
  31.9 4.7 %collective-permute-start.14 = (bf16[16,512]{1,0:T(8,128)(2,1)S(1)}, bf16[16,512]{1,0:T(8,128)(2,1)S(1)}, u32[]{:S(2)}, u32[]{:S(2)}) collective-permute-start(bf16[16,512]{1,0:T(8,128)(2,1)S(1)} %get-tuple-element.122), channel_id=1, source_target_pairs={{0,3},{1,2},{2,1},{3,0},{4,7},{5,6},{6,5},{7,4},{8,11},{9,10},{10,... | collective-permute-start | bytes 49160 | tf_op jit(solution)/shard_map/ppermute | solution.py:372
  31.9 4.8 %collective-permute-start.15 = (bf16[16,512]{1,0:T(8,128)(2,1)S(1)}, bf16[16,512]{1,0:T(8,128)(2,1)S(1)}, u32[]{:S(2)}, u32[]{:S(2)}) collective-permute-start(bf16[16,512]{1,0:T(8,128)(2,1)S(1)} %get-tuple-element.123), channel_id=1, source_target_pairs={{0,2},{1,3},{2,0},{3,1},{4,6},{5,7},{6,4},{7,5},{8,10},{9,11},{10,... | collective-permute-start | bytes 49160 | tf_op jit(solution)/shard_map/ppermute | solution.py:372
  38.1 5.6 %collective-permute-start.16 = (bf16[16,512]{1,0:T(8,128)(2,1)S(1)}, bf16[16,512]{1,0:T(8,128)(2,1)S(1)}, u32[]{:S(2)}, u32[]{:S(2)}) collective-permute-start(bf16[16,512]{1,0:T(8,128)(2,1)S(1)} %get-tuple-element.127), channel_id=1, source_target_pairs={{0,12},{1,13},{2,14},{3,15},{4,8},{5,9},{6,10},{7,11},{8,4},{9,5},... | collective-permute-start | bytes 49160 | tf_op jit(solution)/shard_map/ppermute | solution.py:372
  39.7 4.7 %collective-permute-start.17 = (bf16[16,512]{1,0:T(8,128)(2,1)S(1)}, bf16[16,512]{1,0:T(8,128)(2,1)S(1)}, u32[]{:S(2)}, u32[]{:S(2)}) collective-permute-start(bf16[16,512]{1,0:T(8,128)(2,1)S(1)} %get-tuple-element.128), channel_id=1, source_target_pairs={{0,8},{1,9},{2,10},{3,11},{4,12},{5,13},{6,14},{7,15},{8,0},{9,1},... | collective-permute-start | bytes 49160 | tf_op jit(solution)/shard_map/ppermute | solution.py:372
  39.9 4.5 %collective-permute-start.18 = (bf16[16,512]{1,0:T(8,128)(2,1)S(1)}, bf16[16,512]{1,0:T(8,128)(2,1)S(1)}, u32[]{:S(2)}, u32[]{:S(2)}) collective-permute-start(bf16[16,512]{1,0:T(8,128)(2,1)S(1)} %get-tuple-element.129), channel_id=1, source_target_pairs={{0,4},{1,5},{2,6},{3,7},{4,0},{5,1},{6,2},{7,3},{8,12},{9,13},{10,... | collective-permute-start | bytes 49160 | tf_op jit(solution)/shard_map/ppermute | solution.py:372
  42.6 7.4 %collective-permute-start.19 = (bf16[128,512]{1,0:T(8,128)(2,1)S(1)}, bf16[128,512]{1,0:T(8,128)(2,1)S(1)}, u32[]{:S(2)}, u32[]{:S(2)}) collective-permute-start(bf16[128,512]{1,0:T(8,128)(2,1)S(1)} %get-tuple-element.132), channel_id=1, source_target_pairs={{0,15},{1,2},{2,1},{3,4},{4,3},{5,6},{6,5},{7,8},{8,7},{9,10},{10,... | collective-permute-start | bytes 393224 | tf_op jit(solution)/shard_map/ppermute | solution.py:378
  44.6 4.2 %collective-permute-start.21 = (bf16[16,512]{1,0:T(8,128)(2,1)S(1)}, bf16[16,512]{1,0:T(8,128)(2,1)S(1)}, u32[]{:S(2)}, u32[]{:S(2)}) collective-permute-start(bf16[16,512]{1,0:T(8,128)(2,1)S(1)} %get-tuple-element.138), channel_id=1, source_target_pairs={{0,3},{1,2},{2,1},{3,0},{4,7},{5,6},{6,5},{7,4},{8,11},{9,10},{10,... | collective-permute-start | bytes 49160 | tf_op jit(solution)/shard_map/ppermute | solution.py:372
  44.7 5.3 %collective-permute-start.22 = (bf16[16,512]{1,0:T(8,128)(2,1)S(1)}, bf16[16,512]{1,0:T(8,128)(2,1)S(1)}, u32[]{:S(2)}, u32[]{:S(2)}) collective-permute-start(bf16[16,512]{1,0:T(8,128)(2,1)S(1)} %get-tuple-element.139), channel_id=1, source_target_pairs={{0,2},{1,3},{2,0},{3,1},{4,6},{5,7},{6,4},{7,5},{8,10},{9,11},{10,... | collective-permute-start | bytes 49160 | tf_op jit(solution)/shard_map/ppermute | solution.py:372
  50.8 5.7 %collective-permute-start.23 = (bf16[16,512]{1,0:T(8,128)(2,1)S(1)}, bf16[16,512]{1,0:T(8,128)(2,1)S(1)}, u32[]{:S(2)}, u32[]{:S(2)}) collective-permute-start(bf16[16,512]{1,0:T(8,128)(2,1)S(1)} %get-tuple-element.144), channel_id=1, source_target_pairs={{0,12},{1,13},{2,14},{3,15},{4,8},{5,9},{6,10},{7,11},{8,4},{9,5},... | collective-permute-start | bytes 49160 | tf_op jit(solution)/shard_map/ppermute | solution.py:372
  52.4 4.7 %collective-permute-start.24 = (bf16[16,512]{1,0:T(8,128)(2,1)S(1)}, bf16[16,512]{1,0:T(8,128)(2,1)S(1)}, u32[]{:S(2)}, u32[]{:S(2)}) collective-permute-start(bf16[16,512]{1,0:T(8,128)(2,1)S(1)} %get-tuple-element.145), channel_id=1, source_target_pairs={{0,8},{1,9},{2,10},{3,11},{4,12},{5,13},{6,14},{7,15},{8,0},{9,1},... | collective-permute-start | bytes 49160 | tf_op jit(solution)/shard_map/ppermute | solution.py:372
  53.0 4.2 %collective-permute-start.25 = (bf16[16,512]{1,0:T(8,128)(2,1)S(1)}, bf16[16,512]{1,0:T(8,128)(2,1)S(1)}, u32[]{:S(2)}, u32[]{:S(2)}) collective-permute-start(bf16[16,512]{1,0:T(8,128)(2,1)S(1)} %get-tuple-element.146), channel_id=1, source_target_pairs={{0,4},{1,5},{2,6},{3,7},{4,0},{5,1},{6,2},{7,3},{8,12},{9,13},{10,... | collective-permute-start | bytes 49160 | tf_op jit(solution)/shard_map/ppermute | solution.py:372
  55.2 6.7 %collective-permute-start.26 = (bf16[64,512]{1,0:T(8,128)(2,1)S(1)}, bf16[64,512]{1,0:T(8,128)(2,1)S(1)}, u32[]{:S(2)}, u32[]{:S(2)}) collective-permute-start(bf16[64,512]{1,0:T(8,128)(2,1)S(1)} %get-tuple-element.154), channel_id=1, source_target_pairs={{0,15},{1,2},{2,1},{3,4},{4,3},{5,6},{6,5},{7,8},{8,7},{9,10},{10,... | collective-permute-start | bytes 196616 | tf_op jit(solution)/shard_map/ppermute | solution.py:378
  57.3 4.1 %collective-permute-start.28 = (bf16[16,512]{1,0:T(8,128)(2,1)S(1)}, bf16[16,512]{1,0:T(8,128)(2,1)S(1)}, u32[]{:S(2)}, u32[]{:S(2)}) collective-permute-start(bf16[16,512]{1,0:T(8,128)(2,1)S(1)} %get-tuple-element.156), channel_id=1, source_target_pairs={{0,3},{1,2},{2,1},{3,0},{4,7},{5,6},{6,5},{7,4},{8,11},{9,10},{10,... | collective-permute-start | bytes 49160 | tf_op jit(solution)/shard_map/ppermute | solution.py:372
  57.4 4.5 %collective-permute-start.29 = (bf16[16,512]{1,0:T(8,128)(2,1)S(1)}, bf16[16,512]{1,0:T(8,128)(2,1)S(1)}, u32[]{:S(2)}, u32[]{:S(2)}) collective-permute-start(bf16[16,512]{1,0:T(8,128)(2,1)S(1)} %get-tuple-element.157), channel_id=1, source_target_pairs={{0,2},{1,3},{2,0},{3,1},{4,6},{5,7},{6,4},{7,5},{8,10},{9,11},{10,... | collective-permute-start | bytes 49160 | tf_op jit(solution)/shard_map/ppermute | solution.py:372
  62.6 6.5 %collective-permute-start.30 = (bf16[64,512]{1,0:T(8,128)(2,1)S(1)}, bf16[64,512]{1,0:T(8,128)(2,1)S(1)}, u32[]{:S(2)}, u32[]{:S(2)}) collective-permute-start(bf16[64,512]{1,0:T(8,128)(2,1)S(1)} %get-tuple-element.162), channel_id=1, source_target_pairs={{0,15},{1,2},{2,1},{3,4},{4,3},{5,6},{6,5},{7,8},{8,7},{9,10},{10,... | collective-permute-start | bytes 196616 | tf_op jit(solution)/shard_map/ppermute | solution.py:378
  (20 other events, 67.6 us)

commit v15 on v12

--- a/solution.py
+++ b/solution.py
@@ -14,6 +14,7 @@
 PLANE = 4
 STAGED = 16
 CHUNKS = 4
+Z_ORDER = (2, 3, 1)
 
 
 def mm(a, b):
@@ -225,7 +226,7 @@
 
 def shuffle(inner, own, *refs):
     columns = STAGED // PLANE
-    parts = [own[...]] + [ref[...] for ref in refs[: columns - 1][::-1]]
+    parts = [own[...]] + [refs[Z_ORDER.index(m)][...] for m in range(1, columns)]
     rows = jnp.concatenate(parts, axis=0)
     outs = refs[columns - 1 :]
     count = rows.shape[0]
@@ -372,7 +373,7 @@
         return [across(outer), toggle(inner, 1), blocks.reshape(-1, width)]
     outer, inner, own, *rest = outs
     columns = STAGED // PLANE
-    moved = [toggle(rest[m - 1], m * PLANE) for m in reversed(range(1, columns))]
+    moved = [toggle(rest[m - 1], m * PLANE) for m in Z_ORDER]
     outer_in = across(outer)
     block = columns * cap
     blocks = call(

time: 70.8 us -> 68.2 us (0.963)
  starting transfers between devices: 38.5 us -> 34.6 us
  waiting for transfers between devices: 10.3 us -> 11.7 us
    ppermute x26, starting transfers between devices: 25.5 us -> 21.9 us  [toggle(): return lax.ppermute(value, 'dom', [(i, i ^ bits) for i in range(peers)])]
    ppermute x26, waiting for transfers between devices: 8.5 us -> 9.7 us  [toggle(): return lax.ppermute(value, 'dom', [(i, i ^ bits) for i in range(peers)])]
  transfers between devices with their start and end apart: 32 -> 32, of which waited for: 13 -> 17; matrix products, arithmetic and copies ran while one was open for 0% -> 0% of each run, Pallas kernels for 17% -> 17%
where the time goes in v15:
time: 68.2 us; the launch traced here: 68 us
  starting transfers between devices  34.6 us (51%)
  Pallas kernels  20 us (29%)
  waiting for transfers between devices  11.7 us (17%)
  between operations  0.93 us (1%)
  local copies, waits for them, and re-layouts  0.74 us (1%)
    ppermute x26, starting transfers between devices, toggle(): return lax.ppermute(value, 'dom', [(i, i ^ bits) for i in range(peers)])  21.9 us
    pallas_call x21, Pallas kernels, call(): pl.pallas_call(inner, out_shape=shapes, in_specs=[pl.BlockSpec(memory_spa...  20 us
    ppermute x6, starting transfers between devices, across(): return lax.ppermute(value, 'dom', pairs)  12.7 us
    ppermute x26, waiting for transfers between devices, toggle(): return lax.ppermute(value, 'dom', [(i, i ^ bits) for i in range(peers)])  9.7 us
    ppermute x6, waiting for transfers between devices, across(): return lax.ppermute(value, 'dom', pairs)  1.99 us
  transfers between devices with their start and end apart: 32, of which 17 were waited for; matrix products, arithmetic and copies ran while one was open for 0% of the time, Pallas kernels for 17%

profile of v15, /device:TPU:0, one launch (start us, length us, event | category | flops | bytes accessed | tf_op | source)
XLA Modules:
  0.0 68.0 jit_solution(2802827789701576982)
XLA Ops:
  0.7 2.2 %shard_map.139 = (bf16[64,512]{1,0:T(8,128)(2,1)}, bf16[64,512]{1,0:T(8,128)(2,1)}) custom-call(bf16[1024,512]{1,0:T(8,128)(2,1)} %refs_0_.1, s32[1,2,64]{2,1,0:T(2,128)} %lists.5), custom_call_target="tpu_custom_call" | custom-call | flops 34359738368 | tf_op jit(solution)/shard_map/pallas_call | solution.py:84
  2.9 5.5 %collective-permute-start = (bf16[64,512]{1,0:T(8,128)(2,1)}, bf16[64,512]{1,0:T(8,128)(2,1)S(1)}, u32[]{:S(2)}, u32[]{:S(2)}) collective-permute-start(bf16[64,512]{1,0:T(8,128)(2,1)} %get-tuple-element.86), channel_id=1, source_target_pairs={{0,15},{1,2},{2,1},{3,4},{4,3},{5,6},{6,5},{7,8},{8,7},{9,10},{10,... | collective-permute-start | bytes 196616 | tf_op jit(solution)/shard_map/ppermute | solution.py:363
  9.9 1.9 %shard_map.140 = (f32[512,512]{1,0:T(8,128)S(1)}, bf16[1024,512]{1,0:T(8,128)(2,1)S(1)}, bf16[128,512]{1,0:T(8,128)(2,1)S(1)}, bf16[1024,512]{1,0:T(8,128)(2,1)S(1)}) custom-call(s32[4,512]{1,0:T(4,128)S(1)} %bitcast.8, bf16[512,512]{1,0:T(8,128)(2,1)S(1)} %copy-done.1, bf16[1024,512]{1,0:T(8,128)(2,1)S(1)} %copy-done.3, bf16[512,512]{1,0:T(8,128)(2,1)S(1)} %copy-done.5), custom_call_target="tpu_custom_call" | custom-call | flops 2147483648 | bytes 5382144 | tf_op jit(solution)/shard_map/pallas_call | solution.py:84
  13.1 1.3 %collective-permute-start.3 = (bf16[16,512]{1,0:T(8,128)(2,1)S(1)}, bf16[16,512]{1,0:T(8,128)(2,1)S(1)}, u32[]{:S(2)}, u32[]{:S(2)}) collective-permute-start(bf16[16,512]{1,0:T(8,128)(2,1)S(1)} %get-tuple-element.91), channel_id=1, source_target_pairs={{0,12},{1,13},{2,14},{3,15},{4,8},{5,9},{6,10},{7,11},{8,4},{9,5},... | collective-permute-start | bytes 49160 | tf_op jit(solution)/shard_map/ppermute | solution.py:357
  14.4 1.9 %collective-permute-start.4 = (bf16[16,512]{1,0:T(8,128)(2,1)S(1)}, bf16[16,512]{1,0:T(8,128)(2,1)S(1)}, u32[]{:S(2)}, u32[]{:S(2)}) collective-permute-start(bf16[16,512]{1,0:T(8,128)(2,1)S(1)} %get-tuple-element.92), channel_id=1, source_target_pairs={{0,4},{1,5},{2,6},{3,7},{4,0},{5,1},{6,2},{7,3},{8,12},{9,13},{10,... | collective-permute-start | bytes 49160 | tf_op jit(solution)/shard_map/ppermute | solution.py:357
  16.4 2.3 %collective-permute-start.5 = (bf16[64,512]{1,0:T(8,128)(2,1)S(1)}, bf16[64,512]{1,0:T(8,128)(2,1)S(1)}, u32[]{:S(2)}, u32[]{:S(2)}) collective-permute-start(bf16[64,512]{1,0:T(8,128)(2,1)S(1)} %get-tuple-element.101), channel_id=1, source_target_pairs={{0,15},{1,2},{2,1},{3,4},{4,3},{5,6},{6,5},{7,8},{8,7},{9,10},{10,... | collective-permute-start | bytes 196616 | tf_op jit(solution)/shard_map/ppermute | solution.py:363
  24.1 1.3 %collective-permute-start.9 = (bf16[16,512]{1,0:T(8,128)(2,1)S(1)}, bf16[16,512]{1,0:T(8,128)(2,1)S(1)}, u32[]{:S(2)}, u32[]{:S(2)}) collective-permute-start(bf16[16,512]{1,0:T(8,128)(2,1)S(1)} %get-tuple-element.108), channel_id=1, source_target_pairs={{0,8},{1,9},{2,10},{3,11},{4,12},{5,13},{6,14},{7,15},{8,0},{9,1},... | collective-permute-start | bytes 49160 | tf_op jit(solution)/shard_map/ppermute | solution.py:357
  25.4 2.1 %collective-permute-start.10 = (bf16[16,512]{1,0:T(8,128)(2,1)S(1)}, bf16[16,512]{1,0:T(8,128)(2,1)S(1)}, u32[]{:S(2)}, u32[]{:S(2)}) collective-permute-start(bf16[16,512]{1,0:T(8,128)(2,1)S(1)} %get-tuple-element.109), channel_id=1, source_target_pairs={{0,12},{1,13},{2,14},{3,15},{4,8},{5,9},{6,10},{7,11},{8,4},{9,5},... | collective-permute-start | bytes 49160 | tf_op jit(solution)/shard_map/ppermute | solution.py:357
  27.6 1.6 %collective-permute-start.12 = (bf16[128,512]{1,0:T(8,128)(2,1)S(1)}, bf16[128,512]{1,0:T(8,128)(2,1)S(1)}, u32[]{:S(2)}, u32[]{:S(2)}) collective-permute-start(bf16[128,512]{1,0:T(8,128)(2,1)S(1)} %get-tuple-element.116), channel_id=1, source_target_pairs={{0,15},{1,2},{2,1},{3,4},{4,3},{5,6},{6,5},{7,8},{8,7},{9,10},{10,... | collective-permute-start | bytes 393224 | tf_op jit(solution)/shard_map/ppermute | solution.py:363
  29.2 1.7 %collective-permute-done.10.refs_1_ = bf16[16,512]{1,0:T(8,128)(2,1)S(1)} collective-permute-done((bf16[16,512]{1,0:T(8,128)(2,1)S(1)}, bf16[16,512]{1,0:T(8,128)(2,1)S(1)}, u32[]{:S(2)}, u32[]{:S(2)}) %collective-permute-start.10) | collective-permute-done | bytes 16416 | tf_op jit(solution)/shard_map/ppermute | solution.py:357
  31.9 1.4 %collective-permute-start.13 = (bf16[144,512]{1,0:T(8,128)(2,1)S(1)}, bf16[144,512]{1,0:T(8,128)(2,1)S(1)}, u32[]{:S(2)}, u32[]{:S(2)}) collective-permute-start(bf16[144,512]{1,0:T(8,128)(2,1)S(1)} %get-tuple-element.117), channel_id=1, source_target_pairs={{0,1},{1,0},{2,3},{3,2},{4,5},{5,4},{6,7},{7,6},{8,9},{9,8},{10,11... | collective-permute-start | bytes 442376 | tf_op jit(solution)/shard_map/ppermute | solution.py:357
  35.4 1.3 %shard_map.149 = (bf16[512,512]{1,0:T(8,128)(2,1)S(1)}, bf16[512,512]{1,0:T(8,128)(2,1)S(1)}, bf16[128,512]{1,0:T(8,128)(2,1)S(1)}, bf16[128,512]{1,0:T(8,128)(2...) custom-call(f32[512,512]{1,0:T(8,128)S(1)} %get-tuple-element.112.ne, ...), custom_call_target="tpu_custom_call" | custom-call | flops 1610612736 | bytes 5111808 | tf_op jit(solution)/shard_map/pallas_call | solution.py:84
  37.5 1.9 %collective-permute-start.17 = (bf16[16,512]{1,0:T(8,128)(2,1)S(1)}, bf16[16,512]{1,0:T(8,128)(2,1)S(1)}, u32[]{:S(2)}, u32[]{:S(2)}) collective-permute-start(bf16[16,512]{1,0:T(8,128)(2,1)S(1)} %get-tuple-element.124), channel_id=1, source_target_pairs={{0,12},{1,13},{2,14},{3,15},{4,8},{5,9},{6,10},{7,11},{8,4},{9,5},... | collective-permute-start | bytes 49160 | tf_op jit(solution)/shard_map/ppermute | solution.py:357
  41.5 1.6 %collective-permute-done.17.refs_1_ = bf16[16,512]{1,0:T(8,128)(2,1)S(1)} collective-permute-done((bf16[16,512]{1,0:T(8,128)(2,1)S(1)}, bf16[16,512]{1,0:T(8,128)(2,1)S(1)}, u32[]{:S(2)}, u32[]{:S(2)}) %collective-permute-start.17) | collective-permute-done | bytes 16416 | tf_op jit(solution)/shard_map/ppermute | solution.py:357
  43.5 1.1 %collective-permute-start.22 = (bf16[16,512]{1,0:T(8,128)(2,1)S(1)}, bf16[16,512]{1,0:T(8,128)(2,1)S(1)}, u32[]{:S(2)}, u32[]{:S(2)}) collective-permute-start(bf16[16,512]{1,0:T(8,128)(2,1)S(1)} %get-tuple-element.133), channel_id=1, source_target_pairs={{0,2},{1,3},{2,0},{3,1},{4,6},{5,7},{6,4},{7,5},{8,10},{9,11},{10,... | collective-permute-start | bytes 49160 | tf_op jit(solution)/shard_map/ppermute | solution.py:357
  46.5 1.3 %collective-permute-done.21.refs_8_ = bf16[16,512]{1,0:T(8,128)(2,1)S(1)} collective-permute-done((bf16[16,512]{1,0:T(8,128)(2,1)S(1)}, bf16[16,512]{1,0:T(8,128)(2,1)S(1)}, u32[]{:S(2)}, u32[]{:S(2)}) %collective-permute-start.21) | collective-permute-done | bytes 16416 | tf_op jit(solution)/shard_map/ppermute | solution.py:357
  49.3 2.1 %collective-permute-start.24 = (bf16[16,512]{1,0:T(8,128)(2,1)S(1)}, bf16[16,512]{1,0:T(8,128)(2,1)S(1)}, u32[]{:S(2)}, u32[]{:S(2)}) collective-permute-start(bf16[16,512]{1,0:T(8,128)(2,1)S(1)} %get-tuple-element.137), channel_id=1, source_target_pairs={{0,12},{1,13},{2,14},{3,15},{4,8},{5,9},{6,10},{7,11},{8,4},{9,5},... | collective-permute-start | bytes 49160 | tf_op jit(solution)/shard_map/ppermute | solution.py:357
  51.3 1.1 %collective-permute-start.25 = (bf16[16,512]{1,0:T(8,128)(2,1)S(1)}, bf16[16,512]{1,0:T(8,128)(2,1)S(1)}, u32[]{:S(2)}, u32[]{:S(2)}) collective-permute-start(bf16[16,512]{1,0:T(8,128)(2,1)S(1)} %get-tuple-element.138), channel_id=1, source_target_pairs={{0,4},{1,5},{2,6},{3,7},{4,0},{5,1},{6,2},{7,3},{8,12},{9,13},{10,... | collective-permute-start | bytes 49160 | tf_op jit(solution)/shard_map/ppermute | solution.py:357
  53.6 1.2 %collective-permute-done.24.refs_1_ = bf16[16,512]{1,0:T(8,128)(2,1)S(1)} collective-permute-done((bf16[16,512]{1,0:T(8,128)(2,1)S(1)}, bf16[16,512]{1,0:T(8,128)(2,1)S(1)}, u32[]{:S(2)}, u32[]{:S(2)}) %collective-permute-start.24) | collective-permute-done | bytes 16416 | tf_op jit(solution)/shard_map/ppermute | solution.py:357
  57.6 1.4 %shard_map.155 = (bf16[1024,512]{1,0:T(8,128)(2,1)}, f32[8,128]{1,0:T(8,128)S(1)}) custom-call(f32[1024,512]{1,0:T(8,128)S(1)} %shard_map.151.refs_11_.refs_0_, bf16[128,1024]{1,0:T(8,128)(2,1)S(1)} %get-tuple-element.127.refs_1_, bf16[128,512]{1,0:T(8,128)(2,1)S(1)} %collective-permute-done.19.refs_6_.refs_2_, ...), custom_call_target="tpu_custom_call" | custom-call | flops 134217728 | bytes 3706880 | tf_op jit(solution)/shard_map/pallas_call | solution.py:84
  60.0 1.9 %collective-permute-start.30 = (bf16[64,512]{1,0:T(8,128)(2,1)S(1)}, bf16[64,512]{1,0:T(8,128)(2,1)S(1)}, u32[]{:S(2)}, u32[]{:S(2)}) collective-permute-start(bf16[64,512]{1,0:T(8,128)(2,1)S(1)} %get-tuple-element.154), channel_id=1, source_target_pairs={{0,15},{1,2},{2,1},{3,4},{4,3},{5,6},{6,5},{7,8},{8,7},{9,10},{10,... | collective-permute-start | bytes 196616 | tf_op jit(solution)/shard_map/ppermute | solution.py:363
  62.0 2.5 %shard_map.158 = (f32[1024,512]{1,0:T(8,128)S(1)}, bf16[1024,128]{1,0:T(8,128)(2,1)S(1)}, f32[128,512]{1,0:T(8,128)S(1)}, bf16[512,512]{1,0:T(8,128)(2,1)}) custom-call(bf16[1024,512]{1,0:T(8,128)(2,1)S(1)} %get-tuple-element.141.own_t, bf16[512,512]{1,0:T(8,128)(2,1)S(1)} %get-tuple-element.149.grad, s32[1,2,64]{2,1,0:T(2,128)S(1)} %copy-done.4, ...), custom_call_target="tpu_custom_call" | custom-call | flops 1073741824 | bytes 7340544 | tf_op jit(solution)/shard_map/pallas_call | solution.py:84
  64.5 2.0 %collective-permute-done.30.outer_in = bf16[64,512]{1,0:T(8,128)(2,1)S(1)} collective-permute-done((bf16[64,512]{1,0:T(8,128)(2,1)S(1)}, bf16[64,512]{1,0:T(8,128)(2,1)S(1)}, u32[]{:S(2)}, u32[]{:S(2)}) %collective-permute-start.30) | collective-permute-done | bytes 65568 | tf_op jit(solution)/shard_map/ppermute | solution.py:363
  66.5 1.5 %shard_map.159 = bf16[1024,512]{1,0:T(8,128)(2,1)} custom-call(f32[1024,512]{1,0:T(8,128)S(1)} %get-tuple-element.151.base, bf16[1024,128]{1,0:T(8,128)(2,1)S(1)} %get-tuple-element.152.table, f32[128,512]{1,0:T(8,128)S(1)} %get-tuple-element.153.slope_rows, bf16[512,512]{1,0:T(8,128)(2,1)S(1)} %copy-done.1, ...), custom_call_target="tpu_custom_call" | custom-call | flops 268435456 | bytes 4325376 | tf_op jit(solution)/shard_map/pallas_call | solution.py:84
  (85 shorter events, 22.7 us)
Async XLA Ops:
  2.9 9.0 %collective-permute-start = (bf16[64,512]{1,0:T(8,128)(2,1)}, bf16[64,512]{1,0:T(8,128)(2,1)S(1)}, u32[]{:S(2)}, u32[]{:S(2)}) collective-permute-start(bf16[64,512]{1,0:T(8,128)(2,1)} %get-tuple-element.86), channel_id=1, source_target_pairs={{0,15},{1,2},{2,1},{3,4},{4,3},{5,6},{6,5},{7,8},{8,7},{9,10},{10,... | collective-permute-start | bytes 196616 | tf_op jit(solution)/shard_map/ppermute | solution.py:363
  12.8 5.8 %collective-permute-start.2 = (bf16[16,512]{1,0:T(8,128)(2,1)S(1)}, bf16[16,512]{1,0:T(8,128)(2,1)S(1)}, u32[]{:S(2)}, u32[]{:S(2)}) collective-permute-start(bf16[16,512]{1,0:T(8,128)(2,1)S(1)} %get-tuple-element.90), channel_id=1, source_target_pairs={{0,8},{1,9},{2,10},{3,11},{4,12},{5,13},{6,14},{7,15},{8,0},{9,1},... | collective-permute-start | bytes 49160 | tf_op jit(solution)/shard_map/ppermute | solution.py:357
  13.1 5.6 %collective-permute-start.3 = (bf16[16,512]{1,0:T(8,128)(2,1)S(1)}, bf16[16,512]{1,0:T(8,128)(2,1)S(1)}, u32[]{:S(2)}, u32[]{:S(2)}) collective-permute-start(bf16[16,512]{1,0:T(8,128)(2,1)S(1)} %get-tuple-element.91), channel_id=1, source_target_pairs={{0,12},{1,13},{2,14},{3,15},{4,8},{5,9},{6,10},{7,11},{8,4},{9,5},... | collective-permute-start | bytes 49160 | tf_op jit(solution)/shard_map/ppermute | solution.py:357
  14.4 4.2 %collective-permute-start.4 = (bf16[16,512]{1,0:T(8,128)(2,1)S(1)}, bf16[16,512]{1,0:T(8,128)(2,1)S(1)}, u32[]{:S(2)}, u32[]{:S(2)}) collective-permute-start(bf16[16,512]{1,0:T(8,128)(2,1)S(1)} %get-tuple-element.92), channel_id=1, source_target_pairs={{0,4},{1,5},{2,6},{3,7},{4,0},{5,1},{6,2},{7,3},{8,12},{9,13},{10,... | collective-permute-start | bytes 49160 | tf_op jit(solution)/shard_map/ppermute | solution.py:357
  16.4 7.0 %collective-permute-start.5 = (bf16[64,512]{1,0:T(8,128)(2,1)S(1)}, bf16[64,512]{1,0:T(8,128)(2,1)S(1)}, u32[]{:S(2)}, u32[]{:S(2)}) collective-permute-start(bf16[64,512]{1,0:T(8,128)(2,1)S(1)} %get-tuple-element.101), channel_id=1, source_target_pairs={{0,15},{1,2},{2,1},{3,4},{4,3},{5,6},{6,5},{7,8},{8,7},{9,10},{10,... | collective-permute-start | bytes 196616 | tf_op jit(solution)/shard_map/ppermute | solution.py:363
  18.8 4.1 %collective-permute-start.7 = (bf16[16,512]{1,0:T(8,128)(2,1)S(1)}, bf16[16,512]{1,0:T(8,128)(2,1)S(1)}, u32[]{:S(2)}, u32[]{:S(2)}) collective-permute-start(bf16[16,512]{1,0:T(8,128)(2,1)S(1)} %get-tuple-element.103), channel_id=1, source_target_pairs={{0,3},{1,2},{2,1},{3,0},{4,7},{5,6},{6,5},{7,4},{8,11},{9,10},{10,... | collective-permute-start | bytes 49160 | tf_op jit(solution)/shard_map/ppermute | solution.py:357
  19.5 3.9 %collective-permute-start.8 = (bf16[16,512]{1,0:T(8,128)(2,1)S(1)}, bf16[16,512]{1,0:T(8,128)(2,1)S(1)}, u32[]{:S(2)}, u32[]{:S(2)}) collective-permute-start(bf16[16,512]{1,0:T(8,128)(2,1)S(1)} %get-tuple-element.104), channel_id=1, source_target_pairs={{0,2},{1,3},{2,0},{3,1},{4,6},{5,7},{6,4},{7,5},{8,10},{9,11},{10,... | collective-permute-start | bytes 49160 | tf_op jit(solution)/shard_map/ppermute | solution.py:357
  24.1 5.1 %collective-permute-start.9 = (bf16[16,512]{1,0:T(8,128)(2,1)S(1)}, bf16[16,512]{1,0:T(8,128)(2,1)S(1)}, u32[]{:S(2)}, u32[]{:S(2)}) collective-permute-start(bf16[16,512]{1,0:T(8,128)(2,1)S(1)} %get-tuple-element.108), channel_id=1, source_target_pairs={{0,8},{1,9},{2,10},{3,11},{4,12},{5,13},{6,14},{7,15},{8,0},{9,1},... | collective-permute-start | bytes 49160 | tf_op jit(solution)/shard_map/ppermute | solution.py:357
  25.4 5.5 %collective-permute-start.10 = (bf16[16,512]{1,0:T(8,128)(2,1)S(1)}, bf16[16,512]{1,0:T(8,128)(2,1)S(1)}, u32[]{:S(2)}, u32[]{:S(2)}) collective-permute-start(bf16[16,512]{1,0:T(8,128)(2,1)S(1)} %get-tuple-element.109), channel_id=1, source_target_pairs={{0,12},{1,13},{2,14},{3,15},{4,8},{5,9},{6,10},{7,11},{8,4},{9,5},... | collective-permute-start | bytes 49160 | tf_op jit(solution)/shard_map/ppermute | solution.py:357
  27.6 7.8 %collective-permute-start.12 = (bf16[128,512]{1,0:T(8,128)(2,1)S(1)}, bf16[128,512]{1,0:T(8,128)(2,1)S(1)}, u32[]{:S(2)}, u32[]{:S(2)}) collective-permute-start(bf16[128,512]{1,0:T(8,128)(2,1)S(1)} %get-tuple-element.116), channel_id=1, source_target_pairs={{0,15},{1,2},{2,1},{3,4},{4,3},{5,6},{6,5},{7,8},{8,7},{9,10},{10,... | collective-permute-start | bytes 393224 | tf_op jit(solution)/shard_map/ppermute | solution.py:363
  31.5 4.0 %collective-permute-start.15 = (bf16[16,512]{1,0:T(8,128)(2,1)S(1)}, bf16[16,512]{1,0:T(8,128)(2,1)S(1)}, u32[]{:S(2)}, u32[]{:S(2)}) collective-permute-start(bf16[16,512]{1,0:T(8,128)(2,1)S(1)} %get-tuple-element.119), channel_id=1, source_target_pairs={{0,2},{1,3},{2,0},{3,1},{4,6},{5,7},{6,4},{7,5},{8,10},{9,11},{10,... | collective-permute-start | bytes 49160 | tf_op jit(solution)/shard_map/ppermute | solution.py:357
  36.8 4.7 %collective-permute-start.16 = (bf16[16,512]{1,0:T(8,128)(2,1)S(1)}, bf16[16,512]{1,0:T(8,128)(2,1)S(1)}, u32[]{:S(2)}, u32[]{:S(2)}) collective-permute-start(bf16[16,512]{1,0:T(8,128)(2,1)S(1)} %get-tuple-element.123), channel_id=1, source_target_pairs={{0,8},{1,9},{2,10},{3,11},{4,12},{5,13},{6,14},{7,15},{8,0},{9,1},... | collective-permute-start | bytes 49160 | tf_op jit(solution)/shard_map/ppermute | solution.py:357
  37.5 5.5 %collective-permute-start.17 = (bf16[16,512]{1,0:T(8,128)(2,1)S(1)}, bf16[16,512]{1,0:T(8,128)(2,1)S(1)}, u32[]{:S(2)}, u32[]{:S(2)}) collective-permute-start(bf16[16,512]{1,0:T(8,128)(2,1)S(1)} %get-tuple-element.124), channel_id=1, source_target_pairs={{0,12},{1,13},{2,14},{3,15},{4,8},{5,9},{6,10},{7,11},{8,4},{9,5},... | collective-permute-start | bytes 49160 | tf_op jit(solution)/shard_map/ppermute | solution.py:357
  39.5 3.8 %collective-permute-start.18 = (bf16[16,512]{1,0:T(8,128)(2,1)S(1)}, bf16[16,512]{1,0:T(8,128)(2,1)S(1)}, u32[]{:S(2)}, u32[]{:S(2)}) collective-permute-start(bf16[16,512]{1,0:T(8,128)(2,1)S(1)} %get-tuple-element.125), channel_id=1, source_target_pairs={{0,4},{1,5},{2,6},{3,7},{4,0},{5,1},{6,2},{7,3},{8,12},{9,13},{10,... | collective-permute-start | bytes 49160 | tf_op jit(solution)/shard_map/ppermute | solution.py:357
  40.4 7.8 %collective-permute-start.19 = (bf16[128,512]{1,0:T(8,128)(2,1)S(1)}, bf16[128,512]{1,0:T(8,128)(2,1)S(1)}, u32[]{:S(2)}, u32[]{:S(2)}) collective-permute-start(bf16[128,512]{1,0:T(8,128)(2,1)S(1)} %get-tuple-element.128), channel_id=1, source_target_pairs={{0,15},{1,2},{2,1},{3,4},{4,3},{5,6},{6,5},{7,8},{8,7},{9,10},{10,... | collective-permute-start | bytes 393224 | tf_op jit(solution)/shard_map/ppermute | solution.py:363
  43.4 4.4 %collective-permute-start.21 = (bf16[16,512]{1,0:T(8,128)(2,1)S(1)}, bf16[16,512]{1,0:T(8,128)(2,1)S(1)}, u32[]{:S(2)}, u32[]{:S(2)}) collective-permute-start(bf16[16,512]{1,0:T(8,128)(2,1)S(1)} %get-tuple-element.132), channel_id=1, source_target_pairs={{0,3},{1,2},{2,1},{3,0},{4,7},{5,6},{6,5},{7,4},{8,11},{9,10},{10,... | collective-permute-start | bytes 49160 | tf_op jit(solution)/shard_map/ppermute | solution.py:357
  43.5 4.6 %collective-permute-start.22 = (bf16[16,512]{1,0:T(8,128)(2,1)S(1)}, bf16[16,512]{1,0:T(8,128)(2,1)S(1)}, u32[]{:S(2)}, u32[]{:S(2)}) collective-permute-start(bf16[16,512]{1,0:T(8,128)(2,1)S(1)} %get-tuple-element.133), channel_id=1, source_target_pairs={{0,2},{1,3},{2,0},{3,1},{4,6},{5,7},{6,4},{7,5},{8,10},{9,11},{10,... | collective-permute-start | bytes 49160 | tf_op jit(solution)/shard_map/ppermute | solution.py:357
  48.9 4.7 %collective-permute-start.23 = (bf16[16,512]{1,0:T(8,128)(2,1)S(1)}, bf16[16,512]{1,0:T(8,128)(2,1)S(1)}, u32[]{:S(2)}, u32[]{:S(2)}) collective-permute-start(bf16[16,512]{1,0:T(8,128)(2,1)S(1)} %get-tuple-element.136), channel_id=1, source_target_pairs={{0,8},{1,9},{2,10},{3,11},{4,12},{5,13},{6,14},{7,15},{8,0},{9,1},... | collective-permute-start | bytes 49160 | tf_op jit(solution)/shard_map/ppermute | solution.py:357
  49.3 5.5 %collective-permute-start.24 = (bf16[16,512]{1,0:T(8,128)(2,1)S(1)}, bf16[16,512]{1,0:T(8,128)(2,1)S(1)}, u32[]{:S(2)}, u32[]{:S(2)}) collective-permute-start(bf16[16,512]{1,0:T(8,128)(2,1)S(1)} %get-tuple-element.137), channel_id=1, source_target_pairs={{0,12},{1,13},{2,14},{3,15},{4,8},{5,9},{6,10},{7,11},{8,4},{9,5},... | collective-permute-start | bytes 49160 | tf_op jit(solution)/shard_map/ppermute | solution.py:357
  52.4 6.8 %collective-permute-start.26 = (bf16[64,512]{1,0:T(8,128)(2,1)S(1)}, bf16[64,512]{1,0:T(8,128)(2,1)S(1)}, u32[]{:S(2)}, u32[]{:S(2)}) collective-permute-start(bf16[64,512]{1,0:T(8,128)(2,1)S(1)} %get-tuple-element.144), channel_id=1, source_target_pairs={{0,15},{1,2},{2,1},{3,4},{4,3},{5,6},{6,5},{7,8},{8,7},{9,10},{10,... | collective-permute-start | bytes 196616 | tf_op jit(solution)/shard_map/ppermute | solution.py:363
  55.2 3.9 %collective-permute-start.28 = (bf16[16,512]{1,0:T(8,128)(2,1)S(1)}, bf16[16,512]{1,0:T(8,128)(2,1)S(1)}, u32[]{:S(2)}, u32[]{:S(2)}) collective-permute-start(bf16[16,512]{1,0:T(8,128)(2,1)S(1)} %get-tuple-element.146), channel_id=1, source_target_pairs={{0,3},{1,2},{2,1},{3,0},{4,7},{5,6},{6,5},{7,4},{8,11},{9,10},{10,... | collective-permute-start | bytes 49160 | tf_op jit(solution)/shard_map/ppermute | solution.py:357
  55.3 4.0 %collective-permute-start.29 = (bf16[16,512]{1,0:T(8,128)(2,1)S(1)}, bf16[16,512]{1,0:T(8,128)(2,1)S(1)}, u32[]{:S(2)}, u32[]{:S(2)}) collective-permute-start(bf16[16,512]{1,0:T(8,128)(2,1)S(1)} %get-tuple-element.147), channel_id=1, source_target_pairs={{0,2},{1,3},{2,0},{3,1},{4,6},{5,7},{6,4},{7,5},{8,10},{9,11},{10,... | collective-permute-start | bytes 49160 | tf_op jit(solution)/shard_map/ppermute | solution.py:357
  60.0 6.5 %collective-permute-start.30 = (bf16[64,512]{1,0:T(8,128)(2,1)S(1)}, bf16[64,512]{1,0:T(8,128)(2,1)S(1)}, u32[]{:S(2)}, u32[]{:S(2)}) collective-permute-start(bf16[64,512]{1,0:T(8,128)(2,1)S(1)} %get-tuple-element.154), channel_id=1, source_target_pairs={{0,15},{1,2},{2,1},{3,4},{4,3},{5,6},{6,5},{7,8},{8,7},{9,10},{10,... | collective-permute-start | bytes 196616 | tf_op jit(solution)/shard_map/ppermute | solution.py:363
  62.0 4.5 %collective-permute-start.31 = (bf16[64,512]{1,0:T(8,128)(2,1)S(1)}, bf16[64,512]{1,0:T(8,128)(2,1)S(1)}, u32[]{:S(2)}, u32[]{:S(2)}) collective-permute-start(bf16[64,512]{1,0:T(8,128)(2,1)S(1)} %get-tuple-element.155), channel_id=1, source_target_pairs={{0,1},{1,0},{2,3},{3,2},{4,5},{5,4},{6,7},{7,6},{8,9},{9,8},{10,11... | collective-permute-start | bytes 196616 | tf_op jit(solution)/shard_map/ppermute | solution.py:357
  (20 other events, 65.6 us)

commit v16 on v15

--- a/solution.py
+++ b/solution.py
@@ -10,7 +10,7 @@
 BF = jnp.bfloat16
 F32 = jnp.float32
 VMEM_LIMIT = 24 * 1024 * 1024
-FIRST_LIMIT = 60 * 1024 * 1024
+FIRST_LIMIT = 107 * 512 * 1024
 PLANE = 4
 STAGED = 16
 CHUNKS = 4
@@ -108,22 +108,19 @@
     return [pl.ds(i * step, step) for i in range(CHUNKS)]
 
 
-def grid_send(latent, lists, outer, inner, values, wanted, rows, sems):
+def grid_send(latent, lists, outer, inner, values, sems):
     parts = row_chunks(latent.shape[0])
-    copies = fetch([lists] + [latent.at[part] for part in parts], [wanted] + [values.at[part] for part in parts], sems)
+    copies = fetch([latent.at[part] for part in parts], [values.at[part] for part in parts], sems)
     size = outer.shape[0]
     step = latent.shape[0] // CHUNKS
-    copies[0].wait()
-    listed = jnp.concatenate(pair_order(wanted, lax.axis_index("dom")), axis=1)
+    listed = jnp.concatenate(pair_order(lists, lax.axis_index("dom")), axis=1)
     chosen = pick(latent.shape[0], listed)
-    total = 0.0
+    rows = 0.0
     for i, part in enumerate(parts):
-        copies[i + 1].wait()
-        total += t_mm(chosen[i * step : (i + 1) * step], values[part])
-    rows[...] = total.astype(BF)
-    sides = [rows.at[pl.ds(0, size)], rows.at[pl.ds(size, size)]]
-    for copy in fetch(sides, [outer, inner], sems):
-        copy.wait()
+        copies[i].wait()
+        rows += t_mm(chosen[i * step : (i + 1) * step], values[part])
+    outer[...] = rows[:size].astype(BF)
+    inner[...] = rows[size:].astype(BF)
 
 
 def encoder_local(entries, weight, latent, mesh, near, grid_own_t, grid_rim_t, slope, *, size):
@@ -427,9 +424,8 @@
         [grid_rim, grid_rim],
         64 * square(grid_rows, width),
         grid_latent, grid_halo_rows,
-        hbm=2, hbm_out=2, limit=FIRST_LIMIT,
-        scratch=copies_of([grid_latent, grid_halo_rows])
-        + [pltpu.VMEM((2 * ghalo, width), BF), pltpu.SemaphoreType.DMA((CHUNKS + 1,))],
+        hbm=1, limit=FIRST_LIMIT,
+        scratch=copies_of([grid_latent]) + [pltpu.SemaphoreType.DMA((CHUNKS,))],
     )
     outer_in, inner_in = across(outer), toggle(inner, 1)
 

time: 68.2 us -> 68.1 us (level)
  Pallas kernels: 20 us -> 19.3 us
  transfers between devices with their start and end apart: 32 -> 32, of which waited for: 17 -> 16; matrix products, arithmetic and copies ran while one was open for 0% -> 0% of each run, Pallas kernels for 17% -> 17%
where the time goes in v16:
time: 68.1 us; the launch traced here: 67.9 us
  starting transfers between devices  34.9 us (51%)
  Pallas kernels  19.3 us (28%)
  waiting for transfers between devices  11.4 us (17%)
  local copies, waits for them, and re-layouts  1.4 us (2%)
  between operations  0.92 us (1%)
    ppermute x26, starting transfers between devices, toggle(): return lax.ppermute(value, 'dom', [(i, i ^ bits) for i in range(peers)])  22 us
    pallas_call x21, Pallas kernels, call(): pl.pallas_call(inner, out_shape=shapes, in_specs=[pl.BlockSpec(memory_spa...  19.3 us
    ppermute x6, starting transfers between devices, across(): return lax.ppermute(value, 'dom', pairs)  12.9 us
    ppermute x26, waiting for transfers between devices, toggle(): return lax.ppermute(value, 'dom', [(i, i ^ bits) for i in range(peers)])  9.28 us
    ppermute x6, waiting for transfers between devices, across(): return lax.ppermute(value, 'dom', pairs)  2.1 us
    unnamed x24, local copies, waits for them, and re-layouts  1.4 us
  transfers between devices with their start and end apart: 32, of which 16 were waited for; matrix products, arithmetic and copies ran while one was open for 0% of the time, Pallas kernels for 17%

profile of v16, /device:TPU:0, one launch (start us, length us, event | category | flops | bytes accessed | tf_op | source)
XLA Modules:
  0.0 67.9 jit_solution(5264518430628975666)
XLA Ops:
  1.3 1.5 %shard_map.139 = (bf16[64,512]{1,0:T(8,128)(2,1)S(1)}, bf16[64,512]{1,0:T(8,128)(2,1)S(1)}) custom-call(bf16[1024,512]{1,0:T(8,128)(2,1)} %refs_0_.1, s32[1,2,64]{2,1,0:T(2,128)S(1)} %copy-done.4), custom_call_target="tpu_custom_call" | custom-call | flops 34359738368 | tf_op jit(solution)/shard_map/pallas_call | solution.py:84
  2.9 5.5 %collective-permute-start = (bf16[64,512]{1,0:T(8,128)(2,1)S(1)}, bf16[64,512]{1,0:T(8,128)(2,1)S(1)}, u32[]{:S(2)}, u32[]{:S(2)}) collective-permute-start(bf16[64,512]{1,0:T(8,128)(2,1)S(1)} %get-tuple-element.86), channel_id=1, source_target_pairs={{0,15},{1,2},{2,1},{3,4},{4,3},{5,6},{6,5},{7,8},{8,7},{9,10},{10,... | collective-permute-start | bytes 196616 | tf_op jit(solution)/shard_map/ppermute | solution.py:360
  9.9 1.9 %shard_map.140 = (f32[512,512]{1,0:T(8,128)S(1)}, bf16[1024,512]{1,0:T(8,128)(2,1)S(1)}, bf16[128,512]{1,0:T(8,128)(2,1)S(1)}, bf16[1024,512]{1,0:T(8,128)(2,1)S(1)}) custom-call(s32[4,512]{1,0:T(4,128)S(1)} %bitcast.8, bf16[512,512]{1,0:T(8,128)(2,1)S(1)} %copy-done.1, bf16[1024,512]{1,0:T(8,128)(2,1)S(1)} %copy-done.3, bf16[512,512]{1,0:T(8,128)(2,1)S(1)} %copy-done.5), custom_call_target="tpu_custom_call" | custom-call | flops 2147483648 | bytes 5382144 | tf_op jit(solution)/shard_map/pallas_call | solution.py:84
  13.1 1.4 %collective-permute-start.3 = (bf16[16,512]{1,0:T(8,128)(2,1)S(1)}, bf16[16,512]{1,0:T(8,128)(2,1)S(1)}, u32[]{:S(2)}, u32[]{:S(2)}) collective-permute-start(bf16[16,512]{1,0:T(8,128)(2,1)S(1)} %get-tuple-element.91), channel_id=1, source_target_pairs={{0,12},{1,13},{2,14},{3,15},{4,8},{5,9},{6,10},{7,11},{8,4},{9,5},... | collective-permute-start | bytes 49160 | tf_op jit(solution)/shard_map/ppermute | solution.py:354
  14.4 1.9 %collective-permute-start.4 = (bf16[16,512]{1,0:T(8,128)(2,1)S(1)}, bf16[16,512]{1,0:T(8,128)(2,1)S(1)}, u32[]{:S(2)}, u32[]{:S(2)}) collective-permute-start(bf16[16,512]{1,0:T(8,128)(2,1)S(1)} %get-tuple-element.92), channel_id=1, source_target_pairs={{0,4},{1,5},{2,6},{3,7},{4,0},{5,1},{6,2},{7,3},{8,12},{9,13},{10,... | collective-permute-start | bytes 49160 | tf_op jit(solution)/shard_map/ppermute | solution.py:354
  16.4 2.1 %collective-permute-start.5 = (bf16[64,512]{1,0:T(8,128)(2,1)S(1)}, bf16[64,512]{1,0:T(8,128)(2,1)S(1)}, u32[]{:S(2)}, u32[]{:S(2)}) collective-permute-start(bf16[64,512]{1,0:T(8,128)(2,1)S(1)} %get-tuple-element.101), channel_id=1, source_target_pairs={{0,15},{1,2},{2,1},{3,4},{4,3},{5,6},{6,5},{7,8},{8,7},{9,10},{10,... | collective-permute-start | bytes 196616 | tf_op jit(solution)/shard_map/ppermute | solution.py:360
  19.2 1.2 %collective-permute-start.8 = (bf16[16,512]{1,0:T(8,128)(2,1)S(1)}, bf16[16,512]{1,0:T(8,128)(2,1)S(1)}, u32[]{:S(2)}, u32[]{:S(2)}) collective-permute-start(bf16[16,512]{1,0:T(8,128)(2,1)S(1)} %get-tuple-element.104), channel_id=1, source_target_pairs={{0,2},{1,3},{2,0},{3,1},{4,6},{5,7},{6,4},{7,5},{8,10},{9,11},{10,... | collective-permute-start | bytes 49160 | tf_op jit(solution)/shard_map/ppermute | solution.py:354
  23.8 1.6 %collective-permute-start.9 = (bf16[16,512]{1,0:T(8,128)(2,1)S(1)}, bf16[16,512]{1,0:T(8,128)(2,1)S(1)}, u32[]{:S(2)}, u32[]{:S(2)}) collective-permute-start(bf16[16,512]{1,0:T(8,128)(2,1)S(1)} %get-tuple-element.108), channel_id=1, source_target_pairs={{0,8},{1,9},{2,10},{3,11},{4,12},{5,13},{6,14},{7,15},{8,0},{9,1},... | collective-permute-start | bytes 49160 | tf_op jit(solution)/shard_map/ppermute | solution.py:354
  25.5 2.0 %collective-permute-start.10 = (bf16[16,512]{1,0:T(8,128)(2,1)S(1)}, bf16[16,512]{1,0:T(8,128)(2,1)S(1)}, u32[]{:S(2)}, u32[]{:S(2)}) collective-permute-start(bf16[16,512]{1,0:T(8,128)(2,1)S(1)} %get-tuple-element.109), channel_id=1, source_target_pairs={{0,12},{1,13},{2,14},{3,15},{4,8},{5,9},{6,10},{7,11},{8,4},{9,5},... | collective-permute-start | bytes 49160 | tf_op jit(solution)/shard_map/ppermute | solution.py:354
  27.5 1.6 %collective-permute-start.12 = (bf16[128,512]{1,0:T(8,128)(2,1)S(1)}, bf16[128,512]{1,0:T(8,128)(2,1)S(1)}, u32[]{:S(2)}, u32[]{:S(2)}) collective-permute-start(bf16[128,512]{1,0:T(8,128)(2,1)S(1)} %get-tuple-element.116), channel_id=1, source_target_pairs={{0,15},{1,2},{2,1},{3,4},{4,3},{5,6},{6,5},{7,8},{8,7},{9,10},{10,... | collective-permute-start | bytes 393224 | tf_op jit(solution)/shard_map/ppermute | solution.py:360
  29.1 1.9 %collective-permute-done.10.refs_1_ = bf16[16,512]{1,0:T(8,128)(2,1)S(1)} collective-permute-done((bf16[16,512]{1,0:T(8,128)(2,1)S(1)}, bf16[16,512]{1,0:T(8,128)(2,1)S(1)}, u32[]{:S(2)}, u32[]{:S(2)}) %collective-permute-start.10) | collective-permute-done | bytes 16416 | tf_op jit(solution)/shard_map/ppermute | solution.py:354
  32.0 1.3 %collective-permute-start.13 = (bf16[144,512]{1,0:T(8,128)(2,1)S(1)}, bf16[144,512]{1,0:T(8,128)(2,1)S(1)}, u32[]{:S(2)}, u32[]{:S(2)}) collective-permute-start(bf16[144,512]{1,0:T(8,128)(2,1)S(1)} %get-tuple-element.117), channel_id=1, source_target_pairs={{0,1},{1,0},{2,3},{3,2},{4,5},{5,4},{6,7},{7,6},{8,9},{9,8},{10,11... | collective-permute-start | bytes 442376 | tf_op jit(solution)/shard_map/ppermute | solution.py:354
  35.3 1.3 %shard_map.149 = (bf16[512,512]{1,0:T(8,128)(2,1)S(1)}, bf16[512,512]{1,0:T(8,128)(2,1)S(1)}, bf16[128,512]{1,0:T(8,128)(2,1)S(1)}, bf16[128,512]{1,0:T(8,128)(2...) custom-call(f32[512,512]{1,0:T(8,128)S(1)} %get-tuple-element.112.ne, ...), custom_call_target="tpu_custom_call" | custom-call | flops 1610612736 | bytes 5111808 | tf_op jit(solution)/shard_map/pallas_call | solution.py:84
  37.6 1.9 %collective-permute-start.17 = (bf16[16,512]{1,0:T(8,128)(2,1)S(1)}, bf16[16,512]{1,0:T(8,128)(2,1)S(1)}, u32[]{:S(2)}, u32[]{:S(2)}) collective-permute-start(bf16[16,512]{1,0:T(8,128)(2,1)S(1)} %get-tuple-element.124), channel_id=1, source_target_pairs={{0,12},{1,13},{2,14},{3,15},{4,8},{5,9},{6,10},{7,11},{8,4},{9,5},... | collective-permute-start | bytes 49160 | tf_op jit(solution)/shard_map/ppermute | solution.py:354
  41.4 1.8 %collective-permute-done.17.refs_1_ = bf16[16,512]{1,0:T(8,128)(2,1)S(1)} collective-permute-done((bf16[16,512]{1,0:T(8,128)(2,1)S(1)}, bf16[16,512]{1,0:T(8,128)(2,1)S(1)}, u32[]{:S(2)}, u32[]{:S(2)}) %collective-permute-start.17) | collective-permute-done | bytes 16416 | tf_op jit(solution)/shard_map/ppermute | solution.py:354
  46.6 1.1 %collective-permute-done.21.refs_8_ = bf16[16,512]{1,0:T(8,128)(2,1)S(1)} collective-permute-done((bf16[16,512]{1,0:T(8,128)(2,1)S(1)}, bf16[16,512]{1,0:T(8,128)(2,1)S(1)}, u32[]{:S(2)}, u32[]{:S(2)}) %collective-permute-start.21) | collective-permute-done | bytes 16416 | tf_op jit(solution)/shard_map/ppermute | solution.py:354
  49.3 1.9 %collective-permute-start.24 = (bf16[16,512]{1,0:T(8,128)(2,1)S(1)}, bf16[16,512]{1,0:T(8,128)(2,1)S(1)}, u32[]{:S(2)}, u32[]{:S(2)}) collective-permute-start(bf16[16,512]{1,0:T(8,128)(2,1)S(1)} %get-tuple-element.137), channel_id=1, source_target_pairs={{0,12},{1,13},{2,14},{3,15},{4,8},{5,9},{6,10},{7,11},{8,4},{9,5},... | collective-permute-start | bytes 49160 | tf_op jit(solution)/shard_map/ppermute | solution.py:354
  51.2 1.1 %collective-permute-start.25 = (bf16[16,512]{1,0:T(8,128)(2,1)S(1)}, bf16[16,512]{1,0:T(8,128)(2,1)S(1)}, u32[]{:S(2)}, u32[]{:S(2)}) collective-permute-start(bf16[16,512]{1,0:T(8,128)(2,1)S(1)} %get-tuple-element.138), channel_id=1, source_target_pairs={{0,4},{1,5},{2,6},{3,7},{4,0},{5,1},{6,2},{7,3},{8,12},{9,13},{10,... | collective-permute-start | bytes 49160 | tf_op jit(solution)/shard_map/ppermute | solution.py:354
  53.4 1.4 %collective-permute-done.24.refs_1_ = bf16[16,512]{1,0:T(8,128)(2,1)S(1)} collective-permute-done((bf16[16,512]{1,0:T(8,128)(2,1)S(1)}, bf16[16,512]{1,0:T(8,128)(2,1)S(1)}, u32[]{:S(2)}, u32[]{:S(2)}) %collective-permute-start.24) | collective-permute-done | bytes 16416 | tf_op jit(solution)/shard_map/ppermute | solution.py:354
  57.5 1.4 %shard_map.155 = (bf16[1024,512]{1,0:T(8,128)(2,1)}, f32[8,128]{1,0:T(8,128)S(1)}) custom-call(f32[1024,512]{1,0:T(8,128)S(1)} %shard_map.151.refs_11_.refs_0_, bf16[128,1024]{1,0:T(8,128)(2,1)S(1)} %get-tuple-element.127.refs_1_, bf16[128,512]{1,0:T(8,128)(2,1)S(1)} %collective-permute-done.19.refs_6_.refs_2_, ...), custom_call_target="tpu_custom_call" | custom-call | flops 134217728 | bytes 3706880 | tf_op jit(solution)/shard_map/pallas_call | solution.py:84
  59.9 1.8 %collective-permute-start.30 = (bf16[64,512]{1,0:T(8,128)(2,1)S(1)}, bf16[64,512]{1,0:T(8,128)(2,1)S(1)}, u32[]{:S(2)}, u32[]{:S(2)}) collective-permute-start(bf16[64,512]{1,0:T(8,128)(2,1)S(1)} %get-tuple-element.154), channel_id=1, source_target_pairs={{0,15},{1,2},{2,1},{3,4},{4,3},{5,6},{6,5},{7,8},{8,7},{9,10},{10,... | collective-permute-start | bytes 196616 | tf_op jit(solution)/shard_map/ppermute | solution.py:360
  61.8 2.5 %shard_map.158 = (f32[1024,512]{1,0:T(8,128)S(1)}, bf16[1024,128]{1,0:T(8,128)(2,1)S(1)}, f32[128,512]{1,0:T(8,128)S(1)}, bf16[512,512]{1,0:T(8,128)(2,1)}) custom-call(bf16[1024,512]{1,0:T(8,128)(2,1)S(1)} %get-tuple-element.141.own_t, bf16[512,512]{1,0:T(8,128)(2,1)S(1)} %get-tuple-element.149.grad, s32[1,2,64]{2,1,0:T(2,128)S(1)} %copy-done.4, ...), custom_call_target="tpu_custom_call" | custom-call | flops 1073741824 | bytes 7340544 | tf_op jit(solution)/shard_map/pallas_call | solution.py:84
  64.3 2.1 %collective-permute-done.30.outer_in = bf16[64,512]{1,0:T(8,128)(2,1)S(1)} collective-permute-done((bf16[64,512]{1,0:T(8,128)(2,1)S(1)}, bf16[64,512]{1,0:T(8,128)(2,1)S(1)}, u32[]{:S(2)}, u32[]{:S(2)}) %collective-permute-start.30) | collective-permute-done | bytes 65568 | tf_op jit(solution)/shard_map/ppermute | solution.py:360
  66.4 1.5 %shard_map.159 = bf16[1024,512]{1,0:T(8,128)(2,1)} custom-call(f32[1024,512]{1,0:T(8,128)S(1)} %get-tuple-element.151.base, bf16[1024,128]{1,0:T(8,128)(2,1)S(1)} %get-tuple-element.152.table, f32[128,512]{1,0:T(8,128)S(1)} %get-tuple-element.153.slope_rows, bf16[512,512]{1,0:T(8,128)(2,1)S(1)} %copy-done.1, ...), custom_call_target="tpu_custom_call" | custom-call | flops 268435456 | bytes 4325376 | tf_op jit(solution)/shard_map/pallas_call | solution.py:84
  (85 shorter events, 23.2 us)
Async XLA Ops:
  2.9 9.0 %collective-permute-start = (bf16[64,512]{1,0:T(8,128)(2,1)S(1)}, bf16[64,512]{1,0:T(8,128)(2,1)S(1)}, u32[]{:S(2)}, u32[]{:S(2)}) collective-permute-start(bf16[64,512]{1,0:T(8,128)(2,1)S(1)} %get-tuple-element.86), channel_id=1, source_target_pairs={{0,15},{1,2},{2,1},{3,4},{4,3},{5,6},{6,5},{7,8},{8,7},{9,10},{10,... | collective-permute-start | bytes 196616 | tf_op jit(solution)/shard_map/ppermute | solution.py:360
  12.8 5.6 %collective-permute-start.2 = (bf16[16,512]{1,0:T(8,128)(2,1)S(1)}, bf16[16,512]{1,0:T(8,128)(2,1)S(1)}, u32[]{:S(2)}, u32[]{:S(2)}) collective-permute-start(bf16[16,512]{1,0:T(8,128)(2,1)S(1)} %get-tuple-element.90), channel_id=1, source_target_pairs={{0,8},{1,9},{2,10},{3,11},{4,12},{5,13},{6,14},{7,15},{8,0},{9,1},... | collective-permute-start | bytes 49160 | tf_op jit(solution)/shard_map/ppermute | solution.py:354
  13.1 5.6 %collective-permute-start.3 = (bf16[16,512]{1,0:T(8,128)(2,1)S(1)}, bf16[16,512]{1,0:T(8,128)(2,1)S(1)}, u32[]{:S(2)}, u32[]{:S(2)}) collective-permute-start(bf16[16,512]{1,0:T(8,128)(2,1)S(1)} %get-tuple-element.91), channel_id=1, source_target_pairs={{0,12},{1,13},{2,14},{3,15},{4,8},{5,9},{6,10},{7,11},{8,4},{9,5},... | collective-permute-start | bytes 49160 | tf_op jit(solution)/shard_map/ppermute | solution.py:354
  14.4 4.2 %collective-permute-start.4 = (bf16[16,512]{1,0:T(8,128)(2,1)S(1)}, bf16[16,512]{1,0:T(8,128)(2,1)S(1)}, u32[]{:S(2)}, u32[]{:S(2)}) collective-permute-start(bf16[16,512]{1,0:T(8,128)(2,1)S(1)} %get-tuple-element.92), channel_id=1, source_target_pairs={{0,4},{1,5},{2,6},{3,7},{4,0},{5,1},{6,2},{7,3},{8,12},{9,13},{10,... | collective-permute-start | bytes 49160 | tf_op jit(solution)/shard_map/ppermute | solution.py:354
  16.4 6.7 %collective-permute-start.5 = (bf16[64,512]{1,0:T(8,128)(2,1)S(1)}, bf16[64,512]{1,0:T(8,128)(2,1)S(1)}, u32[]{:S(2)}, u32[]{:S(2)}) collective-permute-start(bf16[64,512]{1,0:T(8,128)(2,1)S(1)} %get-tuple-element.101), channel_id=1, source_target_pairs={{0,15},{1,2},{2,1},{3,4},{4,3},{5,6},{6,5},{7,8},{8,7},{9,10},{10,... | collective-permute-start | bytes 196616 | tf_op jit(solution)/shard_map/ppermute | solution.py:360
  18.8 4.0 %collective-permute-start.7 = (bf16[16,512]{1,0:T(8,128)(2,1)S(1)}, bf16[16,512]{1,0:T(8,128)(2,1)S(1)}, u32[]{:S(2)}, u32[]{:S(2)}) collective-permute-start(bf16[16,512]{1,0:T(8,128)(2,1)S(1)} %get-tuple-element.103), channel_id=1, source_target_pairs={{0,3},{1,2},{2,1},{3,0},{4,7},{5,6},{6,5},{7,4},{8,11},{9,10},{10,... | collective-permute-start | bytes 49160 | tf_op jit(solution)/shard_map/ppermute | solution.py:354
  19.2 3.8 %collective-permute-start.8 = (bf16[16,512]{1,0:T(8,128)(2,1)S(1)}, bf16[16,512]{1,0:T(8,128)(2,1)S(1)}, u32[]{:S(2)}, u32[]{:S(2)}) collective-permute-start(bf16[16,512]{1,0:T(8,128)(2,1)S(1)} %get-tuple-element.104), channel_id=1, source_target_pairs={{0,2},{1,3},{2,0},{3,1},{4,6},{5,7},{6,4},{7,5},{8,10},{9,11},{10,... | collective-permute-start | bytes 49160 | tf_op jit(solution)/shard_map/ppermute | solution.py:354
  23.8 5.3 %collective-permute-start.9 = (bf16[16,512]{1,0:T(8,128)(2,1)S(1)}, bf16[16,512]{1,0:T(8,128)(2,1)S(1)}, u32[]{:S(2)}, u32[]{:S(2)}) collective-permute-start(bf16[16,512]{1,0:T(8,128)(2,1)S(1)} %get-tuple-element.108), channel_id=1, source_target_pairs={{0,8},{1,9},{2,10},{3,11},{4,12},{5,13},{6,14},{7,15},{8,0},{9,1},... | collective-permute-start | bytes 49160 | tf_op jit(solution)/shard_map/ppermute | solution.py:354
  25.5 5.5 %collective-permute-start.10 = (bf16[16,512]{1,0:T(8,128)(2,1)S(1)}, bf16[16,512]{1,0:T(8,128)(2,1)S(1)}, u32[]{:S(2)}, u32[]{:S(2)}) collective-permute-start(bf16[16,512]{1,0:T(8,128)(2,1)S(1)} %get-tuple-element.109), channel_id=1, source_target_pairs={{0,12},{1,13},{2,14},{3,15},{4,8},{5,9},{6,10},{7,11},{8,4},{9,5},... | collective-permute-start | bytes 49160 | tf_op jit(solution)/shard_map/ppermute | solution.py:354
  27.5 7.8 %collective-permute-start.12 = (bf16[128,512]{1,0:T(8,128)(2,1)S(1)}, bf16[128,512]{1,0:T(8,128)(2,1)S(1)}, u32[]{:S(2)}, u32[]{:S(2)}) collective-permute-start(bf16[128,512]{1,0:T(8,128)(2,1)S(1)} %get-tuple-element.116), channel_id=1, source_target_pairs={{0,15},{1,2},{2,1},{3,4},{4,3},{5,6},{6,5},{7,8},{8,7},{9,10},{10,... | collective-permute-start | bytes 393224 | tf_op jit(solution)/shard_map/ppermute | solution.py:360
  31.5 3.8 %collective-permute-start.15 = (bf16[16,512]{1,0:T(8,128)(2,1)S(1)}, bf16[16,512]{1,0:T(8,128)(2,1)S(1)}, u32[]{:S(2)}, u32[]{:S(2)}) collective-permute-start(bf16[16,512]{1,0:T(8,128)(2,1)S(1)} %get-tuple-element.119), channel_id=1, source_target_pairs={{0,2},{1,3},{2,0},{3,1},{4,6},{5,7},{6,4},{7,5},{8,10},{9,11},{10,... | collective-permute-start | bytes 49160 | tf_op jit(solution)/shard_map/ppermute | solution.py:354
  36.6 4.7 %collective-permute-start.16 = (bf16[16,512]{1,0:T(8,128)(2,1)S(1)}, bf16[16,512]{1,0:T(8,128)(2,1)S(1)}, u32[]{:S(2)}, u32[]{:S(2)}) collective-permute-start(bf16[16,512]{1,0:T(8,128)(2,1)S(1)} %get-tuple-element.123), channel_id=1, source_target_pairs={{0,8},{1,9},{2,10},{3,11},{4,12},{5,13},{6,14},{7,15},{8,0},{9,1},... | collective-permute-start | bytes 49160 | tf_op jit(solution)/shard_map/ppermute | solution.py:354
  37.6 5.5 %collective-permute-start.17 = (bf16[16,512]{1,0:T(8,128)(2,1)S(1)}, bf16[16,512]{1,0:T(8,128)(2,1)S(1)}, u32[]{:S(2)}, u32[]{:S(2)}) collective-permute-start(bf16[16,512]{1,0:T(8,128)(2,1)S(1)} %get-tuple-element.124), channel_id=1, source_target_pairs={{0,12},{1,13},{2,14},{3,15},{4,8},{5,9},{6,10},{7,11},{8,4},{9,5},... | collective-permute-start | bytes 49160 | tf_op jit(solution)/shard_map/ppermute | solution.py:354
  39.5 3.8 %collective-permute-start.18 = (bf16[16,512]{1,0:T(8,128)(2,1)S(1)}, bf16[16,512]{1,0:T(8,128)(2,1)S(1)}, u32[]{:S(2)}, u32[]{:S(2)}) collective-permute-start(bf16[16,512]{1,0:T(8,128)(2,1)S(1)} %get-tuple-element.125), channel_id=1, source_target_pairs={{0,4},{1,5},{2,6},{3,7},{4,0},{5,1},{6,2},{7,3},{8,12},{9,13},{10,... | collective-permute-start | bytes 49160 | tf_op jit(solution)/shard_map/ppermute | solution.py:354
  40.2 7.7 %collective-permute-start.19 = (bf16[128,512]{1,0:T(8,128)(2,1)S(1)}, bf16[128,512]{1,0:T(8,128)(2,1)S(1)}, u32[]{:S(2)}, u32[]{:S(2)}) collective-permute-start(bf16[128,512]{1,0:T(8,128)(2,1)S(1)} %get-tuple-element.128), channel_id=1, source_target_pairs={{0,15},{1,2},{2,1},{3,4},{4,3},{5,6},{6,5},{7,8},{8,7},{9,10},{10,... | collective-permute-start | bytes 393224 | tf_op jit(solution)/shard_map/ppermute | solution.py:360
  43.5 4.2 %collective-permute-start.21 = (bf16[16,512]{1,0:T(8,128)(2,1)S(1)}, bf16[16,512]{1,0:T(8,128)(2,1)S(1)}, u32[]{:S(2)}, u32[]{:S(2)}) collective-permute-start(bf16[16,512]{1,0:T(8,128)(2,1)S(1)} %get-tuple-element.132), channel_id=1, source_target_pairs={{0,3},{1,2},{2,1},{3,0},{4,7},{5,6},{6,5},{7,4},{8,11},{9,10},{10,... | collective-permute-start | bytes 49160 | tf_op jit(solution)/shard_map/ppermute | solution.py:354
  43.5 4.4 %collective-permute-start.22 = (bf16[16,512]{1,0:T(8,128)(2,1)S(1)}, bf16[16,512]{1,0:T(8,128)(2,1)S(1)}, u32[]{:S(2)}, u32[]{:S(2)}) collective-permute-start(bf16[16,512]{1,0:T(8,128)(2,1)S(1)} %get-tuple-element.133), channel_id=1, source_target_pairs={{0,2},{1,3},{2,0},{3,1},{4,6},{5,7},{6,4},{7,5},{8,10},{9,11},{10,... | collective-permute-start | bytes 49160 | tf_op jit(solution)/shard_map/ppermute | solution.py:354
  48.7 4.7 %collective-permute-start.23 = (bf16[16,512]{1,0:T(8,128)(2,1)S(1)}, bf16[16,512]{1,0:T(8,128)(2,1)S(1)}, u32[]{:S(2)}, u32[]{:S(2)}) collective-permute-start(bf16[16,512]{1,0:T(8,128)(2,1)S(1)} %get-tuple-element.136), channel_id=1, source_target_pairs={{0,8},{1,9},{2,10},{3,11},{4,12},{5,13},{6,14},{7,15},{8,0},{9,1},... | collective-permute-start | bytes 49160 | tf_op jit(solution)/shard_map/ppermute | solution.py:354
  49.3 5.5 %collective-permute-start.24 = (bf16[16,512]{1,0:T(8,128)(2,1)S(1)}, bf16[16,512]{1,0:T(8,128)(2,1)S(1)}, u32[]{:S(2)}, u32[]{:S(2)}) collective-permute-start(bf16[16,512]{1,0:T(8,128)(2,1)S(1)} %get-tuple-element.137), channel_id=1, source_target_pairs={{0,12},{1,13},{2,14},{3,15},{4,8},{5,9},{6,10},{7,11},{8,4},{9,5},... | collective-permute-start | bytes 49160 | tf_op jit(solution)/shard_map/ppermute | solution.py:354
  51.2 3.8 %collective-permute-start.25 = (bf16[16,512]{1,0:T(8,128)(2,1)S(1)}, bf16[16,512]{1,0:T(8,128)(2,1)S(1)}, u32[]{:S(2)}, u32[]{:S(2)}) collective-permute-start(bf16[16,512]{1,0:T(8,128)(2,1)S(1)} %get-tuple-element.138), channel_id=1, source_target_pairs={{0,4},{1,5},{2,6},{3,7},{4,0},{5,1},{6,2},{7,3},{8,12},{9,13},{10,... | collective-permute-start | bytes 49160 | tf_op jit(solution)/shard_map/ppermute | solution.py:354
  52.3 6.9 %collective-permute-start.26 = (bf16[64,512]{1,0:T(8,128)(2,1)S(1)}, bf16[64,512]{1,0:T(8,128)(2,1)S(1)}, u32[]{:S(2)}, u32[]{:S(2)}) collective-permute-start(bf16[64,512]{1,0:T(8,128)(2,1)S(1)} %get-tuple-element.144), channel_id=1, source_target_pairs={{0,15},{1,2},{2,1},{3,4},{4,3},{5,6},{6,5},{7,8},{8,7},{9,10},{10,... | collective-permute-start | bytes 196616 | tf_op jit(solution)/shard_map/ppermute | solution.py:360
  55.2 4.0 %collective-permute-start.29 = (bf16[16,512]{1,0:T(8,128)(2,1)S(1)}, bf16[16,512]{1,0:T(8,128)(2,1)S(1)}, u32[]{:S(2)}, u32[]{:S(2)}) collective-permute-start(bf16[16,512]{1,0:T(8,128)(2,1)S(1)} %get-tuple-element.147), channel_id=1, source_target_pairs={{0,2},{1,3},{2,0},{3,1},{4,6},{5,7},{6,4},{7,5},{8,10},{9,11},{10,... | collective-permute-start | bytes 49160 | tf_op jit(solution)/shard_map/ppermute | solution.py:354
  59.9 6.5 %collective-permute-start.30 = (bf16[64,512]{1,0:T(8,128)(2,1)S(1)}, bf16[64,512]{1,0:T(8,128)(2,1)S(1)}, u32[]{:S(2)}, u32[]{:S(2)}) collective-permute-start(bf16[64,512]{1,0:T(8,128)(2,1)S(1)} %get-tuple-element.154), channel_id=1, source_target_pairs={{0,15},{1,2},{2,1},{3,4},{4,3},{5,6},{6,5},{7,8},{8,7},{9,10},{10,... | collective-permute-start | bytes 196616 | tf_op jit(solution)/shard_map/ppermute | solution.py:360
  61.8 4.6 %collective-permute-start.31 = (bf16[64,512]{1,0:T(8,128)(2,1)S(1)}, bf16[64,512]{1,0:T(8,128)(2,1)S(1)}, u32[]{:S(2)}, u32[]{:S(2)}) collective-permute-start(bf16[64,512]{1,0:T(8,128)(2,1)S(1)} %get-tuple-element.155), channel_id=1, source_target_pairs={{0,1},{1,0},{2,3},{3,2},{4,5},{5,4},{6,7},{7,6},{8,9},{9,8},{10,11... | collective-permute-start | bytes 196616 | tf_op jit(solution)/shard_map/ppermute | solution.py:354
  (20 other events, 60.9 us)

commit v17 on v16

--- a/solution.py
+++ b/solution.py
@@ -453,7 +453,7 @@
     near, slope_0 = call(
         functools.partial(layer_local, layer=0, scale=scale),
         [total, total],
-        6 * square(mesh_rows, mesh_rows),
+        4 * square(mesh_rows, mesh_rows),
         hidden, own_t, processor_weights, ins[-1],
         free=1,
     )

time: 68.1 us -> 68 us (level)
  transfers between devices with their start and end apart: 32 -> 32, of which waited for: 16 -> 15; matrix products, arithmetic and copies ran while one was open for 0% -> 0% of each run, Pallas kernels for 17% -> 17%
where the time goes in v17:
time: 68 us; the launch traced here: 67.8 us
  starting transfers between devices  35 us (51%)
  Pallas kernels  19.3 us (28%)
  waiting for transfers between devices  11.5 us (17%)
  local copies, waits for them, and re-layouts  1.12 us (2%)
  between operations  0.95 us (1%)
    ppermute x26, starting transfers between devices, toggle(): return lax.ppermute(value, 'dom', [(i, i ^ bits) for i in range(peers)])  21.9 us
    pallas_call x21, Pallas kernels, call(): pl.pallas_call(inner, out_shape=shapes, in_specs=[pl.BlockSpec(memory_spa...  19.3 us
    ppermute x6, starting transfers between devices, across(): return lax.ppermute(value, 'dom', pairs)  13.1 us
    ppermute x26, waiting for transfers between devices, toggle(): return lax.ppermute(value, 'dom', [(i, i ^ bits) for i in range(peers)])  9.47 us
    ppermute x6, waiting for transfers between devices, across(): return lax.ppermute(value, 'dom', pairs)  1.99 us
  transfers between devices with their start and end apart: 32, of which 15 were waited for; matrix products, arithmetic and copies ran while one was open for 0% of the time, Pallas kernels for 17%

profile of v17, /device:TPU:0, one launch (start us, length us, event | category | flops | bytes accessed | tf_op | source)
XLA Modules:
  0.0 67.8 jit_solution(14873520306914292850)
XLA Ops:
  1.3 1.5 %shard_map.139 = (bf16[64,512]{1,0:T(8,128)(2,1)S(1)}, bf16[64,512]{1,0:T(8,128)(2,1)S(1)}) custom-call(bf16[1024,512]{1,0:T(8,128)(2,1)} %refs_0_.1, s32[1,2,64]{2,1,0:T(2,128)S(1)} %copy-done.4), custom_call_target="tpu_custom_call" | custom-call | flops 34359738368 | tf_op jit(solution)/shard_map/pallas_call | solution.py:84
  2.9 5.5 %collective-permute-start = (bf16[64,512]{1,0:T(8,128)(2,1)S(1)}, bf16[64,512]{1,0:T(8,128)(2,1)S(1)}, u32[]{:S(2)}, u32[]{:S(2)}) collective-permute-start(bf16[64,512]{1,0:T(8,128)(2,1)S(1)} %get-tuple-element.86), channel_id=1, source_target_pairs={{0,15},{1,2},{2,1},{3,4},{4,3},{5,6},{6,5},{7,8},{8,7},{9,10},{10,... | collective-permute-start | bytes 196616 | tf_op jit(solution)/shard_map/ppermute | solution.py:360
  9.9 1.9 %shard_map.140 = (f32[512,512]{1,0:T(8,128)S(1)}, bf16[1024,512]{1,0:T(8,128)(2,1)S(1)}, bf16[128,512]{1,0:T(8,128)(2,1)S(1)}, bf16[1024,512]{1,0:T(8,128)(2,1)S(1)}) custom-call(s32[4,512]{1,0:T(4,128)S(1)} %bitcast.8, bf16[512,512]{1,0:T(8,128)(2,1)S(1)} %copy-done.1, bf16[1024,512]{1,0:T(8,128)(2,1)S(1)} %copy-done.3, bf16[512,512]{1,0:T(8,128)(2,1)S(1)} %copy-done.5), custom_call_target="tpu_custom_call" | custom-call | flops 2147483648 | bytes 5382144 | tf_op jit(solution)/shard_map/pallas_call | solution.py:84
  13.1 1.4 %collective-permute-start.3 = (bf16[16,512]{1,0:T(8,128)(2,1)S(1)}, bf16[16,512]{1,0:T(8,128)(2,1)S(1)}, u32[]{:S(2)}, u32[]{:S(2)}) collective-permute-start(bf16[16,512]{1,0:T(8,128)(2,1)S(1)} %get-tuple-element.91), channel_id=1, source_target_pairs={{0,12},{1,13},{2,14},{3,15},{4,8},{5,9},{6,10},{7,11},{8,4},{9,5},... | collective-permute-start | bytes 49160 | tf_op jit(solution)/shard_map/ppermute | solution.py:354
  14.5 1.9 %collective-permute-start.4 = (bf16[16,512]{1,0:T(8,128)(2,1)S(1)}, bf16[16,512]{1,0:T(8,128)(2,1)S(1)}, u32[]{:S(2)}, u32[]{:S(2)}) collective-permute-start(bf16[16,512]{1,0:T(8,128)(2,1)S(1)} %get-tuple-element.92), channel_id=1, source_target_pairs={{0,4},{1,5},{2,6},{3,7},{4,0},{5,1},{6,2},{7,3},{8,12},{9,13},{10,... | collective-permute-start | bytes 49160 | tf_op jit(solution)/shard_map/ppermute | solution.py:354
  16.4 2.1 %collective-permute-start.5 = (bf16[64,512]{1,0:T(8,128)(2,1)S(1)}, bf16[64,512]{1,0:T(8,128)(2,1)S(1)}, u32[]{:S(2)}, u32[]{:S(2)}) collective-permute-start(bf16[64,512]{1,0:T(8,128)(2,1)S(1)} %get-tuple-element.101), channel_id=1, source_target_pairs={{0,15},{1,2},{2,1},{3,4},{4,3},{5,6},{6,5},{7,8},{8,7},{9,10},{10,... | collective-permute-start | bytes 196616 | tf_op jit(solution)/shard_map/ppermute | solution.py:360
  19.3 1.2 %collective-permute-start.8 = (bf16[16,512]{1,0:T(8,128)(2,1)S(1)}, bf16[16,512]{1,0:T(8,128)(2,1)S(1)}, u32[]{:S(2)}, u32[]{:S(2)}) collective-permute-start(bf16[16,512]{1,0:T(8,128)(2,1)S(1)} %get-tuple-element.104), channel_id=1, source_target_pairs={{0,2},{1,3},{2,0},{3,1},{4,6},{5,7},{6,4},{7,5},{8,10},{9,11},{10,... | collective-permute-start | bytes 49160 | tf_op jit(solution)/shard_map/ppermute | solution.py:354
  23.9 1.6 %collective-permute-start.9 = (bf16[16,512]{1,0:T(8,128)(2,1)S(1)}, bf16[16,512]{1,0:T(8,128)(2,1)S(1)}, u32[]{:S(2)}, u32[]{:S(2)}) collective-permute-start(bf16[16,512]{1,0:T(8,128)(2,1)S(1)} %get-tuple-element.108), channel_id=1, source_target_pairs={{0,8},{1,9},{2,10},{3,11},{4,12},{5,13},{6,14},{7,15},{8,0},{9,1},... | collective-permute-start | bytes 49160 | tf_op jit(solution)/shard_map/ppermute | solution.py:354
  25.5 1.9 %collective-permute-start.10 = (bf16[16,512]{1,0:T(8,128)(2,1)S(1)}, bf16[16,512]{1,0:T(8,128)(2,1)S(1)}, u32[]{:S(2)}, u32[]{:S(2)}) collective-permute-start(bf16[16,512]{1,0:T(8,128)(2,1)S(1)} %get-tuple-element.109), channel_id=1, source_target_pairs={{0,12},{1,13},{2,14},{3,15},{4,8},{5,9},{6,10},{7,11},{8,4},{9,5},... | collective-permute-start | bytes 49160 | tf_op jit(solution)/shard_map/ppermute | solution.py:354
  27.4 1.7 %collective-permute-start.12 = (bf16[128,512]{1,0:T(8,128)(2,1)S(1)}, bf16[128,512]{1,0:T(8,128)(2,1)S(1)}, u32[]{:S(2)}, u32[]{:S(2)}) collective-permute-start(bf16[128,512]{1,0:T(8,128)(2,1)S(1)} %get-tuple-element.116), channel_id=1, source_target_pairs={{0,15},{1,2},{2,1},{3,4},{4,3},{5,6},{6,5},{7,8},{8,7},{9,10},{10,... | collective-permute-start | bytes 393224 | tf_op jit(solution)/shard_map/ppermute | solution.py:360
  29.2 1.9 %collective-permute-done.10.refs_1_ = bf16[16,512]{1,0:T(8,128)(2,1)S(1)} collective-permute-done((bf16[16,512]{1,0:T(8,128)(2,1)S(1)}, bf16[16,512]{1,0:T(8,128)(2,1)S(1)}, u32[]{:S(2)}, u32[]{:S(2)}) %collective-permute-start.10) | collective-permute-done | bytes 16416 | tf_op jit(solution)/shard_map/ppermute | solution.py:354
  31.9 1.4 %collective-permute-start.13 = (bf16[144,512]{1,0:T(8,128)(2,1)S(1)}, bf16[144,512]{1,0:T(8,128)(2,1)S(1)}, u32[]{:S(2)}, u32[]{:S(2)}) collective-permute-start(bf16[144,512]{1,0:T(8,128)(2,1)S(1)} %get-tuple-element.117), channel_id=1, source_target_pairs={{0,1},{1,0},{2,3},{3,2},{4,5},{5,4},{6,7},{7,6},{8,9},{9,8},{10,11... | collective-permute-start | bytes 442376 | tf_op jit(solution)/shard_map/ppermute | solution.py:354
  35.2 1.3 %shard_map.149 = (bf16[512,512]{1,0:T(8,128)(2,1)S(1)}, bf16[512,512]{1,0:T(8,128)(2,1)S(1)}, bf16[128,512]{1,0:T(8,128)(2,1)S(1)}, bf16[128,512]{1,0:T(8,128)(2...) custom-call(f32[512,512]{1,0:T(8,128)S(1)} %get-tuple-element.112.ne, ...), custom_call_target="tpu_custom_call" | custom-call | flops 1610612736 | bytes 5111808 | tf_op jit(solution)/shard_map/pallas_call | solution.py:84
  37.6 1.7 %collective-permute-start.17 = (bf16[16,512]{1,0:T(8,128)(2,1)S(1)}, bf16[16,512]{1,0:T(8,128)(2,1)S(1)}, u32[]{:S(2)}, u32[]{:S(2)}) collective-permute-start(bf16[16,512]{1,0:T(8,128)(2,1)S(1)} %get-tuple-element.124), channel_id=1, source_target_pairs={{0,12},{1,13},{2,14},{3,15},{4,8},{5,9},{6,10},{7,11},{8,4},{9,5},... | collective-permute-start | bytes 49160 | tf_op jit(solution)/shard_map/ppermute | solution.py:354
  41.4 1.9 %collective-permute-done.17.refs_1_ = bf16[16,512]{1,0:T(8,128)(2,1)S(1)} collective-permute-done((bf16[16,512]{1,0:T(8,128)(2,1)S(1)}, bf16[16,512]{1,0:T(8,128)(2,1)S(1)}, u32[]{:S(2)}, u32[]{:S(2)}) %collective-permute-start.17) | collective-permute-done | bytes 16416 | tf_op jit(solution)/shard_map/ppermute | solution.py:354
  46.5 1.1 %collective-permute-done.21.refs_8_ = bf16[16,512]{1,0:T(8,128)(2,1)S(1)} collective-permute-done((bf16[16,512]{1,0:T(8,128)(2,1)S(1)}, bf16[16,512]{1,0:T(8,128)(2,1)S(1)}, u32[]{:S(2)}, u32[]{:S(2)}) %collective-permute-start.21) | collective-permute-done | bytes 16416 | tf_op jit(solution)/shard_map/ppermute | solution.py:354
  49.2 1.9 %collective-permute-start.24 = (bf16[16,512]{1,0:T(8,128)(2,1)S(1)}, bf16[16,512]{1,0:T(8,128)(2,1)S(1)}, u32[]{:S(2)}, u32[]{:S(2)}) collective-permute-start(bf16[16,512]{1,0:T(8,128)(2,1)S(1)} %get-tuple-element.137), channel_id=1, source_target_pairs={{0,12},{1,13},{2,14},{3,15},{4,8},{5,9},{6,10},{7,11},{8,4},{9,5},... | collective-permute-start | bytes 49160 | tf_op jit(solution)/shard_map/ppermute | solution.py:354
  51.1 1.1 %collective-permute-start.25 = (bf16[16,512]{1,0:T(8,128)(2,1)S(1)}, bf16[16,512]{1,0:T(8,128)(2,1)S(1)}, u32[]{:S(2)}, u32[]{:S(2)}) collective-permute-start(bf16[16,512]{1,0:T(8,128)(2,1)S(1)} %get-tuple-element.138), channel_id=1, source_target_pairs={{0,4},{1,5},{2,6},{3,7},{4,0},{5,1},{6,2},{7,3},{8,12},{9,13},{10,... | collective-permute-start | bytes 49160 | tf_op jit(solution)/shard_map/ppermute | solution.py:354
  53.5 1.2 %collective-permute-done.24.refs_1_ = bf16[16,512]{1,0:T(8,128)(2,1)S(1)} collective-permute-done((bf16[16,512]{1,0:T(8,128)(2,1)S(1)}, bf16[16,512]{1,0:T(8,128)(2,1)S(1)}, u32[]{:S(2)}, u32[]{:S(2)}) %collective-permute-start.24) | collective-permute-done | bytes 16416 | tf_op jit(solution)/shard_map/ppermute | solution.py:354
  57.4 1.4 %shard_map.155 = (bf16[1024,512]{1,0:T(8,128)(2,1)}, f32[8,128]{1,0:T(8,128)S(1)}) custom-call(f32[1024,512]{1,0:T(8,128)S(1)} %shard_map.151.refs_11_.refs_0_, bf16[128,1024]{1,0:T(8,128)(2,1)S(1)} %get-tuple-element.127.refs_1_, bf16[128,512]{1,0:T(8,128)(2,1)S(1)} %collective-permute-done.19.refs_6_.refs_2_, ...), custom_call_target="tpu_custom_call" | custom-call | flops 134217728 | bytes 3706880 | tf_op jit(solution)/shard_map/pallas_call | solution.py:84
  59.9 2.0 %collective-permute-start.30 = (bf16[64,512]{1,0:T(8,128)(2,1)S(1)}, bf16[64,512]{1,0:T(8,128)(2,1)S(1)}, u32[]{:S(2)}, u32[]{:S(2)}) collective-permute-start(bf16[64,512]{1,0:T(8,128)(2,1)S(1)} %get-tuple-element.154), channel_id=1, source_target_pairs={{0,15},{1,2},{2,1},{3,4},{4,3},{5,6},{6,5},{7,8},{8,7},{9,10},{10,... | collective-permute-start | bytes 196616 | tf_op jit(solution)/shard_map/ppermute | solution.py:360
  61.8 2.5 %shard_map.158 = (f32[1024,512]{1,0:T(8,128)S(1)}, bf16[1024,128]{1,0:T(8,128)(2,1)S(1)}, f32[128,512]{1,0:T(8,128)S(1)}, bf16[512,512]{1,0:T(8,128)(2,1)}) custom-call(bf16[1024,512]{1,0:T(8,128)(2,1)S(1)} %get-tuple-element.141.own_t, bf16[512,512]{1,0:T(8,128)(2,1)S(1)} %get-tuple-element.149.grad, s32[1,2,64]{2,1,0:T(2,128)S(1)} %copy-done.4, ...), custom_call_target="tpu_custom_call" | custom-call | flops 1073741824 | bytes 7340544 | tf_op jit(solution)/shard_map/pallas_call | solution.py:84
  64.4 2.0 %collective-permute-done.30.outer_in = bf16[64,512]{1,0:T(8,128)(2,1)S(1)} collective-permute-done((bf16[64,512]{1,0:T(8,128)(2,1)S(1)}, bf16[64,512]{1,0:T(8,128)(2,1)S(1)}, u32[]{:S(2)}, u32[]{:S(2)}) %collective-permute-start.30) | collective-permute-done | bytes 65568 | tf_op jit(solution)/shard_map/ppermute | solution.py:360
  66.3 1.5 %shard_map.159 = bf16[1024,512]{1,0:T(8,128)(2,1)} custom-call(f32[1024,512]{1,0:T(8,128)S(1)} %get-tuple-element.151.base, bf16[1024,128]{1,0:T(8,128)(2,1)S(1)} %get-tuple-element.152.table, f32[128,512]{1,0:T(8,128)S(1)} %get-tuple-element.153.slope_rows, bf16[512,512]{1,0:T(8,128)(2,1)S(1)} %copy-done.1, ...), custom_call_target="tpu_custom_call" | custom-call | flops 268435456 | bytes 4325376 | tf_op jit(solution)/shard_map/pallas_call | solution.py:84
  (85 shorter events, 23.3 us)
Async XLA Ops:
  2.9 9.0 %collective-permute-start = (bf16[64,512]{1,0:T(8,128)(2,1)S(1)}, bf16[64,512]{1,0:T(8,128)(2,1)S(1)}, u32[]{:S(2)}, u32[]{:S(2)}) collective-permute-start(bf16[64,512]{1,0:T(8,128)(2,1)S(1)} %get-tuple-element.86), channel_id=1, source_target_pairs={{0,15},{1,2},{2,1},{3,4},{4,3},{5,6},{6,5},{7,8},{8,7},{9,10},{10,... | collective-permute-start | bytes 196616 | tf_op jit(solution)/shard_map/ppermute | solution.py:360
  12.8 5.6 %collective-permute-start.2 = (bf16[16,512]{1,0:T(8,128)(2,1)S(1)}, bf16[16,512]{1,0:T(8,128)(2,1)S(1)}, u32[]{:S(2)}, u32[]{:S(2)}) collective-permute-start(bf16[16,512]{1,0:T(8,128)(2,1)S(1)} %get-tuple-element.90), channel_id=1, source_target_pairs={{0,8},{1,9},{2,10},{3,11},{4,12},{5,13},{6,14},{7,15},{8,0},{9,1},... | collective-permute-start | bytes 49160 | tf_op jit(solution)/shard_map/ppermute | solution.py:354
  13.1 5.6 %collective-permute-start.3 = (bf16[16,512]{1,0:T(8,128)(2,1)S(1)}, bf16[16,512]{1,0:T(8,128)(2,1)S(1)}, u32[]{:S(2)}, u32[]{:S(2)}) collective-permute-start(bf16[16,512]{1,0:T(8,128)(2,1)S(1)} %get-tuple-element.91), channel_id=1, source_target_pairs={{0,12},{1,13},{2,14},{3,15},{4,8},{5,9},{6,10},{7,11},{8,4},{9,5},... | collective-permute-start | bytes 49160 | tf_op jit(solution)/shard_map/ppermute | solution.py:354
  14.5 4.2 %collective-permute-start.4 = (bf16[16,512]{1,0:T(8,128)(2,1)S(1)}, bf16[16,512]{1,0:T(8,128)(2,1)S(1)}, u32[]{:S(2)}, u32[]{:S(2)}) collective-permute-start(bf16[16,512]{1,0:T(8,128)(2,1)S(1)} %get-tuple-element.92), channel_id=1, source_target_pairs={{0,4},{1,5},{2,6},{3,7},{4,0},{5,1},{6,2},{7,3},{8,12},{9,13},{10,... | collective-permute-start | bytes 49160 | tf_op jit(solution)/shard_map/ppermute | solution.py:354
  16.4 6.7 %collective-permute-start.5 = (bf16[64,512]{1,0:T(8,128)(2,1)S(1)}, bf16[64,512]{1,0:T(8,128)(2,1)S(1)}, u32[]{:S(2)}, u32[]{:S(2)}) collective-permute-start(bf16[64,512]{1,0:T(8,128)(2,1)S(1)} %get-tuple-element.101), channel_id=1, source_target_pairs={{0,15},{1,2},{2,1},{3,4},{4,3},{5,6},{6,5},{7,8},{8,7},{9,10},{10,... | collective-permute-start | bytes 196616 | tf_op jit(solution)/shard_map/ppermute | solution.py:360
  19.3 3.8 %collective-permute-start.8 = (bf16[16,512]{1,0:T(8,128)(2,1)S(1)}, bf16[16,512]{1,0:T(8,128)(2,1)S(1)}, u32[]{:S(2)}, u32[]{:S(2)}) collective-permute-start(bf16[16,512]{1,0:T(8,128)(2,1)S(1)} %get-tuple-element.104), channel_id=1, source_target_pairs={{0,2},{1,3},{2,0},{3,1},{4,6},{5,7},{6,4},{7,5},{8,10},{9,11},{10,... | collective-permute-start | bytes 49160 | tf_op jit(solution)/shard_map/ppermute | solution.py:354
  23.9 5.3 %collective-permute-start.9 = (bf16[16,512]{1,0:T(8,128)(2,1)S(1)}, bf16[16,512]{1,0:T(8,128)(2,1)S(1)}, u32[]{:S(2)}, u32[]{:S(2)}) collective-permute-start(bf16[16,512]{1,0:T(8,128)(2,1)S(1)} %get-tuple-element.108), channel_id=1, source_target_pairs={{0,8},{1,9},{2,10},{3,11},{4,12},{5,13},{6,14},{7,15},{8,0},{9,1},... | collective-permute-start | bytes 49160 | tf_op jit(solution)/shard_map/ppermute | solution.py:354
  25.5 5.5 %collective-permute-start.10 = (bf16[16,512]{1,0:T(8,128)(2,1)S(1)}, bf16[16,512]{1,0:T(8,128)(2,1)S(1)}, u32[]{:S(2)}, u32[]{:S(2)}) collective-permute-start(bf16[16,512]{1,0:T(8,128)(2,1)S(1)} %get-tuple-element.109), channel_id=1, source_target_pairs={{0,12},{1,13},{2,14},{3,15},{4,8},{5,9},{6,10},{7,11},{8,4},{9,5},... | collective-permute-start | bytes 49160 | tf_op jit(solution)/shard_map/ppermute | solution.py:354
  27.3 3.8 %collective-permute-start.11 = (bf16[16,512]{1,0:T(8,128)(2,1)S(1)}, bf16[16,512]{1,0:T(8,128)(2,1)S(1)}, u32[]{:S(2)}, u32[]{:S(2)}) collective-permute-start(bf16[16,512]{1,0:T(8,128)(2,1)S(1)} %get-tuple-element.110), channel_id=1, source_target_pairs={{0,4},{1,5},{2,6},{3,7},{4,0},{5,1},{6,2},{7,3},{8,12},{9,13},{10,... | collective-permute-start | bytes 49160 | tf_op jit(solution)/shard_map/ppermute | solution.py:354
  27.4 7.8 %collective-permute-start.12 = (bf16[128,512]{1,0:T(8,128)(2,1)S(1)}, bf16[128,512]{1,0:T(8,128)(2,1)S(1)}, u32[]{:S(2)}, u32[]{:S(2)}) collective-permute-start(bf16[128,512]{1,0:T(8,128)(2,1)S(1)} %get-tuple-element.116), channel_id=1, source_target_pairs={{0,15},{1,2},{2,1},{3,4},{4,3},{5,6},{6,5},{7,8},{8,7},{9,10},{10,... | collective-permute-start | bytes 393224 | tf_op jit(solution)/shard_map/ppermute | solution.py:360
  31.4 3.8 %collective-permute-start.15 = (bf16[16,512]{1,0:T(8,128)(2,1)S(1)}, bf16[16,512]{1,0:T(8,128)(2,1)S(1)}, u32[]{:S(2)}, u32[]{:S(2)}) collective-permute-start(bf16[16,512]{1,0:T(8,128)(2,1)S(1)} %get-tuple-element.119), channel_id=1, source_target_pairs={{0,2},{1,3},{2,0},{3,1},{4,6},{5,7},{6,4},{7,5},{8,10},{9,11},{10,... | collective-permute-start | bytes 49160 | tf_op jit(solution)/shard_map/ppermute | solution.py:354
  36.6 4.8 %collective-permute-start.16 = (bf16[16,512]{1,0:T(8,128)(2,1)S(1)}, bf16[16,512]{1,0:T(8,128)(2,1)S(1)}, u32[]{:S(2)}, u32[]{:S(2)}) collective-permute-start(bf16[16,512]{1,0:T(8,128)(2,1)S(1)} %get-tuple-element.123), channel_id=1, source_target_pairs={{0,8},{1,9},{2,10},{3,11},{4,12},{5,13},{6,14},{7,15},{8,0},{9,1},... | collective-permute-start | bytes 49160 | tf_op jit(solution)/shard_map/ppermute | solution.py:354
  37.6 5.6 %collective-permute-start.17 = (bf16[16,512]{1,0:T(8,128)(2,1)S(1)}, bf16[16,512]{1,0:T(8,128)(2,1)S(1)}, u32[]{:S(2)}, u32[]{:S(2)}) collective-permute-start(bf16[16,512]{1,0:T(8,128)(2,1)S(1)} %get-tuple-element.124), channel_id=1, source_target_pairs={{0,12},{1,13},{2,14},{3,15},{4,8},{5,9},{6,10},{7,11},{8,4},{9,5},... | collective-permute-start | bytes 49160 | tf_op jit(solution)/shard_map/ppermute | solution.py:354
  39.4 3.9 %collective-permute-start.18 = (bf16[16,512]{1,0:T(8,128)(2,1)S(1)}, bf16[16,512]{1,0:T(8,128)(2,1)S(1)}, u32[]{:S(2)}, u32[]{:S(2)}) collective-permute-start(bf16[16,512]{1,0:T(8,128)(2,1)S(1)} %get-tuple-element.125), channel_id=1, source_target_pairs={{0,4},{1,5},{2,6},{3,7},{4,0},{5,1},{6,2},{7,3},{8,12},{9,13},{10,... | collective-permute-start | bytes 49160 | tf_op jit(solution)/shard_map/ppermute | solution.py:354
  40.1 7.7 %collective-permute-start.19 = (bf16[128,512]{1,0:T(8,128)(2,1)S(1)}, bf16[128,512]{1,0:T(8,128)(2,1)S(1)}, u32[]{:S(2)}, u32[]{:S(2)}) collective-permute-start(bf16[128,512]{1,0:T(8,128)(2,1)S(1)} %get-tuple-element.128), channel_id=1, source_target_pairs={{0,15},{1,2},{2,1},{3,4},{4,3},{5,6},{6,5},{7,8},{8,7},{9,10},{10,... | collective-permute-start | bytes 393224 | tf_op jit(solution)/shard_map/ppermute | solution.py:360
  43.4 4.2 %collective-permute-start.21 = (bf16[16,512]{1,0:T(8,128)(2,1)S(1)}, bf16[16,512]{1,0:T(8,128)(2,1)S(1)}, u32[]{:S(2)}, u32[]{:S(2)}) collective-permute-start(bf16[16,512]{1,0:T(8,128)(2,1)S(1)} %get-tuple-element.132), channel_id=1, source_target_pairs={{0,3},{1,2},{2,1},{3,0},{4,7},{5,6},{6,5},{7,4},{8,11},{9,10},{10,... | collective-permute-start | bytes 49160 | tf_op jit(solution)/shard_map/ppermute | solution.py:354
  43.5 4.4 %collective-permute-start.22 = (bf16[16,512]{1,0:T(8,128)(2,1)S(1)}, bf16[16,512]{1,0:T(8,128)(2,1)S(1)}, u32[]{:S(2)}, u32[]{:S(2)}) collective-permute-start(bf16[16,512]{1,0:T(8,128)(2,1)S(1)} %get-tuple-element.133), channel_id=1, source_target_pairs={{0,2},{1,3},{2,0},{3,1},{4,6},{5,7},{6,4},{7,5},{8,10},{9,11},{10,... | collective-permute-start | bytes 49160 | tf_op jit(solution)/shard_map/ppermute | solution.py:354
  48.7 4.9 %collective-permute-start.23 = (bf16[16,512]{1,0:T(8,128)(2,1)S(1)}, bf16[16,512]{1,0:T(8,128)(2,1)S(1)}, u32[]{:S(2)}, u32[]{:S(2)}) collective-permute-start(bf16[16,512]{1,0:T(8,128)(2,1)S(1)} %get-tuple-element.136), channel_id=1, source_target_pairs={{0,8},{1,9},{2,10},{3,11},{4,12},{5,13},{6,14},{7,15},{8,0},{9,1},... | collective-permute-start | bytes 49160 | tf_op jit(solution)/shard_map/ppermute | solution.py:354
  49.2 5.5 %collective-permute-start.24 = (bf16[16,512]{1,0:T(8,128)(2,1)S(1)}, bf16[16,512]{1,0:T(8,128)(2,1)S(1)}, u32[]{:S(2)}, u32[]{:S(2)}) collective-permute-start(bf16[16,512]{1,0:T(8,128)(2,1)S(1)} %get-tuple-element.137), channel_id=1, source_target_pairs={{0,12},{1,13},{2,14},{3,15},{4,8},{5,9},{6,10},{7,11},{8,4},{9,5},... | collective-permute-start | bytes 49160 | tf_op jit(solution)/shard_map/ppermute | solution.py:354
  51.1 3.8 %collective-permute-start.25 = (bf16[16,512]{1,0:T(8,128)(2,1)S(1)}, bf16[16,512]{1,0:T(8,128)(2,1)S(1)}, u32[]{:S(2)}, u32[]{:S(2)}) collective-permute-start(bf16[16,512]{1,0:T(8,128)(2,1)S(1)} %get-tuple-element.138), channel_id=1, source_target_pairs={{0,4},{1,5},{2,6},{3,7},{4,0},{5,1},{6,2},{7,3},{8,12},{9,13},{10,... | collective-permute-start | bytes 49160 | tf_op jit(solution)/shard_map/ppermute | solution.py:354
  52.2 6.9 %collective-permute-start.26 = (bf16[64,512]{1,0:T(8,128)(2,1)S(1)}, bf16[64,512]{1,0:T(8,128)(2,1)S(1)}, u32[]{:S(2)}, u32[]{:S(2)}) collective-permute-start(bf16[64,512]{1,0:T(8,128)(2,1)S(1)} %get-tuple-element.144), channel_id=1, source_target_pairs={{0,15},{1,2},{2,1},{3,4},{4,3},{5,6},{6,5},{7,8},{8,7},{9,10},{10,... | collective-permute-start | bytes 196616 | tf_op jit(solution)/shard_map/ppermute | solution.py:360
  55.2 4.0 %collective-permute-start.29 = (bf16[16,512]{1,0:T(8,128)(2,1)S(1)}, bf16[16,512]{1,0:T(8,128)(2,1)S(1)}, u32[]{:S(2)}, u32[]{:S(2)}) collective-permute-start(bf16[16,512]{1,0:T(8,128)(2,1)S(1)} %get-tuple-element.147), channel_id=1, source_target_pairs={{0,2},{1,3},{2,0},{3,1},{4,6},{5,7},{6,4},{7,5},{8,10},{9,11},{10,... | collective-permute-start | bytes 49160 | tf_op jit(solution)/shard_map/ppermute | solution.py:354
  59.9 6.5 %collective-permute-start.30 = (bf16[64,512]{1,0:T(8,128)(2,1)S(1)}, bf16[64,512]{1,0:T(8,128)(2,1)S(1)}, u32[]{:S(2)}, u32[]{:S(2)}) collective-permute-start(bf16[64,512]{1,0:T(8,128)(2,1)S(1)} %get-tuple-element.154), channel_id=1, source_target_pairs={{0,15},{1,2},{2,1},{3,4},{4,3},{5,6},{6,5},{7,8},{8,7},{9,10},{10,... | collective-permute-start | bytes 196616 | tf_op jit(solution)/shard_map/ppermute | solution.py:360
  61.8 4.5 %collective-permute-start.31 = (bf16[64,512]{1,0:T(8,128)(2,1)S(1)}, bf16[64,512]{1,0:T(8,128)(2,1)S(1)}, u32[]{:S(2)}, u32[]{:S(2)}) collective-permute-start(bf16[64,512]{1,0:T(8,128)(2,1)S(1)} %get-tuple-element.155), channel_id=1, source_target_pairs={{0,1},{1,0},{2,3},{3,2},{4,5},{5,4},{6,7},{7,6},{8,9},{9,8},{10,11... | collective-permute-start | bytes 196616 | tf_op jit(solution)/shard_map/ppermute | solution.py:354
  (20 other events, 76.0 us)

commit v18 on v17

--- a/solution.py
+++ b/solution.py
@@ -13,7 +13,7 @@
 FIRST_LIMIT = 107 * 512 * 1024
 PLANE = 4
 STAGED = 16
-CHUNKS = 4
+CHUNKS = 8
 Z_ORDER = (2, 3, 1)
 
 

time: 68 us -> 68.4 us (level)
  no operation moved by 1% of the time
where the time goes in v18:
time: 68.4 us; the launch traced here: 68.2 us
  starting transfers between devices  34.9 us (51%)
  Pallas kernels  19.7 us (29%)
  waiting for transfers between devices  11.5 us (17%)
  local copies, waits for them, and re-layouts  1.12 us (2%)
  between operations  0.95 us (1%)
    ppermute x26, starting transfers between devices, toggle(): return lax.ppermute(value, 'dom', [(i, i ^ bits) for i in range(peers)])  21.9 us
    pallas_call x21, Pallas kernels, call(): pl.pallas_call(inner, out_shape=shapes, in_specs=[pl.BlockSpec(memory_spa...  19.7 us
    ppermute x6, starting transfers between devices, across(): return lax.ppermute(value, 'dom', pairs)  13 us
    ppermute x26, waiting for transfers between devices, toggle(): return lax.ppermute(value, 'dom', [(i, i ^ bits) for i in range(peers)])  9.52 us
    ppermute x6, waiting for transfers between devices, across(): return lax.ppermute(value, 'dom', pairs)  1.99 us
  transfers between devices with their start and end apart: 32, of which 15 were waited for; matrix products, arithmetic and copies ran while one was open for 0% of the time, Pallas kernels for 17%

profile of v18, /device:TPU:0, one launch (start us, length us, event | category | flops | bytes accessed | tf_op | source)
XLA Modules:
  0.0 68.2 jit_solution(5318875960749893412)
XLA Ops:
  1.3 1.9 %shard_map.139 = (bf16[64,512]{1,0:T(8,128)(2,1)S(1)}, bf16[64,512]{1,0:T(8,128)(2,1)S(1)}) custom-call(bf16[1024,512]{1,0:T(8,128)(2,1)} %refs_0_.1, s32[1,2,64]{2,1,0:T(2,128)S(1)} %copy-done.4), custom_call_target="tpu_custom_call" | custom-call | flops 34359738368 | tf_op jit(solution)/shard_map/pallas_call | solution.py:84
  3.3 5.5 %collective-permute-start = (bf16[64,512]{1,0:T(8,128)(2,1)S(1)}, bf16[64,512]{1,0:T(8,128)(2,1)S(1)}, u32[]{:S(2)}, u32[]{:S(2)}) collective-permute-start(bf16[64,512]{1,0:T(8,128)(2,1)S(1)} %get-tuple-element.86), channel_id=1, source_target_pairs={{0,15},{1,2},{2,1},{3,4},{4,3},{5,6},{6,5},{7,8},{8,7},{9,10},{10,... | collective-permute-start | bytes 196616 | tf_op jit(solution)/shard_map/ppermute | solution.py:360
  10.3 1.9 %shard_map.140 = (f32[512,512]{1,0:T(8,128)S(1)}, bf16[1024,512]{1,0:T(8,128)(2,1)S(1)}, bf16[128,512]{1,0:T(8,128)(2,1)S(1)}, bf16[1024,512]{1,0:T(8,128)(2,1)S(1)}) custom-call(s32[4,512]{1,0:T(4,128)S(1)} %bitcast.8, bf16[512,512]{1,0:T(8,128)(2,1)S(1)} %copy-done.1, bf16[1024,512]{1,0:T(8,128)(2,1)S(1)} %copy-done.3, bf16[512,512]{1,0:T(8,128)(2,1)S(1)} %copy-done.5), custom_call_target="tpu_custom_call" | custom-call | flops 2147483648 | bytes 5382144 | tf_op jit(solution)/shard_map/pallas_call | solution.py:84
  13.5 1.4 %collective-permute-start.3 = (bf16[16,512]{1,0:T(8,128)(2,1)S(1)}, bf16[16,512]{1,0:T(8,128)(2,1)S(1)}, u32[]{:S(2)}, u32[]{:S(2)}) collective-permute-start(bf16[16,512]{1,0:T(8,128)(2,1)S(1)} %get-tuple-element.91), channel_id=1, source_target_pairs={{0,12},{1,13},{2,14},{3,15},{4,8},{5,9},{6,10},{7,11},{8,4},{9,5},... | collective-permute-start | bytes 49160 | tf_op jit(solution)/shard_map/ppermute | solution.py:354
  14.8 1.9 %collective-permute-start.4 = (bf16[16,512]{1,0:T(8,128)(2,1)S(1)}, bf16[16,512]{1,0:T(8,128)(2,1)S(1)}, u32[]{:S(2)}, u32[]{:S(2)}) collective-permute-start(bf16[16,512]{1,0:T(8,128)(2,1)S(1)} %get-tuple-element.92), channel_id=1, source_target_pairs={{0,4},{1,5},{2,6},{3,7},{4,0},{5,1},{6,2},{7,3},{8,12},{9,13},{10,... | collective-permute-start | bytes 49160 | tf_op jit(solution)/shard_map/ppermute | solution.py:354
  16.8 2.1 %collective-permute-start.5 = (bf16[64,512]{1,0:T(8,128)(2,1)S(1)}, bf16[64,512]{1,0:T(8,128)(2,1)S(1)}, u32[]{:S(2)}, u32[]{:S(2)}) collective-permute-start(bf16[64,512]{1,0:T(8,128)(2,1)S(1)} %get-tuple-element.101), channel_id=1, source_target_pairs={{0,15},{1,2},{2,1},{3,4},{4,3},{5,6},{6,5},{7,8},{8,7},{9,10},{10,... | collective-permute-start | bytes 196616 | tf_op jit(solution)/shard_map/ppermute | solution.py:360
  19.6 1.2 %collective-permute-start.8 = (bf16[16,512]{1,0:T(8,128)(2,1)S(1)}, bf16[16,512]{1,0:T(8,128)(2,1)S(1)}, u32[]{:S(2)}, u32[]{:S(2)}) collective-permute-start(bf16[16,512]{1,0:T(8,128)(2,1)S(1)} %get-tuple-element.104), channel_id=1, source_target_pairs={{0,2},{1,3},{2,0},{3,1},{4,6},{5,7},{6,4},{7,5},{8,10},{9,11},{10,... | collective-permute-start | bytes 49160 | tf_op jit(solution)/shard_map/ppermute | solution.py:354
  24.2 1.6 %collective-permute-start.9 = (bf16[16,512]{1,0:T(8,128)(2,1)S(1)}, bf16[16,512]{1,0:T(8,128)(2,1)S(1)}, u32[]{:S(2)}, u32[]{:S(2)}) collective-permute-start(bf16[16,512]{1,0:T(8,128)(2,1)S(1)} %get-tuple-element.108), channel_id=1, source_target_pairs={{0,8},{1,9},{2,10},{3,11},{4,12},{5,13},{6,14},{7,15},{8,0},{9,1},... | collective-permute-start | bytes 49160 | tf_op jit(solution)/shard_map/ppermute | solution.py:354
  25.9 1.9 %collective-permute-start.10 = (bf16[16,512]{1,0:T(8,128)(2,1)S(1)}, bf16[16,512]{1,0:T(8,128)(2,1)S(1)}, u32[]{:S(2)}, u32[]{:S(2)}) collective-permute-start(bf16[16,512]{1,0:T(8,128)(2,1)S(1)} %get-tuple-element.109), channel_id=1, source_target_pairs={{0,12},{1,13},{2,14},{3,15},{4,8},{5,9},{6,10},{7,11},{8,4},{9,5},... | collective-permute-start | bytes 49160 | tf_op jit(solution)/shard_map/ppermute | solution.py:354
  27.8 1.7 %collective-permute-start.12 = (bf16[128,512]{1,0:T(8,128)(2,1)S(1)}, bf16[128,512]{1,0:T(8,128)(2,1)S(1)}, u32[]{:S(2)}, u32[]{:S(2)}) collective-permute-start(bf16[128,512]{1,0:T(8,128)(2,1)S(1)} %get-tuple-element.116), channel_id=1, source_target_pairs={{0,15},{1,2},{2,1},{3,4},{4,3},{5,6},{6,5},{7,8},{8,7},{9,10},{10,... | collective-permute-start | bytes 393224 | tf_op jit(solution)/shard_map/ppermute | solution.py:360
  29.5 1.9 %collective-permute-done.10.refs_1_ = bf16[16,512]{1,0:T(8,128)(2,1)S(1)} collective-permute-done((bf16[16,512]{1,0:T(8,128)(2,1)S(1)}, bf16[16,512]{1,0:T(8,128)(2,1)S(1)}, u32[]{:S(2)}, u32[]{:S(2)}) %collective-permute-start.10) | collective-permute-done | bytes 16416 | tf_op jit(solution)/shard_map/ppermute | solution.py:354
  32.3 1.4 %collective-permute-start.13 = (bf16[144,512]{1,0:T(8,128)(2,1)S(1)}, bf16[144,512]{1,0:T(8,128)(2,1)S(1)}, u32[]{:S(2)}, u32[]{:S(2)}) collective-permute-start(bf16[144,512]{1,0:T(8,128)(2,1)S(1)} %get-tuple-element.117), channel_id=1, source_target_pairs={{0,1},{1,0},{2,3},{3,2},{4,5},{5,4},{6,7},{7,6},{8,9},{9,8},{10,11... | collective-permute-start | bytes 442376 | tf_op jit(solution)/shard_map/ppermute | solution.py:354
  35.6 1.3 %shard_map.149 = (bf16[512,512]{1,0:T(8,128)(2,1)S(1)}, bf16[512,512]{1,0:T(8,128)(2,1)S(1)}, bf16[128,512]{1,0:T(8,128)(2,1)S(1)}, bf16[128,512]{1,0:T(8,128)(2...) custom-call(f32[512,512]{1,0:T(8,128)S(1)} %get-tuple-element.112.ne, ...), custom_call_target="tpu_custom_call" | custom-call | flops 1610612736 | bytes 5111808 | tf_op jit(solution)/shard_map/pallas_call | solution.py:84
  37.0 1.1 %collective-permute-start.16 = (bf16[16,512]{1,0:T(8,128)(2,1)S(1)}, bf16[16,512]{1,0:T(8,128)(2,1)S(1)}, u32[]{:S(2)}, u32[]{:S(2)}) collective-permute-start(bf16[16,512]{1,0:T(8,128)(2,1)S(1)} %get-tuple-element.123), channel_id=1, source_target_pairs={{0,8},{1,9},{2,10},{3,11},{4,12},{5,13},{6,14},{7,15},{8,0},{9,1},... | collective-permute-start | bytes 49160 | tf_op jit(solution)/shard_map/ppermute | solution.py:354
  38.0 1.7 %collective-permute-start.17 = (bf16[16,512]{1,0:T(8,128)(2,1)S(1)}, bf16[16,512]{1,0:T(8,128)(2,1)S(1)}, u32[]{:S(2)}, u32[]{:S(2)}) collective-permute-start(bf16[16,512]{1,0:T(8,128)(2,1)S(1)} %get-tuple-element.124), channel_id=1, source_target_pairs={{0,12},{1,13},{2,14},{3,15},{4,8},{5,9},{6,10},{7,11},{8,4},{9,5},... | collective-permute-start | bytes 49160 | tf_op jit(solution)/shard_map/ppermute | solution.py:354
  41.7 2.0 %collective-permute-done.17.refs_1_ = bf16[16,512]{1,0:T(8,128)(2,1)S(1)} collective-permute-done((bf16[16,512]{1,0:T(8,128)(2,1)S(1)}, bf16[16,512]{1,0:T(8,128)(2,1)S(1)}, u32[]{:S(2)}, u32[]{:S(2)}) %collective-permute-start.17) | collective-permute-done | bytes 16416 | tf_op jit(solution)/shard_map/ppermute | solution.py:354
  49.6 1.9 %collective-permute-start.24 = (bf16[16,512]{1,0:T(8,128)(2,1)S(1)}, bf16[16,512]{1,0:T(8,128)(2,1)S(1)}, u32[]{:S(2)}, u32[]{:S(2)}) collective-permute-start(bf16[16,512]{1,0:T(8,128)(2,1)S(1)} %get-tuple-element.137), channel_id=1, source_target_pairs={{0,12},{1,13},{2,14},{3,15},{4,8},{5,9},{6,10},{7,11},{8,4},{9,5},... | collective-permute-start | bytes 49160 | tf_op jit(solution)/shard_map/ppermute | solution.py:354
  51.5 1.1 %collective-permute-start.25 = (bf16[16,512]{1,0:T(8,128)(2,1)S(1)}, bf16[16,512]{1,0:T(8,128)(2,1)S(1)}, u32[]{:S(2)}, u32[]{:S(2)}) collective-permute-start(bf16[16,512]{1,0:T(8,128)(2,1)S(1)} %get-tuple-element.138), channel_id=1, source_target_pairs={{0,4},{1,5},{2,6},{3,7},{4,0},{5,1},{6,2},{7,3},{8,12},{9,13},{10,... | collective-permute-start | bytes 49160 | tf_op jit(solution)/shard_map/ppermute | solution.py:354
  53.9 1.2 %collective-permute-done.24.refs_1_ = bf16[16,512]{1,0:T(8,128)(2,1)S(1)} collective-permute-done((bf16[16,512]{1,0:T(8,128)(2,1)S(1)}, bf16[16,512]{1,0:T(8,128)(2,1)S(1)}, u32[]{:S(2)}, u32[]{:S(2)}) %collective-permute-start.24) | collective-permute-done | bytes 16416 | tf_op jit(solution)/shard_map/ppermute | solution.py:354
  57.8 1.4 %shard_map.155 = (bf16[1024,512]{1,0:T(8,128)(2,1)}, f32[8,128]{1,0:T(8,128)S(1)}) custom-call(f32[1024,512]{1,0:T(8,128)S(1)} %shard_map.151.refs_11_.refs_0_, bf16[128,1024]{1,0:T(8,128)(2,1)S(1)} %get-tuple-element.127.refs_1_, bf16[128,512]{1,0:T(8,128)(2,1)S(1)} %collective-permute-done.19.refs_6_.refs_2_, ...), custom_call_target="tpu_custom_call" | custom-call | flops 134217728 | bytes 3706880 | tf_op jit(solution)/shard_map/pallas_call | solution.py:84
  60.2 2.0 %collective-permute-start.30 = (bf16[64,512]{1,0:T(8,128)(2,1)S(1)}, bf16[64,512]{1,0:T(8,128)(2,1)S(1)}, u32[]{:S(2)}, u32[]{:S(2)}) collective-permute-start(bf16[64,512]{1,0:T(8,128)(2,1)S(1)} %get-tuple-element.154), channel_id=1, source_target_pairs={{0,15},{1,2},{2,1},{3,4},{4,3},{5,6},{6,5},{7,8},{8,7},{9,10},{10,... | collective-permute-start | bytes 196616 | tf_op jit(solution)/shard_map/ppermute | solution.py:360
  62.2 2.5 %shard_map.158 = (f32[1024,512]{1,0:T(8,128)S(1)}, bf16[1024,128]{1,0:T(8,128)(2,1)S(1)}, f32[128,512]{1,0:T(8,128)S(1)}, bf16[512,512]{1,0:T(8,128)(2,1)}) custom-call(bf16[1024,512]{1,0:T(8,128)(2,1)S(1)} %get-tuple-element.141.own_t, bf16[512,512]{1,0:T(8,128)(2,1)S(1)} %get-tuple-element.149.grad, s32[1,2,64]{2,1,0:T(2,128)S(1)} %copy-done.4, ...), custom_call_target="tpu_custom_call" | custom-call | flops 1073741824 | bytes 7340544 | tf_op jit(solution)/shard_map/pallas_call | solution.py:84
  64.7 2.0 %collective-permute-done.30.outer_in = bf16[64,512]{1,0:T(8,128)(2,1)S(1)} collective-permute-done((bf16[64,512]{1,0:T(8,128)(2,1)S(1)}, bf16[64,512]{1,0:T(8,128)(2,1)S(1)}, u32[]{:S(2)}, u32[]{:S(2)}) %collective-permute-start.30) | collective-permute-done | bytes 65568 | tf_op jit(solution)/shard_map/ppermute | solution.py:360
  66.7 1.5 %shard_map.159 = bf16[1024,512]{1,0:T(8,128)(2,1)} custom-call(f32[1024,512]{1,0:T(8,128)S(1)} %get-tuple-element.151.base, bf16[1024,128]{1,0:T(8,128)(2,1)S(1)} %get-tuple-element.152.table, f32[128,512]{1,0:T(8,128)S(1)} %get-tuple-element.153.slope_rows, bf16[512,512]{1,0:T(8,128)(2,1)S(1)} %copy-done.1, ...), custom_call_target="tpu_custom_call" | custom-call | flops 268435456 | bytes 4325376 | tf_op jit(solution)/shard_map/pallas_call | solution.py:84
  (85 shorter events, 23.3 us)
Async XLA Ops:
  3.3 9.0 %collective-permute-start = (bf16[64,512]{1,0:T(8,128)(2,1)S(1)}, bf16[64,512]{1,0:T(8,128)(2,1)S(1)}, u32[]{:S(2)}, u32[]{:S(2)}) collective-permute-start(bf16[64,512]{1,0:T(8,128)(2,1)S(1)} %get-tuple-element.86), channel_id=1, source_target_pairs={{0,15},{1,2},{2,1},{3,4},{4,3},{5,6},{6,5},{7,8},{8,7},{9,10},{10,... | collective-permute-start | bytes 196616 | tf_op jit(solution)/shard_map/ppermute | solution.py:360
  13.2 5.6 %collective-permute-start.2 = (bf16[16,512]{1,0:T(8,128)(2,1)S(1)}, bf16[16,512]{1,0:T(8,128)(2,1)S(1)}, u32[]{:S(2)}, u32[]{:S(2)}) collective-permute-start(bf16[16,512]{1,0:T(8,128)(2,1)S(1)} %get-tuple-element.90), channel_id=1, source_target_pairs={{0,8},{1,9},{2,10},{3,11},{4,12},{5,13},{6,14},{7,15},{8,0},{9,1},... | collective-permute-start | bytes 49160 | tf_op jit(solution)/shard_map/ppermute | solution.py:354
  13.5 5.6 %collective-permute-start.3 = (bf16[16,512]{1,0:T(8,128)(2,1)S(1)}, bf16[16,512]{1,0:T(8,128)(2,1)S(1)}, u32[]{:S(2)}, u32[]{:S(2)}) collective-permute-start(bf16[16,512]{1,0:T(8,128)(2,1)S(1)} %get-tuple-element.91), channel_id=1, source_target_pairs={{0,12},{1,13},{2,14},{3,15},{4,8},{5,9},{6,10},{7,11},{8,4},{9,5},... | collective-permute-start | bytes 49160 | tf_op jit(solution)/shard_map/ppermute | solution.py:354
  14.8 4.2 %collective-permute-start.4 = (bf16[16,512]{1,0:T(8,128)(2,1)S(1)}, bf16[16,512]{1,0:T(8,128)(2,1)S(1)}, u32[]{:S(2)}, u32[]{:S(2)}) collective-permute-start(bf16[16,512]{1,0:T(8,128)(2,1)S(1)} %get-tuple-element.92), channel_id=1, source_target_pairs={{0,4},{1,5},{2,6},{3,7},{4,0},{5,1},{6,2},{7,3},{8,12},{9,13},{10,... | collective-permute-start | bytes 49160 | tf_op jit(solution)/shard_map/ppermute | solution.py:354
  16.8 6.7 %collective-permute-start.5 = (bf16[64,512]{1,0:T(8,128)(2,1)S(1)}, bf16[64,512]{1,0:T(8,128)(2,1)S(1)}, u32[]{:S(2)}, u32[]{:S(2)}) collective-permute-start(bf16[64,512]{1,0:T(8,128)(2,1)S(1)} %get-tuple-element.101), channel_id=1, source_target_pairs={{0,15},{1,2},{2,1},{3,4},{4,3},{5,6},{6,5},{7,8},{8,7},{9,10},{10,... | collective-permute-start | bytes 196616 | tf_op jit(solution)/shard_map/ppermute | solution.py:360
  19.6 3.8 %collective-permute-start.8 = (bf16[16,512]{1,0:T(8,128)(2,1)S(1)}, bf16[16,512]{1,0:T(8,128)(2,1)S(1)}, u32[]{:S(2)}, u32[]{:S(2)}) collective-permute-start(bf16[16,512]{1,0:T(8,128)(2,1)S(1)} %get-tuple-element.104), channel_id=1, source_target_pairs={{0,2},{1,3},{2,0},{3,1},{4,6},{5,7},{6,4},{7,5},{8,10},{9,11},{10,... | collective-permute-start | bytes 49160 | tf_op jit(solution)/shard_map/ppermute | solution.py:354
  24.2 5.3 %collective-permute-start.9 = (bf16[16,512]{1,0:T(8,128)(2,1)S(1)}, bf16[16,512]{1,0:T(8,128)(2,1)S(1)}, u32[]{:S(2)}, u32[]{:S(2)}) collective-permute-start(bf16[16,512]{1,0:T(8,128)(2,1)S(1)} %get-tuple-element.108), channel_id=1, source_target_pairs={{0,8},{1,9},{2,10},{3,11},{4,12},{5,13},{6,14},{7,15},{8,0},{9,1},... | collective-permute-start | bytes 49160 | tf_op jit(solution)/shard_map/ppermute | solution.py:354
  25.9 5.5 %collective-permute-start.10 = (bf16[16,512]{1,0:T(8,128)(2,1)S(1)}, bf16[16,512]{1,0:T(8,128)(2,1)S(1)}, u32[]{:S(2)}, u32[]{:S(2)}) collective-permute-start(bf16[16,512]{1,0:T(8,128)(2,1)S(1)} %get-tuple-element.109), channel_id=1, source_target_pairs={{0,12},{1,13},{2,14},{3,15},{4,8},{5,9},{6,10},{7,11},{8,4},{9,5},... | collective-permute-start | bytes 49160 | tf_op jit(solution)/shard_map/ppermute | solution.py:354
  27.7 3.8 %collective-permute-start.11 = (bf16[16,512]{1,0:T(8,128)(2,1)S(1)}, bf16[16,512]{1,0:T(8,128)(2,1)S(1)}, u32[]{:S(2)}, u32[]{:S(2)}) collective-permute-start(bf16[16,512]{1,0:T(8,128)(2,1)S(1)} %get-tuple-element.110), channel_id=1, source_target_pairs={{0,4},{1,5},{2,6},{3,7},{4,0},{5,1},{6,2},{7,3},{8,12},{9,13},{10,... | collective-permute-start | bytes 49160 | tf_op jit(solution)/shard_map/ppermute | solution.py:354
  27.8 7.8 %collective-permute-start.12 = (bf16[128,512]{1,0:T(8,128)(2,1)S(1)}, bf16[128,512]{1,0:T(8,128)(2,1)S(1)}, u32[]{:S(2)}, u32[]{:S(2)}) collective-permute-start(bf16[128,512]{1,0:T(8,128)(2,1)S(1)} %get-tuple-element.116), channel_id=1, source_target_pairs={{0,15},{1,2},{2,1},{3,4},{4,3},{5,6},{6,5},{7,8},{8,7},{9,10},{10,... | collective-permute-start | bytes 393224 | tf_op jit(solution)/shard_map/ppermute | solution.py:360
  31.8 3.8 %collective-permute-start.15 = (bf16[16,512]{1,0:T(8,128)(2,1)S(1)}, bf16[16,512]{1,0:T(8,128)(2,1)S(1)}, u32[]{:S(2)}, u32[]{:S(2)}) collective-permute-start(bf16[16,512]{1,0:T(8,128)(2,1)S(1)} %get-tuple-element.119), channel_id=1, source_target_pairs={{0,2},{1,3},{2,0},{3,1},{4,6},{5,7},{6,4},{7,5},{8,10},{9,11},{10,... | collective-permute-start | bytes 49160 | tf_op jit(solution)/shard_map/ppermute | solution.py:354
  37.0 4.8 %collective-permute-start.16 = (bf16[16,512]{1,0:T(8,128)(2,1)S(1)}, bf16[16,512]{1,0:T(8,128)(2,1)S(1)}, u32[]{:S(2)}, u32[]{:S(2)}) collective-permute-start(bf16[16,512]{1,0:T(8,128)(2,1)S(1)} %get-tuple-element.123), channel_id=1, source_target_pairs={{0,8},{1,9},{2,10},{3,11},{4,12},{5,13},{6,14},{7,15},{8,0},{9,1},... | collective-permute-start | bytes 49160 | tf_op jit(solution)/shard_map/ppermute | solution.py:354
  38.0 5.6 %collective-permute-start.17 = (bf16[16,512]{1,0:T(8,128)(2,1)S(1)}, bf16[16,512]{1,0:T(8,128)(2,1)S(1)}, u32[]{:S(2)}, u32[]{:S(2)}) collective-permute-start(bf16[16,512]{1,0:T(8,128)(2,1)S(1)} %get-tuple-element.124), channel_id=1, source_target_pairs={{0,12},{1,13},{2,14},{3,15},{4,8},{5,9},{6,10},{7,11},{8,4},{9,5},... | collective-permute-start | bytes 49160 | tf_op jit(solution)/shard_map/ppermute | solution.py:354
  39.7 3.9 %collective-permute-start.18 = (bf16[16,512]{1,0:T(8,128)(2,1)S(1)}, bf16[16,512]{1,0:T(8,128)(2,1)S(1)}, u32[]{:S(2)}, u32[]{:S(2)}) collective-permute-start(bf16[16,512]{1,0:T(8,128)(2,1)S(1)} %get-tuple-element.125), channel_id=1, source_target_pairs={{0,4},{1,5},{2,6},{3,7},{4,0},{5,1},{6,2},{7,3},{8,12},{9,13},{10,... | collective-permute-start | bytes 49160 | tf_op jit(solution)/shard_map/ppermute | solution.py:354
  40.5 7.7 %collective-permute-start.19 = (bf16[128,512]{1,0:T(8,128)(2,1)S(1)}, bf16[128,512]{1,0:T(8,128)(2,1)S(1)}, u32[]{:S(2)}, u32[]{:S(2)}) collective-permute-start(bf16[128,512]{1,0:T(8,128)(2,1)S(1)} %get-tuple-element.128), channel_id=1, source_target_pairs={{0,15},{1,2},{2,1},{3,4},{4,3},{5,6},{6,5},{7,8},{8,7},{9,10},{10,... | collective-permute-start | bytes 393224 | tf_op jit(solution)/shard_map/ppermute | solution.py:360
  43.8 4.2 %collective-permute-start.21 = (bf16[16,512]{1,0:T(8,128)(2,1)S(1)}, bf16[16,512]{1,0:T(8,128)(2,1)S(1)}, u32[]{:S(2)}, u32[]{:S(2)}) collective-permute-start(bf16[16,512]{1,0:T(8,128)(2,1)S(1)} %get-tuple-element.132), channel_id=1, source_target_pairs={{0,3},{1,2},{2,1},{3,0},{4,7},{5,6},{6,5},{7,4},{8,11},{9,10},{10,... | collective-permute-start | bytes 49160 | tf_op jit(solution)/shard_map/ppermute | solution.py:354
  43.9 4.4 %collective-permute-start.22 = (bf16[16,512]{1,0:T(8,128)(2,1)S(1)}, bf16[16,512]{1,0:T(8,128)(2,1)S(1)}, u32[]{:S(2)}, u32[]{:S(2)}) collective-permute-start(bf16[16,512]{1,0:T(8,128)(2,1)S(1)} %get-tuple-element.133), channel_id=1, source_target_pairs={{0,2},{1,3},{2,0},{3,1},{4,6},{5,7},{6,4},{7,5},{8,10},{9,11},{10,... | collective-permute-start | bytes 49160 | tf_op jit(solution)/shard_map/ppermute | solution.py:354
  49.0 4.9 %collective-permute-start.23 = (bf16[16,512]{1,0:T(8,128)(2,1)S(1)}, bf16[16,512]{1,0:T(8,128)(2,1)S(1)}, u32[]{:S(2)}, u32[]{:S(2)}) collective-permute-start(bf16[16,512]{1,0:T(8,128)(2,1)S(1)} %get-tuple-element.136), channel_id=1, source_target_pairs={{0,8},{1,9},{2,10},{3,11},{4,12},{5,13},{6,14},{7,15},{8,0},{9,1},... | collective-permute-start | bytes 49160 | tf_op jit(solution)/shard_map/ppermute | solution.py:354
  49.6 5.5 %collective-permute-start.24 = (bf16[16,512]{1,0:T(8,128)(2,1)S(1)}, bf16[16,512]{1,0:T(8,128)(2,1)S(1)}, u32[]{:S(2)}, u32[]{:S(2)}) collective-permute-start(bf16[16,512]{1,0:T(8,128)(2,1)S(1)} %get-tuple-element.137), channel_id=1, source_target_pairs={{0,12},{1,13},{2,14},{3,15},{4,8},{5,9},{6,10},{7,11},{8,4},{9,5},... | collective-permute-start | bytes 49160 | tf_op jit(solution)/shard_map/ppermute | solution.py:354
  51.5 3.8 %collective-permute-start.25 = (bf16[16,512]{1,0:T(8,128)(2,1)S(1)}, bf16[16,512]{1,0:T(8,128)(2,1)S(1)}, u32[]{:S(2)}, u32[]{:S(2)}) collective-permute-start(bf16[16,512]{1,0:T(8,128)(2,1)S(1)} %get-tuple-element.138), channel_id=1, source_target_pairs={{0,4},{1,5},{2,6},{3,7},{4,0},{5,1},{6,2},{7,3},{8,12},{9,13},{10,... | collective-permute-start | bytes 49160 | tf_op jit(solution)/shard_map/ppermute | solution.py:354
  52.6 6.9 %collective-permute-start.26 = (bf16[64,512]{1,0:T(8,128)(2,1)S(1)}, bf16[64,512]{1,0:T(8,128)(2,1)S(1)}, u32[]{:S(2)}, u32[]{:S(2)}) collective-permute-start(bf16[64,512]{1,0:T(8,128)(2,1)S(1)} %get-tuple-element.144), channel_id=1, source_target_pairs={{0,15},{1,2},{2,1},{3,4},{4,3},{5,6},{6,5},{7,8},{8,7},{9,10},{10,... | collective-permute-start | bytes 196616 | tf_op jit(solution)/shard_map/ppermute | solution.py:360
  55.5 4.0 %collective-permute-start.29 = (bf16[16,512]{1,0:T(8,128)(2,1)S(1)}, bf16[16,512]{1,0:T(8,128)(2,1)S(1)}, u32[]{:S(2)}, u32[]{:S(2)}) collective-permute-start(bf16[16,512]{1,0:T(8,128)(2,1)S(1)} %get-tuple-element.147), channel_id=1, source_target_pairs={{0,2},{1,3},{2,0},{3,1},{4,6},{5,7},{6,4},{7,5},{8,10},{9,11},{10,... | collective-permute-start | bytes 49160 | tf_op jit(solution)/shard_map/ppermute | solution.py:354
  60.2 6.5 %collective-permute-start.30 = (bf16[64,512]{1,0:T(8,128)(2,1)S(1)}, bf16[64,512]{1,0:T(8,128)(2,1)S(1)}, u32[]{:S(2)}, u32[]{:S(2)}) collective-permute-start(bf16[64,512]{1,0:T(8,128)(2,1)S(1)} %get-tuple-element.154), channel_id=1, source_target_pairs={{0,15},{1,2},{2,1},{3,4},{4,3},{5,6},{6,5},{7,8},{8,7},{9,10},{10,... | collective-permute-start | bytes 196616 | tf_op jit(solution)/shard_map/ppermute | solution.py:360
  62.2 4.5 %collective-permute-start.31 = (bf16[64,512]{1,0:T(8,128)(2,1)S(1)}, bf16[64,512]{1,0:T(8,128)(2,1)S(1)}, u32[]{:S(2)}, u32[]{:S(2)}) collective-permute-start(bf16[64,512]{1,0:T(8,128)(2,1)S(1)} %get-tuple-element.155), channel_id=1, source_target_pairs={{0,1},{1,0},{2,3},{3,2},{4,5},{5,4},{6,7},{7,6},{8,9},{9,8},{10,11... | collective-permute-start | bytes 196616 | tf_op jit(solution)/shard_map/ppermute | solution.py:354
  (20 other events, 77.1 us)
